TPU v7x, 32 devices: a whole 2x2x4 slice. The times are simulated.
32 devices in a mesh: dp: 8 (over y, x, core), mp: 4 (over z).
Axes of the slice: x: 2, y: 2, z: 4, core: 2. Of those that a mesh axis runs over, the one named last changes fastest.
Arguments:
- tokens: bfloat16 [96, 160, 768], P('dp', 'mp'), may hold values from -6 to 6
- word_len: int32 [96], P('dp'), may hold values from 1 to 60, as said below
- region_count: int32 [96], P('dp'), may hold values from 10 to 100, as said below
- w_qkv: bfloat16 [3, 768, 768], P(None, None, 'mp'), may hold values from -0.3125 to 0.3125
- qv_bias: bfloat16 [2, 768], P(None, 'mp'), may hold values from -3 to 3
- w_out: bfloat16 [768, 768], P('mp'), may hold values from -0.625 to 0.625
- out_bias: bfloat16 [768], replicated, may hold values from -3 to 3
- norm1_gain: bfloat16 [768], replicated, may hold values from 0.5 to 1.5
- norm1_bias: bfloat16 [768], replicated, may hold values from -3 to 3
- w_in: bfloat16 [768, 3072], P(None, 'mp'), may hold values from -0.21875 to 0.21875
- in_bias: bfloat16 [3072], P('mp'), may hold values from -3 to 3
- w_down: bfloat16 [3072, 768], P('mp'), may hold values from -0.15625 to 0.15625
- down_bias: bfloat16 [768], replicated, may hold values from -3 to 3
- norm2_gain: bfloat16 [768], replicated, may hold values from 0.5 to 1.5
- norm2_bias: bfloat16 [768], replicated, may hold values from -3 to 3
- cotangent: bfloat16 [96, 160, 768], P('dp', 'mp'), may hold values from -6 to 6
Outputs:
- layer_out: bfloat16 [96, 160, 768], P('dp', 'mp')
- grad_input: float32 [96, 160, 768], P('dp', 'mp')
- grad_qkv: float32 [3, 768, 768], P(None, None, 'mp')
- grad_qv_bias: float32 [2, 768], P(None, 'mp')
- grad_out: float32 [768, 768], P('mp')
- grad_out_bias: float32 [768], replicated
- grad_norm1_gain: float32 [768], replicated
- grad_norm1_bias: float32 [768], replicated
- grad_in: float32 [768, 3072], P(None, 'mp')
- grad_in_bias: float32 [3072], P('mp')
- grad_down: float32 [3072, 768], P('mp')
- grad_down_bias: float32 [768], replicated
- grad_norm2_gain: float32 [768], replicated
- grad_norm2_bias: float32 [768], replicated
Inputs may be any that keep to these rules, and one draw needn't show every extreme that they name: `word_len`: words of a pair; in each aligned block of 12 pairs one pair, chosen at random, has 60 words and 100 regions. `region_count`: regions of a pair.
All inputs are finite; a program needn't handle non-finite values.
Results may differ from a plain program's by a relative error of at most 0.014.
The roundings to bfloat16 on the way count: a program that leaves them out, or rounds other values in their place, can miss the bound.
Values may be sent and summed in bfloat16 or wider, within the bound.
No kernel may reach another device: no remote copies, remote signals or barrier semaphores. Data moves between devices by JAX's collectives and lax.ppermute only.
A program may use at most 128 MiB of HBM per device.

v0:
```python
from functools import partial

import jax
import jax.numpy as jnp
from jax import lax
from jax.sharding import PartitionSpec as P

HEAD = 64
WORDS = 60


EPSILON = 1e-05


def normalize(total, gain, shift):
    centered = total - jnp.mean(total, axis=-1, keepdims=True)
    inv_scale = lax.rsqrt(jnp.mean(centered * centered, axis=-1, keepdims=True) + EPSILON)
    normed = centered * inv_scale
    return (normed * gain + shift, normed, inv_scale)


def normalize_back(upstream, normed, inv_scale, gain):
    scaled_up = upstream * gain
    mean_one = jnp.mean(scaled_up, axis=-1, keepdims=True)
    mean_two = jnp.mean(scaled_up * normed, axis=-1, keepdims=True)
    return inv_scale * (scaled_up - mean_one - normed * mean_two)


def shards(
    tokens,
    word_len,
    region_count,
    w_qkv,
    qv_bias,
    w_out,
    out_bias,
    norm1_gain,
    norm1_bias,
    w_in,
    in_bias,
    w_down,
    down_bias,
    norm2_gain,
    norm2_bias,
    cotangent,
):
    pair_count = tokens.shape[0]
    rows_local = tokens.shape[1]
    slot_total = rows_local * lax.axis_size("mp")
    head_local = w_qkv.shape[2] // HEAD
    col_local = w_qkv.shape[2]
    head_scale = HEAD ** (-0.5)
    slot_index = jnp.arange(slot_total, dtype=jnp.int32)
    key_valid = jnp.where(
        slot_index[None, :] < WORDS,
        slot_index[None, :] < word_len[:, None],
        slot_index[None, :] - WORDS < region_count[:, None],
    )
    gain_one = norm1_gain.astype(jnp.float32)
    gain_two = norm2_gain.astype(jnp.float32)
    head_shape = (pair_count, slot_total, head_local, HEAD)
    whole = lax.all_gather(tokens, "mp", axis=1, tiled=True)
    projected = jnp.einsum("psd,jdc->jpsc", whole, w_qkv, preferred_element_type=jnp.float32)
    queries = (projected[0] + qv_bias[0]).astype(jnp.bfloat16).reshape(head_shape)
    key_heads = projected[1].astype(jnp.bfloat16).reshape(head_shape)
    values = (projected[2] + qv_bias[1]).astype(jnp.bfloat16).reshape(head_shape)

    def masked_scores():
        raw_scores = (
            jnp.einsum("pqhd,pkhd->phqk", queries, key_heads, preferred_element_type=jnp.float32)
            * head_scale
        )
        return jnp.where(key_valid[:, None, None, :], raw_scores, -1e30)

    masked = masked_scores()
    row_max = jnp.max(masked, axis=-1, keepdims=True)
    exp_scores = jnp.exp(masked - row_max)
    row_total = jnp.sum(exp_scores, axis=-1, keepdims=True)
    prob_low = (exp_scores / row_total).astype(jnp.bfloat16)
    log_total = row_max + jnp.log(row_total)
    context = jnp.einsum(
        "phqk,pkhd->pqhd", prob_low, values, preferred_element_type=jnp.float32
    ).astype(jnp.bfloat16)
    context = context.reshape(pair_count, slot_total, col_local)
    branch = jnp.einsum("psc,cd->psd", context, w_out, preferred_element_type=jnp.float32)
    first_sum = lax.psum_scatter(branch, "mp", scatter_dimension=1, tiled=True) + out_bias + tokens
    hidden, normed_one, scale_one = normalize(first_sum, gain_one, norm1_bias.astype(jnp.float32))
    hidden_all = lax.all_gather(hidden.astype(jnp.bfloat16), "mp", axis=1, tiled=True)
    pre_act = (
        jnp.einsum("psd,df->psf", hidden_all, w_in, preferred_element_type=jnp.float32) + in_bias
    )
    activation, gelu_back = jax.vjp(partial(jax.nn.gelu, approximate=False), pre_act)
    act_low = activation.astype(jnp.bfloat16)
    ffn_term = jnp.einsum("psf,fd->psd", act_low, w_down, preferred_element_type=jnp.float32)
    second = lax.psum_scatter(ffn_term, "mp", scatter_dimension=1, tiled=True) + down_bias + hidden
    output, normed_two, scale_two = normalize(second, gain_two, norm2_bias.astype(jnp.float32))
    layer_out = output.astype(jnp.bfloat16)
    upstream = cotangent.astype(jnp.float32)
    grad_norm2_gain = jnp.sum(upstream * normed_two, axis=(0, 1))
    grad_norm2_bias = jnp.sum(upstream, axis=(0, 1))
    delta_ffn = normalize_back(upstream, normed_two, scale_two, gain_two)
    grad_down_bias = jnp.sum(delta_ffn, axis=(0, 1))
    ffn_all = lax.all_gather(delta_ffn.astype(jnp.bfloat16), "mp", axis=1, tiled=True)
    grad_down = jnp.einsum("psf,psd->fd", act_low, ffn_all, preferred_element_type=jnp.float32)
    act_grad = jnp.einsum("psd,fd->psf", ffn_all, w_down, preferred_element_type=jnp.float32)
    pre_grad = gelu_back(act_grad)[0].astype(jnp.bfloat16)
    grad_in = jnp.einsum("psd,psf->df", hidden_all, pre_grad, preferred_element_type=jnp.float32)
    grad_in_bias = jnp.sum(pre_grad.astype(jnp.float32), axis=(0, 1))
    back_term = jnp.einsum("psf,df->psd", pre_grad, w_in, preferred_element_type=jnp.float32)
    hidden_grad = lax.psum_scatter(back_term, "mp", scatter_dimension=1, tiled=True) + delta_ffn
    grad_norm1_gain = jnp.sum(hidden_grad * normed_one, axis=(0, 1))
    grad_norm1_bias = jnp.sum(hidden_grad, axis=(0, 1))
    delta_attn = normalize_back(hidden_grad, normed_one, scale_one, gain_one)
    grad_out_bias = jnp.sum(delta_attn, axis=(0, 1))
    attn_all = lax.all_gather(delta_attn.astype(jnp.bfloat16), "mp", axis=1, tiled=True)
    grad_out = jnp.einsum("psc,psd->cd", context, attn_all, preferred_element_type=jnp.float32)
    context_grad = (
        jnp.einsum("psd,cd->psc", attn_all, w_out, preferred_element_type=jnp.float32)
        .astype(jnp.bfloat16)
        .reshape(head_shape)
    )
    weights = jnp.exp(masked_scores() - log_total)
    prob_grad = jnp.einsum(
        "pqhd,pkhd->phqk", context_grad, values, preferred_element_type=jnp.float32
    )
    inner_sum = jnp.sum(prob_grad * weights, axis=-1, keepdims=True)
    score_grad = (weights * (prob_grad - inner_sum)).astype(jnp.bfloat16)
    value_grad = jnp.einsum(
        "phqk,pqhd->pkhd", prob_low, context_grad, preferred_element_type=jnp.float32
    ).astype(jnp.bfloat16)
    query_grad = (
        jnp.einsum("phqk,pkhd->pqhd", score_grad, key_heads, preferred_element_type=jnp.float32)
        * head_scale
    ).astype(jnp.bfloat16)
    key_grad = (
        jnp.einsum("phqk,pqhd->pkhd", score_grad, queries, preferred_element_type=jnp.float32)
        * head_scale
    ).astype(jnp.bfloat16)
    stacked = jnp.stack([query_grad, key_grad, value_grad]).reshape(
        3, pair_count, slot_total, col_local
    )
    grad_qkv = jnp.einsum("psd,jpsc->jdc", whole, stacked, preferred_element_type=jnp.float32)
    grad_qv_bias = jnp.stack(
        [
            jnp.sum(stacked[0].astype(jnp.float32), axis=(0, 1)),
            jnp.sum(stacked[2].astype(jnp.float32), axis=(0, 1)),
        ]
    )
    input_term = jnp.einsum("jpsc,jdc->psd", stacked, w_qkv, preferred_element_type=jnp.float32)
    grad_input = lax.psum_scatter(input_term, "mp", scatter_dimension=1, tiled=True) + delta_attn
    grad_qkv, grad_qv_bias, grad_out, grad_in, grad_in_bias, grad_down = lax.psum(
        (grad_qkv, grad_qv_bias, grad_out, grad_in, grad_in_bias, grad_down), "dp"
    )
    (
        grad_out_bias,
        grad_norm1_gain,
        grad_norm1_bias,
        grad_down_bias,
        grad_norm2_gain,
        grad_norm2_bias,
    ) = lax.psum(
        (
            grad_out_bias,
            grad_norm1_gain,
            grad_norm1_bias,
            grad_down_bias,
            grad_norm2_gain,
            grad_norm2_bias,
        ),
        ("dp", "mp"),
    )
    return (
        layer_out,
        grad_input,
        grad_qkv,
        grad_qv_bias,
        grad_out,
        grad_out_bias,
        grad_norm1_gain,
        grad_norm1_bias,
        grad_in,
        grad_in_bias,
        grad_down,
        grad_down_bias,
        grad_norm2_gain,
        grad_norm2_bias,
    )


def solution(mesh):
    in_specs = (
        P("dp", "mp", None),
        P("dp"),
        P("dp"),
        P(None, None, "mp"),
        P(None, "mp"),
        P("mp", None),
        P(),
        P(),
        P(),
        P(None, "mp"),
        P("mp"),
        P("mp", None),
        P(),
        P(),
        P(),
        P("dp", "mp", None),
    )
    out_specs = (
        P("dp", "mp", None),
        P("dp", "mp", None),
        P(None, None, "mp"),
        P(None, "mp"),
        P("mp", None),
        P(),
        P(),
        P(),
        P(None, "mp"),
        P("mp"),
        P("mp", None),
        P(),
        P(),
        P(),
    )
    return jax.shard_map(shards, mesh=mesh, in_specs=in_specs, out_specs=out_specs, check_vma=False)
```

profile of v0, /device:TPU:0, one launch (start us, length us, event | category | flops | bytes accessed | tf_op | source)
XLA Modules:
  0.0 916.2 jit_solution(11628647580971805979)
XLA Ops:
  9.7 62.9 %all-gather.5.cloned.1.call-done = bf16[12,160,768]{2,1,0:T(8,128)(2,1)} async-done(((bf16[12,40,768]{2,1,0:T(8,128)(2,1)}), bf16[12,160,768]{2,1,0:T(8,128)(2,1)}) %all-gather.5.cloned.1.call-update) | async-done | bytes 2949136 | tf_op jit(solution)/shard_map/all_gather | solution.py:62
  72.6 4.6 fusion.14
  78.2 1.5 fusion.53
  79.8 2.4 copy.48
  82.2 2.1 copy.46
  84.2 2.1 copy.47
  86.4 3.2 fusion.7
  89.6 1.7 fusion.6
  92.2 1.6 divide_convert_fusion
  96.5 3.6 fusion.40
  100.9 102.6 %reduce-scatter.5.cloned.1.call-done = f32[12,40,768]{2,1,0:T(8,128)} async-done(((f32[12,160,768]{2,1,0:T(8,128)}), f32[12,40,768]{2,1,0:T(8,128)}) %reduce-scatter.5.cloned.1.call-update) | async-done | bytes 1474576 | tf_op jit(solution)/shard_map/reduce_scatter | solution.py:86
  203.4 1.6 fusion.52
  206.8 60.6 %all-gather.7.cloned.1.call-done = bf16[12,160,768]{2,1,0:T(8,128)(2,1)} async-done(((bf16[12,40,768]{2,1,0:T(8,128)(2,1)}), bf16[12,160,768]{2,1,0:T(8,128)(2,1)}) %all-gather.7.cloned.1.call-update) | async-done | bytes 2949136 | tf_op jit(solution)/shard_map/all_gather | solution.py:88
  267.5 5.8 fusion.13
  273.3 14.3 %multiply_convert_fusion.1 = (bf16[12,160,768]{2,1,0:T(8,128)(2,1)S(1)}, f32[12,160,768]{2,1,0:T(8,128)}) fusion(f32[12,160,768]{2,1,0:T(8,128)S(1)} %get-tuple-element.58, f32[768]{0:T(1024)S(1)} %convert_element_type.139, u16[160,768]{1,0:T(8,128)(2,1)S(1)} %get-tuple-element.15, u16[160,768]{1,0:T(8,128)(2,1)S(1)} %get-tuple-element.14), kind=kLoop, calls=%fused_computation.12 | loop fusion | flops 104693760 | bytes 15240192 | tf_op jit(solution)/shard_map/convert_element_type | solution.py:93
  287.6 1.6 copy-done.17
  289.2 5.1 fusion.29
  295.0 102.6 %reduce-scatter.7.cloned.1.call-done = f32[12,40,768]{2,1,0:T(8,128)} async-done(((f32[12,160,768]{2,1,0:T(8,128)}), f32[12,40,768]{2,1,0:T(8,128)}) %reduce-scatter.7.cloned.1.call-update) | async-done | bytes 1474576 | tf_op jit(solution)/shard_map/reduce_scatter | solution.py:95
  397.6 1.9 fusion.50
  400.6 1.3 fusion.47
  402.2 60.6 %all-gather.9.cloned.1.call-done = bf16[12,160,768]{2,1,0:T(8,128)(2,1)} async-done(((bf16[12,40,768]{2,1,0:T(8,128)(2,1)}), bf16[12,160,768]{2,1,0:T(8,128)(2,1)}) %all-gather.9.cloned.1.call-update) | async-done | bytes 2949136 | tf_op jit(solution)/shard_map/all_gather | solution.py:103
  462.9 10.5 %convert_reduce_fusion = (f32[768]{0:T(1024)}, bf16[12,160,768]{2,1,0:T(8,128)(2,1)S(1)}) fusion(f32[12,160,768]{2,1,0:T(8,128)} %get-tuple-element.45, bf16[12,160,768]{2,1,0:T(8,128)(2,1)} %all-gather.9.cloned.1.call-done, bf16[768,768]{1,0:T(8,128)(2,1)} %param.27, f32[12,160,768]{2,1,0:T(8,128)} %copy-done.13, f32[768]{0:T(1024)S(1)} %convert_element_type.139), kind=kOutput, calls=%fused_computation.7 | convolution fusion | flops 2289990912 | bytes 18880512 | tf_op jit(solution)/shard_map/psd,fd->psf/dot_general | solution.py:105
  473.4 1.6 copy-done.48
  475.0 5.1 fusion.31
  480.8 102.6 %reduce-scatter.9.cloned.1.call-done = f32[12,40,768]{2,1,0:T(8,128)} async-done(((f32[12,160,768]{2,1,0:T(8,128)}), f32[12,40,768]{2,1,0:T(8,128)}) %reduce-scatter.9.cloned.1.call-update) | async-done | bytes 1474576 | tf_op jit(solution)/shard_map/reduce_scatter | solution.py:110
  583.4 4.3 fusion.26
  591.3 60.5 %all-gather.11.cloned.1.call-done = bf16[12,160,768]{2,1,0:T(8,128)(2,1)} async-done(((bf16[12,40,768]{2,1,0:T(8,128)(2,1)}), bf16[12,160,768]{2,1,0:T(8,128)(2,1)}) %all-gather.11.cloned.1.call-update) | async-done | bytes 2949136 | tf_op jit(solution)/shard_map/all_gather | solution.py:115
  651.8 2.8 convolution_convert_fusion.2
  655.3 3.7 convert_reduce_fusion.1
  659.0 4.7 multiply_reduce_fusion
  663.8 2.0 multiply_convert_fusion
  665.8 1.2 multiply_convert_fusion.2
  667.1 1.6 convert_reduce_fusion.2
  668.7 1.4 copy.57
  670.2 1.4 copy.55
  672.3 7.1 convolution_bitcast_fusion
  679.7 6.9 convolution_bitcast_fusion.1
  686.7 4.2 convolution_bitcast_fusion.2
  690.9 1.7 convolution_bitcast_fusion.3
  693.5 3.5 fusion.20
  697.7 46.3 %all-reduce = (f32[768]{0:T(1024)}, f32[768]{0:T(1024)}, f32[768]{0:T(1024)}, f32[768]{0:T(1024)}, f32[768]{0:T(1024)}, /*index=5*/f32[768]{0:T(1024)}) all-reduce(f32[768]{0:T(1024)S(1)} %copy-done.34, f32[768]{0:T(1024)S(1)} %copy-done.33, f32[768]{0:T(1024)S(1)} %copy-done.32, ...), channel_id=1, replica_groups=mesh['dp'=8,'mp'=4] {'dp','mp'}, use_global_device_ids=true, to_apply=%region_21.22 | all-reduce | flops 4608 | bytes 36864 | tf_op jit(solution)/shard_map/psum | solution.py:161
  744.2 14.6 %all-reduce.1 = (f32[2,192]{1,0:T(2,128)}, f32[768]{0:T(1024)}) all-reduce(f32[2,192]{1,0:T(2,128)S(1)} %pad_maximum_fusion.3, f32[768]{0:T(1024)S(1)} %copy-done.36), channel_id=1, replica_groups=mesh['dp'=8,'mp'=4] {'dp'}, use_global_device_ids=true, to_apply=%region_18.19 | all-reduce | flops 1152 | bytes 9216 | tf_op jit(solution)/shard_map/psum | solution.py:151
  758.9 24.8 %reduce-scatter.11.cloned.1.call-done = f32[12,40,768]{2,1,0:T(8,128)} async-done(((f32[12,160,768]{2,1,0:T(8,128)}), f32[12,40,768]{2,1,0:T(8,128)}) %reduce-scatter.11.cloned.1.call-update) | async-done | bytes 1474576 | tf_op jit(solution)/shard_map/reduce_scatter | solution.py:150
  783.7 2.7 add.152
  786.3 116.2 %all-reduce.5.cloned.1.call-done = (f32[3,768,192]{1,2,0:T(8,128)}, f32[192,768]{1,0:T(8,128)}, f32[768,768]{1,0:T(8,128)}, f32[768,768]{1,0:T(8,128)}) async-done(((f32[3,768,192]{1,2,0:T(8,128)}, f32[192,768]{1,0:T(8,128)}, f32[768,768]{1,0:T(8,128)}, f32[768,768]{1,0:T(8,128)}), (f32[3,768,192]{1,2,0:T(8,128)}, f32[192,768]{1,0:T(8,128)}, f32[768,768]{1,0:T(8,128)}, ...) | async-done | bytes 7077904 | tf_op jit(solution)/shard_map/psum | solution.py:151
  902.5 2.9 copy.74
  906.3 1.4 copy.76
  907.7 1.4 copy.77
  (156 shorter events, 20.1 us)
Async XLA Ops:
  7.2 260.3 %copy-start = (bf16[768,768]{1,0:T(8,128)(2,1)S(1)}, bf16[768,768]{1,0:T(8,128)(2,1)}, u32[]{:S(2)}) copy-start(bf16[768,768]{1,0:T(8,128)(2,1)} %param.25) | copy-start | bytes 3538948
  7.2 65.4 %all-gather.5.cloned.1.call-start = ((), (), s32[]{:S(2)}) async-start(), calls=%async_computation.4 | async-start | bytes 3686400 | tf_op jit(solution)/shard_map/all_gather | solution.py:62
  7.9 195.5 %reduce-scatter.5.cloned.1.call-start = ((), (), s32[]{:S(2)}) async-start(), calls=%async_computation.5 | async-start | bytes 7372800 | tf_op jit(solution)/shard_map/reduce_scatter | solution.py:86
  86.4 3.2 copy-start.5
  89.6 2.5 copy-start.2
  89.6 2.6 copy-start.25
  92.2 1.7 copy-start.7
  93.8 1.6 copy-start.4
  93.8 2.6 copy-start.28
  100.1 103.3 %copy-start.18 = (bf16[12,40,768]{2,1,0:T(8,128)(2,1)S(1)}, bf16[12,40,768]{2,1,0:T(8,128)(2,1)}, u32[]{:S(2)}) copy-start(bf16[12,40,768]{2,1,0:T(8,128)(2,1)} %param.16) | copy-start | bytes 2211844
  100.2 167.3 %all-gather.7.cloned.1.call-start = ((), (), s32[]{:S(2)}) async-start(), calls=%async_computation.6 | async-start | bytes 3686400 | tf_op jit(solution)/shard_map/all_gather | solution.py:88
  205.1 1.7 copy-start.40
  206.6 191.0 %reduce-scatter.7.cloned.1.call-start = ((), (), s32[]{:S(2)}) async-start(), calls=%async_computation.7 | async-start | bytes 7372800 | tf_op jit(solution)/shard_map/reduce_scatter | solution.py:95
  273.3 14.4 %copy-start.13 = (f32[12,160,768]{2,1,0:T(8,128)}, f32[12,160,768]{2,1,0:T(8,128)S(1)}, u32[]{:S(2)}) copy-start(f32[12,160,768]{2,1,0:T(8,128)S(1)} %get-tuple-element.58) | copy-start | bytes 17694724
  273.3 15.9 %copy-start.47 = (bf16[768,768]{1,0:T(8,128)(2,1)S(1)}, bf16[768,768]{1,0:T(8,128)(2,1)}, u32[]{:S(2)}) copy-start(bf16[768,768]{1,0:T(8,128)(2,1)} %param.27) | copy-start | bytes 3538948
  287.6 1.6 copy-start.17
  294.3 168.5 %all-gather.9.cloned.1.call-start = ((), (), s32[]{:S(2)}) async-start(), calls=%async_computation.8 | async-start | bytes 3686400 | tf_op jit(solution)/shard_map/all_gather | solution.py:103
  295.0 104.8 %copy-start.12 = (bf16[12,40,768]{2,1,0:T(8,128)(2,1)S(1)}, bf16[12,40,768]{2,1,0:T(8,128)(2,1)}, u32[]{:S(2)}) copy-start(bf16[12,40,768]{2,1,0:T(8,128)(2,1)} %param.31) | copy-start | bytes 2211844
  399.5 1.1 copy-start.3
  402.0 181.5 %reduce-scatter.9.cloned.1.call-start = ((), (), s32[]{:S(2)}) async-start(), calls=%async_computation.9 | async-start | bytes 7372800 | tf_op jit(solution)/shard_map/reduce_scatter | solution.py:110
  473.4 1.6 copy-start.48
  480.2 171.6 %all-gather.11.cloned.1.call-start = ((), (), s32[]{:S(2)}) async-start(), calls=%async_computation.10 | async-start | bytes 3686400 | tf_op jit(solution)/shard_map/all_gather | solution.py:115
  587.8 3.5 copy-start.26
  587.8 64.1 %copy-start.29 = (bf16[192,768]{1,0:T(8,128)(2,1)S(1)}, bf16[192,768]{1,0:T(8,128)(2,1)}, u32[]{:S(2)}) copy-start(bf16[192,768]{1,0:T(8,128)(2,1)} %param.21) | copy-start | bytes 884740
  591.0 192.7 %reduce-scatter.11.cloned.1.call-start = ((), (), s32[]{:S(2)}) async-start(), calls=%async_computation.11 | async-start | bytes 7372800 | tf_op jit(solution)/shard_map/reduce_scatter | solution.py:150
  655.3 3.7 copy-start.8
  655.3 8.5 slice-start
  659.0 4.8 slice-start.1
  663.8 2.0 copy-start.6
  665.8 1.3 copy-start.11
  668.7 1.4 copy-start.16
  670.1 2.1 copy-start.21
  672.3 7.1 copy-start.23
  679.4 223.2 %all-reduce.5.cloned.1.call-start = ((), (), s32[]{:S(2)}) async-start(), calls=%async_computation.12 | async-start | bytes 14155776 | tf_op jit(solution)/shard_map/psum | solution.py:151
  679.7 7.0 copy-start.45
  679.7 7.0 copy-start.49
  686.7 4.2 copy-start.15
  686.7 4.2 copy-start.46
  690.8 1.7 copy-start.22
  690.9 1.7 copy-start.24
  690.9 2.6 copy-start.44
  697.0 47.1 %copy-start.35 = (f32[3,64]{1,0:T(4,128)S(1)}, f32[3,64]{1,0:T(4,128)}, u32[]{:S(2)}) copy-start(f32[3,64]{1,0:T(4,128)} %get-tuple-element.61) | copy-start | bytes 2308
  697.0 47.2 %copy-start.36 = (f32[768]{0:T(1024)S(1)}, f32[768]{0:T(1024)}, u32[]{:S(2)}) copy-start(f32[768]{0:T(1024)} %get-tuple-element.65) | copy-start | bytes 9220
  697.0 86.7 %copy-start.10 = (f32[12,40,768]{2,1,0:T(8,128)S(1)}, f32[12,40,768]{2,1,0:T(8,128)}, u32[]{:S(2)}) copy-start(f32[12,40,768]{2,1,0:T(8,128)} %copy-done.9) | copy-start | bytes 4423684
  902.5 3.0 copy-start.27
  902.5 3.8 copy-start.20
  905.5 2.2 copy-start.19
  906.3 2.8 copy-start.1
  (13 other events, 9.9 us)
Sparse Core Ops, SparseCore 0:
  9.6 62.9 all-gather.4
  100.3 103.0 reduce-scatter.4
  206.7 60.7 all-gather.6
  294.5 103.0 reduce-scatter.6
  402.1 60.7 all-gather.8
  480.3 103.0 reduce-scatter.8
  591.1 60.7 all-gather.10
  679.5 104.1 reduce-scatter.10
  788.5 113.9 all-reduce.4
where the time goes:
time: 923 us; the launch traced here: 916 us
  waiting for transfers between devices  694 us (75%)
  matrix products  76.1 us (8%)
  blocking collectives  61 us (7%)
  other arithmetic  37.5 us (4%)
  local copies, waits for them, and re-layouts  31.2 us (3%)
  between operations  14.8 us (2%)
    psum x1, waiting for transfers between devices, shards(): lax.psum((grad_qkv, grad_qv_bias, grad_out, grad_in, grad_in_bias, grad_d...  116 us
    reduce_scatter x1, waiting for transfers between devices, shards(): lax.psum_scatter(back_term, 'mp', scatter_dimension=1, tiled=True)  103 us
    reduce_scatter x1, waiting for transfers between devices, shards(): lax.psum_scatter(ffn_term, 'mp', scatter_dimension=1, tiled=True)  103 us
    reduce_scatter x1, waiting for transfers between devices, shards(): lax.psum_scatter(branch, 'mp', scatter_dimension=1, tiled=True) + out_bias  103 us
    all_gather x1, waiting for transfers between devices, shards(): whole = lax.all_gather(tokens, 'mp', axis=1, tiled=True)  62.9 us
    all_gather x1, waiting for transfers between devices, shards(): lax.all_gather(hidden.astype(jnp.bfloat16), 'mp', axis=1, tiled=True)  60.6 us
    all_gather x1, waiting for transfers between devices, shards(): lax.all_gather(delta_ffn.astype(jnp.bfloat16), 'mp', axis=1, tiled=True)  60.6 us
    all_gather x1, waiting for transfers between devices, shards(): lax.all_gather(delta_attn.astype(jnp.bfloat16), 'mp', axis=1, tiled=True)  60.5 us
  transfers between devices with their start and end apart: 9, of which 9 were waited for; matrix products, arithmetic and copies ran while one was open for 2% of the time, Pallas kernels for 0%

commit v1 on v0

v1 whole, which is shorter than its diff:
```python
from functools import partial

import jax
import jax.numpy as jnp
from jax import lax
from jax.sharding import PartitionSpec as P

HEAD = 64
WORDS = 60
EPSILON = 1e-05
F32 = jnp.float32
BF16 = jnp.bfloat16


def normalize(total, gain, shift):
    centered = total - jnp.mean(total, axis=-1, keepdims=True)
    inv_scale = lax.rsqrt(jnp.mean(centered * centered, axis=-1, keepdims=True) + EPSILON)
    normed = centered * inv_scale
    return (normed * gain + shift, normed, inv_scale)


def normalize_back(upstream, normed, inv_scale, gain):
    scaled_up = upstream * gain
    mean_one = jnp.mean(scaled_up, axis=-1, keepdims=True)
    mean_two = jnp.mean(scaled_up * normed, axis=-1, keepdims=True)
    return inv_scale * (scaled_up - mean_one - normed * mean_two)


def flip(array, axis, bit):
    size = lax.axis_size(axis)
    return lax.ppermute(array, axis, [(i, i ^ bit) for i in range(size)])


def tie(*arrays):
    return lax.optimization_barrier(arrays)


def dp_bits():
    size = lax.axis_size("dp")
    bits = size.bit_length() - 1
    return bits


def pick(array, axis, index):
    return lax.dynamic_index_in_dim(array, index, axis, keepdims=False)


def gather_steps(halves):
    bits = dp_bits()
    me = lax.axis_index("dp")
    outer = list(range(1, bits))
    orders = [outer, outer[::-1]]
    held = [h.reshape((1,) * bits + h.shape) for h in halves]
    for step in range(len(outer)):
        held = list(tie(*held))
        got = [flip(h, "dp", 1 << order[step]) for h, order in zip(held, orders)]
        got = list(tie(*got))
        for side, order in enumerate(orders):
            bit = order[step]
            axis = bits - 1 - bit
            mine = ((me >> bit) & 1) == 0
            held[side] = jnp.concatenate(
                [jnp.where(mine, held[side], got[side]), jnp.where(mine, got[side], held[side])],
                axis=axis,
            )
    both = jnp.concatenate(held, axis=bits + 1)
    other = flip(both, "dp", 1)
    mine = (me & 1) == 0
    full = jnp.concatenate(
        [jnp.where(mine, both, other), jnp.where(mine, other, both)], axis=bits - 1
    )
    return full.reshape((lax.axis_size("dp"),) + full.shape[bits:])


def gather_dp(pieces):
    n, rows, cols = pieces.shape
    half = rows // 2
    full = gather_steps([pieces[:, :half], pieces[:, half:]])
    return full.transpose(1, 0, 2, 3).reshape(n, -1, cols)


def add_low(one, two):
    return (one.astype(F32) + two.astype(F32)).astype(BF16)


def reduce_dp(packs):
    bits = dp_bits()
    me = lax.axis_index("dp")
    shards_, rows, cols = packs.shape
    part = rows // lax.axis_size("dp")
    array = packs.reshape((shards_,) + (2,) * bits + (part, cols))
    low = me & 1
    other = flip(pick(array, bits, 1 - low), "dp", 1)
    array = add_low(pick(array, bits, low), other)
    half = shards_ // 2
    held = [array[:half], array[half:]]
    outer = list(range(1, bits))
    orders = [outer, outer[::-1]]
    left = [list(reversed(outer)) for _ in orders]
    for step in range(len(outer)):
        sends = []
        for side, order in enumerate(orders):
            bit = order[step]
            axis = 1 + left[side].index(bit)
            sends.append(pick(held[side], axis, 1 - ((me >> bit) & 1)))
        sends = tie(*sends)
        got = [flip(s, "dp", 1 << order[step]) for s, order in zip(sends, orders)]
        got = tie(*got)
        for side, order in enumerate(orders):
            bit = order[step]
            axis = 1 + left[side].index(bit)
            held[side] = add_low(pick(held[side], axis, (me >> bit) & 1), got[side])
            left[side].remove(bit)
    return jnp.concatenate(held, axis=0)


def reduce_mp(parts):
    sends = tie(*[parts[k] for k in range(1, parts.shape[0])])
    got = [flip(s, "mp", k + 1) for k, s in enumerate(sends)]
    got = tie(*got)
    total = parts[0].astype(F32)
    for g in got:
        total = total + g.astype(F32)
    return total.astype(BF16)


def exchange_rows(array):
    size = lax.axis_size("mp")
    me = lax.axis_index("mp")
    blocks = array.reshape((size, array.shape[0] // size) + array.shape[1:])
    sends = tie(*[pick(blocks, 0, me ^ k) for k in range(size)])
    got = [sends[0]] + [flip(sends[k], "mp", k) for k in range(1, size)]
    return jnp.concatenate(got, axis=1)


def return_rows(array):
    size = lax.axis_size("mp")
    me = lax.axis_index("mp")
    pairs, slots, cols = array.shape
    rows = slots // size
    sends = [array[:, k * rows : (k + 1) * rows] for k in range(size)]
    sends = tie(*sends)
    got = jnp.stack([sends[0]] + [flip(sends[k], "mp", k) for k in range(1, size)])
    got = jnp.take(got, jnp.arange(size) ^ me, axis=0)
    return got.reshape(size * pairs, rows, cols)


def shards(
    tokens,
    word_len,
    region_count,
    w_qkv,
    qv_bias,
    w_out,
    out_bias,
    norm1_gain,
    norm1_bias,
    w_in,
    in_bias,
    w_down,
    down_bias,
    norm2_gain,
    norm2_bias,
    cotangent,
):
    mp = lax.axis_size("mp")
    dp = lax.axis_size("dp")
    mi = lax.axis_index("mp")
    di = lax.axis_index("dp")
    width = tokens.shape[2]
    rows_local = tokens.shape[1]
    slot_total = rows_local * mp
    pair_count = tokens.shape[0] // mp
    cols = w_qkv.shape[2]
    units = w_in.shape[1]
    heads = cols // HEAD
    head_scale = HEAD ** (-0.5)
    order = jnp.arange(mp) ^ mi

    att_own = jnp.concatenate([w_qkv.transpose(0, 2, 1).reshape(3 * cols, width), w_out], axis=0)
    att_rows = att_own.shape[0]
    att_part = att_rows // dp
    in_own = w_in.T
    in_part = units // dp
    piece = lax.dynamic_slice_in_dim(att_own, di * att_part, att_part, 0)
    in_piece = lax.dynamic_slice_in_dim(in_own, di * in_part, in_part, 0)
    down_piece = lax.dynamic_slice_in_dim(w_down, di * in_part, in_part, 0)

    small = jnp.concatenate([qv_bias.reshape(-1), in_bias])
    small_rows = -(-small.shape[0] // width)
    pad_rows = -(-small_rows // 8) * 8
    small = jnp.pad(small, (0, pad_rows * width - small.shape[0])).reshape(pad_rows, width)
    payload = jnp.concatenate([piece, small], axis=0)

    x = exchange_rows(tokens)
    payload, x = tie(payload, x)
    got = tie(*[flip(payload, "mp", k) for k in range(1, mp)])
    w_in_all = lax.all_gather(in_piece, ("mp", "dp"), axis=0, tiled=True)
    w_down_all = lax.all_gather(down_piece, ("mp", "dp"), axis=0, tiled=True)
    smalls = jnp.stack([small] + [g[att_part:] for g in got]).reshape(mp, -1)
    qv_all = smalls[:, : 2 * cols].reshape(mp, 2, cols)
    in_bias_all = jnp.take(smalls[:, 2 * cols : 2 * cols + units], order, axis=0).reshape(-1)
    others = gather_dp(jnp.stack([g[:att_part] for g in got]))
    att_all = jnp.concatenate([att_own[None], others], axis=0)
    qkv_all = att_all[:, : 3 * cols].reshape(mp, 3, cols, width)
    out_all = att_all[:, 3 * cols :]

    words = lax.dynamic_slice_in_dim(word_len, mi * pair_count, pair_count, 0)
    regions = lax.dynamic_slice_in_dim(region_count, mi * pair_count, pair_count, 0)
    slot_index = (order[:, None] * rows_local + jnp.arange(rows_local)[None, :]).reshape(-1)
    key_valid = jnp.where(
        slot_index[None, :] < WORDS,
        slot_index[None, :] < words[:, None],
        slot_index[None, :] - WORDS < regions[:, None],
    )
    gain_one = norm1_gain.astype(F32)
    gain_two = norm2_gain.astype(F32)
    head_shape = (mp, pair_count, slot_total, heads, HEAD)
    projected = jnp.einsum("psd,kjcd->jkpsc", x, qkv_all, preferred_element_type=F32)
    queries = (projected[0] + qv_all[:, 0][:, None, None]).astype(BF16).reshape(head_shape)
    key_heads = projected[1].astype(BF16).reshape(head_shape)
    values = (projected[2] + qv_all[:, 1][:, None, None]).astype(BF16).reshape(head_shape)

    def masked_scores():
        raw_scores = (
            jnp.einsum("kpqhd,kpthd->kphqt", queries, key_heads, preferred_element_type=F32)
            * head_scale
        )
        return jnp.where(key_valid[None, :, None, None, :], raw_scores, -1e30)

    masked = masked_scores()
    row_max = jnp.max(masked, axis=-1, keepdims=True)
    exp_scores = jnp.exp(masked - row_max)
    weights = exp_scores / jnp.sum(exp_scores, axis=-1, keepdims=True)
    prob_low = weights.astype(BF16)
    context = jnp.einsum("kphqt,kpthd->kpqhd", prob_low, values, preferred_element_type=F32)
    context = context.astype(BF16).reshape(mp, pair_count, slot_total, cols)
    branch = jnp.einsum("kpsc,kcd->psd", context, out_all, preferred_element_type=F32)
    first_sum = branch + out_bias + x
    hidden, normed_one, scale_one = normalize(first_sum, gain_one, norm1_bias.astype(F32))
    hidden_low = hidden.astype(BF16)

    cot = exchange_rows(tie(cotangent, hidden_low)[0])

    pre_act = jnp.einsum("psd,fd->psf", hidden_low, w_in_all, preferred_element_type=F32)
    pre_act = pre_act + in_bias_all
    activation, gelu_back = jax.vjp(partial(jax.nn.gelu, approximate=False), pre_act)
    act_low = activation.astype(BF16)
    ffn_term = jnp.einsum("psf,fd->psd", act_low, w_down_all, preferred_element_type=F32)
    second = ffn_term + down_bias + hidden
    output, normed_two, scale_two = normalize(second, gain_two, norm2_bias.astype(F32))
    upstream = cot.astype(F32)
    grad_norm2_gain = jnp.sum(upstream * normed_two, axis=(0, 1))
    grad_norm2_bias = jnp.sum(upstream, axis=(0, 1))
    delta_ffn = normalize_back(upstream, normed_two, scale_two, gain_two)
    grad_down_bias = jnp.sum(delta_ffn, axis=(0, 1))
    ffn_low = delta_ffn.astype(BF16)

    grad_down = jnp.einsum("psf,psd->fd", act_low, ffn_low, preferred_element_type=F32)
    act_grad = jnp.einsum("psd,fd->psf", ffn_low, w_down_all, preferred_element_type=F32)
    pre_grad = gelu_back(act_grad)[0].astype(BF16)
    grad_in = jnp.einsum("psf,psd->fd", pre_grad, hidden_low, preferred_element_type=F32)
    grad_in_bias = jnp.sum(pre_grad.astype(F32), axis=(0, 1))
    ffn_pack = jnp.stack(
        [grad_in.astype(BF16).reshape(mp, units, width), grad_down.astype(BF16).reshape(mp, units, width)],
        axis=1,
    )
    ffn_pack = jnp.take(ffn_pack, order, axis=0).reshape(2 * mp, units, width)
    ffn_part = reduce_dp(ffn_pack)
    ffn_part = reduce_mp(ffn_part.reshape(mp, 2 * in_part, width))
    ffn_grads = gather_dp(ffn_part.reshape(2, in_part, width))

    back_term = jnp.einsum("psf,fd->psd", pre_grad, w_in_all, preferred_element_type=F32)
    hidden_grad = back_term + delta_ffn
    grad_norm1_gain = jnp.sum(hidden_grad * normed_one, axis=(0, 1))
    grad_norm1_bias = jnp.sum(hidden_grad, axis=(0, 1))
    delta_attn = normalize_back(hidden_grad, normed_one, scale_one, gain_one)
    grad_out_bias = jnp.sum(delta_attn, axis=(0, 1))
    attn_low = delta_attn.astype(BF16)
    grad_out = jnp.einsum("kpsc,psd->kcd", context, attn_low, preferred_element_type=F32)
    context_grad = jnp.einsum("psd,kcd->kpsc", attn_low, out_all, preferred_element_type=F32)
    context_grad = context_grad.astype(BF16).reshape(head_shape)
    prob_grad = jnp.einsum("kpqhd,kpthd->kphqt", context_grad, values, preferred_element_type=F32)
    inner_sum = jnp.sum(prob_grad * weights, axis=-1, keepdims=True)
    score_grad = (weights * (prob_grad - inner_sum)).astype(BF16)
    value_grad = jnp.einsum(
        "kphqt,kpqhd->kpthd", prob_low, context_grad, preferred_element_type=F32
    ).astype(BF16)
    query_grad = (
        jnp.einsum("kphqt,kpthd->kpqhd", score_grad, key_heads, preferred_element_type=F32)
        * head_scale
    ).astype(BF16)
    key_grad = (
        jnp.einsum("kphqt,kpqhd->kpthd", score_grad, queries, preferred_element_type=F32)
        * head_scale
    ).astype(BF16)
    stacked = jnp.stack([query_grad, key_grad, value_grad], axis=1).reshape(
        mp, 3, pair_count, slot_total, cols
    )
    grad_qkv = jnp.einsum("kjpsc,psd->kjcd", stacked, x, preferred_element_type=F32)
    att_pack = jnp.concatenate(
        [grad_qkv.astype(BF16).reshape(mp, 3 * cols, width), grad_out.astype(BF16)], axis=1
    )
    att_part_sum = reduce_mp(reduce_dp(att_pack))
    att_grads = gather_dp(att_part_sum[None])[0]
    sums_qv = jnp.stack(
        [
            jnp.sum(query_grad.astype(F32), axis=(1, 2)).reshape(mp, cols),
            jnp.sum(value_grad.astype(F32), axis=(1, 2)).reshape(mp, cols),
        ],
        axis=1,
    )
    input_term = jnp.einsum("kjpsc,kjcd->psd", stacked, qkv_all, preferred_element_type=F32)
    grad_rows = (input_term + delta_attn).astype(BF16)

    layer_out = return_rows(output.astype(BF16))
    grad_input = return_rows(grad_rows).astype(F32)

    flat = jnp.concatenate(
        [
            grad_out_bias,
            grad_norm1_gain,
            grad_norm1_bias,
            grad_down_bias,
            grad_norm2_gain,
            grad_norm2_bias,
            grad_in_bias,
            jnp.take(sums_qv, order, axis=0).reshape(-1),
        ]
    )
    flat = lax.psum(flat, ("dp", "mp"))
    vectors = flat[: 6 * width].reshape(6, width)
    sum_in_bias = lax.dynamic_slice_in_dim(flat, 6 * width + mi * units, units, 0)
    sum_qv = lax.dynamic_slice_in_dim(
        flat, 6 * width + mp * units + mi * 2 * cols, 2 * cols, 0
    ).reshape(2, cols)

    grad_qkv_own = att_grads[: 3 * cols].reshape(3, cols, width).astype(F32).transpose(0, 2, 1)
    grad_out_own = att_grads[3 * cols :].astype(F32)
    grad_in_own = ffn_grads[0].astype(F32).T
    grad_down_own = ffn_grads[1].astype(F32)
    return (
        layer_out,
        grad_input,
        grad_qkv_own,
        sum_qv,
        grad_out_own,
        vectors[0],
        vectors[1],
        vectors[2],
        grad_in_own,
        sum_in_bias,
        grad_down_own,
        vectors[3],
        vectors[4],
        vectors[5],
    )


def solution(mesh):
    in_specs = (
        P("dp", "mp", None),
        P("dp"),
        P("dp"),
        P(None, None, "mp"),
        P(None, "mp"),
        P("mp", None),
        P(),
        P(),
        P(),
        P(None, "mp"),
        P("mp"),
        P("mp", None),
        P(),
        P(),
        P(),
        P("dp", "mp", None),
    )
    out_specs = (
        P("dp", "mp", None),
        P("dp", "mp", None),
        P(None, None, "mp"),
        P(None, "mp"),
        P("mp", None),
        P(),
        P(),
        P(),
        P(None, "mp"),
        P("mp"),
        P("mp", None),
        P(),
        P(),
        P(),
    )
    return jax.shard_map(shards, mesh=mesh, in_specs=in_specs, out_specs=out_specs, check_vma=False)
```

time: 923 us -> 474 us (0.51)
  waiting for transfers between devices: 694 us -> 130 us
  starting transfers between devices: 1.3 us -> 58.9 us
  other arithmetic: 37.5 us -> 84.4 us
  local copies, waits for them, and re-layouts: 31.2 us -> 71.6 us
  blocking collectives: 61 us -> 39.8 us
  matrix products: 76.1 us -> 65.7 us
    reduce_scatter x4 -> x0, waiting for transfers between devices: 333 us -> none  [the longest x1 103 us: shards(): lax.psum_scatter(back_term, 'mp', scatter_dimension=1, tiled=True)]
    all_gather x4 -> x2, waiting for transfers between devices: 245 us -> 18.7 us  [the longest x1 18.7 us: shards(): w_down_all = lax.all_gather(down_piece, ('mp', 'dp'), axis=0, tiled=True)]
    psum x1 -> x0, waiting for transfers between devices: 116 us -> none  [shards(): lax.psum((grad_qkv, grad_qv_bias, grad_out, grad_in, grad_in_bias, grad_d...]
    ppermute x0 -> x46, waiting for transfers between devices: none -> 111 us  [flip(): return lax.ppermute(array, axis, [(i, i ^ bit) for i in range(size)])]
    ppermute x0 -> x46, starting transfers between devices: none -> 58.8 us  [flip(): return lax.ppermute(array, axis, [(i, i ^ bit) for i in range(size)])]
    psum x2 -> x1, blocking collectives: 61 us -> 39.8 us  [shards(): flat = lax.psum(flat, ('dp', 'mp'))]
    convert_element_type x14 -> x26, other arithmetic: 22.2 us -> 39.9 us  [the longest x1 14.8 us: shards(): act_low = activation.astype(BF16)]
    gather x0 -> x6, local copies, waits for them, and re-layouts: none -> 15.4 us  [the longest x2 11 us: shards(): ffn_pack = jnp.take(ffn_pack, order, axis=0).reshape(2 * mp, units, width)]
  transfers between devices with their start and end apart: 9 -> 48, of which waited for: 9 -> 22; matrix products, arithmetic and copies ran while one was open for 2% -> 30% of each run, Pallas kernels for 0% -> 0%
where the time goes in v1:
time: 474 us; the launch traced here: 466 us
  waiting for transfers between devices  130 us (27%)
  other arithmetic  84.4 us (18%)
  local copies, waits for them, and re-layouts  71.6 us (15%)
  matrix products  65.7 us (14%)
  starting transfers between devices  58.9 us (12%)
  blocking collectives  39.8 us (8%)
  between operations  16.2 us (3%)
    ppermute x46, waiting for transfers between devices, flip(): return lax.ppermute(array, axis, [(i, i ^ bit) for i in range(size)])  111 us
    ppermute x46, starting transfers between devices, flip(): return lax.ppermute(array, axis, [(i, i ^ bit) for i in range(size)])  58.8 us
    psum x1, blocking collectives, shards(): flat = lax.psum(flat, ('dp', 'mp'))  39.8 us
    all_gather x1, waiting for transfers between devices, shards(): w_down_all = lax.all_gather(down_piece, ('mp', 'dp'), axis=0, tiled=True)  18.7 us
    convert_element_type x1, other arithmetic, shards(): act_low = activation.astype(BF16)  14.8 us
    convert_element_type x10, other arithmetic, add_low(): return (one.astype(F32) + two.astype(F32)).astype(BF16)  14.5 us
    unnamed x216, local copies, waits for them, and re-layouts  14.4 us
    squeeze x11, local copies, waits for them, and re-layouts, pick(): return lax.dynamic_index_in_dim(array, index, axis, keepdims=False)  11.6 us
  transfers between devices with their start and end apart: 48, of which 22 were waited for; matrix products, arithmetic and copies ran while one was open for 30% of the time, Pallas kernels for 0%

profile of v1, /device:TPU:0, one launch (start us, length us, event | category | flops | bytes accessed | tf_op | source)
XLA Modules:
  0.0 466.1 jit_solution(420698085004636553)
XLA Ops:
  10.9 5.1 %collective-permute-start.2 = (bf16[3,40,768]{2,1,0:T(8,128)(2,1)S(1)}, bf16[3,40,768]{2,1,0:T(8,128)(2,1)S(1)}, u32[]{:S(2)}, u32[]{:S(2)}) collective-permute-start(bf16[3,40,768]{2,1,0:T(8,128)(2,1)S(1)} %get-tuple-element.92), channel_id=1, source_target_pairs={{0,3},{1,2},{2,1},{3,0},{4,7},{5,6},{6,5},{7,4},{8,11},{9,10},{10,... | collective-permute-start | bytes 552968 | tf_op jit(solution)/shard_map/ppermute | solution.py:31
  18.6 2.9 collective-permute-done.2
  21.6 13.0 %collective-permute-done.1 = bf16[3,40,768]{2,1,0:T(8,128)(2,1)S(1)} collective-permute-done((bf16[3,40,768]{2,1,0:T(8,128)(2,1)S(1)}, bf16[3,40,768]{2,1,0:T(8,128)(2,1)S(1)}, u32[]{:S(2)}, u32[]{:S(2)}) %collective-permute-start.1) | collective-permute-done | bytes 184352 | tf_op jit(solution)/shard_map/ppermute | solution.py:31
  35.5 3.2 collective-permute-start.4
  43.8 9.3 %collective-permute-done.4 = bf16[104,768]{1,0:T(8,128)(2,1)S(1)} collective-permute-done((bf16[104,768]{1,0:T(8,128)(2,1)S(1)}, bf16[104,768]{1,0:T(8,128)(2,1)S(1)}, u32[]{:S(2)}, u32[]{:S(2)}) %collective-permute-start.4) | collective-permute-done | bytes 159776 | tf_op jit(solution)/shard_map/ppermute | solution.py:31
  57.5 3.4 collective-permute-done.6
  60.9 2.3 collective-permute-done.7
  65.5 13.6 %collective-permute-done.8 = bf16[1,2,1,3,48,768]{5,4,3,2,1,0:T(8,128)(2,1)S(1)} collective-permute-done((bf16[1,2,1,3,48,768]{5,4,3,2,1,0:T(8,128)(2,1)S(1)}, bf16[1,2,1,3,48,768]{5,4,3,2,1,0:T(8,128)(2,1)S(1)}, u32[]{:S(2)}, u32[]{:S(2)}) %collective-permute-start.8) | collective-permute-done | bytes 442400 | tf_op jit(solution)/shard_map/ppermute | solution.py:31
  84.7 2.2 broadcast_select_fusion.2
  89.4 2.5 convolution_bitcast_fusion
  102.7 2.5 fusion.103
  111.3 3.3 collective-permute-start.16
  114.6 2.6 collective-permute-start.15
  117.2 6.5 %fusion.42 = (u8[160,3072]{1,0:T(8,128)(4,1)S(1)}, u8[160,3072]{1,0:T(8,128)(4,1)S(1)}, f32[3,160,3072]{2,1,0:T(8,128)S(1)}) fusion(f32[3072]{0:T(1024)} %reshape.434, bf16[3,160,768]{2,1,0:T(8,128)(2,1)} %fusion.51, bf16[3072,768]{1,0:T(8,128)(2,1)} %all-gather.3.cloned.1.call-done), kind=kOutput, calls=%fused_computation.119 | convolution fusion | flops 2284584960 | bytes 12349440 | tf_op jit(solution)/shard_map/psd,fd->psf/dot_general | solution.py:245
  123.7 2.5 copy-done.11
  126.2 14.8 %multiply_convert_fusion.1 = (bf16[3,160,3072]{2,1,0:T(8,128)(2,1)}, f32[3,160,3072]{2,1,0:T(8,128)}) fusion(f32[3,160,3072]{2,1,0:T(8,128)S(1)} %get-tuple-element.278, f32[3072]{0:T(1024)S(1)} %copy-done.51, u8[160,3072]{1,0:T(8,128)(4,1)S(1)} %get-tuple-element.178, u8[160,3072]{1,0:T(8,128)(4,1)S(1)} %get-tuple-element.177), kind=kLoop, calls=%fused_computation.27 | loop fusion | flops 104693760 | bytes 15740928 | tf_op jit(solution)/shard_map/convert_element_type | solution.py:248
  141.0 18.7 %all-gather.5.cloned.1.call-done = bf16[3072,768]{1,0:T(8,128)(2,1)} async-done(((bf16[96,768]{1,0:T(8,128)(2,1)}), bf16[3072,768]{1,0:T(8,128)(2,1)}) %all-gather.5.cloned.1.call-update) | async-done | bytes 4718608 | tf_op jit(solution)/shard_map/all_gather | solution.py:199
  159.8 6.4 %fusion.105 = (f32[3,160]{1,0:T(4,128)S(1)}, f32[3,160,768]{2,1,0:T(8,128)S(1)}) fusion(f32[768]{0:T(1024)} %convert_element_type.341, f32[768]{0:T(1024)S(1)} %convert_element_type.340, f32[3,160]{1,0:T(4,128)} %copy-done.60, f32[3,160,768]{2,1,0:T(8,128)} %copy-done.5, f32[3,160]{1,0:T(4,128)S(1)} %broadcast_multiply_fusion.5, ...), kind=kOutput, calls=%fused_computation.309 | convolution fusion | flops 2267504128 | bytes 10631808 | tf_op jit(solution)/shard_map/psf,fd->psd/dot_general | solution.py:249
  168.5 9.4 %convert_reduce_fusion = (f32[3072]{0:T(1024)}, bf16[3,160,3072]{2,1,0:T(8,128)(2,1)}) fusion(f32[3,160,3072]{2,1,0:T(8,128)S(1)} %bitcast.302, bf16[3072,768]{1,0:T(8,128)(2,1)} %all-gather.5.cloned.1.call-done, f32[3,160]{1,0:T(4,128)S(1)} %broadcast_multiply_fusion.2, f32[3,160,768]{2,1,0:T(8,128)S(1)} %get-tuple-element.280, ...), kind=kOutput, calls=%fused_computation.23 | convolution fusion | flops 2295886848 | bytes 21711360 | tf_op jit(solution)/shard_map/psd,fd->psf/dot_general | solution.py:260
  177.9 7.1 %multiply_reduce_fusion.1 = (f32[768]{0:T(1024)}, f32[3,160]{1,0:T(4,128)S(1)}, f32[3,160]{1,0:T(4,128)S(1)}, f32[768]{0:T(1024)}, f32[3,160,768]{2,1,0:T(8,128)S(1)}) fusion(f32[3,160,768]{2,1,0:T(8,128)S(1)} %copy-done.6, f32[3,160]{1,0:T(4,128)S(1)} %copy-done.61, f32[3,160]{1,0:T(4,128)S(1)} %broadcast_multiply_fusion.5, f32[768]{0:T(1024)S(1)} %copy-done.59, ...), kind=kOutput, calls=%fused_computation.108 | convolution fusion | flops 2274137600 | bytes 12856320 | tf_op jit(solution)/shard_map/psf,fd->psd/dot_general | solution.py:273
  189.1 2.8 copy.63
  192.0 5.9 %convert_reduce_fusion.1 = (f32[4,3,64]{2,1,0:T(4,128)}, bf16[4,3,3,64,160]{4,3,2,1,0:T(8,128)(2,1)}) fusion(bf16[4,3,160,3,64]{2,4,3,1,0:T(8,128)(2,1)} %bitcast.319, f32[4,3,3,160,160]{3,4,2,1,0:T(8,128)} %copy-done.10, f32[4,3,3,160]{3,2,1,0:T(4,128)} %copy-done.49), kind=kOutput, calls=%fused_computation.79 | convolution fusion | flops 120913152 | bytes 5187072 | tf_op jit(solution)/shard_map/kphqt,kpqhd->kpthd/dot_general | solution.py:286
  197.9 4.4 multiply_reduce_fusion
  210.0 4.4 bitcast_convert_fusion.1
  214.3 2.5 copy.69
  219.1 4.1 fusion.52
  227.9 4.4 bitcast_convert_fusion
  232.3 3.8 fusion.8
  236.1 5.5 %gather_fusion.3 = bf16[4,2,384,768]{3,2,1,0:T(8,128)(2,1)} fusion(bf16[4,2,384,768]{3,2,0,1:T(8,128)(2,1)} %get-tuple-element.193, s32[1024]{0:T(1024)} %copy-done.70), kind=kCustom, calls=%fused_computation.5 | custom fusion | bytes 9437200 | tf_op jit(solution)/shard_map/jit(_take)/gather | solution.py:268
  241.6 5.5 %gather_fusion.2 = bf16[4,2,384,768]{3,2,1,0:T(8,128)(2,1)} fusion(bf16[4,2,384,768]{3,2,0,1:T(8,128)(2,1)} %get-tuple-element.192, s32[1024]{0:T(1024)} %copy-done.70), kind=kCustom, calls=%fused_computation.4 | custom fusion | bytes 9437200 | tf_op jit(solution)/shard_map/jit(_take)/gather | solution.py:268
  247.1 7.7 %pad_maximum_fusion = bf16[4,2,768,768]{3,2,1,0:T(8,128)(2,1)} fusion(bf16[4,2,384,768]{3,2,1,0:T(8,128)(2,1)} %gather_fusion.3, bf16[4,2,384,768]{3,2,1,0:T(8,128)(2,1)} %gather_fusion.2), kind=kLoop, calls=%fused_computation.9 | loop fusion | flops 18874368 | bytes 18874368
  254.8 8.3 %broadcast_select_fusion = bf16[8,2,2,2,96,768]{5,4,3,2,1,0:T(8,128)(2,1)} fusion(bf16[8,2,2,2,96,768]{5,4,3,2,1,0:T(8,128)(2,1)} %bitcast.286, pred[8]{0:T(512)(128)(4,1)S(1)} %copy-done.87), kind=kLoop, calls=%fused_computation.14 | loop fusion | flops 4718592 | bytes 18874376 | tf_op jit(solution)/shard_map/jit(_take)/select_n | solution.py:268
  263.2 5.3 %dynamic-slice_bitcast_fusion = bf16[8,2,2,96,768]{4,3,2,1,0:T(8,128)(2,1)} fusion(bf16[8,2,2,2,96,768]{5,4,3,2,1,0:T(8,128)(2,1)} %broadcast_select_fusion, s32[]{:T(128)S(6)} %select_n.337), kind=kLoop, calls=%fused_computation.57 | loop fusion | bytes 9437188 | tf_op jit(solution)/shard_map/jit(dynamic_index_in_dim)/squeeze | solution.py:45
  279.1 2.4 fusion.9
  285.6 13.1 %collective-permute-done.21 = bf16[2,2,96,768]{3,2,0,1:T(8,128)(2,1)} collective-permute-done((bf16[2,2,96,768]{3,2,0,1:T(8,128)(2,1)}, bf16[2,2,96,768]{3,2,0,1:T(8,128)(2,1)}, u32[]{:S(2)}, u32[]{:S(2)}) %collective-permute-start.21) | collective-permute-done | bytes 589856 | tf_op jit(solution)/shard_map/ppermute | solution.py:31
  304.7 39.8 %psum.7 = f32[9216]{0:T(1024)} all-reduce(f32[9216]{0:T(1024)S(1)} %constant_dynamic-update-slice_fusion), channel_id=1, replica_groups=mesh['dp'=8,'mp'=4] {'dp','mp'}, use_global_device_ids=true, to_apply=%region_20.22 | all-reduce | flops 9216 | bytes 73728 | tf_op jit(solution)/shard_map/psum | solution.py:331
  347.2 5.5 %fusion.1 = bf16[8,2,2,96,768]{4,3,2,1,0:T(8,128)(2,1)S(1)} fusion(bf16[8,2,2,96,768]{4,3,2,1,0:T(8,128)(2,1)} %collective-permute-done.33, bf16[8,2,2,2,96,768]{5,4,3,2,1,0:T(8,128)(2,1)} %broadcast_select_fusion, s32[]{:T(128)S(6)} %select_n.336), kind=kLoop, calls=%fused_computation.11 | loop fusion | flops 9437184 | bytes 14155780 | tf_op jit(solution)/shard_map/convert_element_type | solution.py:83
  355.4 2.3 collective-permute-start.34
  368.8 7.3 %collective-permute-done.26 = bf16[96,768]{1,0:T(8,128)(2,1)} collective-permute-done((bf16[96,768]{1,0:T(8,128)(2,1)}, bf16[96,768]{1,0:T(8,128)(2,1)}, u32[]{:S(2)}, u32[]{:S(2)}) %collective-permute-start.26) | collective-permute-done | bytes 147488 | tf_op jit(solution)/shard_map/ppermute | solution.py:31
  376.0 5.9 %collective-permute-start.11 = (bf16[3,40,768]{2,1,0:T(8,128)(2,1)}, bf16[3,40,768]{2,1,0:T(8,128)(2,1)S(1)}, u32[]{:S(2)}, u32[]{:S(2)}) collective-permute-start(bf16[3,40,768]{2,1,0:T(8,128)(2,1)} %get-tuple-element.107), channel_id=1, source_target_pairs={{0,1},{1,0},{2,3},{3,2},{4,5},{5,4},{6,7},{7,6},{8,9},{9,8},{10,11... | collective-permute-start | bytes 552968 | tf_op jit(solution)/shard_map/ppermute | solution.py:31
  383.4 6.0 %collective-permute-done.12 = bf16[3,40,768]{2,1,0:T(8,128)(2,1)S(1)} collective-permute-done((bf16[3,40,768]{2,1,0:T(8,128)(2,1)}, bf16[3,40,768]{2,1,0:T(8,128)(2,1)S(1)}, u32[]{:S(2)}, u32[]{:S(2)}) %collective-permute-start.12) | collective-permute-done | bytes 184352 | tf_op jit(solution)/shard_map/ppermute | solution.py:31
  401.9 10.0 %collective-permute-done.36 = bf16[4,96,768]{2,1,0:T(8,128)(2,1)S(1)} collective-permute-done((bf16[4,96,768]{2,1,0:T(8,128)(2,1)S(1)}, bf16[4,96,768]{2,1,0:T(8,128)(2,1)S(1)}, u32[]{:S(2)}, u32[]{:S(2)}) %collective-permute-start.36) | collective-permute-done | bytes 589856 | tf_op jit(solution)/shard_map/ppermute | solution.py:31
  413.3 3.2 collective-permute-start.39
  418.7 5.1 %collective-permute-done.38 = bf16[192,768]{1,0:T(8,128)(2,1)S(1)} collective-permute-done((bf16[192,768]{1,0:T(8,128)(2,1)S(1)}, bf16[192,768]{1,0:T(8,128)(2,1)S(1)}, u32[]{:S(2)}, u32[]{:S(2)}) %collective-permute-start.38) | collective-permute-done | bytes 294944 | tf_op jit(solution)/shard_map/ppermute | solution.py:31
  423.8 11.1 %collective-permute-done.39 = bf16[192,768]{1,0:T(8,128)(2,1)S(1)} collective-permute-done((bf16[192,768]{1,0:T(8,128)(2,1)S(1)}, bf16[192,768]{1,0:T(8,128)(2,1)S(1)}, u32[]{:S(2)}, u32[]{:S(2)}) %collective-permute-start.39) | collective-permute-done | bytes 294944 | tf_op jit(solution)/shard_map/ppermute | solution.py:31
  435.9 4.4 collective-permute-done.41
  443.3 4.0 collective-permute-done.43
  456.2 2.8 bitcast_convert_fusion.4
  (457 shorter events, 131.2 us)
Async XLA Ops:
  7.2 110.0 %all-gather.3.cloned.1.call-start = ((), (), s32[]{:S(2)}) async-start(), calls=%async_computation | async-start | bytes 4866048 | tf_op jit(solution)/shard_map/all_gather | solution.py:198
  9.4 150.3 %all-gather.5.cloned.1.call-start = ((), (), s32[]{:S(2)}) async-start(), calls=%async_computation.1 | async-start | bytes 4866048 | tf_op jit(solution)/shard_map/all_gather | solution.py:199
  10.9 10.7 %collective-permute-start.2 = (bf16[3,40,768]{2,1,0:T(8,128)(2,1)S(1)}, bf16[3,40,768]{2,1,0:T(8,128)(2,1)S(1)}, u32[]{:S(2)}, u32[]{:S(2)}) collective-permute-start(bf16[3,40,768]{2,1,0:T(8,128)(2,1)S(1)} %get-tuple-element.92), channel_id=1, source_target_pairs={{0,3},{1,2},{2,1},{3,0},{4,7},{5,6},{6,5},{7,4},{8,11},{9,10},{10,... | collective-permute-start | bytes 552968 | tf_op jit(solution)/shard_map/ppermute | solution.py:31
  16.0 18.6 %collective-permute-start.1 = (bf16[3,40,768]{2,1,0:T(8,128)(2,1)S(1)}, bf16[3,40,768]{2,1,0:T(8,128)(2,1)S(1)}, u32[]{:S(2)}, u32[]{:S(2)}) collective-permute-start(bf16[3,40,768]{2,1,0:T(8,128)(2,1)S(1)} %get-tuple-element.91), channel_id=1, source_target_pairs={{0,2},{1,3},{2,0},{3,1},{4,6},{5,7},{6,4},{7,5},{8,10},{9,11},{10,... | collective-permute-start | bytes 552968 | tf_op jit(solution)/shard_map/ppermute | solution.py:31
  16.0 18.6 %collective-permute-start = (bf16[3,40,768]{2,1,0:T(8,128)(2,1)S(1)}, bf16[3,40,768]{2,1,0:T(8,128)(2,1)S(1)}, u32[]{:S(2)}, u32[]{:S(2)}) collective-permute-start(bf16[3,40,768]{2,1,0:T(8,128)(2,1)S(1)} %get-tuple-element.90), channel_id=1, source_target_pairs={{0,1},{1,0},{2,3},{3,2},{4,5},{5,4},{6,7},{7,6},{8,9},{9,8},{10,11... | collective-permute-start | bytes 552968 | tf_op jit(solution)/shard_map/ppermute | solution.py:31
  35.5 8.3 %collective-permute-start.3 = (bf16[104,768]{1,0:T(8,128)(2,1)S(1)}, bf16[104,768]{1,0:T(8,128)(2,1)S(1)}, u32[]{:S(2)}, u32[]{:S(2)}) collective-permute-start(bf16[104,768]{1,0:T(8,128)(2,1)S(1)} %pad_maximum_fusion.21), channel_id=1, source_target_pairs={{0,1},{1,0},{2,3},{3,2},{4,5},{5,4},{6,7},{7,6},{8,9},{9,8},{10,11... | collective-permute-start | bytes 479240 | tf_op jit(solution)/shard_map/ppermute | solution.py:31
  35.5 17.6 %collective-permute-start.4 = (bf16[104,768]{1,0:T(8,128)(2,1)S(1)}, bf16[104,768]{1,0:T(8,128)(2,1)S(1)}, u32[]{:S(2)}, u32[]{:S(2)}) collective-permute-start(bf16[104,768]{1,0:T(8,128)(2,1)S(1)} %pad_maximum_fusion.21), channel_id=1, source_target_pairs={{0,2},{1,3},{2,0},{3,1},{4,6},{5,7},{6,4},{7,5},{8,10},{9,11},{10,... | collective-permute-start | bytes 479240 | tf_op jit(solution)/shard_map/ppermute | solution.py:31
  38.7 14.4 %collective-permute-start.5 = (bf16[104,768]{1,0:T(8,128)(2,1)S(1)}, bf16[104,768]{1,0:T(8,128)(2,1)S(1)}, u32[]{:S(2)}, u32[]{:S(2)}) collective-permute-start(bf16[104,768]{1,0:T(8,128)(2,1)S(1)} %pad_maximum_fusion.21), channel_id=1, source_target_pairs={{0,3},{1,2},{2,1},{3,0},{4,7},{5,6},{6,5},{7,4},{8,11},{9,10},{10,... | collective-permute-start | bytes 479240 | tf_op jit(solution)/shard_map/ppermute | solution.py:31
  53.2 7.7 %collective-permute-start.6 = (bf16[1,1,1,3,48,768]{5,4,3,2,1,0:T(8,128)(2,1)S(1)}, bf16[1,1,1,3,48,768]{5,4,3,2,1,0:T(8,128)(2,1)S(1)}, u32[]{:S(2)}, u32[]{:S(2)}) collective-permute-start(bf16[1,1,1,3,48,768]{5,4,3,2,1,0:T(8,128)(2,1)S(1)} %get-tuple-element.97), channel_id=1, source_target_pairs={{0,8},{4,12},{8,0},{12,4},{16,24},{20,28},{24,16},{28,20},{1,9},{5... | collective-permute-start | bytes 663560 | tf_op jit(solution)/shard_map/ppermute | solution.py:31
  54.8 8.4 %collective-permute-start.7 = (bf16[1,1,1,3,48,768]{5,4,3,2,1,0:T(8,128)(2,1)S(1)}, bf16[1,1,1,3,48,768]{5,4,3,2,1,0:T(8,128)(2,1)S(1)}, u32[]{:S(2)}, u32[]{:S(2)}) collective-permute-start(bf16[1,1,1,3,48,768]{5,4,3,2,1,0:T(8,128)(2,1)S(1)} %get-tuple-element.98), channel_id=1, source_target_pairs={{0,16},{4,20},{8,24},{12,28},{16,0},{20,4},{24,8},{28,12},{1,17},{... | collective-permute-start | bytes 663560 | tf_op jit(solution)/shard_map/ppermute | solution.py:31
  63.4 15.8 %collective-permute-start.8 = (bf16[1,2,1,3,48,768]{5,4,3,2,1,0:T(8,128)(2,1)S(1)}, bf16[1,2,1,3,48,768]{5,4,3,2,1,0:T(8,128)(2,1)S(1)}, u32[]{:S(2)}, u32[]{:S(2)}) collective-permute-start(bf16[1,2,1,3,48,768]{5,4,3,2,1,0:T(8,128)(2,1)S(1)} %pad_maximum_fusion.17), channel_id=1, source_target_pairs={{0,16},{4,20},{8,24},{12,28},{16,0},{20,4},{24,8},{28,12},{1,17},{... | collective-permute-start | bytes 1327112 | tf_op jit(solution)/shard_map/ppermute | solution.py:31
  65.2 13.9 %collective-permute-start.9 = (bf16[2,1,1,3,48,768]{5,4,3,2,1,0:T(8,128)(2,1)S(1)}, bf16[2,1,1,3,48,768]{5,4,3,2,1,0:T(8,128)(2,1)S(1)}, u32[]{:S(2)}, u32[]{:S(2)}) collective-permute-start(bf16[2,1,1,3,48,768]{5,4,3,2,1,0:T(8,128)(2,1)S(1)} %pad_maximum_fusion.18), channel_id=1, source_target_pairs={{0,8},{4,12},{8,0},{12,4},{16,24},{20,28},{24,16},{28,20},{1,9},{5... | collective-permute-start | bytes 1327112 | tf_op jit(solution)/shard_map/ppermute | solution.py:31
  80.7 4.0 collective-permute-start.10
  111.3 55.3 %collective-permute-start.16 = (bf16[3,40,768]{2,1,0:T(8,128)(2,1)}, bf16[3,40,768]{2,1,0:T(8,128)(2,1)}, u32[]{:S(2)}, u32[]{:S(2)}) collective-permute-start(bf16[3,40,768]{2,1,0:T(8,128)(2,1)} %get-tuple-element.114), channel_id=1, source_target_pairs={{0,3},{1,2},{2,1},{3,0},{4,7},{5,6},{6,5},{7,4},{8,11},{9,10},{10,... | collective-permute-start | bytes 552968 | tf_op jit(solution)/shard_map/ppermute | solution.py:31
  114.6 52.0 %collective-permute-start.15 = (bf16[3,40,768]{2,1,0:T(8,128)(2,1)}, bf16[3,40,768]{2,1,0:T(8,128)(2,1)}, u32[]{:S(2)}, u32[]{:S(2)}) collective-permute-start(bf16[3,40,768]{2,1,0:T(8,128)(2,1)} %get-tuple-element.113), channel_id=1, source_target_pairs={{0,2},{1,3},{2,0},{3,1},{4,6},{5,7},{6,4},{7,5},{8,10},{9,11},{10,... | collective-permute-start | bytes 552968 | tf_op jit(solution)/shard_map/ppermute | solution.py:31
  117.2 49.4 %collective-permute-start.14 = (bf16[3,40,768]{2,1,0:T(8,128)(2,1)}, bf16[3,40,768]{2,1,0:T(8,128)(2,1)}, u32[]{:S(2)}, u32[]{:S(2)}) collective-permute-start(bf16[3,40,768]{2,1,0:T(8,128)(2,1)} %get-tuple-element.112), channel_id=1, source_target_pairs={{0,1},{1,0},{2,3},{3,2},{4,5},{5,4},{6,7},{7,6},{8,9},{9,8},{10,11... | collective-permute-start | bytes 552968 | tf_op jit(solution)/shard_map/ppermute | solution.py:31
  227.2 51.9 %collective-permute-start.20 = (bf16[4,2,2,96,768]{4,3,0,1,2:T(8,128)(2,1)}, bf16[4,2,2,96,768]{4,3,0,1,2:T(8,128)(2,1)}, u32[]{:S(2)}, u32[]{:S(2)}) collective-permute-start(bf16[4,2,2,96,768]{4,3,0,1,2:T(8,128)(2,1)} %bitcast.285), channel_id=1, source_target_pairs={{0,4},{4,0},{8,12},{12,8},{16,20},{20,16},{24,28},{28,24},{1,5},{5... | collective-permute-start | bytes 7077896 | tf_op jit(solution)/shard_map/ppermute | solution.py:31
  268.5 78.7 %collective-permute-start.33 = (bf16[8,2,2,96,768]{4,3,2,1,0:T(8,128)(2,1)}, bf16[8,2,2,96,768]{4,3,2,1,0:T(8,128)(2,1)}, u32[]{:S(2)}, u32[]{:S(2)}) collective-permute-start(bf16[8,2,2,96,768]{4,3,2,1,0:T(8,128)(2,1)} %dynamic-slice_bitcast_fusion), channel_id=1, source_target_pairs={{0,4},{4,0},{8,12},{12,8},{16,20},{20,16},{24,28},{28,24},{1,5},{5... | collective-permute-start | bytes 14155784 | tf_op jit(solution)/shard_map/ppermute | solution.py:31
  272.7 85.6 %collective-permute-start.19 = (bf16[3,40,768]{2,1,0:T(8,128)(2,1)}, bf16[3,40,768]{2,1,0:T(8,128)(2,1)}, u32[]{:S(2)}, u32[]{:S(2)}) collective-permute-start(bf16[3,40,768]{2,1,0:T(8,128)(2,1)} %get-tuple-element.118), channel_id=1, source_target_pairs={{0,3},{1,2},{2,1},{3,0},{4,7},{5,6},{6,5},{7,4},{8,11},{9,10},{10,... | collective-permute-start | bytes 552968 | tf_op jit(solution)/shard_map/ppermute | solution.py:31
  274.8 84.6 %collective-permute-start.18 = (bf16[3,40,768]{2,1,0:T(8,128)(2,1)}, bf16[3,40,768]{2,1,0:T(8,128)(2,1)}, u32[]{:S(2)}, u32[]{:S(2)}) collective-permute-start(bf16[3,40,768]{2,1,0:T(8,128)(2,1)} %get-tuple-element.117), channel_id=1, source_target_pairs={{0,2},{1,3},{2,0},{3,1},{4,6},{5,7},{6,4},{7,5},{8,10},{9,11},{10,... | collective-permute-start | bytes 552968 | tf_op jit(solution)/shard_map/ppermute | solution.py:31
  283.4 15.3 %collective-permute-start.21 = (bf16[2,2,96,768]{3,2,0,1:T(8,128)(2,1)}, bf16[2,2,96,768]{3,2,0,1:T(8,128)(2,1)}, u32[]{:S(2)}, u32[]{:S(2)}) collective-permute-start(bf16[2,2,96,768]{3,2,0,1:T(8,128)(2,1)} %dynamic-slice_bitcast_fusion.6), channel_id=1, source_target_pairs={{0,8},{4,12},{8,0},{12,4},{16,24},{20,28},{24,16},{28,20},{1,9},{5... | collective-permute-start | bytes 1769480 | tf_op jit(solution)/shard_map/ppermute | solution.py:31
  284.8 15.0 %collective-permute-start.22 = (bf16[2,2,96,768]{3,2,0,1:T(8,128)(2,1)}, bf16[2,2,96,768]{3,2,0,1:T(8,128)(2,1)}, u32[]{:S(2)}, u32[]{:S(2)}) collective-permute-start(bf16[2,2,96,768]{3,2,0,1:T(8,128)(2,1)} %dynamic-slice_bitcast_fusion.5), channel_id=1, source_target_pairs={{0,16},{4,20},{8,24},{12,28},{16,0},{20,4},{24,8},{28,12},{1,17},{... | collective-permute-start | bytes 1769480 | tf_op jit(solution)/shard_map/ppermute | solution.py:31
  302.5 42.8 %collective-permute-start.23 = (bf16[2,96,768]{2,1,0:T(8,128)(2,1)S(1)}, bf16[2,96,768]{2,1,0:T(8,128)(2,1)S(1)}, u32[]{:S(2)}, u32[]{:S(2)}) collective-permute-start(bf16[2,96,768]{2,1,0:T(8,128)(2,1)S(1)} %dynamic-slice_bitcast_fusion.8), channel_id=1, source_target_pairs={{0,16},{4,20},{8,24},{12,28},{16,0},{20,4},{24,8},{28,12},{1,17},{... | collective-permute-start | bytes 884744 | tf_op jit(solution)/shard_map/ppermute | solution.py:31
  303.2 43.1 %collective-permute-start.24 = (bf16[2,96,768]{2,1,0:T(8,128)(2,1)S(1)}, bf16[2,96,768]{2,1,0:T(8,128)(2,1)S(1)}, u32[]{:S(2)}, u32[]{:S(2)}) collective-permute-start(bf16[2,96,768]{2,1,0:T(8,128)(2,1)S(1)} %dynamic-slice_bitcast_fusion.7), channel_id=1, source_target_pairs={{0,8},{4,12},{8,0},{12,4},{16,24},{20,28},{24,16},{28,20},{1,9},{5... | collective-permute-start | bytes 884744 | tf_op jit(solution)/shard_map/ppermute | solution.py:31
  345.3 15.3 %collective-permute-start.17 = (bf16[3,40,768]{2,1,0:T(8,128)(2,1)}, bf16[3,40,768]{2,1,0:T(8,128)(2,1)}, u32[]{:S(2)}, u32[]{:S(2)}) collective-permute-start(bf16[3,40,768]{2,1,0:T(8,128)(2,1)} %get-tuple-element.116), channel_id=1, source_target_pairs={{0,1},{1,0},{2,3},{3,2},{4,5},{5,4},{6,7},{7,6},{8,9},{9,8},{10,11... | collective-permute-start | bytes 552968 | tf_op jit(solution)/shard_map/ppermute | solution.py:31
  355.4 38.4 %collective-permute-start.34 = (bf16[4,2,96,768]{3,2,1,0:T(8,128)(2,1)}, bf16[4,2,96,768]{3,2,1,0:T(8,128)(2,1)}, u32[]{:S(2)}, u32[]{:S(2)}) collective-permute-start(bf16[4,2,96,768]{3,2,1,0:T(8,128)(2,1)} %dynamic-slice_bitcast_fusion.2), channel_id=1, source_target_pairs={{0,8},{4,12},{8,0},{12,4},{16,24},{20,28},{24,16},{28,20},{1,9},{5... | collective-permute-start | bytes 3538952 | tf_op jit(solution)/shard_map/ppermute | solution.py:31
  357.7 36.1 %collective-permute-start.35 = (bf16[4,2,96,768]{3,2,1,0:T(8,128)(2,1)}, bf16[4,2,96,768]{3,2,1,0:T(8,128)(2,1)}, u32[]{:S(2)}, u32[]{:S(2)}) collective-permute-start(bf16[4,2,96,768]{3,2,1,0:T(8,128)(2,1)} %dynamic-slice_bitcast_fusion.1), channel_id=1, source_target_pairs={{0,16},{4,20},{8,24},{12,28},{16,0},{20,4},{24,8},{28,12},{1,17},{... | collective-permute-start | bytes 3538952 | tf_op jit(solution)/shard_map/ppermute | solution.py:31
  358.3 8.8 %collective-permute-start.25 = (bf16[96,768]{1,0:T(8,128)(2,1)S(1)}, bf16[96,768]{1,0:T(8,128)(2,1)}, u32[]{:S(2)}, u32[]{:S(2)}) collective-permute-start(bf16[96,768]{1,0:T(8,128)(2,1)S(1)} %slice_bitcast_fusion.6), channel_id=1, source_target_pairs={{0,1},{1,0},{2,3},{3,2},{4,5},{5,4},{6,7},{7,6},{8,9},{9,8},{10,11... | collective-permute-start | bytes 442376 | tf_op jit(solution)/shard_map/ppermute | solution.py:31
  359.4 16.6 %collective-permute-start.26 = (bf16[96,768]{1,0:T(8,128)(2,1)}, bf16[96,768]{1,0:T(8,128)(2,1)}, u32[]{:S(2)}, u32[]{:S(2)}) collective-permute-start(bf16[96,768]{1,0:T(8,128)(2,1)} %get-tuple-element.128), channel_id=1, source_target_pairs={{0,2},{1,3},{2,0},{3,1},{4,6},{5,7},{6,4},{7,5},{8,10},{9,11},{10,... | collective-permute-start | bytes 442376 | tf_op jit(solution)/shard_map/ppermute | solution.py:31
  360.6 15.4 %collective-permute-start.27 = (bf16[96,768]{1,0:T(8,128)(2,1)}, bf16[96,768]{1,0:T(8,128)(2,1)}, u32[]{:S(2)}, u32[]{:S(2)}) collective-permute-start(bf16[96,768]{1,0:T(8,128)(2,1)} %get-tuple-element.129), channel_id=1, source_target_pairs={{0,3},{1,2},{2,1},{3,0},{4,7},{5,6},{6,5},{7,4},{8,11},{9,10},{10,... | collective-permute-start | bytes 442376 | tf_op jit(solution)/shard_map/ppermute | solution.py:31
  367.0 16.1 %collective-permute-start.13 = (bf16[3,40,768]{2,1,0:T(8,128)(2,1)}, bf16[3,40,768]{2,1,0:T(8,128)(2,1)S(1)}, u32[]{:S(2)}, u32[]{:S(2)}) collective-permute-start(bf16[3,40,768]{2,1,0:T(8,128)(2,1)} %get-tuple-element.109), channel_id=1, source_target_pairs={{0,3},{1,2},{2,1},{3,0},{4,7},{5,6},{6,5},{7,4},{8,11},{9,10},{10,... | collective-permute-start | bytes 552968 | tf_op jit(solution)/shard_map/ppermute | solution.py:31
  376.0 13.4 %collective-permute-start.12 = (bf16[3,40,768]{2,1,0:T(8,128)(2,1)}, bf16[3,40,768]{2,1,0:T(8,128)(2,1)S(1)}, u32[]{:S(2)}, u32[]{:S(2)}) collective-permute-start(bf16[3,40,768]{2,1,0:T(8,128)(2,1)} %get-tuple-element.108), channel_id=1, source_target_pairs={{0,2},{1,3},{2,0},{3,1},{4,6},{5,7},{6,4},{7,5},{8,10},{9,11},{10,... | collective-permute-start | bytes 552968 | tf_op jit(solution)/shard_map/ppermute | solution.py:31
  376.0 14.0 %collective-permute-start.11 = (bf16[3,40,768]{2,1,0:T(8,128)(2,1)}, bf16[3,40,768]{2,1,0:T(8,128)(2,1)S(1)}, u32[]{:S(2)}, u32[]{:S(2)}) collective-permute-start(bf16[3,40,768]{2,1,0:T(8,128)(2,1)} %get-tuple-element.107), channel_id=1, source_target_pairs={{0,1},{1,0},{2,3},{3,2},{4,5},{5,4},{6,7},{7,6},{8,9},{9,8},{10,11... | collective-permute-start | bytes 552968 | tf_op jit(solution)/shard_map/ppermute | solution.py:31
  383.1 9.5 %collective-permute-start.28 = (bf16[1,1,1,1,48,768]{5,4,3,2,1,0:T(8,128)(2,1)S(1)}, bf16[1,1,1,1,48,768]{5,4,3,2,1,0:T(8,128)(2,1)S(1)}, u32[]{:S(2)}, u32[]{:S(2)}) collective-permute-start(bf16[1,1,1,1,48,768]{5,4,3,2,1,0:T(8,128)(2,1)S(1)} %get-tuple-element.133), channel_id=1, source_target_pairs={{0,8},{4,12},{8,0},{12,4},{16,24},{20,28},{24,16},{28,20},{1,9},{5... | collective-permute-start | bytes 221192 | tf_op jit(solution)/shard_map/ppermute | solution.py:31
  389.4 4.4 collective-permute-start.29
  397.6 14.3 %collective-permute-start.36 = (bf16[4,96,768]{2,1,0:T(8,128)(2,1)S(1)}, bf16[4,96,768]{2,1,0:T(8,128)(2,1)S(1)}, u32[]{:S(2)}, u32[]{:S(2)}) collective-permute-start(bf16[4,96,768]{2,1,0:T(8,128)(2,1)S(1)} %dynamic-slice_bitcast_fusion.4), channel_id=1, source_target_pairs={{0,16},{4,20},{8,24},{12,28},{16,0},{20,4},{24,8},{28,12},{1,17},{... | collective-permute-start | bytes 1769480 | tf_op jit(solution)/shard_map/ppermute | solution.py:31
  398.2 14.5 %collective-permute-start.37 = (bf16[4,96,768]{2,1,0:T(8,128)(2,1)S(1)}, bf16[4,96,768]{2,1,0:T(8,128)(2,1)S(1)}, u32[]{:S(2)}, u32[]{:S(2)}) collective-permute-start(bf16[4,96,768]{2,1,0:T(8,128)(2,1)S(1)} %dynamic-slice_bitcast_fusion.3), channel_id=1, source_target_pairs={{0,8},{4,12},{8,0},{12,4},{16,24},{20,28},{24,16},{28,20},{1,9},{5... | collective-permute-start | bytes 1769480 | tf_op jit(solution)/shard_map/ppermute | solution.py:31
  399.0 19.7 %collective-permute-start.30 = (bf16[1,2,1,1,48,768]{5,4,3,2,1,0:T(8,128)(2,1)S(1)}, bf16[1,2,1,1,48,768]{5,4,3,2,1,0:T(8,128)(2,1)S(1)}, u32[]{:S(2)}, u32[]{:S(2)}) collective-permute-start(bf16[1,2,1,1,48,768]{5,4,3,2,1,0:T(8,128)(2,1)S(1)} %pad_maximum_fusion.22), channel_id=1, source_target_pairs={{0,16},{4,20},{8,24},{12,28},{16,0},{20,4},{24,8},{28,12},{1,17},{... | collective-permute-start | bytes 442376 | tf_op jit(solution)/shard_map/ppermute | solution.py:31
  400.4 18.3 %collective-permute-start.31 = (bf16[2,1,1,1,48,768]{5,4,2,1,0,3:T(8,128)(2,1)S(1)}, bf16[2,1,1,1,48,768]{5,4,2,1,0,3:T(8,128)(2,1)S(1)}, u32[]{:S(2)}, u32[]{:S(2)}) collective-permute-start(bf16[2,1,1,1,48,768]{5,4,2,1,0,3:T(8,128)(2,1)S(1)} %pad_maximum_fusion.23), channel_id=1, source_target_pairs={{0,8},{4,12},{8,0},{12,4},{16,24},{20,28},{24,16},{28,20},{1,9},{5... | collective-permute-start | bytes 442376 | tf_op jit(solution)/shard_map/ppermute | solution.py:31
  413.2 10.6 %collective-permute-start.38 = (bf16[192,768]{1,0:T(8,128)(2,1)S(1)}, bf16[192,768]{1,0:T(8,128)(2,1)S(1)}, u32[]{:S(2)}, u32[]{:S(2)}) collective-permute-start(bf16[192,768]{1,0:T(8,128)(2,1)S(1)} %bitcast.328), channel_id=1, source_target_pairs={{0,1},{1,0},{2,3},{3,2},{4,5},{5,4},{6,7},{7,6},{8,9},{9,8},{10,11... | collective-permute-start | bytes 884744 | tf_op jit(solution)/shard_map/ppermute | solution.py:31
  413.3 21.6 %collective-permute-start.39 = (bf16[192,768]{1,0:T(8,128)(2,1)S(1)}, bf16[192,768]{1,0:T(8,128)(2,1)S(1)}, u32[]{:S(2)}, u32[]{:S(2)}) collective-permute-start(bf16[192,768]{1,0:T(8,128)(2,1)S(1)} %bitcast.330), channel_id=1, source_target_pairs={{0,2},{1,3},{2,0},{3,1},{4,6},{5,7},{6,4},{7,5},{8,10},{9,11},{10,... | collective-permute-start | bytes 884744 | tf_op jit(solution)/shard_map/ppermute | solution.py:31
  416.5 18.4 %collective-permute-start.40 = (bf16[192,768]{1,0:T(8,128)(2,1)S(1)}, bf16[192,768]{1,0:T(8,128)(2,1)S(1)}, u32[]{:S(2)}, u32[]{:S(2)}) collective-permute-start(bf16[192,768]{1,0:T(8,128)(2,1)S(1)} %bitcast.329), channel_id=1, source_target_pairs={{0,3},{1,2},{2,1},{3,0},{4,7},{5,6},{6,5},{7,4},{8,11},{9,10},{10,... | collective-permute-start | bytes 884744 | tf_op jit(solution)/shard_map/ppermute | solution.py:31
  435.1 5.2 %collective-permute-start.41 = (bf16[1,1,1,2,48,768]{5,4,3,2,1,0:T(8,128)(2,1)S(1)}, bf16[1,1,1,2,48,768]{5,4,3,2,1,0:T(8,128)(2,1)S(1)}, u32[]{:S(2)}, u32[]{:S(2)}) collective-permute-start(bf16[1,1,1,2,48,768]{5,4,3,2,1,0:T(8,128)(2,1)S(1)} %get-tuple-element.155), channel_id=1, source_target_pairs={{0,8},{4,12},{8,0},{12,4},{16,24},{20,28},{24,16},{28,20},{1,9},{5... | collective-permute-start | bytes 442376 | tf_op jit(solution)/shard_map/ppermute | solution.py:31
  435.3 5.1 %collective-permute-start.42 = (bf16[1,1,1,2,48,768]{5,4,2,1,0,3:T(8,128)(2,1)S(1)}, bf16[1,1,1,2,48,768]{5,4,2,1,0,3:T(8,128)(2,1)S(1)}, u32[]{:S(2)}, u32[]{:S(2)}) collective-permute-start(bf16[1,1,1,2,48,768]{5,4,2,1,0,3:T(8,128)(2,1)S(1)} %get-tuple-element.156), channel_id=1, source_target_pairs={{0,16},{4,20},{8,24},{12,28},{16,0},{20,4},{24,8},{28,12},{1,17},{... | collective-permute-start | bytes 442376 | tf_op jit(solution)/shard_map/ppermute | solution.py:31
  440.6 6.8 %collective-permute-start.43 = (bf16[1,2,1,2,48,768]{5,4,3,2,1,0:T(8,128)(2,1)S(1)}, bf16[1,2,1,2,48,768]{5,4,3,2,1,0:T(8,128)(2,1)S(1)}, u32[]{:S(2)}, u32[]{:S(2)}) collective-permute-start(bf16[1,2,1,2,48,768]{5,4,3,2,1,0:T(8,128)(2,1)S(1)} %pad_maximum_fusion.19), channel_id=1, source_target_pairs={{0,16},{4,20},{8,24},{12,28},{16,0},{20,4},{24,8},{28,12},{1,17},{... | collective-permute-start | bytes 884744 | tf_op jit(solution)/shard_map/ppermute | solution.py:31
  441.2 6.7 %collective-permute-start.44 = (bf16[2,1,1,2,48,768]{5,4,2,1,0,3:T(8,128)(2,1)S(1)}, bf16[2,1,1,2,48,768]{5,4,2,1,0,3:T(8,128)(2,1)S(1)}, u32[]{:S(2)}, u32[]{:S(2)}) collective-permute-start(bf16[2,1,1,2,48,768]{5,4,2,1,0,3:T(8,128)(2,1)S(1)} %pad_maximum_fusion.20), channel_id=1, source_target_pairs={{0,8},{4,12},{8,0},{12,4},{16,24},{20,28},{24,16},{28,20},{1,9},{5... | collective-permute-start | bytes 884744 | tf_op jit(solution)/shard_map/ppermute | solution.py:31
  443.3 6.2 %collective-permute-start.32 = (bf16[2,2,1,1,96,768]{5,4,2,1,0,3:T(8,128)(2,1)S(1)}, bf16[2,2,1,1,96,768]{5,4,2,1,0,3:T(8,128)(2,1)S(1)}, u32[]{:S(2)}, u32[]{:S(2)}) collective-permute-start(bf16[2,2,1,1,96,768]{5,4,2,1,0,3:T(8,128)(2,1)S(1)} %maximum_maximum_fusion.2), channel_id=1, source_target_pairs={{0,4},{4,0},{8,12},{12,8},{16,20},{20,16},{24,28},{28,24},{1,5},{5... | collective-permute-start | bytes 1769480 | tf_op jit(solution)/shard_map/ppermute | solution.py:31
  448.1 4.0 collective-permute-start.45
  (101 other events, 999.7 us)
Sparse Core Ops, SparseCore 0:
  11.0 78.1 all-gather.2
  92.0 67.6 all-gather.4

commit v2 on v0

v2 whole, which is shorter than its diff:
```python
from functools import partial

import jax
import jax.numpy as jnp
from jax import lax
from jax.experimental import pallas as pl
from jax.experimental.pallas import tpu as pltpu
from jax.sharding import PartitionSpec as P

HEAD = 64
WORDS = 60
EPSILON = 1e-05
SQRT_HALF = 0.7071067811865476
DENSITY = 0.3989422804014327
F32 = jnp.float32
BF16 = jnp.bfloat16
VMEM_BYTES = 58 * 1024 * 1024
SMALL_VMEM_BYTES = 16 * 1024 * 1024


def dot(one, two, one_axis, two_axis):
    return lax.dot_general(
        one, two, (((one_axis,), (two_axis,)), ((), ())), preferred_element_type=F32
    )


def normalize(total, gain, shift):
    centered = total - jnp.mean(total, axis=-1, keepdims=True)
    inv_scale = lax.rsqrt(jnp.mean(centered * centered, axis=-1, keepdims=True) + EPSILON)
    normed = centered * inv_scale
    return normed * gain + shift, normed, inv_scale


def normalize_back(upstream, normed, inv_scale, gain):
    scaled_up = upstream * gain
    mean_one = jnp.mean(scaled_up, axis=-1, keepdims=True)
    mean_two = jnp.mean(scaled_up * normed, axis=-1, keepdims=True)
    return inv_scale * (scaled_up - mean_one - normed * mean_two)


def column_sum(array):
    return jnp.sum(array, axis=0, keepdims=True)


def head_stack(array, heads):
    head = lax.broadcasted_iota(jnp.int32, array.shape, 1) // HEAD
    zero = jnp.zeros_like(array)
    return jnp.concatenate([jnp.where(head == h, array, zero) for h in range(heads)], axis=0)


def head_pick(stacked, heads):
    rows = stacked.shape[0] // heads
    head = lax.broadcasted_iota(jnp.int32, (rows, stacked.shape[1]), 1) // HEAD
    total = stacked[:rows]
    for h in range(1, heads):
        total = jnp.where(head == h, stacked[h * rows : (h + 1) * rows], total)
    return total


def attention_kernel(
    pairs, x_ref, qk_ref, vo_ref, small_ref, valid_ref, vectors_ref,
    q_ref, k_ref, v_ref, weights_ref, context_ref, low_ref, normed_ref, scale_ref, total_ref,
):
    step = pl.program_id(0)
    cols = q_ref.shape[2]
    heads = cols // HEAD
    slots = x_ref.shape[0] // pairs
    x = x_ref[...]
    q_ref[0] = (dot(x, qk_ref[0, :cols], 1, 1) + small_ref[0, 0:1, :cols]).astype(BF16)
    k_ref[0] = dot(x, qk_ref[0, cols:], 1, 1).astype(BF16)
    v_ref[0] = (dot(x, vo_ref[0, :cols], 1, 1) + small_ref[0, 1:2, :cols]).astype(BF16)
    for p in range(pairs):
        rows = slice(p * slots, (p + 1) * slots)
        scores = dot(head_stack(q_ref[0, rows], heads), k_ref[0, rows], 1, 1) * HEAD ** (-0.5)
        scores = jnp.where(valid_ref[p] > 0.5, scores, -1e30)
        exp_scores = jnp.exp(scores - jnp.max(scores, axis=-1, keepdims=True))
        weights = exp_scores / jnp.sum(exp_scores, axis=-1, keepdims=True)
        weights_ref[0, p] = weights
        mixed = dot(weights.astype(BF16), v_ref[0, rows], 1, 0)
        context_ref[0, rows] = head_pick(mixed, heads).astype(BF16)
    branch = dot(context_ref[0], vo_ref[0, cols:], 1, 0)

    @pl.when(step == 0)
    def _():
        total_ref[...] = branch

    @pl.when(step > 0)
    def _():
        total_ref[...] += branch

    @pl.when(step == pl.num_programs(0) - 1)
    def _():
        first_sum = total_ref[...] + vectors_ref[0:1] + x.astype(F32)
        hidden, normed, scale = normalize(first_sum, vectors_ref[1:2], vectors_ref[2:3])
        low_ref[...] = hidden.astype(BF16)
        normed_ref[...] = normed
        scale_ref[...] = scale


def unit_rows(one, two, start, stop):
    half = one.shape[1]
    parts = []
    if start < half:
        parts.append(one[0, start : min(stop, half)])
    if stop > half:
        parts.append(two[0, max(start - half, 0) : stop - half])
    return parts[0] if len(parts) == 1 else jnp.concatenate(parts, axis=0)


def blocks_of(units):
    size = min(256, units)
    return [(start, start + size) for start in range(0, units, size)]


def by_owner(step, body, own, others):
    @pl.when(step == 0)
    def _():
        body(True, *own)

    @pl.when(step > 0)
    def _():
        body(False, *others)


def ffn_kernel(
    here_ref, low_ref, normed_ref, own_in_one, own_in_two, in_one, in_two, own_down_one, own_down_two, down_one,
    down_two, bias_one, bias_two, cot_ref, vectors_ref,
    act_ref, slope_ref, out_ref, delta_ref, ffn_low_ref, sums_ref, total_ref,
):
    step = pl.program_id(0)
    low = low_ref[...]
    half = in_one.shape[1]

    def body(first, w_in_one, w_in_two, w_down_one, w_down_two):
        bias = jnp.concatenate([bias_one[0, 2:3], bias_two[0, 2:3]], axis=1)
        branch = None
        for start, stop in blocks_of(2 * half):
            pre_act = dot(low, unit_rows(w_in_one, w_in_two, start, stop), 1, 1) + bias[:, start:stop]
            share = 0.5 * (1.0 + lax.erf(pre_act * SQRT_HALF))
            act = (pre_act * share).astype(BF16)
            act_ref[0, :, start:stop] = act
            slope_ref[0, :, start:stop] = share + pre_act * (DENSITY * jnp.exp(-0.5 * pre_act * pre_act))
            term = dot(act, unit_rows(w_down_one, w_down_two, start, stop), 1, 0)
            branch = term if branch is None else branch + term
        if first:
            total_ref[...] = branch
        else:
            total_ref[...] += branch

    by_owner(
        step,
        body,
        (own_in_one, own_in_two, own_down_one, own_down_two),
        (in_one, in_two, down_one, down_two),
    )

    @pl.when(step == pl.num_programs(0) - 1)
    def _():
        hidden = normed_ref[...] * vectors_ref[1:2] + vectors_ref[2:3]
        second = total_ref[...] + vectors_ref[3:4] + hidden
        gain = vectors_ref[4:5]
        output, normed, scale = normalize(second, gain, vectors_ref[5:6])
        out_ref[...] = output.astype(BF16)
        upstream = cot_ref[...].astype(F32)
        delta = normalize_back(upstream, normed, scale, gain)
        delta_ref[...] = delta
        ffn_low_ref[...] = delta.astype(BF16)
        sums_ref[...] = jnp.zeros_like(sums_ref)
        sums_ref[0:1] = column_sum(upstream * normed)
        sums_ref[1:2] = column_sum(upstream)
        sums_ref[2:3] = column_sum(delta)


def down_grad_kernel(act_ref, ffn_low_ref, keep_ref, send_ref):
    half = keep_ref.shape[1]
    low = ffn_low_ref[...]
    send_ref[0] = dot(act_ref[0, :, half:], low, 0, 0).astype(BF16)
    keep_ref[0] = dot(act_ref[0, :, :half], low, 0, 0).astype(BF16)


def in_grad_kernel(
    here_ref, ffn_low_ref, low_ref, slope_ref, own_down_one, own_down_two, down_one, down_two,
    keep_ref, send_ref, pre_grad_ref, sum_in_ref,
):
    core = here_ref[0]
    half = keep_ref.shape[1]
    ffn_low = ffn_low_ref[...]

    def body(first, w_down_one, w_down_two):
        for start, stop in blocks_of(2 * half):
            act_grad = dot(ffn_low, unit_rows(w_down_one, w_down_two, start, stop), 1, 1)
            pre_grad_ref[0, :, start:stop] = (act_grad * slope_ref[0, :, start:stop]).astype(BF16)

    by_owner(pl.program_id(0), body, (own_down_one, own_down_two), (down_one, down_two))
    low = low_ref[...]
    one, two = pre_grad_ref[0, :, :half], pre_grad_ref[0, :, half:]
    sum_in_ref[0, :, pl.ds(pl.multiple_of(core * half, half), half)] = column_sum(one.astype(F32))
    sum_in_ref[0, :, pl.ds(pl.multiple_of((1 - core) * half, half), half)] = column_sum(two.astype(F32))
    send_ref[0] = dot(two, low, 0, 0).astype(BF16)
    keep_ref[0] = dot(one, low, 0, 0).astype(BF16)


def ffn_back_kernel(
    here_ref, pre_grad_ref, own_in_one, own_in_two, in_one, in_two, delta_ref, normed_ref, scale_ref, vectors_ref,
    delta_attn_ref, attn_low_ref, sums_ref, total_ref,
):
    step = pl.program_id(0)
    units = pre_grad_ref.shape[2]

    def body(first, w_in_one, w_in_two):
        branch = None
        for start, stop in blocks_of(units):
            term = dot(pre_grad_ref[0, :, start:stop], unit_rows(w_in_one, w_in_two, start, stop), 1, 0)
            branch = term if branch is None else branch + term
        if first:
            total_ref[...] = branch
        else:
            total_ref[...] += branch

    by_owner(step, body, (own_in_one, own_in_two), (in_one, in_two))

    @pl.when(step == pl.num_programs(0) - 1)
    def _():
        hidden_grad = total_ref[...] + delta_ref[...]
        normed = normed_ref[...]
        delta = normalize_back(hidden_grad, normed, scale_ref[...], vectors_ref[1:2])
        delta_attn_ref[...] = delta
        attn_low_ref[...] = delta.astype(BF16)
        sums_ref[...] = jnp.zeros_like(sums_ref)
        sums_ref[0:1] = column_sum(delta)
        sums_ref[1:2] = column_sum(hidden_grad * normed)
        sums_ref[2:3] = column_sum(hidden_grad)


def attention_back_kernel(
    pairs, here_ref, x_ref, attn_low_ref, delta_ref, qk_ref, vo_ref, q_ref, k_ref, v_ref, weights_ref, context_ref,
    sums_one_ref, sums_two_ref, sum_in_ref,
    qk_keep_ref, vo_keep_ref, send_ref, sums_ref, rows_ref, dq_ref, dk_ref, dv_ref, total_ref,
):
    step = pl.program_id(0)
    core = here_ref[0]
    cols = q_ref.shape[2]
    heads = cols // HEAD
    slots = x_ref.shape[0] // pairs
    scale = HEAD ** (-0.5)
    x = x_ref[...]
    attn_low = attn_low_ref[...]
    context_grad = dot(attn_low, vo_ref[0, cols:], 1, 1).astype(BF16)
    grad_out = dot(context_ref[0], attn_low, 0, 0).astype(BF16)
    for p in range(pairs):
        rows = slice(p * slots, (p + 1) * slots)
        up = head_stack(context_grad[rows], heads)
        weights = weights_ref[0, p]
        prob_grad = dot(up, v_ref[0, rows], 1, 1)
        inner = jnp.sum(prob_grad * weights, axis=-1, keepdims=True)
        score_grad = (weights * (prob_grad - inner)).astype(BF16)
        dv_ref[rows] = dot(weights.astype(BF16), up, 0, 0).astype(BF16)
        query_grad = head_pick(dot(score_grad, k_ref[0, rows], 1, 0), heads)
        dq_ref[rows] = (query_grad * scale).astype(BF16)
        key_grad = dot(score_grad, head_stack(q_ref[0, rows], heads), 0, 0)
        dk_ref[rows] = (key_grad * scale).astype(BF16)
    dq, dk, dv = dq_ref[...], dk_ref[...], dv_ref[...]
    shards_ = pl.num_programs(0)

    @pl.when(step == 0)
    def _():
        sums_ref[...] = jnp.zeros_like(sums_ref)
        sums_ref[0:8] = sums_one_ref[...]
        sums_ref[8:16] = sums_two_ref[...]
        for j in range(sum_in_ref.shape[0]):
            sums_ref[16 + j : 17 + j] = sum_in_ref[j]

    row = pl.ds(16 + shards_ + (step ^ here_ref[1]), 1)
    sums_ref[row, :cols] = column_sum(dq.astype(F32))
    sums_ref[row, 2 * cols : 3 * cols] = column_sum(dv.astype(F32))
    grad_q = dot(dq, x, 0, 0).astype(BF16)
    grad_k = dot(dk, x, 0, 0).astype(BF16)
    grad_v = dot(dv, x, 0, 0).astype(BF16)

    @pl.when(core == 0)
    def _():
        qk_keep_ref[0], send_ref[0, 0] = grad_q, grad_k
        vo_keep_ref[0], send_ref[1, 0] = grad_v, grad_out

    @pl.when(core != 0)
    def _():
        qk_keep_ref[0], send_ref[0, 0] = grad_k, grad_q
        vo_keep_ref[0], send_ref[1, 0] = grad_out, grad_v

    branch = dot(dq, qk_ref[0, :cols], 1, 0) + dot(dk, qk_ref[0, cols:], 1, 0)
    branch = branch + dot(dv, vo_ref[0, :cols], 1, 0)

    @pl.when(step == 0)
    def _():
        total_ref[...] = branch + delta_ref[...]

    @pl.when(step > 0)
    def _():
        total_ref[...] += branch

    @pl.when(step == pl.num_programs(0) - 1)
    def _():
        rows_ref[...] = total_ref[...].astype(BF16)


def whole(array):
    return pl.BlockSpec(array.shape, lambda *_: (0,) * len(array.shape))


def per_step(array):
    return pl.BlockSpec((1,) + array.shape[1:], lambda s, *_: (s,) + (0,) * (len(array.shape) - 1))


def call(kernel, steps, name, inputs, outputs, scratch, scalar=None):
    spec = pltpu.PrefetchScalarGridSpec(
        num_scalar_prefetch=0 if scalar is None else 1,
        grid=(steps,),
        in_specs=[make if isinstance(make, pl.BlockSpec) else make(a) for make, a in inputs],
        out_specs=[make if isinstance(make, pl.BlockSpec) else make(a) for make, a in outputs],
        scratch_shapes=scratch,
    )
    return pl.pallas_call(
        kernel,
        grid_spec=spec,
        out_shape=[a for _, a in outputs],
        name=name,
        cost_estimate=pl.CostEstimate(flops=0, bytes_accessed=0, transcendentals=0),
        compiler_params=pltpu.CompilerParams(vmem_limit_bytes=VMEM_BYTES),
    )(*(() if scalar is None else (scalar,)), *[a for _, a in inputs])


def shape(dims, dtype):
    return jax.ShapeDtypeStruct(dims, dtype)


def add_kernel(count, *refs):
    total = refs[1][...].astype(F32)
    for ref in refs[2 : 1 + count]:
        total = total + ref[...].astype(F32)
    refs[1 + count][...] = total.astype(BF16)


def add_terms(terms, me, fixed):
    first, bits = terms[0]
    left = [b for b in bits if b not in fixed]
    n, _, rows, cols = first.shape

    def place(own_bits):
        def index(g, me_ref):
            at = 0
            for b in own_bits:
                if b in fixed:
                    value = (me_ref[0] >> b) & 1
                    value = value if fixed[b] else 1 - value
                else:
                    value = (g >> (len(left) - 1 - left.index(b))) & 1
                at = at * 2 + value
            return (0, at, 0, 0)

        return index

    spec = pltpu.PrefetchScalarGridSpec(
        num_scalar_prefetch=1,
        grid=(1 << len(left),),
        in_specs=[pl.BlockSpec((n, 1, rows, cols), place(b)) for _, b in terms],
        out_specs=pl.BlockSpec((n, 1, rows, cols), lambda g, _: (0, g, 0, 0)),
    )
    out = pl.pallas_call(
        partial(add_kernel, len(terms)),
        grid_spec=spec,
        out_shape=shape((n, 1 << len(left), rows, cols), BF16),
        name="add",
        cost_estimate=pl.CostEstimate(flops=0, bytes_accessed=0, transcendentals=0),
        compiler_params=pltpu.CompilerParams(vmem_limit_bytes=SMALL_VMEM_BYTES),
    )(me, *[a for a, _ in terms])
    return out, left


def flip(array, axis, mask):
    size = lax.axis_size(axis)
    return lax.ppermute(array, axis, [(i, i ^ mask) for i in range(size)])


def tie(*arrays):
    return lax.optimization_barrier(arrays)


def pick(array, axis, index):
    return lax.dynamic_index_in_dim(array, index, axis, keepdims=False)


def outer_bits():
    bits = list(range(1, lax.axis_size("dp").bit_length() - 1))
    return bits, (bits, bits[::-1])


def share_of():
    me = lax.axis_index("dp")
    return (me & 1) * (lax.axis_size("dp") // 2) + (me >> 1)


class Gather:
    def __init__(self, pair):
        self.bits, self.orders = outer_bits()
        self.steps = len(self.bits)
        self.n, _, self.cols = pair[0].shape
        self.held = [
            a.reshape((self.n,) + (1,) * self.steps + a.shape[1:]) for a in pair
        ]

    def send(self, step):
        return [flip(h, "dp", 1 << order[step]) for h, order in zip(self.held, self.orders)]

    def take(self, step, got):
        me = lax.axis_index("dp")
        merged = []
        for mine, theirs, order in zip(self.held, got, self.orders):
            bit = order[step]
            low = ((me >> bit) & 1) == 0
            parts = [jnp.where(low, mine, theirs), jnp.where(low, theirs, mine)]
            merged.append(jnp.concatenate(parts, axis=1 + self.steps - bit))
        self.held = merged

    def send_core(self):
        self.halves = jnp.stack([h.reshape(self.n, -1, self.cols) for h in self.held])
        return flip(self.halves, "dp", 1)

    def finish(self, got):
        low = (lax.axis_index("dp") & 1) == 0
        one, two = jnp.where(low, self.halves, got), jnp.where(low, got, self.halves)
        return [jnp.concatenate([one[i], two[i]], axis=1) for i in range(2)]


class Reduce:
    def __init__(self, keeps, gots):
        self.bits, self.orders = outer_bits()
        self.steps = len(self.bits)
        self.me = lax.axis_index("dp").astype(jnp.int32).reshape(1)
        high_first = self.bits[::-1]
        n, rows, cols = keeps[0].shape
        form = (n, 1 << self.steps, rows >> self.steps, cols)
        self.terms = [
            [(k.reshape(form), high_first), (g.reshape(form), high_first)]
            for k, g in zip(keeps, gots)
        ]
        self.left = [None, None]

    def pack(self, step):
        sends = []
        for side, order in enumerate(self.orders):
            fixed = {b: True for b in order[:step]}
            fixed[order[step]] = False
            out, self.left[side] = add_terms(self.terms[side], self.me, fixed)
            sends.append(out)
        return sends

    def send(self, step, packs):
        return [flip(p, "dp", 1 << order[step]) for p, order in zip(packs, self.orders)]

    def take(self, got):
        for side in range(2):
            self.terms[side].append((got[side], self.left[side]))

    def finish(self):
        fixed = {b: True for b in self.bits}
        return [add_terms(t, self.me, fixed)[0][:, 0] for t in self.terms]


def add_parts(*parts):
    total = parts[0].astype(F32)
    for part in parts[1:]:
        total = total + part.astype(F32)
    return total.astype(BF16)


def shards(
    tokens,
    word_len,
    region_count,
    w_qkv,
    qv_bias,
    w_out,
    out_bias,
    norm1_gain,
    norm1_bias,
    w_in,
    in_bias,
    w_down,
    down_bias,
    norm2_gain,
    norm2_bias,
    cotangent,
):
    mp = lax.axis_size("mp")
    dp = lax.axis_size("dp")
    mi = lax.axis_index("mp")
    width = tokens.shape[2]
    rows_local = tokens.shape[1]
    slots = rows_local * mp
    pairs = tokens.shape[0] // mp
    rows = pairs * slots
    cols = w_qkv.shape[2]
    units = w_in.shape[1]
    half_units = units // 2
    order = jnp.arange(mp) ^ mi
    here = jnp.stack([lax.axis_index("dp") & 1, mi]).astype(jnp.int32)
    share = share_of()

    turned = w_qkv.transpose(0, 2, 1)
    own = {
        "qk": turned[:2].reshape(2 * cols, width),
        "vo": jnp.concatenate([turned[2], w_out], axis=0),
        "in": w_in.T,
        "down": w_down,
    }

    def piece(name):
        part = own[name].shape[0] // dp
        return lax.dynamic_slice_in_dim(own[name], share * part, part, 0)

    def row_blocks(array):
        blocks = array.reshape((mp, pairs) + array.shape[1:])
        return [pick(blocks, 0, mi ^ k) for k in range(mp)]

    def join(blocks):
        return jnp.concatenate(blocks, axis=1).reshape(rows, width)

    fill = lambda v: jnp.pad(v, ((0, 0), (0, width - v.shape[1])))
    small = jnp.concatenate([fill(qv_bias), in_bias.reshape(1, units), jnp.zeros((5, width), BF16)])
    att_part, ffn_part = 2 * cols // dp, units // dp
    att_send = jnp.concatenate([piece("qk"), piece("vo"), small], axis=0)
    ffn_send = jnp.concatenate([piece("in"), piece("down")], axis=0)
    tok = row_blocks(tokens)
    cot = row_blocks(cotangent)
    vectors = jnp.stack(
        [out_bias, norm1_gain, norm1_bias, down_bias, norm2_gain, norm2_bias, out_bias, out_bias]
    ).astype(F32)
    words = lax.dynamic_slice_in_dim(word_len, mi * pairs, pairs, 0)
    regions = lax.dynamic_slice_in_dim(region_count, mi * pairs, pairs, 0)
    slot_index = (order[:, None] * rows_local + jnp.arange(rows_local)[None, :]).reshape(-1)
    key_valid = jnp.where(
        slot_index[None, :] < WORDS,
        slot_index[None, :] < words[:, None],
        slot_index[None, :] - WORDS < regions[:, None],
    ).astype(F32)[:, None, :]

    att_two = flip(att_send, "mp", 2)
    att_two, ffn_send, tok, vectors, key_valid = tie(att_two, ffn_send, tok, vectors, key_valid)
    att_odd = flip(jnp.stack([att_send, att_two]), "mp", 1)
    ffn_two = flip(ffn_send, "mp", 2)
    att_odd, ffn_two = tie(att_odd, ffn_two)
    att_got = [att_odd[0], att_two, att_odd[1]]
    att = Gather(
        [
            jnp.stack([g[:att_part] for g in att_got]),
            jnp.stack([g[att_part : 2 * att_part] for g in att_got]),
        ]
    )
    ffn_odd = flip(jnp.stack([ffn_send, ffn_two]), "mp", 1)
    got = att.send(0)
    smalls = jnp.stack([small] + [g[2 * att_part :] for g in att_got]).astype(F32)
    ffn_odd, got, tok, smalls = tie(ffn_odd, got, tok, smalls)
    for step in range(1, att.steps):
        att.take(step - 1, got)
        got = att.send(step)
        if step == 1:
            tok_one, tok_three = flip(tok[1], "mp", 1), flip(tok[3], "mp", 3)
        got, tok_one, tok_three, tok = tie(got, tok_one, tok_three, tok)
    att.take(att.steps - 1, got)
    ffn_got = [ffn_odd[0], ffn_two, ffn_odd[1]]
    ffn = Gather(
        [
            jnp.stack([g[:ffn_part] for g in ffn_got]),
            jnp.stack([g[ffn_part:] for g in ffn_got]),
        ]
    )
    got = ffn.send(0)
    core_got = att.send_core()
    tok_two = flip(tok[2], "mp", 2)
    got, core_got, tok_two, cot = tie(got, core_got, tok_two, cot)
    qk_others, vo_others = att.finish(core_got)
    qk_all = jnp.concatenate([own["qk"][None], qk_others])
    vo_all = jnp.concatenate([own["vo"][None], vo_others])
    x = join([tok[0], tok_one, tok_two, tok_three])
    heads_low = shape((mp, rows, cols), BF16)
    low_shape = shape((rows, width), BF16)
    rows_shape = shape((rows, width), F32)
    sums_shape = shape((8, width), F32)
    for step in range(1, ffn.steps):
        ffn.take(step - 1, got)
        got = ffn.send(step)
        if step == 1:
            cot_one, cot_three = flip(cot[1], "mp", 1), flip(cot[3], "mp", 3)
            got, qk_all, vo_all, x = tie(got, qk_all, vo_all, x) if ffn.steps > 2 else (got, qk_all, vo_all, x)
    q, k, v, weights, context, hidden_low, normed_one, scale_one = call(
        partial(attention_kernel, pairs),
        mp,
        "attention",
        [
            (whole, x),
            (per_step, qk_all),
            (per_step, vo_all),
            (per_step, smalls),
            (whole, key_valid),
            (whole, vectors),
        ],
        [
            (per_step, heads_low),
            (per_step, heads_low),
            (per_step, heads_low),
            (per_step, shape((mp, pairs, cols // HEAD * slots, slots), F32)),
            (per_step, heads_low),
            (whole, low_shape),
            (whole, rows_shape),
            (whole, shape((rows, 1), F32)),
        ],
        [pltpu.VMEM((rows, width), F32)],
    )
    got, hidden_low, cot_one, cot_three, cot = tie(got, hidden_low, cot_one, cot_three, cot)
    ffn.take(ffn.steps - 1, got)
    in_one, down_one = [h.reshape(mp - 1, half_units, width) for h in ffn.held]
    in_two, down_two = flip(in_one, "dp", 1), flip(down_one, "dp", 1)
    cot_two = flip(cot[2], "mp", 2)
    in_two, down_two, cot_two, hidden_low = tie(in_two, down_two, cot_two, hidden_low)
    cot_rows = join([cot[0], cot_one, cot_two, cot_three])

    one_block, two_block = (1, half_units, width), (1, half_units, width)
    mine = pl.BlockSpec(one_block, lambda s, h: (h[0], 0, 0))
    other = pl.BlockSpec(one_block, lambda s, h: (1 - h[0], 0, 0))
    later = pl.BlockSpec(two_block, lambda s, h: (jnp.maximum(s - 1, 0), 0, 0))
    own_in = own["in"].reshape(2, half_units, width)
    own_down = own["down"].reshape(2, half_units, width)
    in_args = [(mine, own_in), (other, own_in), (later, in_one), (later, in_two)]
    down_args = [(mine, own_down), (other, own_down), (later, down_one), (later, down_two)]
    act, slope, output, delta_ffn, ffn_low, sums_two = call(
        ffn_kernel,
        mp,
        "ffn",
        [
            (whole, hidden_low),
            (whole, normed_one),
            *in_args,
            *down_args,
            (pl.BlockSpec((1, 8, half_units), lambda s, h: (s, 0, h[0])), smalls),
            (pl.BlockSpec((1, 8, half_units), lambda s, h: (s, 0, 1 - h[0])), smalls),
            (whole, cot_rows),
            (whole, vectors),
        ],
        [
            (per_step, shape((mp, rows, units), BF16)),
            (per_step, shape((mp, rows, units), F32)),
            (whole, low_shape),
            (whole, rows_shape),
            (whole, low_shape),
            (whole, sums_shape),
        ],
        [pltpu.VMEM((rows, width), F32)],
        here,
    )
    half = shape((mp, half_units, width), BF16)
    down_keep, down_send = call(
        down_grad_kernel,
        mp,
        "down_grad",
        [(per_step, act), (whole, ffn_low)],
        [(per_step, half), (per_step, half)],
        [],
    )
    down_send, ffn_low = tie(down_send, ffn_low)
    down_got = flip(down_send, "dp", 1)
    in_keep, in_send, pre_grad, sum_in = call(
        in_grad_kernel,
        mp,
        "in_grad",
        [(whole, ffn_low), (whole, hidden_low), (per_step, slope), *down_args],
        [
            (per_step, half),
            (per_step, half),
            (per_step, shape((mp, rows, units), BF16)),
            (
                pl.BlockSpec((1, 1, units), lambda s, h: (s ^ h[1], 0, 0)),
                shape((mp, 1, units), F32),
            ),
        ],
        [],
        here,
    )
    out_rows = output.reshape(pairs, mp, rows_local, width)
    out_blocks = [out_rows[:, k] for k in range(mp)]
    down_got, in_send, pre_grad, out_blocks = tie(down_got, in_send, pre_grad, out_blocks)
    in_got = flip(in_send, "dp", 1)
    delta_attn, attn_low, sums_one = call(
        ffn_back_kernel,
        mp,
        "ffn_back",
        [
            (per_step, pre_grad),
            *in_args,
            (whole, delta_ffn),
            (whole, normed_one),
            (whole, scale_one),
            (whole, vectors),
        ],
        [(whole, rows_shape), (whole, low_shape), (whole, sums_shape)],
        [pltpu.VMEM((rows, width), F32)],
        here,
    )
    in_got, attn_low = tie(in_got, attn_low)
    ffn = Reduce([in_keep, down_keep], [in_got, down_got])
    packs = ffn.pack(0)
    packs, attn_low = tie(packs, attn_low)
    got = ffn.send(0, packs)
    out_got = [out_blocks[0]] + [flip(out_blocks[k], "mp", k) for k in range(1, mp)]
    small_half = shape((mp, cols, width), BF16)
    qk_keep, vo_keep, att_send, sums, grad_rows = call(
        partial(attention_back_kernel, pairs),
        mp,
        "attention_back",
        [
            (whole, x),
            (whole, attn_low),
            (whole, delta_attn),
            (per_step, qk_all),
            (per_step, vo_all),
            (per_step, q),
            (per_step, k),
            (per_step, v),
            (per_step, weights),
            (per_step, context),
            (whole, sums_one),
            (whole, sums_two),
            (whole, sum_in),
        ],
        [
            (per_step, small_half),
            (per_step, small_half),
            (
                pl.BlockSpec((2, 1, cols, width), lambda s, h: (0, s, 0, 0)),
                shape((2, mp, cols, width), BF16),
            ),
            (whole, shape((16 + 2 * mp, width), F32)),
            (whole, low_shape),
        ],
        [pltpu.VMEM((rows, cols), BF16)] * 3 + [pltpu.VMEM((rows, width), F32)],
        here,
    )
    grad_rows = grad_rows.reshape(pairs, mp, rows_local, width)
    row_sends = [grad_rows[:, k] for k in range(mp)]
    got, out_got, att_send, row_sends, sums = tie(got, out_got, att_send, row_sends, sums)
    for step in range(1, ffn.steps):
        ffn.take(got)
        packs = ffn.pack(step)
        got = ffn.send(step, packs)
        if step == 1:
            att_got = flip(att_send, "dp", 1)
            sums_got = flip(sums, "dp", 1)
            row_three = flip(row_sends[3], "mp", 3)
        got, att_got, sums_got, row_three, row_sends = tie(got, att_got, sums_got, row_three, row_sends)
    ffn.take(got)
    sums = sums + sums_got
    ffn_parts = ffn.finish()
    ffn_odd = jnp.concatenate([p[1::2] for p in ffn_parts], axis=1)
    ffn_even = jnp.concatenate([p[0::2] for p in ffn_parts], axis=1)
    att = Reduce([qk_keep, vo_keep], [att_got[0], att_got[1]])
    packs = att.pack(0)
    ffn_odd, ffn_even, packs, sums = tie(ffn_odd, ffn_even, packs, sums)
    got = att.send(0, packs)
    ffn_got = flip(ffn_odd, "mp", 1)
    row_one = flip(row_sends[1], "mp", 1)
    sums_got = flip(sums, "dp", 2)
    got, ffn_got, row_one, sums_got = tie(got, ffn_got, row_one, sums_got)
    sums = sums + sums_got
    for mask in [1 << b for b in range(2, dp.bit_length() - 2)]:
        sums = sums + flip(sums, "dp", mask)
    ffn_two = add_parts(ffn_even[1], ffn_got[1])
    for step in range(1, att.steps):
        att.take(got)
        packs = att.pack(step)
        got = att.send(step, packs)
        if step == 1:
            ffn_last = flip(ffn_two, "mp", 2)
            sums_got = flip(sums, "dp", dp // 2)
        got, ffn_last, sums_got, row_sends = tie(got, ffn_last, sums_got, row_sends)
    att.take(got)
    sums = sums + sums_got
    att_parts = att.finish()
    att_odd = jnp.concatenate([p[1::2] for p in att_parts], axis=1)
    att_even = jnp.concatenate([p[0::2] for p in att_parts], axis=1)
    ffn_sum = add_parts(ffn_even[0], ffn_got[0], ffn_last)
    ffn = Gather([ffn_sum[None, :ffn_part], ffn_sum[None, ffn_part:]])
    ffn.held, att_odd, att_even, sums = tie(ffn.held, att_odd, att_even, sums)
    got = ffn.send(0)
    att_got = flip(att_odd, "mp", 1)
    row_two = flip(row_sends[2], "mp", 2)
    sums_got = flip(sums, "mp", 1)
    got, att_got, row_two, sums_got = tie(got, att_got, row_two, sums_got)
    sums = sums + sums_got
    att_two = add_parts(att_even[1], att_got[1])
    for step in range(1, ffn.steps):
        ffn.take(step - 1, got)
        got = ffn.send(step)
        if step == 1:
            att_last = flip(att_two, "mp", 2)
            sums_got = flip(sums, "mp", 2)
        got, att_last, sums_got = tie(got, att_last, sums_got)
    ffn.take(ffn.steps - 1, got)
    sums = sums + sums_got
    att_sum = add_parts(att_even[0], att_got[0], att_last)
    att = Gather([att_sum[None, :att_part], att_sum[None, att_part:]])
    core_got = ffn.send_core()
    got = att.send(0)
    core_got, got = tie(core_got, got)
    grad_in, grad_down = ffn.finish(core_got)
    for step in range(1, att.steps):
        att.take(step - 1, got)
        got = tie(*att.send(step))
    att.take(att.steps - 1, got)
    grad_qk, grad_vo = att.finish(att.send_core())

    def leave(blocks):
        return jnp.take(jnp.stack(blocks), order, axis=0).reshape(mp * pairs, rows_local, width)

    layer_out = leave(out_got)
    grad_input = leave([row_sends[0], row_one, row_two, row_three]).astype(F32)
    sum_in_bias = lax.dynamic_index_in_dim(sums, 16 + mi, 0, keepdims=False)
    sum_qv = lax.dynamic_index_in_dim(sums, 16 + mp + mi, 0, keepdims=False)
    sum_qv = jnp.stack([sum_qv[:cols], sum_qv[2 * cols : 3 * cols]])
    grad_qkv = jnp.concatenate([grad_qk[0], grad_vo[0, :cols]], axis=0).reshape(3, cols, width)
    return (
        layer_out,
        grad_input,
        grad_qkv.astype(F32).transpose(0, 2, 1),
        sum_qv,
        grad_vo[0, cols:].astype(F32),
        sums[0],
        sums[1],
        sums[2],
        grad_in[0].astype(F32).T,
        sum_in_bias,
        grad_down[0].astype(F32),
        sums[10],
        sums[8],
        sums[9],
    )


def solution(mesh):
    in_specs = (
        P("dp", "mp", None),
        P("dp"),
        P("dp"),
        P(None, None, "mp"),
        P(None, "mp"),
        P("mp", None),
        P(),
        P(),
        P(),
        P(None, "mp"),
        P("mp"),
        P("mp", None),
        P(),
        P(),
        P(),
        P("dp", "mp", None),
    )
    out_specs = (
        P("dp", "mp", None),
        P("dp", "mp", None),
        P(None, None, "mp"),
        P(None, "mp"),
        P("mp", None),
        P(),
        P(),
        P(),
        P(None, "mp"),
        P("mp"),
        P("mp", None),
        P(),
        P(),
        P(),
    )
    return jax.shard_map(shards, mesh=mesh, in_specs=in_specs, out_specs=out_specs, check_vma=False)
```

time: 923 us -> 322 us (0.35)
  waiting for transfers between devices: 694 us -> 104 us
  Pallas kernels: 0 us -> 88.3 us
  matrix products: 76.1 us -> 0 us
  starting transfers between devices: 1.3 us -> 62.7 us
  blocking collectives: 61 us -> 0 us
  between operations: 14.8 us -> 1.88 us
    reduce_scatter x4 -> x0, waiting for transfers between devices: 333 us -> none  [the longest x1 103 us: shards(): lax.psum_scatter(back_term, 'mp', scatter_dimension=1, tiled=True)]
    all_gather x4 -> x0, waiting for transfers between devices: 245 us -> none  [the longest x1 62.9 us: shards(): whole = lax.all_gather(tokens, 'mp', axis=1, tiled=True)]
    psum x1 -> x0, waiting for transfers between devices: 116 us -> none  [shards(): lax.psum((grad_qkv, grad_qv_bias, grad_out, grad_in, grad_in_bias, grad_d...]
    ppermute x0 -> x57, waiting for transfers between devices: none -> 104 us  [flip(): return lax.ppermute(array, axis, [(i, i ^ mask) for i in range(size)])]
    pallas_call x0 -> x18, Pallas kernels: none -> 88.3 us  [the longest x6 79.4 us: call(): pl.pallas_call(kernel, grid_spec=spec, out_shape=[a for _, a in outputs],...]
    dot_general x18 -> x0, matrix products: 76.1 us -> none  [the longest x1 10.5 us: shards(): jnp.einsum('psd,fd->psf', ffn_all, w_down, preferred_element_type=jnp.flo...]
    ppermute x0 -> x57, starting transfers between devices: none -> 62.7 us  [flip(): return lax.ppermute(array, axis, [(i, i ^ mask) for i in range(size)])]
    psum x2 -> x0, blocking collectives: 61 us -> none  [the longest x1 46.3 us: shards(): lax.psum((grad_out_bias, grad_norm1_gain, grad_norm1_bias, grad_down_bias...]
  transfers between devices with their start and end apart: 9 -> 57, of which waited for: 9 -> 25; matrix products, arithmetic and copies ran while one was open for 2% -> 13% of each run, Pallas kernels for 0% -> 19%
where the time goes in v2:
time: 322 us; the launch traced here: 321 us
  waiting for transfers between devices  104 us (32%)
  Pallas kernels  88.3 us (27%)
  starting transfers between devices  62.7 us (19%)
  other arithmetic  40.9 us (13%)
  local copies, waits for them, and re-layouts  22.9 us (7%)
    ppermute x57, waiting for transfers between devices, flip(): return lax.ppermute(array, axis, [(i, i ^ mask) for i in range(size)])  104 us
    pallas_call x6, Pallas kernels, call(): pl.pallas_call(kernel, grid_spec=spec, out_shape=[a for _, a in outputs],...  79.4 us
    ppermute x57, starting transfers between devices, flip(): return lax.ppermute(array, axis, [(i, i ^ mask) for i in range(size)])  62.7 us
    pallas_call x12, Pallas kernels, add_terms(): pl.pallas_call(partial(add_kernel, len(terms)), grid_spec=spec, out_shape...  8.84 us
    select_n x15, other arithmetic, take(): parts = [jnp.where(low, mine, theirs), jnp.where(low, theirs, mine)]  8.04 us
  transfers between devices with their start and end apart: 57, of which 25 were waited for; matrix products, arithmetic and copies ran while one was open for 13% of the time, Pallas kernels for 19%

profile of v2, /device:TPU:0, one launch (start us, length us, event | category | flops | bytes accessed | tf_op | source)
XLA Modules:
  0.0 320.9 jit_solution(6030488164491198167)
XLA Ops:
  3.2 4.1 %collective-permute-start = (bf16[104,768]{1,0:T(8,128)(2,1)S(1)}, bf16[104,768]{1,0:T(8,128)(2,1)S(1)}, u32[]{:S(2)}, u32[]{:S(2)}) collective-permute-start(bf16[104,768]{1,0:T(8,128)(2,1)S(1)} %concatenate.104), channel_id=1, source_target_pairs={{0,2},{1,3},{2,0},{3,1},{4,6},{5,7},{6,4},{7,5},{8,10},{9,11},{10,... | collective-permute-start | bytes 479240 | tf_op jit(solution)/shard_map/ppermute | solution.py:381
  12.2 2.7 collective-permute-done
  15.6 3.4 %collective-permute-start.2 = (bf16[192,768]{1,0:T(8,128)(2,1)S(1)}, bf16[192,768]{1,0:T(8,128)(2,1)S(1)}, u32[]{:S(2)}, u32[]{:S(2)}) collective-permute-start(bf16[192,768]{1,0:T(8,128)(2,1)S(1)} %pad_maximum_fusion.23), channel_id=1, source_target_pairs={{0,2},{1,3},{2,0},{3,1},{4,6},{5,7},{6,4},{7,5},{8,10},{9,11},{10,... | collective-permute-start | bytes 884744 | tf_op jit(solution)/shard_map/ppermute | solution.py:381
  19.0 9.9 %collective-permute-done.2 = bf16[192,768]{1,0:T(8,128)(2,1)S(1)} collective-permute-done((bf16[192,768]{1,0:T(8,128)(2,1)S(1)}, bf16[192,768]{1,0:T(8,128)(2,1)S(1)}, u32[]{:S(2)}, u32[]{:S(2)}) %collective-permute-start.2) | collective-permute-done | bytes 294944 | tf_op jit(solution)/shard_map/ppermute | solution.py:381
  30.0 3.2 collective-permute-start.3
  37.1 2.8 collective-permute-done.5
  41.2 5.0 %collective-permute-done.3 = bf16[2,192,768]{2,1,0:T(8,128)(2,1)S(1)} collective-permute-done((bf16[2,192,768]{2,1,0:T(8,128)(2,1)S(1)}, bf16[2,192,768]{2,1,0:T(8,128)(2,1)S(1)}, u32[]{:S(2)}, u32[]{:S(2)}) %collective-permute-start.3) | collective-permute-done | bytes 589856 | tf_op jit(solution)/shard_map/ppermute | solution.py:381
  49.5 1.7 collective-permute-start.10
  51.3 1.6 collective-permute-start.11
  52.9 4.1 %collective-permute-done.10 = bf16[3,40,768]{2,1,0:T(8,128)(2,1)S(1)} collective-permute-done((bf16[3,40,768]{2,1,0:T(8,128)(2,1)S(1)}, bf16[3,40,768]{2,1,0:T(8,128)(2,1)S(1)}, u32[]{:S(2)}, u32[]{:S(2)}) %collective-permute-start.10) | collective-permute-done | bytes 184352 | tf_op jit(solution)/shard_map/ppermute | solution.py:381
  57.0 2.5 collective-permute-done.11
  64.8 1.7 collective-permute-start.13
  66.6 2.1 dynamic-slice_bitcast_fusion
  68.7 7.2 %collective-permute-done.7 = bf16[3,1,1,96,768]{4,3,0,2,1:T(8,128)(2,1)} collective-permute-done((bf16[3,1,1,96,768]{4,3,0,2,1:T(8,128)(2,1)}, bf16[3,1,1,96,768]{4,3,0,2,1:T(8,128)(2,1)}, u32[]{:S(2)}, u32[]{:S(2)}) %collective-permute-start.7) | collective-permute-done | bytes 442400 | tf_op jit(solution)/shard_map/ppermute | solution.py:381
  83.1 1.7 broadcast_select_fusion.1
  85.1 2.5 collective-permute-start.17
  89.3 1.8 pad_maximum_fusion.9
  92.7 13.9 %attention.1 = (bf16[4,480,192]{2,1,0:T(8,128)(2,1)}, bf16[4,480,192]{2,1,0:T(8,128)(2,1)}, bf16[4,480,192]{2,1,0:T(8,128)(2,1)}, f32[4,3,480,160]{3,2,1,0:T(8,1...) custom-call(bf16[480,768]{1,0:T(8,128)(2,1)} %bitcast.252, ...), custom_call_target="tpu_custom_call" | custom-call | tf_op jit(solution)/shard_map/attention/pallas_call | solution.py:322
  108.4 1.8 broadcast_select_fusion.7
  111.7 2.4 copy.35
  114.7 8.2 %collective-permute-done.20 = bf16[3,40,768]{2,1,0:T(8,128)(2,1)} collective-permute-done((bf16[3,40,768]{2,1,0:T(8,128)(2,1)}, bf16[3,40,768]{2,1,0:T(8,128)(2,1)}, u32[]{:S(2)}, u32[]{:S(2)}) %collective-permute-start.20) | collective-permute-done | bytes 184352 | tf_op jit(solution)/shard_map/ppermute | solution.py:381
  122.9 2.1 pad_maximum_fusion.10
  125.0 15.8 %ffn.1 = (bf16[4,480,768]{2,1,0:T(8,128)(2,1)}, f32[4,480,768]{2,1,0:T(8,128)}, bf16[480,768]{1,0:T(8,128)(2,1)}, f32[480,768]{1,0:T(8,128)}, bf16[480,768]{1,0:T(8,128)(2,1)}, /*index=5*/f32[8,768]{1,0:T(8,128)}) custom-call(s32[2]{0:T(128)} %pad_add_fusion.here_ref, bf16[480,768]{1,0:T(8,128)(2,1)} %get-tuple-element.192.low_ref, ...), custom_call_target="tpu_custom_call" | custom-call | tf_op jit(solution)/shard_map/ffn/pallas_call | solution.py:322
  140.9 6.1 %down_grad.1 = (bf16[4,384,768]{2,1,0:T(8,128)(2,1)}, bf16[4,384,768]{2,1,0:T(8,128)(2,1)}) custom-call(bf16[4,480,768]{2,1,0:T(8,128)(2,1)} %get-tuple-element.200.act_ref, bf16[480,768]{1,0:T(8,128)(2,1)} %get-tuple-element.203.ffn_low_ref), custom_call_target="tpu_custom_call" | custom-call | tf_op jit(solution)/shard_map/down_grad/pallas_call | solution.py:322
  147.0 11.7 %in_grad.1 = (bf16[4,384,768]{2,1,0:T(8,128)(2,1)}, bf16[4,384,768]{2,1,0:T(8,128)(2,1)}, bf16[4,480,768]{2,1,0:T(8,128)(2,1)}, f32[4,1,768]{2,1,0:T(1,128)}) custom-call(s32[2]{0:T(128)} %pad_add_fusion.here_ref, bf16[480,768]{1,0:T(8,128)(2,1)} %get-tuple-element.203.ffn_low_ref, bf16[480,768]{1,0:T(8,128)(2,1)} %get-tuple-element.192.low_ref, ...), custom_call_target="tpu_custom_call" | custom-call | tf_op jit(solution)/shard_map/in_grad/pallas_call | solution.py:322
  161.4 9.9 %ffn_back.1 = (f32[480,768]{1,0:T(8,128)}, bf16[480,768]{1,0:T(8,128)(2,1)}, f32[8,768]{1,0:T(8,128)}) custom-call(s32[2]{0:T(128)} %pad_add_fusion.here_ref, bf16[4,480,768]{2,1,0:T(8,128)(2,1)} %get-tuple-element.211.pre_grad_ref, bf16[2,384,768]{2,1,0:T(8,128)(2,1)} %bitcast.236, bf16[2,384,768]{2,1,0:T(8,128)(2,1)} %bitcast.237, ...), custom_call_target="tpu_custom_call" | custom-call | tf_op jit(solution)/shard_map/ffn_back/pallas_call | solution.py:322
  171.4 1.7 copy-done.1
  173.1 2.3 add.195
  177.0 2.2 collective-permute-start.26
  179.2 2.2 collective-permute-start.27
  181.4 22.0 %attention_back.1 = (bf16[4,192,768]{2,1,0:T(8,128)(2,1)}, bf16[4,192,768]{2,1,0:T(8,128)(2,1)}, bf16[2,4,192,768]{3,2,1,0:T(8,128)(2,1)}, f32[24,768]{1,0:T(8,128)}, bf16[480,768]{1,0:T(8,128)(2,1)}) custom-call(s32[2]{0:T(128)} %pad_add_fusion.here_ref, bf16[480,768]{1,0:T(8,128)(2,1)} %bitcast.253, bf16[480,768]{1,0:T(8,128)(2,1)} %get-tuple-element.225.attn_low_ref, ...), custom_call_target="tpu_custom_call" | custom-call | tf_op jit(solution)/shard_map/attention_back/pallas_call | solution.py:322
  203.4 2.0 slice_bitcast_fusion.13
  213.1 5.1 %collective-permute-done.32 = bf16[3,40,768]{2,1,0:T(8,128)(2,1)S(1)} collective-permute-done((bf16[3,40,768]{2,1,0:T(8,128)(2,1)S(1)}, bf16[3,40,768]{2,1,0:T(8,128)(2,1)S(1)}, u32[]{:S(2)}, u32[]{:S(2)}) %collective-permute-start.32) | collective-permute-done | bytes 184352 | tf_op jit(solution)/shard_map/ppermute | solution.py:381
  218.2 3.4 %collective-permute-done.29.refs_4_ = bf16[4,1,96,768]{3,2,1,0:T(8,128)(2,1)S(1)} collective-permute-done((bf16[4,1,96,768]{3,2,1,0:T(8,128)(2,1)S(1)}, bf16[4,1,96,768]{3,2,1,0:T(8,128)(2,1)S(1)}, u32[]{:S(2)}, u32[]{:S(2)}) %collective-permute-start.29) | collective-permute-done | bytes 589856 | tf_op jit(solution)/shard_map/ppermute | solution.py:381
  221.5 2.2 collective-permute-done.28.refs_4_
  231.0 2.0 collective-permute-start.36
  233.9 10.2 %collective-permute-done.37 = f32[24,768]{1,0:T(8,128)S(1)} collective-permute-done((f32[24,768]{1,0:T(8,128)S(1)}, f32[24,768]{1,0:T(8,128)S(1)}, u32[]{:S(2)}, u32[]{:S(2)}) %collective-permute-start.37) | collective-permute-done | bytes 73760 | tf_op jit(solution)/shard_map/ppermute | solution.py:381
  244.1 4.7 %collective-permute-done.36 = bf16[3,40,768]{2,1,0:T(8,128)(2,1)S(1)} collective-permute-done((bf16[3,40,768]{2,1,0:T(8,128)(2,1)S(1)}, bf16[3,40,768]{2,1,0:T(8,128)(2,1)S(1)}, u32[]{:S(2)}, u32[]{:S(2)}) %collective-permute-start.36) | collective-permute-done | bytes 184352 | tf_op jit(solution)/shard_map/ppermute | solution.py:381
  252.4 5.9 %collective-permute-done.41 = f32[24,768]{1,0:T(8,128)S(1)} collective-permute-done((f32[24,768]{1,0:T(8,128)S(1)}, f32[24,768]{1,0:T(8,128)S(1)}, u32[]{:S(2)}, u32[]{:S(2)}) %collective-permute-start.41) | collective-permute-done | bytes 73760 | tf_op jit(solution)/shard_map/ppermute | solution.py:381
  258.4 4.4 %collective-permute-done.40 = bf16[192,768]{1,0:T(8,128)(2,1)S(1)} collective-permute-done((bf16[192,768]{1,0:T(8,128)(2,1)S(1)}, bf16[192,768]{1,0:T(8,128)(2,1)S(1)}, u32[]{:S(2)}, u32[]{:S(2)}) %collective-permute-start.40) | collective-permute-done | bytes 294944 | tf_op jit(solution)/shard_map/ppermute | solution.py:381
  264.5 2.1 collective-permute-start.45
  266.7 11.2 %collective-permute-done.46 = f32[24,768]{1,0:T(8,128)S(1)} collective-permute-done((f32[24,768]{1,0:T(8,128)S(1)}, f32[24,768]{1,0:T(8,128)S(1)}, u32[]{:S(2)}, u32[]{:S(2)}) %collective-permute-start.46) | collective-permute-done | bytes 73760 | tf_op jit(solution)/shard_map/ppermute | solution.py:381
  283.6 2.5 collective-permute-start.50
  287.9 5.0 %collective-permute-done.50 = f32[24,768]{1,0:T(8,128)S(1)} collective-permute-done((f32[24,768]{1,0:T(8,128)S(1)}, f32[24,768]{1,0:T(8,128)S(1)}, u32[]{:S(2)}, u32[]{:S(2)}) %collective-permute-start.50) | collective-permute-done | bytes 73760 | tf_op jit(solution)/shard_map/ppermute | solution.py:381
  298.6 1.8 collective-permute-start.52
  307.2 3.1 collective-permute-done.55
  312.8 2.0 copy.42
  314.7 2.6 fusion
  (298 shorter events, 88.4 us)
Async XLA Ops:
  3.2 11.6 %collective-permute-start = (bf16[104,768]{1,0:T(8,128)(2,1)S(1)}, bf16[104,768]{1,0:T(8,128)(2,1)S(1)}, u32[]{:S(2)}, u32[]{:S(2)}) collective-permute-start(bf16[104,768]{1,0:T(8,128)(2,1)S(1)} %concatenate.104), channel_id=1, source_target_pairs={{0,2},{1,3},{2,0},{3,1},{4,6},{5,7},{6,4},{7,5},{8,10},{9,11},{10,... | collective-permute-start | bytes 479240 | tf_op jit(solution)/shard_map/ppermute | solution.py:381
  14.9 15.1 %collective-permute-start.1 = (bf16[2,104,768]{2,1,0:T(8,128)(2,1)S(1)}, bf16[2,104,768]{2,1,0:T(8,128)(2,1)S(1)}, u32[]{:S(2)}, u32[]{:S(2)}) collective-permute-start(bf16[2,104,768]{2,1,0:T(8,128)(2,1)S(1)} %pad_maximum_fusion.22), channel_id=1, source_target_pairs={{0,1},{1,0},{2,3},{3,2},{4,5},{5,4},{6,7},{7,6},{8,9},{9,8},{10,11... | collective-permute-start | bytes 958472 | tf_op jit(solution)/shard_map/ppermute | solution.py:381
  15.6 13.3 %collective-permute-start.2 = (bf16[192,768]{1,0:T(8,128)(2,1)S(1)}, bf16[192,768]{1,0:T(8,128)(2,1)S(1)}, u32[]{:S(2)}, u32[]{:S(2)}) collective-permute-start(bf16[192,768]{1,0:T(8,128)(2,1)S(1)} %pad_maximum_fusion.23), channel_id=1, source_target_pairs={{0,2},{1,3},{2,0},{3,1},{4,6},{5,7},{6,4},{7,5},{8,10},{9,11},{10,... | collective-permute-start | bytes 884744 | tf_op jit(solution)/shard_map/ppermute | solution.py:381
  30.0 16.1 %collective-permute-start.3 = (bf16[2,192,768]{2,1,0:T(8,128)(2,1)S(1)}, bf16[2,192,768]{2,1,0:T(8,128)(2,1)S(1)}, u32[]{:S(2)}, u32[]{:S(2)}) collective-permute-start(bf16[2,192,768]{2,1,0:T(8,128)(2,1)S(1)} %pad_maximum_fusion.14), channel_id=1, source_target_pairs={{0,1},{1,0},{2,3},{3,2},{4,5},{5,4},{6,7},{7,6},{8,9},{9,8},{10,11... | collective-permute-start | bytes 1769480 | tf_op jit(solution)/shard_map/ppermute | solution.py:381
  46.3 13.2 %collective-permute-start.9 = (bf16[3,2,1,48,768]{4,3,0,2,1:T(8,128)(2,1)S(1)}, bf16[3,2,1,48,768]{4,3,0,2,1:T(8,128)(2,1)S(1)}, u32[]{:S(2)}, u32[]{:S(2)}) collective-permute-start(bf16[3,2,1,48,768]{4,3,0,2,1:T(8,128)(2,1)S(1)} %pad_maximum_fusion.21), channel_id=1, source_target_pairs={{0,8},{4,12},{8,0},{12,4},{16,24},{20,28},{24,16},{28,20},{1,9},{5... | collective-permute-start | bytes 1327112 | tf_op jit(solution)/shard_map/ppermute | solution.py:381
  47.9 12.2 %collective-permute-start.8 = (bf16[3,1,2,48,768]{4,3,0,2,1:T(8,128)(2,1)S(1)}, bf16[3,1,2,48,768]{4,3,0,2,1:T(8,128)(2,1)S(1)}, u32[]{:S(2)}, u32[]{:S(2)}) collective-permute-start(bf16[3,1,2,48,768]{4,3,0,2,1:T(8,128)(2,1)S(1)} %pad_maximum_fusion.20), channel_id=1, source_target_pairs={{0,16},{4,20},{8,24},{12,28},{16,0},{20,4},{24,8},{28,12},{1,17},{... | collective-permute-start | bytes 1327112 | tf_op jit(solution)/shard_map/ppermute | solution.py:381
  49.5 7.5 %collective-permute-start.10 = (bf16[3,40,768]{2,1,0:T(8,128)(2,1)S(1)}, bf16[3,40,768]{2,1,0:T(8,128)(2,1)S(1)}, u32[]{:S(2)}, u32[]{:S(2)}) collective-permute-start(bf16[3,40,768]{2,1,0:T(8,128)(2,1)S(1)} %get-tuple-element.166), channel_id=1, source_target_pairs={{0,1},{1,0},{2,3},{3,2},{4,5},{5,4},{6,7},{7,6},{8,9},{9,8},{10,11... | collective-permute-start | bytes 552968 | tf_op jit(solution)/shard_map/ppermute | solution.py:381
  51.3 8.2 %collective-permute-start.11 = (bf16[3,40,768]{2,1,0:T(8,128)(2,1)S(1)}, bf16[3,40,768]{2,1,0:T(8,128)(2,1)S(1)}, u32[]{:S(2)}, u32[]{:S(2)}) collective-permute-start(bf16[3,40,768]{2,1,0:T(8,128)(2,1)S(1)} %get-tuple-element.167), channel_id=1, source_target_pairs={{0,3},{1,2},{2,1},{3,0},{4,7},{5,6},{6,5},{7,4},{8,11},{9,10},{10,... | collective-permute-start | bytes 552968 | tf_op jit(solution)/shard_map/ppermute | solution.py:381
  62.0 14.9 %collective-permute-start.12 = (bf16[2,3,192,768]{3,2,1,0:T(8,128)(2,1)}, bf16[2,3,192,768]{3,2,1,0:T(8,128)(2,1)}, u32[]{:S(2)}, u32[]{:S(2)}) collective-permute-start(bf16[2,3,192,768]{3,2,1,0:T(8,128)(2,1)} %pad_maximum_fusion), channel_id=1, source_target_pairs={{0,4},{4,0},{8,12},{12,8},{16,20},{20,16},{24,28},{28,24},{1,5},{5... | collective-permute-start | bytes 5308424 | tf_op jit(solution)/shard_map/ppermute | solution.py:381
  63.0 12.9 %collective-permute-start.7 = (bf16[3,1,1,96,768]{4,3,0,2,1:T(8,128)(2,1)}, bf16[3,1,1,96,768]{4,3,0,2,1:T(8,128)(2,1)}, u32[]{:S(2)}, u32[]{:S(2)}) collective-permute-start(bf16[3,1,1,96,768]{4,3,0,2,1:T(8,128)(2,1)} %maximum_bitcast_fusion.4), channel_id=1, source_target_pairs={{0,16},{4,20},{8,24},{12,28},{16,0},{20,4},{24,8},{28,12},{1,17},{... | collective-permute-start | bytes 1327112 | tf_op jit(solution)/shard_map/ppermute | solution.py:381
  64.3 12.7 %collective-permute-start.6 = (bf16[3,1,1,96,768]{4,3,0,2,1:T(8,128)(2,1)}, bf16[3,1,1,96,768]{4,3,0,2,1:T(8,128)(2,1)}, u32[]{:S(2)}, u32[]{:S(2)}) collective-permute-start(bf16[3,1,1,96,768]{4,3,0,2,1:T(8,128)(2,1)} %maximum_bitcast_fusion.3), channel_id=1, source_target_pairs={{0,8},{4,12},{8,0},{12,4},{16,24},{20,28},{24,16},{28,20},{1,9},{5... | collective-permute-start | bytes 1327112 | tf_op jit(solution)/shard_map/ppermute | solution.py:381
  64.8 12.1 %collective-permute-start.13 = (bf16[3,40,768]{2,1,0:T(8,128)(2,1)}, bf16[3,40,768]{2,1,0:T(8,128)(2,1)}, u32[]{:S(2)}, u32[]{:S(2)}) collective-permute-start(bf16[3,40,768]{2,1,0:T(8,128)(2,1)} %get-tuple-element.172), channel_id=1, source_target_pairs={{0,2},{1,3},{2,0},{3,1},{4,6},{5,7},{6,4},{7,5},{8,10},{9,11},{10,... | collective-permute-start | bytes 552968 | tf_op jit(solution)/shard_map/ppermute | solution.py:381
  78.3 28.3 %collective-permute-start.15 = (bf16[3,2,1,96,768]{4,3,0,2,1:T(8,128)(2,1)S(1)}, bf16[3,2,1,96,768]{4,3,0,2,1:T(8,128)(2,1)}, u32[]{:S(2)}, u32[]{:S(2)}) collective-permute-start(bf16[3,2,1,96,768]{4,3,0,2,1:T(8,128)(2,1)S(1)} %pad_maximum_fusion.7), channel_id=1, source_target_pairs={{0,8},{4,12},{8,0},{12,4},{16,24},{20,28},{24,16},{28,20},{1,9},{5... | collective-permute-start | bytes 2654216 | tf_op jit(solution)/shard_map/ppermute | solution.py:381
  81.6 25.0 %collective-permute-start.14 = (bf16[3,1,2,96,768]{4,3,0,2,1:T(8,128)(2,1)}, bf16[3,1,2,96,768]{4,3,0,2,1:T(8,128)(2,1)}, u32[]{:S(2)}, u32[]{:S(2)}) collective-permute-start(bf16[3,1,2,96,768]{4,3,0,2,1:T(8,128)(2,1)} %pad_maximum_fusion.6), channel_id=1, source_target_pairs={{0,16},{4,20},{8,24},{12,28},{16,0},{20,4},{24,8},{28,12},{1,17},{... | collective-permute-start | bytes 2654216 | tf_op jit(solution)/shard_map/ppermute | solution.py:381
  85.0 21.6 %collective-permute-start.16 = (bf16[3,40,768]{2,1,0:T(8,128)(2,1)}, bf16[3,40,768]{2,1,0:T(8,128)(2,1)S(1)}, u32[]{:S(2)}, u32[]{:S(2)}) collective-permute-start(bf16[3,40,768]{2,1,0:T(8,128)(2,1)} %get-tuple-element.184), channel_id=1, source_target_pairs={{0,1},{1,0},{2,3},{3,2},{4,5},{5,4},{6,7},{7,6},{8,9},{9,8},{10,11... | collective-permute-start | bytes 552968 | tf_op jit(solution)/shard_map/ppermute | solution.py:381
  85.1 21.6 %collective-permute-start.17 = (bf16[3,40,768]{2,1,0:T(8,128)(2,1)}, bf16[3,40,768]{2,1,0:T(8,128)(2,1)S(1)}, u32[]{:S(2)}, u32[]{:S(2)}) collective-permute-start(bf16[3,40,768]{2,1,0:T(8,128)(2,1)} %get-tuple-element.185), channel_id=1, source_target_pairs={{0,3},{1,2},{2,1},{3,0},{4,7},{5,6},{6,5},{7,4},{8,11},{9,10},{10,... | collective-permute-start | bytes 552968 | tf_op jit(solution)/shard_map/ppermute | solution.py:381
  108.4 14.6 %collective-permute-start.19 = (bf16[3,384,768]{2,1,0:T(8,128)(2,1)S(1)}, bf16[3,384,768]{2,1,0:T(8,128)(2,1)}, u32[]{:S(2)}, u32[]{:S(2)}) collective-permute-start(bf16[3,384,768]{2,1,0:T(8,128)(2,1)S(1)} %bitcast.242), channel_id=1, source_target_pairs={{0,4},{4,0},{8,12},{12,8},{16,20},{20,16},{24,28},{28,24},{1,5},{5... | collective-permute-start | bytes 5308424 | tf_op jit(solution)/shard_map/ppermute | solution.py:381
  110.6 12.3 %collective-permute-start.18 = (bf16[3,384,768]{2,1,0:T(8,128)(2,1)S(1)}, bf16[3,384,768]{2,1,0:T(8,128)(2,1)}, u32[]{:S(2)}, u32[]{:S(2)}) collective-permute-start(bf16[3,384,768]{2,1,0:T(8,128)(2,1)S(1)} %bitcast.245), channel_id=1, source_target_pairs={{0,4},{4,0},{8,12},{12,8},{16,20},{20,16},{24,28},{28,24},{1,5},{5... | collective-permute-start | bytes 5308424 | tf_op jit(solution)/shard_map/ppermute | solution.py:381
  110.7 12.2 %collective-permute-start.20 = (bf16[3,40,768]{2,1,0:T(8,128)(2,1)}, bf16[3,40,768]{2,1,0:T(8,128)(2,1)}, u32[]{:S(2)}, u32[]{:S(2)}) collective-permute-start(bf16[3,40,768]{2,1,0:T(8,128)(2,1)} %get-tuple-element.190), channel_id=1, source_target_pairs={{0,2},{1,3},{2,0},{3,1},{4,6},{5,7},{6,4},{7,5},{8,10},{9,11},{10,... | collective-permute-start | bytes 552968 | tf_op jit(solution)/shard_map/ppermute | solution.py:381
  146.9 12.6 %collective-permute-start.21 = (bf16[4,384,768]{2,1,0:T(8,128)(2,1)}, bf16[4,384,768]{2,1,0:T(8,128)(2,1)S(1)}, u32[]{:S(2)}, u32[]{:S(2)}) collective-permute-start(bf16[4,384,768]{2,1,0:T(8,128)(2,1)} %get-tuple-element.206), channel_id=1, source_target_pairs={{0,4},{4,0},{8,12},{12,8},{16,20},{20,16},{24,28},{28,24},{1,5},{5... | collective-permute-start | bytes 7077896 | tf_op jit(solution)/shard_map/ppermute | solution.py:381
  159.5 11.9 %collective-permute-start.22 = (bf16[4,384,768]{2,1,0:T(8,128)(2,1)}, bf16[4,384,768]{2,1,0:T(8,128)(2,1)}, u32[]{:S(2)}, u32[]{:S(2)}) collective-permute-start(bf16[4,384,768]{2,1,0:T(8,128)(2,1)} %get-tuple-element.210), channel_id=1, source_target_pairs={{0,4},{4,0},{8,12},{12,8},{16,20},{20,16},{24,28},{28,24},{1,5},{5... | collective-permute-start | bytes 7077896 | tf_op jit(solution)/shard_map/ppermute | solution.py:381
  175.3 30.1 %collective-permute-start.23 = (bf16[4,2,96,768]{3,2,1,0:T(8,128)(2,1)}, bf16[4,2,96,768]{3,2,1,0:T(8,128)(2,1)}, u32[]{:S(2)}, u32[]{:S(2)}) collective-permute-start(bf16[4,2,96,768]{3,2,1,0:T(8,128)(2,1)} %add.195), channel_id=1, source_target_pairs={{0,8},{4,12},{8,0},{12,4},{16,24},{20,28},{24,16},{28,20},{1,9},{5... | collective-permute-start | bytes 3538952 | tf_op jit(solution)/shard_map/ppermute | solution.py:381
  176.5 29.0 %collective-permute-start.24 = (bf16[4,2,96,768]{3,2,1,0:T(8,128)(2,1)}, bf16[4,2,96,768]{3,2,1,0:T(8,128)(2,1)S(1)}, u32[]{:S(2)}, u32[]{:S(2)}) collective-permute-start(bf16[4,2,96,768]{3,2,1,0:T(8,128)(2,1)} %add.196), channel_id=1, source_target_pairs={{0,16},{4,20},{8,24},{12,28},{16,0},{20,4},{24,8},{28,12},{1,17},{... | collective-permute-start | bytes 3538952 | tf_op jit(solution)/shard_map/ppermute | solution.py:381
  177.0 28.4 %collective-permute-start.25 = (bf16[3,40,768]{2,1,0:T(8,128)(2,1)}, bf16[3,40,768]{2,1,0:T(8,128)(2,1)}, u32[]{:S(2)}, u32[]{:S(2)}) collective-permute-start(bf16[3,40,768]{2,1,0:T(8,128)(2,1)} %get-tuple-element.222), channel_id=1, source_target_pairs={{0,1},{1,0},{2,3},{3,2},{4,5},{5,4},{6,7},{7,6},{8,9},{9,8},{10,11... | collective-permute-start | bytes 552968 | tf_op jit(solution)/shard_map/ppermute | solution.py:381
  177.0 28.4 %collective-permute-start.26 = (bf16[3,40,768]{2,1,0:T(8,128)(2,1)}, bf16[3,40,768]{2,1,0:T(8,128)(2,1)}, u32[]{:S(2)}, u32[]{:S(2)}) collective-permute-start(bf16[3,40,768]{2,1,0:T(8,128)(2,1)} %get-tuple-element.223), channel_id=1, source_target_pairs={{0,2},{1,3},{2,0},{3,1},{4,6},{5,7},{6,4},{7,5},{8,10},{9,11},{10,... | collective-permute-start | bytes 552968 | tf_op jit(solution)/shard_map/ppermute | solution.py:381
  179.2 26.2 %collective-permute-start.27 = (bf16[3,40,768]{2,1,0:T(8,128)(2,1)}, bf16[3,40,768]{2,1,0:T(8,128)(2,1)}, u32[]{:S(2)}, u32[]{:S(2)}) collective-permute-start(bf16[3,40,768]{2,1,0:T(8,128)(2,1)} %get-tuple-element.224), channel_id=1, source_target_pairs={{0,3},{1,2},{2,1},{3,0},{4,7},{5,6},{6,5},{7,4},{8,11},{9,10},{10,... | collective-permute-start | bytes 552968 | tf_op jit(solution)/shard_map/ppermute | solution.py:381
  205.4 18.3 %collective-permute-start.30 = (bf16[2,4,192,768]{3,2,1,0:T(8,128)(2,1)}, bf16[2,4,192,768]{3,2,1,0:T(8,128)(2,1)S(1)}, u32[]{:S(2)}, u32[]{:S(2)}) collective-permute-start(bf16[2,4,192,768]{3,2,1,0:T(8,128)(2,1)} %get-tuple-element.245), channel_id=1, source_target_pairs={{0,4},{4,0},{8,12},{12,8},{16,20},{20,16},{24,28},{28,24},{1,5},{5... | collective-permute-start | bytes 7077896 | tf_op jit(solution)/shard_map/ppermute | solution.py:381
  205.7 15.8 %collective-permute-start.29 = (bf16[4,1,96,768]{3,2,1,0:T(8,128)(2,1)S(1)}, bf16[4,1,96,768]{3,2,1,0:T(8,128)(2,1)S(1)}, u32[]{:S(2)}, u32[]{:S(2)}) collective-permute-start(bf16[4,1,96,768]{3,2,1,0:T(8,128)(2,1)S(1)} %add.198), channel_id=1, source_target_pairs={{0,8},{4,12},{8,0},{12,4},{16,24},{20,28},{24,16},{28,20},{1,9},{5... | collective-permute-start | bytes 1769480 | tf_op jit(solution)/shard_map/ppermute | solution.py:381
  208.6 15.1 %collective-permute-start.28 = (bf16[4,1,96,768]{3,2,1,0:T(8,128)(2,1)S(1)}, bf16[4,1,96,768]{3,2,1,0:T(8,128)(2,1)S(1)}, u32[]{:S(2)}, u32[]{:S(2)}) collective-permute-start(bf16[4,1,96,768]{3,2,1,0:T(8,128)(2,1)S(1)} %add.197), channel_id=1, source_target_pairs={{0,16},{4,20},{8,24},{12,28},{16,0},{20,4},{24,8},{28,12},{1,17},{... | collective-permute-start | bytes 1769480 | tf_op jit(solution)/shard_map/ppermute | solution.py:381
  210.2 8.0 %collective-permute-start.32 = (bf16[3,40,768]{2,1,0:T(8,128)(2,1)S(1)}, bf16[3,40,768]{2,1,0:T(8,128)(2,1)S(1)}, u32[]{:S(2)}, u32[]{:S(2)}) collective-permute-start(bf16[3,40,768]{2,1,0:T(8,128)(2,1)S(1)} %get-tuple-element.247), channel_id=1, source_target_pairs={{0,3},{1,2},{2,1},{3,0},{4,7},{5,6},{6,5},{7,4},{8,11},{9,10},{10,... | collective-permute-start | bytes 552968 | tf_op jit(solution)/shard_map/ppermute | solution.py:381
  228.2 20.5 %collective-permute-start.33 = (bf16[4,2,48,768]{3,2,1,0:T(8,128)(2,1)S(1)}, bf16[4,2,48,768]{3,2,1,0:T(8,128)(2,1)S(1)}, u32[]{:S(2)}, u32[]{:S(2)}) collective-permute-start(bf16[4,2,48,768]{3,2,1,0:T(8,128)(2,1)S(1)} %add.201), channel_id=1, source_target_pairs={{0,8},{4,12},{8,0},{12,4},{16,24},{20,28},{24,16},{28,20},{1,9},{5... | collective-permute-start | bytes 1769480 | tf_op jit(solution)/shard_map/ppermute | solution.py:381
  229.4 19.3 %collective-permute-start.34 = (bf16[4,2,48,768]{3,2,1,0:T(8,128)(2,1)S(1)}, bf16[4,2,48,768]{3,2,1,0:T(8,128)(2,1)S(1)}, u32[]{:S(2)}, u32[]{:S(2)}) collective-permute-start(bf16[4,2,48,768]{3,2,1,0:T(8,128)(2,1)S(1)} %add.202), channel_id=1, source_target_pairs={{0,16},{4,20},{8,24},{12,28},{16,0},{20,4},{24,8},{28,12},{1,17},{... | collective-permute-start | bytes 1769480 | tf_op jit(solution)/shard_map/ppermute | solution.py:381
  230.9 17.8 %collective-permute-start.35 = (bf16[2,192,768]{2,1,0:T(8,128)(2,1)S(1)}, bf16[2,192,768]{2,1,0:T(8,128)(2,1)S(1)}, u32[]{:S(2)}, u32[]{:S(2)}) collective-permute-start(bf16[2,192,768]{2,1,0:T(8,128)(2,1)S(1)} %pad_maximum_fusion.15), channel_id=1, source_target_pairs={{0,1},{1,0},{2,3},{3,2},{4,5},{5,4},{6,7},{7,6},{8,9},{9,8},{10,11... | collective-permute-start | bytes 1769480 | tf_op jit(solution)/shard_map/ppermute | solution.py:381
  231.0 17.8 %collective-permute-start.36 = (bf16[3,40,768]{2,1,0:T(8,128)(2,1)S(1)}, bf16[3,40,768]{2,1,0:T(8,128)(2,1)S(1)}, u32[]{:S(2)}, u32[]{:S(2)}) collective-permute-start(bf16[3,40,768]{2,1,0:T(8,128)(2,1)S(1)} %get-tuple-element.259), channel_id=1, source_target_pairs={{0,1},{1,0},{2,3},{3,2},{4,5},{5,4},{6,7},{7,6},{8,9},{9,8},{10,11... | collective-permute-start | bytes 552968 | tf_op jit(solution)/shard_map/ppermute | solution.py:381
  233.0 11.1 %collective-permute-start.37 = (f32[24,768]{1,0:T(8,128)S(1)}, f32[24,768]{1,0:T(8,128)S(1)}, u32[]{:S(2)}, u32[]{:S(2)}) collective-permute-start(f32[24,768]{1,0:T(8,128)S(1)} %add.147), channel_id=1, source_target_pairs={{0,8},{4,12},{8,0},{12,4},{16,24},{20,28},{24,16},{28,20},{1,9},{5... | collective-permute-start | bytes 221192 | tf_op jit(solution)/shard_map/ppermute | solution.py:381
  248.9 13.9 %collective-permute-start.40 = (bf16[192,768]{1,0:T(8,128)(2,1)S(1)}, bf16[192,768]{1,0:T(8,128)(2,1)S(1)}, u32[]{:S(2)}, u32[]{:S(2)}) collective-permute-start(bf16[192,768]{1,0:T(8,128)(2,1)S(1)} %fusion.3), channel_id=1, source_target_pairs={{0,2},{1,3},{2,0},{3,1},{4,6},{5,7},{6,4},{7,5},{8,10},{9,11},{10,... | collective-permute-start | bytes 884744 | tf_op jit(solution)/shard_map/ppermute | solution.py:381
  249.7 13.1 %collective-permute-start.39 = (bf16[4,1,48,768]{3,2,1,0:T(8,128)(2,1)S(1)}, bf16[4,1,48,768]{3,2,1,0:T(8,128)(2,1)S(1)}, u32[]{:S(2)}, u32[]{:S(2)}) collective-permute-start(bf16[4,1,48,768]{3,2,1,0:T(8,128)(2,1)S(1)} %add.204), channel_id=1, source_target_pairs={{0,8},{4,12},{8,0},{12,4},{16,24},{20,28},{24,16},{28,20},{1,9},{5... | collective-permute-start | bytes 884744 | tf_op jit(solution)/shard_map/ppermute | solution.py:381
  250.3 12.5 %collective-permute-start.38 = (bf16[4,1,48,768]{3,2,1,0:T(8,128)(2,1)S(1)}, bf16[4,1,48,768]{3,2,1,0:T(8,128)(2,1)S(1)}, u32[]{:S(2)}, u32[]{:S(2)}) collective-permute-start(bf16[4,1,48,768]{3,2,1,0:T(8,128)(2,1)S(1)} %add.203), channel_id=1, source_target_pairs={{0,16},{4,20},{8,24},{12,28},{16,0},{20,4},{24,8},{28,12},{1,17},{... | collective-permute-start | bytes 884744 | tf_op jit(solution)/shard_map/ppermute | solution.py:381
  263.4 14.6 %collective-permute-start.44 = (bf16[2,96,768]{2,1,0:T(8,128)(2,1)S(1)}, bf16[2,96,768]{2,1,0:T(8,128)(2,1)S(1)}, u32[]{:S(2)}, u32[]{:S(2)}) collective-permute-start(bf16[2,96,768]{2,1,0:T(8,128)(2,1)S(1)} %pad_maximum_fusion.24), channel_id=1, source_target_pairs={{0,1},{1,0},{2,3},{3,2},{4,5},{5,4},{6,7},{7,6},{8,9},{9,8},{10,11... | collective-permute-start | bytes 884744 | tf_op jit(solution)/shard_map/ppermute | solution.py:381
  263.5 14.4 %collective-permute-start.42 = (bf16[1,1,1,96,768]{4,3,2,1,0:T(8,128)(2,1)S(1)}, bf16[1,1,1,96,768]{4,3,2,1,0:T(8,128)(2,1)S(1)}, u32[]{:S(2)}, u32[]{:S(2)}) collective-permute-start(bf16[1,1,1,96,768]{4,3,2,1,0:T(8,128)(2,1)S(1)} %get-tuple-element.274), channel_id=1, source_target_pairs={{0,8},{4,12},{8,0},{12,4},{16,24},{20,28},{24,16},{28,20},{1,9},{5... | collective-permute-start | bytes 442376 | tf_op jit(solution)/shard_map/ppermute | solution.py:381
  264.0 13.9 %collective-permute-start.43 = (bf16[1,1,1,96,768]{4,3,2,1,0:T(8,128)(2,1)S(1)}, bf16[1,1,1,96,768]{4,3,2,1,0:T(8,128)(2,1)S(1)}, u32[]{:S(2)}, u32[]{:S(2)}) collective-permute-start(bf16[1,1,1,96,768]{4,3,2,1,0:T(8,128)(2,1)S(1)} %get-tuple-element.275), channel_id=1, source_target_pairs={{0,16},{4,20},{8,24},{12,28},{16,0},{20,4},{24,8},{28,12},{1,17},{... | collective-permute-start | bytes 442376 | tf_op jit(solution)/shard_map/ppermute | solution.py:381
  264.5 13.4 %collective-permute-start.45 = (bf16[3,40,768]{2,1,0:T(8,128)(2,1)}, bf16[3,40,768]{2,1,0:T(8,128)(2,1)S(1)}, u32[]{:S(2)}, u32[]{:S(2)}) collective-permute-start(bf16[3,40,768]{2,1,0:T(8,128)(2,1)} %get-tuple-element.277), channel_id=1, source_target_pairs={{0,2},{1,3},{2,0},{3,1},{4,6},{5,7},{6,4},{7,5},{8,10},{9,11},{10,... | collective-permute-start | bytes 552968 | tf_op jit(solution)/shard_map/ppermute | solution.py:381
  266.6 11.3 %collective-permute-start.46 = (f32[24,768]{1,0:T(8,128)S(1)}, f32[24,768]{1,0:T(8,128)S(1)}, u32[]{:S(2)}, u32[]{:S(2)}) collective-permute-start(f32[24,768]{1,0:T(8,128)S(1)} %add.153), channel_id=1, source_target_pairs={{0,1},{1,0},{2,3},{3,2},{4,5},{5,4},{6,7},{7,6},{8,9},{9,8},{10,11... | collective-permute-start | bytes 221192 | tf_op jit(solution)/shard_map/ppermute | solution.py:381
  278.8 14.1 %collective-permute-start.48 = (bf16[1,2,1,96,768]{4,3,2,1,0:T(8,128)(2,1)}, bf16[1,2,1,96,768]{4,3,2,1,0:T(8,128)(2,1)}, u32[]{:S(2)}, u32[]{:S(2)}) collective-permute-start(bf16[1,2,1,96,768]{4,3,2,1,0:T(8,128)(2,1)} %pad_maximum_fusion.27), channel_id=1, source_target_pairs={{0,8},{4,12},{8,0},{12,4},{16,24},{20,28},{24,16},{28,20},{1,9},{5... | collective-permute-start | bytes 884744 | tf_op jit(solution)/shard_map/ppermute | solution.py:381
  280.1 12.9 %collective-permute-start.47 = (bf16[1,1,2,96,768]{4,3,2,1,0:T(8,128)(2,1)}, bf16[1,1,2,96,768]{4,3,2,1,0:T(8,128)(2,1)}, u32[]{:S(2)}, u32[]{:S(2)}) collective-permute-start(bf16[1,1,2,96,768]{4,3,2,1,0:T(8,128)(2,1)} %pad_maximum_fusion.26), channel_id=1, source_target_pairs={{0,16},{4,20},{8,24},{12,28},{16,0},{20,4},{24,8},{28,12},{1,17},{... | collective-permute-start | bytes 884744 | tf_op jit(solution)/shard_map/ppermute | solution.py:381
  281.2 11.7 %collective-permute-start.49 = (bf16[96,768]{1,0:T(8,128)(2,1)}, bf16[96,768]{1,0:T(8,128)(2,1)}, u32[]{:S(2)}, u32[]{:S(2)}) collective-permute-start(bf16[96,768]{1,0:T(8,128)(2,1)} %fusion.6), channel_id=1, source_target_pairs={{0,2},{1,3},{2,0},{3,1},{4,6},{5,7},{6,4},{7,5},{8,10},{9,11},{10,... | collective-permute-start | bytes 442376 | tf_op jit(solution)/shard_map/ppermute | solution.py:381
  283.6 9.3 %collective-permute-start.50 = (f32[24,768]{1,0:T(8,128)S(1)}, f32[24,768]{1,0:T(8,128)S(1)}, u32[]{:S(2)}, u32[]{:S(2)}) collective-permute-start(f32[24,768]{1,0:T(8,128)S(1)} %add.157), channel_id=1, source_target_pairs={{0,2},{1,3},{2,0},{3,1},{4,6},{5,7},{6,4},{7,5},{8,10},{9,11},{10,... | collective-permute-start | bytes 221192 | tf_op jit(solution)/shard_map/ppermute | solution.py:381
  295.2 9.6 %collective-permute-start.51 = (bf16[2,1,384,768]{3,2,1,0:T(8,128)(2,1)S(1)}, bf16[2,1,384,768]{3,2,1,0:T(8,128)(2,1)S(1)}, u32[]{:S(2)}, u32[]{:S(2)}) collective-permute-start(bf16[2,1,384,768]{3,2,1,0:T(8,128)(2,1)S(1)} %pad_maximum_fusion.3), channel_id=1, source_target_pairs={{0,4},{4,0},{8,12},{12,8},{16,20},{20,16},{24,28},{28,24},{1,5},{5... | collective-permute-start | bytes 3538952 | tf_op jit(solution)/shard_map/ppermute | solution.py:381
  (48 other events, 228.1 us)

commit v3 on v2

--- a/solution.py
+++ b/solution.py
@@ -14,8 +14,7 @@
 DENSITY = 0.3989422804014327
 F32 = jnp.float32
 BF16 = jnp.bfloat16
-VMEM_BYTES = 58 * 1024 * 1024
-SMALL_VMEM_BYTES = 16 * 1024 * 1024
+MIB = 1024 * 1024
 
 
 def dot(one, two, one_axis, two_axis):
@@ -57,8 +56,18 @@
     return total
 
 
+def head_weights(here_ref, own_ref, one_ref, two_ref):
+    first, low = pl.program_id(0) == 0, here_ref[0] == 0
+    half = one_ref.shape[1]
+    one, two = one_ref[0], two_ref[0]
+    return (
+        jnp.where(first, own_ref[:half], jnp.where(low, one, two)),
+        jnp.where(first, own_ref[half:], jnp.where(low, two, one)),
+    )
+
+
 def attention_kernel(
-    pairs, x_ref, qk_ref, vo_ref, small_ref, valid_ref, vectors_ref,
+    pairs, here_ref, x_ref, own_qk, qk_one, qk_two, own_vo, vo_one, vo_two, small_ref, valid_ref, vectors_ref,
     q_ref, k_ref, v_ref, weights_ref, context_ref, low_ref, normed_ref, scale_ref, total_ref,
 ):
     step = pl.program_id(0)
@@ -66,9 +75,11 @@
     heads = cols // HEAD
     slots = x_ref.shape[0] // pairs
     x = x_ref[...]
-    q_ref[0] = (dot(x, qk_ref[0, :cols], 1, 1) + small_ref[0, 0:1, :cols]).astype(BF16)
-    k_ref[0] = dot(x, qk_ref[0, cols:], 1, 1).astype(BF16)
-    v_ref[0] = (dot(x, vo_ref[0, :cols], 1, 1) + small_ref[0, 1:2, :cols]).astype(BF16)
+    w_q, w_k = head_weights(here_ref, own_qk, qk_one, qk_two)
+    w_v, w_o = head_weights(here_ref, own_vo, vo_one, vo_two)
+    q_ref[0] = (dot(x, w_q, 1, 1) + small_ref[0, 0:1, :cols]).astype(BF16)
+    k_ref[0] = dot(x, w_k, 1, 1).astype(BF16)
+    v_ref[0] = (dot(x, w_v, 1, 1) + small_ref[0, 1:2, :cols]).astype(BF16)
     for p in range(pairs):
         rows = slice(p * slots, (p + 1) * slots)
         scores = dot(head_stack(q_ref[0, rows], heads), k_ref[0, rows], 1, 1) * HEAD ** (-0.5)
@@ -78,7 +89,7 @@
         weights_ref[0, p] = weights
         mixed = dot(weights.astype(BF16), v_ref[0, rows], 1, 0)
         context_ref[0, rows] = head_pick(mixed, heads).astype(BF16)
-    branch = dot(context_ref[0], vo_ref[0, cols:], 1, 0)
+    branch = dot(context_ref[0], w_o, 1, 0)
 
     @pl.when(step == 0)
     def _():
@@ -112,49 +123,62 @@
     return [(start, start + size) for start in range(0, units, size)]
 
 
-def by_owner(step, body, own, others):
-    @pl.when(step == 0)
-    def _():
-        body(True, *own)
-
-    @pl.when(step > 0)
-    def _():
-        body(False, *others)
-
-
 def ffn_kernel(
     here_ref, low_ref, normed_ref, own_in_one, own_in_two, in_one, in_two, own_down_one, own_down_two, down_one,
     down_two, bias_one, bias_two, cot_ref, vectors_ref,
-    act_ref, slope_ref, out_ref, delta_ref, ffn_low_ref, sums_ref, total_ref,
+    out_ref, delta_ref, pre_grad_ref, in_keep_ref, in_send_ref, down_keep_ref, down_send_ref, sum_in_ref, sums_ref,
+    act_ref, slope_ref, ffn_low_ref, total_ref,
 ):
     step = pl.program_id(0)
-    low = low_ref[...]
+    shards_ = pl.num_programs(0) // 2
+    core = here_ref[0]
     half = in_one.shape[1]
 
-    def body(first, w_in_one, w_in_two, w_down_one, w_down_two):
+    def down_of(first, slot):
+        if first:
+            return own_down_one, own_down_two
+        other = pl.ds(slot - 1, 1)
+        return down_one.at[other], down_two.at[other]
+
+    def forward(first):
+        low = low_ref[...]
         bias = jnp.concatenate([bias_one[0, 2:3], bias_two[0, 2:3]], axis=1)
+        w_in = (own_in_one, own_in_two) if first else (in_one, in_two)
+        w_down = down_of(first, step)
         branch = None
         for start, stop in blocks_of(2 * half):
-            pre_act = dot(low, unit_rows(w_in_one, w_in_two, start, stop), 1, 1) + bias[:, start:stop]
+            pre_act = dot(low, unit_rows(*w_in, start, stop), 1, 1) + bias[:, start:stop]
             share = 0.5 * (1.0 + lax.erf(pre_act * SQRT_HALF))
             act = (pre_act * share).astype(BF16)
-            act_ref[0, :, start:stop] = act
-            slope_ref[0, :, start:stop] = share + pre_act * (DENSITY * jnp.exp(-0.5 * pre_act * pre_act))
-            term = dot(act, unit_rows(w_down_one, w_down_two, start, stop), 1, 0)
+            act_ref[step, :, start:stop] = act
+            slope_ref[step, :, start:stop] = share + pre_act * (DENSITY * jnp.exp(-0.5 * pre_act * pre_act))
+            term = dot(act, unit_rows(*w_down, start, stop), 1, 0)
             branch = term if branch is None else branch + term
         if first:
             total_ref[...] = branch
         else:
             total_ref[...] += branch
 
-    by_owner(
-        step,
-        body,
-        (own_in_one, own_in_two, own_down_one, own_down_two),
-        (in_one, in_two, down_one, down_two),
-    )
-
-    @pl.when(step == pl.num_programs(0) - 1)
+    def backward(first):
+        slot = 0 if first else step - shards_
+        ffn_low = ffn_low_ref[...]
+        w_down = down_of(first, slot)
+        for start, stop in blocks_of(2 * half):
+            act_grad = dot(ffn_low, unit_rows(*w_down, start, stop), 1, 1)
+            pre_grad_ref[0, :, start:stop] = (act_grad * slope_ref[slot, :, start:stop]).astype(BF16)
+        down_send_ref[0] = dot(act_ref[slot, :, half:], ffn_low, 0, 0).astype(BF16)
+        down_keep_ref[0] = dot(act_ref[slot, :, :half], ffn_low, 0, 0).astype(BF16)
+        low = low_ref[...]
+        one, two = pre_grad_ref[0, :, :half], pre_grad_ref[0, :, half:]
+        sum_in_ref[0, :, pl.ds(pl.multiple_of(core * half, half), half)] = column_sum(one.astype(F32))
+        sum_in_ref[0, :, pl.ds(pl.multiple_of((1 - core) * half, half), half)] = column_sum(two.astype(F32))
+        in_send_ref[0] = dot(two, low, 0, 0).astype(BF16)
+        in_keep_ref[0] = dot(one, low, 0, 0).astype(BF16)
+
+    pl.when(step == 0)(partial(forward, True))
+    pl.when((step > 0) & (step < shards_))(partial(forward, False))
+
+    @pl.when(step == shards_ - 1)
     def _():
         hidden = normed_ref[...] * vectors_ref[1:2] + vectors_ref[2:3]
         second = total_ref[...] + vectors_ref[3:4] + hidden
@@ -170,34 +194,8 @@
         sums_ref[1:2] = column_sum(upstream)
         sums_ref[2:3] = column_sum(delta)
 
-
-def down_grad_kernel(act_ref, ffn_low_ref, keep_ref, send_ref):
-    half = keep_ref.shape[1]
-    low = ffn_low_ref[...]
-    send_ref[0] = dot(act_ref[0, :, half:], low, 0, 0).astype(BF16)
-    keep_ref[0] = dot(act_ref[0, :, :half], low, 0, 0).astype(BF16)
-
-
-def in_grad_kernel(
-    here_ref, ffn_low_ref, low_ref, slope_ref, own_down_one, own_down_two, down_one, down_two,
-    keep_ref, send_ref, pre_grad_ref, sum_in_ref,
-):
-    core = here_ref[0]
-    half = keep_ref.shape[1]
-    ffn_low = ffn_low_ref[...]
-
-    def body(first, w_down_one, w_down_two):
-        for start, stop in blocks_of(2 * half):
-            act_grad = dot(ffn_low, unit_rows(w_down_one, w_down_two, start, stop), 1, 1)
-            pre_grad_ref[0, :, start:stop] = (act_grad * slope_ref[0, :, start:stop]).astype(BF16)
-
-    by_owner(pl.program_id(0), body, (own_down_one, own_down_two), (down_one, down_two))
-    low = low_ref[...]
-    one, two = pre_grad_ref[0, :, :half], pre_grad_ref[0, :, half:]
-    sum_in_ref[0, :, pl.ds(pl.multiple_of(core * half, half), half)] = column_sum(one.astype(F32))
-    sum_in_ref[0, :, pl.ds(pl.multiple_of((1 - core) * half, half), half)] = column_sum(two.astype(F32))
-    send_ref[0] = dot(two, low, 0, 0).astype(BF16)
-    keep_ref[0] = dot(one, low, 0, 0).astype(BF16)
+    pl.when(step == shards_)(partial(backward, True))
+    pl.when(step > shards_)(partial(backward, False))
 
 
 def ffn_back_kernel(
@@ -217,7 +215,8 @@
         else:
             total_ref[...] += branch
 
-    by_owner(step, body, (own_in_one, own_in_two), (in_one, in_two))
+    pl.when(step == 0)(partial(body, True, own_in_one, own_in_two))
+    pl.when(step > 0)(partial(body, False, in_one, in_two))
 
     @pl.when(step == pl.num_programs(0) - 1)
     def _():
@@ -233,7 +232,7 @@
 
 
 def attention_back_kernel(
-    pairs, here_ref, x_ref, attn_low_ref, delta_ref, qk_ref, vo_ref, q_ref, k_ref, v_ref, weights_ref, context_ref,
+    pairs, here_ref, x_ref, attn_low_ref, delta_ref, own_qk, qk_one, qk_two, own_vo, vo_one, vo_two, q_ref, k_ref, v_ref, weights_ref, context_ref,
     sums_one_ref, sums_two_ref, sum_in_ref,
     qk_keep_ref, vo_keep_ref, send_ref, sums_ref, rows_ref, dq_ref, dk_ref, dv_ref, total_ref,
 ):
@@ -245,7 +244,9 @@
     scale = HEAD ** (-0.5)
     x = x_ref[...]
     attn_low = attn_low_ref[...]
-    context_grad = dot(attn_low, vo_ref[0, cols:], 1, 1).astype(BF16)
+    w_q, w_k = head_weights(here_ref, own_qk, qk_one, qk_two)
+    w_v, w_o = head_weights(here_ref, own_vo, vo_one, vo_two)
+    context_grad = dot(attn_low, w_o, 1, 1).astype(BF16)
     grad_out = dot(context_ref[0], attn_low, 0, 0).astype(BF16)
     for p in range(pairs):
         rows = slice(p * slots, (p + 1) * slots)
@@ -287,8 +288,7 @@
         qk_keep_ref[0], send_ref[0, 0] = grad_k, grad_q
         vo_keep_ref[0], send_ref[1, 0] = grad_out, grad_v
 
-    branch = dot(dq, qk_ref[0, :cols], 1, 0) + dot(dk, qk_ref[0, cols:], 1, 0)
-    branch = branch + dot(dv, vo_ref[0, :cols], 1, 0)
+    branch = dot(dq, w_q, 1, 0) + dot(dk, w_k, 1, 0) + dot(dv, w_v, 1, 0)
 
     @pl.when(step == 0)
     def _():
@@ -311,9 +311,9 @@
     return pl.BlockSpec((1,) + array.shape[1:], lambda s, *_: (s,) + (0,) * (len(array.shape) - 1))
 
 
-def call(kernel, steps, name, inputs, outputs, scratch, scalar=None):
+def call(kernel, steps, name, vmem, inputs, outputs, scratch, scalar, kept=()):
     spec = pltpu.PrefetchScalarGridSpec(
-        num_scalar_prefetch=0 if scalar is None else 1,
+        num_scalar_prefetch=1,
         grid=(steps,),
         in_specs=[make if isinstance(make, pl.BlockSpec) else make(a) for make, a in inputs],
         out_specs=[make if isinstance(make, pl.BlockSpec) else make(a) for make, a in outputs],
@@ -322,11 +322,11 @@
     return pl.pallas_call(
         kernel,
         grid_spec=spec,
-        out_shape=[a for _, a in outputs],
+        out_shape=[pltpu.HBM(a.shape, a.dtype) if i in kept else a for i, (_, a) in enumerate(outputs)],
         name=name,
         cost_estimate=pl.CostEstimate(flops=0, bytes_accessed=0, transcendentals=0),
-        compiler_params=pltpu.CompilerParams(vmem_limit_bytes=VMEM_BYTES),
-    )(*(() if scalar is None else (scalar,)), *[a for _, a in inputs])
+        compiler_params=pltpu.CompilerParams(vmem_limit_bytes=vmem * MIB),
+    )(scalar, *[a for _, a in inputs])
 
 
 def shape(dims, dtype):
@@ -371,7 +371,7 @@
         out_shape=shape((n, 1 << len(left), rows, cols), BF16),
         name="add",
         cost_estimate=pl.CostEstimate(flops=0, bytes_accessed=0, transcendentals=0),
-        compiler_params=pltpu.CompilerParams(vmem_limit_bytes=SMALL_VMEM_BYTES),
+        compiler_params=pltpu.CompilerParams(vmem_limit_bytes=16 * MIB),
     )(me, *[a for a, _ in terms])
     return out, left
 
@@ -421,14 +421,15 @@
             merged.append(jnp.concatenate(parts, axis=1 + self.steps - bit))
         self.held = merged
 
-    def send_core(self):
-        self.halves = jnp.stack([h.reshape(self.n, -1, self.cols) for h in self.held])
-        return flip(self.halves, "dp", 1)
-
-    def finish(self, got):
+    def halves(self):
+        return [h.reshape(self.n, -1, self.cols) for h in self.held]
+
+    def finish(self, halves, got):
         low = (lax.axis_index("dp") & 1) == 0
-        one, two = jnp.where(low, self.halves, got), jnp.where(low, got, self.halves)
-        return [jnp.concatenate([one[i], two[i]], axis=1) for i in range(2)]
+        return [
+            jnp.concatenate([jnp.where(low, h, g), jnp.where(low, g, h)], axis=1)
+            for h, g in zip(halves, got)
+        ]
 
 
 class Reduce:
@@ -545,7 +546,9 @@
     ).astype(F32)[:, None, :]
 
     att_two = flip(att_send, "mp", 2)
-    att_two, ffn_send, tok, vectors, key_valid = tie(att_two, ffn_send, tok, vectors, key_valid)
+    att_two, ffn_send, tok, vectors, key_valid, here, own = tie(
+        att_two, ffn_send, tok, vectors, key_valid, here, own
+    )
     att_odd = flip(jnp.stack([att_send, att_two]), "mp", 1)
     ffn_two = flip(ffn_send, "mp", 2)
     att_odd, ffn_two = tie(att_odd, ffn_two)
@@ -575,12 +578,10 @@
         ]
     )
     got = ffn.send(0)
-    core_got = att.send_core()
+    qk_one, vo_one = att.halves()
+    qk_two, vo_two = flip(qk_one, "dp", 1), flip(vo_one, "dp", 1)
     tok_two = flip(tok[2], "mp", 2)
-    got, core_got, tok_two, cot = tie(got, core_got, tok_two, cot)
-    qk_others, vo_others = att.finish(core_got)
-    qk_all = jnp.concatenate([own["qk"][None], qk_others])
-    vo_all = jnp.concatenate([own["vo"][None], vo_others])
+    got, qk_two, vo_two, tok_two, cot = tie(got, qk_two, vo_two, tok_two, cot)
     x = join([tok[0], tok_one, tok_two, tok_three])
     heads_low = shape((mp, rows, cols), BF16)
     low_shape = shape((rows, width), BF16)
@@ -590,16 +591,26 @@
         ffn.take(step - 1, got)
         got = ffn.send(step)
         if step == 1:
-            cot_one, cot_three = flip(cot[1], "mp", 1), flip(cot[3], "mp", 3)
-            got, qk_all, vo_all, x = tie(got, qk_all, vo_all, x) if ffn.steps > 2 else (got, qk_all, vo_all, x)
+            cot_one, cot_two, cot_three = [flip(cot[k], "mp", k) for k in range(1, mp)]
+        if step < ffn.steps - 1:
+            got = tie(*got)
+    later = lambda a: pl.BlockSpec((1,) + a.shape[1:], lambda s, h: (jnp.clip(s - 1, 0, mp - 2), 0, 0))
+    head_args = [
+        (whole, own["qk"]),
+        (later, qk_one),
+        (later, qk_two),
+        (whole, own["vo"]),
+        (later, vo_one),
+        (later, vo_two),
+    ]
     q, k, v, weights, context, hidden_low, normed_one, scale_one = call(
         partial(attention_kernel, pairs),
         mp,
         "attention",
+        32,
         [
             (whole, x),
-            (per_step, qk_all),
-            (per_step, vo_all),
+            *head_args,
             (per_step, smalls),
             (whole, key_valid),
             (whole, vectors),
@@ -615,84 +626,71 @@
             (whole, shape((rows, 1), F32)),
         ],
         [pltpu.VMEM((rows, width), F32)],
-    )
-    got, hidden_low, cot_one, cot_three, cot = tie(got, hidden_low, cot_one, cot_three, cot)
+        here,
+        range(5),
+    )
+    got, hidden_low, cot_one, cot_two, cot_three = tie(got, hidden_low, cot_one, cot_two, cot_three)
     ffn.take(ffn.steps - 1, got)
-    in_one, down_one = [h.reshape(mp - 1, half_units, width) for h in ffn.held]
+    in_one, down_one = ffn.halves()
     in_two, down_two = flip(in_one, "dp", 1), flip(down_one, "dp", 1)
-    cot_two = flip(cot[2], "mp", 2)
-    in_two, down_two, cot_two, hidden_low = tie(in_two, down_two, cot_two, hidden_low)
     cot_rows = join([cot[0], cot_one, cot_two, cot_three])
-
-    one_block, two_block = (1, half_units, width), (1, half_units, width)
-    mine = pl.BlockSpec(one_block, lambda s, h: (h[0], 0, 0))
-    other = pl.BlockSpec(one_block, lambda s, h: (1 - h[0], 0, 0))
-    later = pl.BlockSpec(two_block, lambda s, h: (jnp.maximum(s - 1, 0), 0, 0))
+    in_two, down_two, hidden_low, cot_rows = tie(in_two, down_two, hidden_low, cot_rows)
+
+    half_block = (1, half_units, width)
+    mine = pl.BlockSpec(half_block, lambda s, h: (h[0], 0, 0))
+    other = pl.BlockSpec(half_block, lambda s, h: (1 - h[0], 0, 0))
     own_in = own["in"].reshape(2, half_units, width)
     own_down = own["down"].reshape(2, half_units, width)
     in_args = [(mine, own_in), (other, own_in), (later, in_one), (later, in_two)]
-    down_args = [(mine, own_down), (other, own_down), (later, down_one), (later, down_two)]
-    act, slope, output, delta_ffn, ffn_low, sums_two = call(
+    down_args = [(mine, own_down), (other, own_down), (whole, down_one), (whole, down_two)]
+    half = shape((mp, half_units, width), BF16)
+    bias_block = (1, 8, half_units)
+    back_step = lambda s: jnp.maximum(s - mp, 0)
+    back = lambda a: pl.BlockSpec((1,) + a.shape[1:], lambda s, h: (back_step(s), 0, 0))
+    output, delta_ffn, pre_grad, in_keep, in_send, down_keep, down_send, sum_in, sums_two = call(
         ffn_kernel,
-        mp,
+        2 * mp,
         "ffn",
+        52,
         [
             (whole, hidden_low),
             (whole, normed_one),
             *in_args,
             *down_args,
-            (pl.BlockSpec((1, 8, half_units), lambda s, h: (s, 0, h[0])), smalls),
-            (pl.BlockSpec((1, 8, half_units), lambda s, h: (s, 0, 1 - h[0])), smalls),
+            (pl.BlockSpec(bias_block, lambda s, h: (jnp.minimum(s, mp - 1), 0, h[0])), smalls),
+            (pl.BlockSpec(bias_block, lambda s, h: (jnp.minimum(s, mp - 1), 0, 1 - h[0])), smalls),
             (whole, cot_rows),
             (whole, vectors),
         ],
         [
-            (per_step, shape((mp, rows, units), BF16)),
-            (per_step, shape((mp, rows, units), F32)),
             (whole, low_shape),
             (whole, rows_shape),
-            (whole, low_shape),
+            (back, shape((mp, rows, units), BF16)),
+            (back, half),
+            (back, half),
+            (back, half),
+            (back, half),
+            (
+                pl.BlockSpec((1, 1, units), lambda s, h: (back_step(s) ^ h[1], 0, 0)),
+                shape((mp, 1, units), F32),
+            ),
             (whole, sums_shape),
         ],
-        [pltpu.VMEM((rows, width), F32)],
+        [
+            pltpu.VMEM((mp, rows, units), BF16),
+            pltpu.VMEM((mp, rows, units), F32),
+            pltpu.VMEM((rows, width), BF16),
+            pltpu.VMEM((rows, width), F32),
+        ],
         here,
-    )
-    half = shape((mp, half_units, width), BF16)
-    down_keep, down_send = call(
-        down_grad_kernel,
-        mp,
-        "down_grad",
-        [(per_step, act), (whole, ffn_low)],
-        [(per_step, half), (per_step, half)],
-        [],
-    )
-    down_send, ffn_low = tie(down_send, ffn_low)
-    down_got = flip(down_send, "dp", 1)
-    in_keep, in_send, pre_grad, sum_in = call(
-        in_grad_kernel,
-        mp,
-        "in_grad",
-        [(whole, ffn_low), (whole, hidden_low), (per_step, slope), *down_args],
-        [
-            (per_step, half),
-            (per_step, half),
-            (per_step, shape((mp, rows, units), BF16)),
-            (
-                pl.BlockSpec((1, 1, units), lambda s, h: (s ^ h[1], 0, 0)),
-                shape((mp, 1, units), F32),
-            ),
-        ],
-        [],
-        here,
-    )
-    out_rows = output.reshape(pairs, mp, rows_local, width)
-    out_blocks = [out_rows[:, k] for k in range(mp)]
-    down_got, in_send, pre_grad, out_blocks = tie(down_got, in_send, pre_grad, out_blocks)
-    in_got = flip(in_send, "dp", 1)
+        range(2, 7),
+    )
+    in_got, down_got = flip(in_send, "dp", 1), flip(down_send, "dp", 1)
     delta_attn, attn_low, sums_one = call(
         ffn_back_kernel,
         mp,
         "ffn_back",
+        24,
         [
             (per_step, pre_grad),
             *in_args,
@@ -705,7 +703,9 @@
         [pltpu.VMEM((rows, width), F32)],
         here,
     )
-    in_got, attn_low = tie(in_got, attn_low)
+    out_rows = output.reshape(pairs, mp, rows_local, width)
+    out_blocks = [out_rows[:, k] for k in range(mp)]
+    in_got, down_got, attn_low, out_blocks = tie(in_got, down_got, attn_low, out_blocks)
     ffn = Reduce([in_keep, down_keep], [in_got, down_got])
     packs = ffn.pack(0)
     packs, attn_low = tie(packs, attn_low)
@@ -716,12 +716,12 @@
         partial(attention_back_kernel, pairs),
         mp,
         "attention_back",
+        32,
         [
             (whole, x),
             (whole, attn_low),
             (whole, delta_attn),
-            (per_step, qk_all),
-            (per_step, vo_all),
+            *head_args,
             (per_step, q),
             (per_step, k),
             (per_step, v),
@@ -753,11 +753,9 @@
         got = ffn.send(step, packs)
         if step == 1:
             att_got = flip(att_send, "dp", 1)
-            sums_got = flip(sums, "dp", 1)
-            row_three = flip(row_sends[3], "mp", 3)
-        got, att_got, sums_got, row_three, row_sends = tie(got, att_got, sums_got, row_three, row_sends)
+            row_two, row_three = flip(row_sends[2], "mp", 2), flip(row_sends[3], "mp", 3)
+        got, att_got, row_two, row_three, row_sends = tie(got, att_got, row_two, row_three, row_sends)
     ffn.take(got)
-    sums = sums + sums_got
     ffn_parts = ffn.finish()
     ffn_odd = jnp.concatenate([p[1::2] for p in ffn_parts], axis=1)
     ffn_even = jnp.concatenate([p[0::2] for p in ffn_parts], axis=1)
@@ -766,9 +764,8 @@
     ffn_odd, ffn_even, packs, sums = tie(ffn_odd, ffn_even, packs, sums)
     got = att.send(0, packs)
     ffn_got = flip(ffn_odd, "mp", 1)
-    row_one = flip(row_sends[1], "mp", 1)
-    sums_got = flip(sums, "dp", 2)
-    got, ffn_got, row_one, sums_got = tie(got, ffn_got, row_one, sums_got)
+    sums_got = flip(sums, "dp", 1)
+    got, ffn_got, sums_got, row_sends, out_got = tie(got, ffn_got, sums_got, row_sends, out_got)
     sums = sums + sums_got
     for mask in [1 << b for b in range(2, dp.bit_length() - 2)]:
         sums = sums + flip(sums, "dp", mask)
@@ -779,8 +776,9 @@
         got = att.send(step, packs)
         if step == 1:
             ffn_last = flip(ffn_two, "mp", 2)
-            sums_got = flip(sums, "dp", dp // 2)
-        got, ffn_last, sums_got, row_sends = tie(got, ffn_last, sums_got, row_sends)
+            row_one = flip(row_sends[1], "mp", 1)
+            sums_got = flip(sums, "dp", 2)
+        got, ffn_last, row_one, sums_got = tie(got, ffn_last, row_one, sums_got)
     att.take(got)
     sums = sums + sums_got
     att_parts = att.finish()
@@ -791,9 +789,8 @@
     ffn.held, att_odd, att_even, sums = tie(ffn.held, att_odd, att_even, sums)
     got = ffn.send(0)
     att_got = flip(att_odd, "mp", 1)
-    row_two = flip(row_sends[2], "mp", 2)
-    sums_got = flip(sums, "mp", 1)
-    got, att_got, row_two, sums_got = tie(got, att_got, row_two, sums_got)
+    sums_got = flip(sums, "dp", dp // 2)
+    got, att_got, sums_got = tie(got, att_got, sums_got)
     sums = sums + sums_got
     att_two = add_parts(att_even[1], att_got[1])
     for step in range(1, ffn.steps):
@@ -801,21 +798,29 @@
         got = ffn.send(step)
         if step == 1:
             att_last = flip(att_two, "mp", 2)
-            sums_got = flip(sums, "mp", 2)
+            sums_got = flip(sums, "mp", 1)
         got, att_last, sums_got = tie(got, att_last, sums_got)
     ffn.take(ffn.steps - 1, got)
     sums = sums + sums_got
     att_sum = add_parts(att_even[0], att_got[0], att_last)
     att = Gather([att_sum[None, :att_part], att_sum[None, att_part:]])
-    core_got = ffn.send_core()
+    ffn_halves = ffn.halves()
+    core_got = [flip(h, "dp", 1) for h in ffn_halves]
     got = att.send(0)
-    core_got, got = tie(core_got, got)
-    grad_in, grad_down = ffn.finish(core_got)
+    sums_got = flip(sums, "mp", 2)
+    core_got, got, sums_got, row_one, row_two, row_three = tie(
+        core_got, got, sums_got, row_one, row_two, row_three
+    )
+    sums = sums + sums_got
+    grad_in, grad_down = ffn.finish(ffn_halves, core_got)
+    grad_in, grad_down = grad_in[0].astype(F32).T, grad_down[0].astype(F32)
     for step in range(1, att.steps):
         att.take(step - 1, got)
         got = tie(*att.send(step))
+    grad_in, grad_down, got, row_one = tie(grad_in, grad_down, got, row_one)
     att.take(att.steps - 1, got)
-    grad_qk, grad_vo = att.finish(att.send_core())
+    att_halves = att.halves()
+    grad_qk, grad_vo = att.finish(att_halves, [flip(h, "dp", 1) for h in att_halves])
 
     def leave(blocks):
         return jnp.take(jnp.stack(blocks), order, axis=0).reshape(mp * pairs, rows_local, width)
@@ -835,9 +840,9 @@
         sums[0],
         sums[1],
         sums[2],
-        grad_in[0].astype(F32).T,
+        grad_in,
         sum_in_bias,
-        grad_down[0].astype(F32),
+        grad_down,
         sums[10],
         sums[8],
         sums[9],

time: 322 us -> 277 us (0.86)
  Pallas kernels: 88.3 us -> 66.5 us
  other arithmetic: 40.9 us -> 19.8 us
  waiting for transfers between devices: 104 us -> 90.3 us
  starting transfers between devices: 62.7 us -> 72.7 us
    pallas_call x6 -> x4, Pallas kernels: 79.4 us -> 62.8 us  [call(): pl.pallas_call(kernel, grid_spec=spec, out_shape=[pltpu.HBM(a.shape, a.dt...]
    ppermute x57 -> x60, waiting for transfers between devices: 104 us -> 90.3 us  [flip(): return lax.ppermute(array, axis, [(i, i ^ mask) for i in range(size)])]
    ppermute x57 -> x60, starting transfers between devices: 62.7 us -> 72.7 us  [flip(): return lax.ppermute(array, axis, [(i, i ^ mask) for i in range(size)])]
    select_n x15, other arithmetic: 8.04 us -> 0.88 us  [take(): parts = [jnp.where(low, mine, theirs), jnp.where(low, theirs, mine)]]
    pallas_call x12, Pallas kernels: 8.84 us -> 3.77 us  [add_terms(): pl.pallas_call(partial(add_kernel, len(terms)), grid_spec=spec, out_shape...]
    unnamed x80 -> x126, local copies, waits for them, and re-layouts: 6.19 us -> 8.95 us
  transfers between devices with their start and end apart: 57 -> 60, of which waited for: 25 -> 28; matrix products, arithmetic and copies ran while one was open for 13% -> 10% of each run, Pallas kernels for 19% -> 14%
where the time goes in v3:
time: 277 us; the launch traced here: 276 us
  waiting for transfers between devices  90.3 us (33%)
  starting transfers between devices  72.7 us (26%)
  Pallas kernels  66.5 us (24%)
  local copies, waits for them, and re-layouts  24.5 us (9%)
  other arithmetic  19.8 us (7%)
    ppermute x60, waiting for transfers between devices, flip(): return lax.ppermute(array, axis, [(i, i ^ mask) for i in range(size)])  90.3 us
    ppermute x60, starting transfers between devices, flip(): return lax.ppermute(array, axis, [(i, i ^ mask) for i in range(size)])  72.7 us
    pallas_call x4, Pallas kernels, call(): pl.pallas_call(kernel, grid_spec=spec, out_shape=[pltpu.HBM(a.shape, a.dt...  62.8 us
    unnamed x126, local copies, waits for them, and re-layouts  8.95 us
  transfers between devices with their start and end apart: 60, of which 28 were waited for; matrix products, arithmetic and copies ran while one was open for 10% of the time, Pallas kernels for 14%

profile of v3, /device:TPU:0, one launch (start us, length us, event | category | flops | bytes accessed | tf_op | source)
XLA Modules:
  0.0 275.9 jit_solution(14366611595584947716)
XLA Ops:
  3.3 4.1 %collective-permute-start = (bf16[104,768]{1,0:T(8,128)(2,1)S(1)}, bf16[104,768]{1,0:T(8,128)(2,1)S(1)}, u32[]{:S(2)}, u32[]{:S(2)}) collective-permute-start(bf16[104,768]{1,0:T(8,128)(2,1)S(1)} %concatenate.92), channel_id=1, source_target_pairs={{0,2},{1,3},{2,0},{3,1},{4,6},{5,7},{6,4},{7,5},{8,10},{9,11},{10,... | collective-permute-start | bytes 479240 | tf_op jit(solution)/shard_map/ppermute | solution.py:381
  10.7 4.2 %collective-permute-done = bf16[104,768]{1,0:T(8,128)(2,1)S(1)} collective-permute-done((bf16[104,768]{1,0:T(8,128)(2,1)S(1)}, bf16[104,768]{1,0:T(8,128)(2,1)S(1)}, u32[]{:S(2)}, u32[]{:S(2)}) %collective-permute-start) | collective-permute-done | bytes 159776 | tf_op jit(solution)/shard_map/ppermute | solution.py:381
  15.8 3.4 %collective-permute-start.2 = (bf16[192,768]{1,0:T(8,128)(2,1)S(1)}, bf16[192,768]{1,0:T(8,128)(2,1)S(1)}, u32[]{:S(2)}, u32[]{:S(2)}) collective-permute-start(bf16[192,768]{1,0:T(8,128)(2,1)S(1)} %pad_maximum_fusion.20), channel_id=1, source_target_pairs={{0,2},{1,3},{2,0},{3,1},{4,6},{5,7},{6,4},{7,5},{8,10},{9,11},{10,... | collective-permute-start | bytes 884744 | tf_op jit(solution)/shard_map/ppermute | solution.py:381
  19.2 9.9 %collective-permute-done.2 = bf16[192,768]{1,0:T(8,128)(2,1)S(1)} collective-permute-done((bf16[192,768]{1,0:T(8,128)(2,1)S(1)}, bf16[192,768]{1,0:T(8,128)(2,1)S(1)}, u32[]{:S(2)}, u32[]{:S(2)}) %collective-permute-start.2) | collective-permute-done | bytes 294944 | tf_op jit(solution)/shard_map/ppermute | solution.py:381
  30.2 3.2 %collective-permute-start.3 = (bf16[2,192,768]{2,1,0:T(8,128)(2,1)S(1)}, bf16[2,192,768]{2,1,0:T(8,128)(2,1)S(1)}, u32[]{:S(2)}, u32[]{:S(2)}) collective-permute-start(bf16[2,192,768]{2,1,0:T(8,128)(2,1)S(1)} %pad_maximum_fusion.12), channel_id=1, source_target_pairs={{0,1},{1,0},{2,3},{3,2},{4,5},{5,4},{6,7},{7,6},{8,9},{9,8},{10,11... | collective-permute-start | bytes 1769480 | tf_op jit(solution)/shard_map/ppermute | solution.py:381
  33.4 1.6 collective-permute-start.5
  36.6 3.4 %collective-permute-done.5 = bf16[3,1,1,48,768]{4,3,0,2,1:T(8,128)(2,1)S(1)} collective-permute-done((bf16[3,1,1,48,768]{4,3,0,2,1:T(8,128)(2,1)S(1)}, bf16[3,1,1,48,768]{4,3,0,2,1:T(8,128)(2,1)S(1)}, u32[]{:S(2)}, u32[]{:S(2)}) %collective-permute-start.5) | collective-permute-done | bytes 221216 | tf_op jit(solution)/shard_map/ppermute | solution.py:381
  41.4 5.0 %collective-permute-done.3 = bf16[2,192,768]{2,1,0:T(8,128)(2,1)S(1)} collective-permute-done((bf16[2,192,768]{2,1,0:T(8,128)(2,1)S(1)}, bf16[2,192,768]{2,1,0:T(8,128)(2,1)S(1)}, u32[]{:S(2)}, u32[]{:S(2)}) %collective-permute-start.3) | collective-permute-done | bytes 589856 | tf_op jit(solution)/shard_map/ppermute | solution.py:381
  48.1 1.6 collective-permute-start.8
  49.7 1.7 collective-permute-start.10
  51.4 1.6 collective-permute-start.11
  53.1 4.1 %collective-permute-done.10 = bf16[3,40,768]{2,1,0:T(8,128)(2,1)S(1)} collective-permute-done((bf16[3,40,768]{2,1,0:T(8,128)(2,1)S(1)}, bf16[3,40,768]{2,1,0:T(8,128)(2,1)S(1)}, u32[]{:S(2)}, u32[]{:S(2)}) %collective-permute-start.10) | collective-permute-done | bytes 184352 | tf_op jit(solution)/shard_map/ppermute | solution.py:381
  57.2 2.5 collective-permute-done.11
  62.3 1.6 collective-permute-start.14
  64.6 8.4 %collective-permute-done.7 = bf16[3,1,1,96,768]{4,3,0,2,1:T(8,128)(2,1)S(1)} collective-permute-done((bf16[3,1,1,96,768]{4,3,0,2,1:T(8,128)(2,1)S(1)}, bf16[3,1,1,96,768]{4,3,0,2,1:T(8,128)(2,1)S(1)}, u32[]{:S(2)}, u32[]{:S(2)}) %collective-permute-start.7) | collective-permute-done | bytes 442400 | tf_op jit(solution)/shard_map/ppermute | solution.py:381
  76.6 2.7 collective-permute-start.18
  79.3 1.6 collective-permute-start.19
  81.0 12.2 %attention.1 = (bf16[4,480,192]{2,1,0:T(8,128)(2,1)}, bf16[4,480,192]{2,1,0:T(8,128)(2,1)}, bf16[4,480,192]{2,1,0:T(8,128)(2,1)}, f32[4,3,480,160]{3,2,1,0:T(8,1...) custom-call(s32[2]{0:T(128)S(1)} %pad_add_fusion.here_ref, ...), custom_call_target="tpu_custom_call" | custom-call | tf_op jit(solution)/shard_map/attention/pallas_call | solution.py:322
  94.3 1.7 collective-permute-done.15
  98.7 2.4 copy.47
  101.1 2.3 pad_maximum_fusion.8
  104.1 24.5 %ffn.1 = (bf16[480,768]{1,0:T(8,128)(2,1)S(1)}, f32[480,768]{1,0:T(8,128)}, bf16[4,480,768]{2,1,0:T(8,128)(2,1)}, bf16[4,384,768]{2,1,0:T(8,128)(2,1)}, bf16[4,3...) custom-call(s32[2]{0:T(128)S(1)} %pad_add_fusion.here_ref, ...), custom_call_target="tpu_custom_call" | custom-call | tf_op jit(solution)/shard_map/ffn/pallas_call | solution.py:322
  130.6 1.8 copy-done.17
  133.8 6.3 %ffn_back.1 = (f32[480,768]{1,0:T(8,128)S(1)}, bf16[480,768]{1,0:T(8,128)(2,1)S(1)}, f32[8,768]{1,0:T(8,128)S(1)}) custom-call(s32[2]{0:T(128)S(1)} %pad_add_fusion.here_ref, bf16[4,480,768]{2,1,0:T(8,128)(2,1)S(1)} %copy-done.17, bf16[2,384,768]{2,1,0:T(8,128)(2,1)S(1)} %bitcast.194, bf16[2,384,768]{2,1,0:T(8,128)(2,1)S(1)} %bitcast.195, ...), custom_call_target="tpu_custom_call" | custom-call | tf_op jit(solution)/shard_map/ffn_back/pallas_call | solution.py:322
  143.7 1.7 collective-permute-start.25
  145.5 2.4 collective-permute-start.27
  147.9 2.0 collective-permute-start.28
  149.9 19.8 %attention_back.1 = (bf16[4,192,768]{2,1,0:T(8,128)(2,1)S(1)}, bf16[4,192,768]{2,1,0:T(8,128)(2,1)S(1)}, bf16[2,4,192,768]{3,2,1,0:T(8,128)(2,1)}, f32[24,768]{1,0:T(8,128)S(1)}, bf16[480,768]{1,0:T(8,128)(2,1)S(1)}) custom-call(s32[2]{0:T(128)S(1)} %pad_add_fusion.here_ref, bf16[480,768]{1,0:T(8,128)(2,1)S(1)} %bitcast.230, ...), custom_call_target="tpu_custom_call" | custom-call | tf_op jit(solution)/shard_map/attention_back/pallas_call | solution.py:322
  171.7 1.6 collective-permute-start.30
  173.5 1.8 collective-permute-start.29
  177.1 12.7 %collective-permute-done.32 = bf16[3,40,768]{2,1,0:T(8,128)(2,1)S(1)} collective-permute-done((bf16[3,40,768]{2,1,0:T(8,128)(2,1)S(1)}, bf16[3,40,768]{2,1,0:T(8,128)(2,1)S(1)}, u32[]{:S(2)}, u32[]{:S(2)}) %collective-permute-start.32) | collective-permute-done | bytes 184352 | tf_op jit(solution)/shard_map/ppermute | solution.py:381
  194.7 3.9 %collective-permute-start.36 = (bf16[2,192,768]{2,1,0:T(8,128)(2,1)S(1)}, bf16[2,192,768]{2,1,0:T(8,128)(2,1)S(1)}, u32[]{:S(2)}, u32[]{:S(2)}) collective-permute-start(bf16[2,192,768]{2,1,0:T(8,128)(2,1)S(1)} %pad_maximum_fusion.13), channel_id=1, source_target_pairs={{0,1},{1,0},{2,3},{3,2},{4,5},{5,4},{6,7},{7,6},{8,9},{9,8},{10,11... | collective-permute-start | bytes 1769480 | tf_op jit(solution)/shard_map/ppermute | solution.py:381
  199.8 7.8 %collective-permute-done.34.refs_3_ = bf16[4,2,48,768]{3,2,1,0:T(8,128)(2,1)S(1)} collective-permute-done((bf16[4,2,48,768]{3,2,1,0:T(8,128)(2,1)S(1)}, bf16[4,2,48,768]{3,2,1,0:T(8,128)(2,1)S(1)}, u32[]{:S(2)}, u32[]{:S(2)}) %collective-permute-start.34) | collective-permute-done | bytes 589856 | tf_op jit(solution)/shard_map/ppermute | solution.py:381
  208.0 3.1 %collective-permute-done.36 = bf16[2,192,768]{2,1,0:T(8,128)(2,1)S(1)} collective-permute-done((bf16[2,192,768]{2,1,0:T(8,128)(2,1)S(1)}, bf16[2,192,768]{2,1,0:T(8,128)(2,1)S(1)}, u32[]{:S(2)}, u32[]{:S(2)}) %collective-permute-start.36) | collective-permute-done | bytes 589856 | tf_op jit(solution)/shard_map/ppermute | solution.py:381
  211.2 2.8 %collective-permute-start.40 = (bf16[192,768]{1,0:T(8,128)(2,1)S(1)}, bf16[192,768]{1,0:T(8,128)(2,1)S(1)}, u32[]{:S(2)}, u32[]{:S(2)}) collective-permute-start(bf16[192,768]{1,0:T(8,128)(2,1)S(1)} %fusion.2), channel_id=1, source_target_pairs={{0,2},{1,3},{2,0},{3,1},{4,6},{5,7},{6,4},{7,5},{8,10},{9,11},{10,... | collective-permute-start | bytes 884744 | tf_op jit(solution)/shard_map/ppermute | solution.py:381
  218.0 4.9 %collective-permute-done.42 = f32[24,768]{1,0:T(8,128)S(1)} collective-permute-done((f32[24,768]{1,0:T(8,128)S(1)}, f32[24,768]{1,0:T(8,128)S(1)}, u32[]{:S(2)}, u32[]{:S(2)}) %collective-permute-start.42) | collective-permute-done | bytes 73760 | tf_op jit(solution)/shard_map/ppermute | solution.py:381
  222.9 3.5 %collective-permute-done.41 = bf16[3,40,768]{2,1,0:T(8,128)(2,1)S(1)} collective-permute-done((bf16[3,40,768]{2,1,0:T(8,128)(2,1)S(1)}, bf16[3,40,768]{2,1,0:T(8,128)(2,1)S(1)}, u32[]{:S(2)}, u32[]{:S(2)}) %collective-permute-start.41) | collective-permute-done | bytes 184352 | tf_op jit(solution)/shard_map/ppermute | solution.py:381
  231.0 3.9 %collective-permute-done.46 = f32[24,768]{1,0:T(8,128)S(1)} collective-permute-done((f32[24,768]{1,0:T(8,128)S(1)}, f32[24,768]{1,0:T(8,128)S(1)}, u32[]{:S(2)}, u32[]{:S(2)}) %collective-permute-start.46) | collective-permute-done | bytes 73760 | tf_op jit(solution)/shard_map/ppermute | solution.py:381
  237.9 1.6 collective-permute-start.49
  240.6 3.3 %collective-permute-done.50 = f32[24,768]{1,0:T(8,128)S(1)} collective-permute-done((f32[24,768]{1,0:T(8,128)S(1)}, f32[24,768]{1,0:T(8,128)S(1)}, u32[]{:S(2)}, u32[]{:S(2)}) %collective-permute-start.50) | collective-permute-done | bytes 73760 | tf_op jit(solution)/shard_map/ppermute | solution.py:381
  244.0 2.8 %collective-permute-done.49 = bf16[96,768]{1,0:T(8,128)(2,1)S(1)} collective-permute-done((bf16[96,768]{1,0:T(8,128)(2,1)S(1)}, bf16[96,768]{1,0:T(8,128)(2,1)S(1)}, u32[]{:S(2)}, u32[]{:S(2)}) %collective-permute-start.49) | collective-permute-done | bytes 147488 | tf_op jit(solution)/shard_map/ppermute | solution.py:381
  248.2 1.9 collective-permute-start.54
  252.6 1.8 collective-permute-start.57
  259.0 1.6 fusion
  263.3 2.6 gather_fusion.1
  265.8 2.4 broadcast_select_fusion.4
  268.3 1.9 copy.54
  272.5 1.9 bitcast_convert_fusion.1
  (338 shorter events, 68.1 us)
Async XLA Ops:
  3.3 11.6 %collective-permute-start = (bf16[104,768]{1,0:T(8,128)(2,1)S(1)}, bf16[104,768]{1,0:T(8,128)(2,1)S(1)}, u32[]{:S(2)}, u32[]{:S(2)}) collective-permute-start(bf16[104,768]{1,0:T(8,128)(2,1)S(1)} %concatenate.92), channel_id=1, source_target_pairs={{0,2},{1,3},{2,0},{3,1},{4,6},{5,7},{6,4},{7,5},{8,10},{9,11},{10,... | collective-permute-start | bytes 479240 | tf_op jit(solution)/shard_map/ppermute | solution.py:381
  15.0 15.1 %collective-permute-start.1 = (bf16[2,104,768]{2,1,0:T(8,128)(2,1)S(1)}, bf16[2,104,768]{2,1,0:T(8,128)(2,1)S(1)}, u32[]{:S(2)}, u32[]{:S(2)}) collective-permute-start(bf16[2,104,768]{2,1,0:T(8,128)(2,1)S(1)} %pad_maximum_fusion.19), channel_id=1, source_target_pairs={{0,1},{1,0},{2,3},{3,2},{4,5},{5,4},{6,7},{7,6},{8,9},{9,8},{10,11... | collective-permute-start | bytes 958472 | tf_op jit(solution)/shard_map/ppermute | solution.py:381
  15.8 13.3 %collective-permute-start.2 = (bf16[192,768]{1,0:T(8,128)(2,1)S(1)}, bf16[192,768]{1,0:T(8,128)(2,1)S(1)}, u32[]{:S(2)}, u32[]{:S(2)}) collective-permute-start(bf16[192,768]{1,0:T(8,128)(2,1)S(1)} %pad_maximum_fusion.20), channel_id=1, source_target_pairs={{0,2},{1,3},{2,0},{3,1},{4,6},{5,7},{6,4},{7,5},{8,10},{9,11},{10,... | collective-permute-start | bytes 884744 | tf_op jit(solution)/shard_map/ppermute | solution.py:381
  30.2 16.1 %collective-permute-start.3 = (bf16[2,192,768]{2,1,0:T(8,128)(2,1)S(1)}, bf16[2,192,768]{2,1,0:T(8,128)(2,1)S(1)}, u32[]{:S(2)}, u32[]{:S(2)}) collective-permute-start(bf16[2,192,768]{2,1,0:T(8,128)(2,1)S(1)} %pad_maximum_fusion.12), channel_id=1, source_target_pairs={{0,1},{1,0},{2,3},{3,2},{4,5},{5,4},{6,7},{7,6},{8,9},{9,8},{10,11... | collective-permute-start | bytes 1769480 | tf_op jit(solution)/shard_map/ppermute | solution.py:381
  33.4 6.6 %collective-permute-start.5 = (bf16[3,1,1,48,768]{4,3,0,2,1:T(8,128)(2,1)S(1)}, bf16[3,1,1,48,768]{4,3,0,2,1:T(8,128)(2,1)S(1)}, u32[]{:S(2)}, u32[]{:S(2)}) collective-permute-start(bf16[3,1,1,48,768]{4,3,0,2,1:T(8,128)(2,1)S(1)} %maximum_bitcast_fusion.6), channel_id=1, source_target_pairs={{0,16},{4,20},{8,24},{12,28},{16,0},{20,4},{24,8},{28,12},{1,17},{... | collective-permute-start | bytes 663560 | tf_op jit(solution)/shard_map/ppermute | solution.py:381
  35.0 6.3 %collective-permute-start.4 = (bf16[3,1,1,48,768]{4,3,0,2,1:T(8,128)(2,1)S(1)}, bf16[3,1,1,48,768]{4,3,0,2,1:T(8,128)(2,1)S(1)}, u32[]{:S(2)}, u32[]{:S(2)}) collective-permute-start(bf16[3,1,1,48,768]{4,3,0,2,1:T(8,128)(2,1)S(1)} %maximum_bitcast_fusion.5), channel_id=1, source_target_pairs={{0,8},{4,12},{8,0},{12,4},{16,24},{20,28},{24,16},{28,20},{1,9},{5... | collective-permute-start | bytes 663560 | tf_op jit(solution)/shard_map/ppermute | solution.py:381
  46.4 13.2 %collective-permute-start.9 = (bf16[3,2,1,48,768]{4,3,0,2,1:T(8,128)(2,1)S(1)}, bf16[3,2,1,48,768]{4,3,0,2,1:T(8,128)(2,1)S(1)}, u32[]{:S(2)}, u32[]{:S(2)}) collective-permute-start(bf16[3,2,1,48,768]{4,3,0,2,1:T(8,128)(2,1)S(1)} %pad_maximum_fusion.18), channel_id=1, source_target_pairs={{0,8},{4,12},{8,0},{12,4},{16,24},{20,28},{24,16},{28,20},{1,9},{5... | collective-permute-start | bytes 1327112 | tf_op jit(solution)/shard_map/ppermute | solution.py:381
  48.1 11.6 %collective-permute-start.8 = (bf16[3,1,2,48,768]{4,3,0,2,1:T(8,128)(2,1)S(1)}, bf16[3,1,2,48,768]{4,3,0,2,1:T(8,128)(2,1)S(1)}, u32[]{:S(2)}, u32[]{:S(2)}) collective-permute-start(bf16[3,1,2,48,768]{4,3,0,2,1:T(8,128)(2,1)S(1)} %pad_maximum_fusion.17), channel_id=1, source_target_pairs={{0,16},{4,20},{8,24},{12,28},{16,0},{20,4},{24,8},{28,12},{1,17},{... | collective-permute-start | bytes 1327112 | tf_op jit(solution)/shard_map/ppermute | solution.py:381
  49.7 7.5 %collective-permute-start.10 = (bf16[3,40,768]{2,1,0:T(8,128)(2,1)S(1)}, bf16[3,40,768]{2,1,0:T(8,128)(2,1)S(1)}, u32[]{:S(2)}, u32[]{:S(2)}) collective-permute-start(bf16[3,40,768]{2,1,0:T(8,128)(2,1)S(1)} %get-tuple-element.177), channel_id=1, source_target_pairs={{0,1},{1,0},{2,3},{3,2},{4,5},{5,4},{6,7},{7,6},{8,9},{9,8},{10,11... | collective-permute-start | bytes 552968 | tf_op jit(solution)/shard_map/ppermute | solution.py:381
  51.4 8.2 %collective-permute-start.11 = (bf16[3,40,768]{2,1,0:T(8,128)(2,1)S(1)}, bf16[3,40,768]{2,1,0:T(8,128)(2,1)S(1)}, u32[]{:S(2)}, u32[]{:S(2)}) collective-permute-start(bf16[3,40,768]{2,1,0:T(8,128)(2,1)S(1)} %get-tuple-element.178), channel_id=1, source_target_pairs={{0,3},{1,2},{2,1},{3,0},{4,7},{5,6},{6,5},{7,4},{8,11},{9,10},{10,... | collective-permute-start | bytes 552968 | tf_op jit(solution)/shard_map/ppermute | solution.py:381
  59.9 13.7 %collective-permute-start.13 = (bf16[3,192,768]{2,1,0:T(8,128)(2,1)S(1)}, bf16[3,192,768]{2,1,0:T(8,128)(2,1)S(1)}, u32[]{:S(2)}, u32[]{:S(2)}) collective-permute-start(bf16[3,192,768]{2,1,0:T(8,128)(2,1)S(1)} %bitcast.223), channel_id=1, source_target_pairs={{0,4},{4,0},{8,12},{12,8},{16,20},{20,16},{24,28},{28,24},{1,5},{5... | collective-permute-start | bytes 2654216 | tf_op jit(solution)/shard_map/ppermute | solution.py:381
  60.2 13.4 %collective-permute-start.12 = (bf16[3,192,768]{2,1,0:T(8,128)(2,1)S(1)}, bf16[3,192,768]{2,1,0:T(8,128)(2,1)S(1)}, u32[]{:S(2)}, u32[]{:S(2)}) collective-permute-start(bf16[3,192,768]{2,1,0:T(8,128)(2,1)S(1)} %bitcast.226), channel_id=1, source_target_pairs={{0,4},{4,0},{8,12},{12,8},{16,20},{20,16},{24,28},{28,24},{1,5},{5... | collective-permute-start | bytes 2654216 | tf_op jit(solution)/shard_map/ppermute | solution.py:381
  60.9 12.2 %collective-permute-start.7 = (bf16[3,1,1,96,768]{4,3,0,2,1:T(8,128)(2,1)S(1)}, bf16[3,1,1,96,768]{4,3,0,2,1:T(8,128)(2,1)S(1)}, u32[]{:S(2)}, u32[]{:S(2)}) collective-permute-start(bf16[3,1,1,96,768]{4,3,0,2,1:T(8,128)(2,1)S(1)} %maximum_bitcast_fusion.4), channel_id=1, source_target_pairs={{0,16},{4,20},{8,24},{12,28},{16,0},{20,4},{24,8},{28,12},{1,17},{... | collective-permute-start | bytes 1327112 | tf_op jit(solution)/shard_map/ppermute | solution.py:381
  61.7 11.9 %collective-permute-start.6 = (bf16[3,1,1,96,768]{4,3,0,2,1:T(8,128)(2,1)S(1)}, bf16[3,1,1,96,768]{4,3,0,2,1:T(8,128)(2,1)S(1)}, u32[]{:S(2)}, u32[]{:S(2)}) collective-permute-start(bf16[3,1,1,96,768]{4,3,0,2,1:T(8,128)(2,1)S(1)} %maximum_bitcast_fusion.3), channel_id=1, source_target_pairs={{0,8},{4,12},{8,0},{12,4},{16,24},{20,28},{24,16},{28,20},{1,9},{5... | collective-permute-start | bytes 1327112 | tf_op jit(solution)/shard_map/ppermute | solution.py:381
  62.3 11.3 %collective-permute-start.14 = (bf16[3,40,768]{2,1,0:T(8,128)(2,1)S(1)}, bf16[3,40,768]{2,1,0:T(8,128)(2,1)S(1)}, u32[]{:S(2)}, u32[]{:S(2)}) collective-permute-start(bf16[3,40,768]{2,1,0:T(8,128)(2,1)S(1)} %get-tuple-element.183), channel_id=1, source_target_pairs={{0,2},{1,3},{2,0},{3,1},{4,6},{5,7},{6,4},{7,5},{8,10},{9,11},{10,... | collective-permute-start | bytes 552968 | tf_op jit(solution)/shard_map/ppermute | solution.py:381
  73.8 20.5 %collective-permute-start.16 = (bf16[3,2,1,96,768]{4,3,0,2,1:T(8,128)(2,1)S(1)}, bf16[3,2,1,96,768]{4,3,0,2,1:T(8,128)(2,1)S(1)}, u32[]{:S(2)}, u32[]{:S(2)}) collective-permute-start(bf16[3,2,1,96,768]{4,3,0,2,1:T(8,128)(2,1)S(1)} %pad_maximum_fusion.5), channel_id=1, source_target_pairs={{0,8},{4,12},{8,0},{12,4},{16,24},{20,28},{24,16},{28,20},{1,9},{5... | collective-permute-start | bytes 2654216 | tf_op jit(solution)/shard_map/ppermute | solution.py:381
  75.1 20.9 %collective-permute-start.15 = (bf16[3,1,2,96,768]{4,3,0,2,1:T(8,128)(2,1)S(1)}, bf16[3,1,2,96,768]{4,3,0,2,1:T(8,128)(2,1)S(1)}, u32[]{:S(2)}, u32[]{:S(2)}) collective-permute-start(bf16[3,1,2,96,768]{4,3,0,2,1:T(8,128)(2,1)S(1)} %pad_maximum_fusion.4), channel_id=1, source_target_pairs={{0,16},{4,20},{8,24},{12,28},{16,0},{20,4},{24,8},{28,12},{1,17},{... | collective-permute-start | bytes 2654216 | tf_op jit(solution)/shard_map/ppermute | solution.py:381
  76.5 16.8 %collective-permute-start.17 = (bf16[3,40,768]{2,1,0:T(8,128)(2,1)S(1)}, bf16[3,40,768]{2,1,0:T(8,128)(2,1)S(1)}, u32[]{:S(2)}, u32[]{:S(2)}) collective-permute-start(bf16[3,40,768]{2,1,0:T(8,128)(2,1)S(1)} %get-tuple-element.198), channel_id=1, source_target_pairs={{0,1},{1,0},{2,3},{3,2},{4,5},{5,4},{6,7},{7,6},{8,9},{9,8},{10,11... | collective-permute-start | bytes 552968 | tf_op jit(solution)/shard_map/ppermute | solution.py:381
  76.6 16.7 %collective-permute-start.18 = (bf16[3,40,768]{2,1,0:T(8,128)(2,1)S(1)}, bf16[3,40,768]{2,1,0:T(8,128)(2,1)S(1)}, u32[]{:S(2)}, u32[]{:S(2)}) collective-permute-start(bf16[3,40,768]{2,1,0:T(8,128)(2,1)S(1)} %get-tuple-element.199), channel_id=1, source_target_pairs={{0,2},{1,3},{2,0},{3,1},{4,6},{5,7},{6,4},{7,5},{8,10},{9,11},{10,... | collective-permute-start | bytes 552968 | tf_op jit(solution)/shard_map/ppermute | solution.py:381
  79.3 14.0 %collective-permute-start.19 = (bf16[3,40,768]{2,1,0:T(8,128)(2,1)S(1)}, bf16[3,40,768]{2,1,0:T(8,128)(2,1)S(1)}, u32[]{:S(2)}, u32[]{:S(2)}) collective-permute-start(bf16[3,40,768]{2,1,0:T(8,128)(2,1)S(1)} %get-tuple-element.200), channel_id=1, source_target_pairs={{0,3},{1,2},{2,1},{3,0},{4,7},{5,6},{6,5},{7,4},{8,11},{9,10},{10,... | collective-permute-start | bytes 552968 | tf_op jit(solution)/shard_map/ppermute | solution.py:381
  128.6 12.2 %collective-permute-start.22 = (bf16[4,384,768]{2,1,0:T(8,128)(2,1)}, bf16[4,384,768]{2,1,0:T(8,128)(2,1)S(1)}, u32[]{:S(2)}, u32[]{:S(2)}) collective-permute-start(bf16[4,384,768]{2,1,0:T(8,128)(2,1)} %get-tuple-element.216), channel_id=1, source_target_pairs={{0,4},{4,0},{8,12},{12,8},{16,20},{20,16},{24,28},{28,24},{1,5},{5... | collective-permute-start | bytes 7077896 | tf_op jit(solution)/shard_map/ppermute | solution.py:381
  128.8 12.0 %collective-permute-start.23 = (bf16[4,384,768]{2,1,0:T(8,128)(2,1)}, bf16[4,384,768]{2,1,0:T(8,128)(2,1)S(1)}, u32[]{:S(2)}, u32[]{:S(2)}) collective-permute-start(bf16[4,384,768]{2,1,0:T(8,128)(2,1)} %get-tuple-element.217), channel_id=1, source_target_pairs={{0,4},{4,0},{8,12},{12,8},{16,20},{20,16},{24,28},{28,24},{1,5},{5... | collective-permute-start | bytes 7077896 | tf_op jit(solution)/shard_map/ppermute | solution.py:381
  143.1 28.1 %collective-permute-start.24 = (bf16[4,2,96,768]{3,2,1,0:T(8,128)(2,1)S(1)}, bf16[4,2,96,768]{3,2,1,0:T(8,128)(2,1)S(1)}, u32[]{:S(2)}, u32[]{:S(2)}) collective-permute-start(bf16[4,2,96,768]{3,2,1,0:T(8,128)(2,1)S(1)} %add.195), channel_id=1, source_target_pairs={{0,8},{4,12},{8,0},{12,4},{16,24},{20,28},{24,16},{28,20},{1,9},{5... | collective-permute-start | bytes 3538952 | tf_op jit(solution)/shard_map/ppermute | solution.py:381
  143.7 27.7 %collective-permute-start.25 = (bf16[4,2,96,768]{3,2,1,0:T(8,128)(2,1)S(1)}, bf16[4,2,96,768]{3,2,1,0:T(8,128)(2,1)S(1)}, u32[]{:S(2)}, u32[]{:S(2)}) collective-permute-start(bf16[4,2,96,768]{3,2,1,0:T(8,128)(2,1)S(1)} %add.196), channel_id=1, source_target_pairs={{0,16},{4,20},{8,24},{12,28},{16,0},{20,4},{24,8},{28,12},{1,17},{... | collective-permute-start | bytes 3538952 | tf_op jit(solution)/shard_map/ppermute | solution.py:381
  145.5 25.0 %collective-permute-start.26 = (bf16[3,40,768]{2,1,0:T(8,128)(2,1)S(1)}, bf16[3,40,768]{2,1,0:T(8,128)(2,1)S(1)}, u32[]{:S(2)}, u32[]{:S(2)}) collective-permute-start(bf16[3,40,768]{2,1,0:T(8,128)(2,1)S(1)} %get-tuple-element.230), channel_id=1, source_target_pairs={{0,1},{1,0},{2,3},{3,2},{4,5},{5,4},{6,7},{7,6},{8,9},{9,8},{10,11... | collective-permute-start | bytes 552968 | tf_op jit(solution)/shard_map/ppermute | solution.py:381
  145.5 25.0 %collective-permute-start.27 = (bf16[3,40,768]{2,1,0:T(8,128)(2,1)S(1)}, bf16[3,40,768]{2,1,0:T(8,128)(2,1)S(1)}, u32[]{:S(2)}, u32[]{:S(2)}) collective-permute-start(bf16[3,40,768]{2,1,0:T(8,128)(2,1)S(1)} %get-tuple-element.231), channel_id=1, source_target_pairs={{0,2},{1,3},{2,0},{3,1},{4,6},{5,7},{6,4},{7,5},{8,10},{9,11},{10,... | collective-permute-start | bytes 552968 | tf_op jit(solution)/shard_map/ppermute | solution.py:381
  147.9 22.6 %collective-permute-start.28 = (bf16[3,40,768]{2,1,0:T(8,128)(2,1)S(1)}, bf16[3,40,768]{2,1,0:T(8,128)(2,1)S(1)}, u32[]{:S(2)}, u32[]{:S(2)}) collective-permute-start(bf16[3,40,768]{2,1,0:T(8,128)(2,1)S(1)} %get-tuple-element.232), channel_id=1, source_target_pairs={{0,3},{1,2},{2,1},{3,0},{4,7},{5,6},{6,5},{7,4},{8,11},{9,10},{10,... | collective-permute-start | bytes 552968 | tf_op jit(solution)/shard_map/ppermute | solution.py:381
  171.5 18.4 %collective-permute-start.31 = (bf16[2,4,192,768]{3,2,1,0:T(8,128)(2,1)}, bf16[2,4,192,768]{3,2,1,0:T(8,128)(2,1)S(1)}, u32[]{:S(2)}, u32[]{:S(2)}) collective-permute-start(bf16[2,4,192,768]{3,2,1,0:T(8,128)(2,1)} %get-tuple-element.248), channel_id=1, source_target_pairs={{0,4},{4,0},{8,12},{12,8},{16,20},{20,16},{24,28},{28,24},{1,5},{5... | collective-permute-start | bytes 7077896 | tf_op jit(solution)/shard_map/ppermute | solution.py:381
  171.7 18.2 %collective-permute-start.30 = (bf16[4,1,96,768]{3,2,1,0:T(8,128)(2,1)S(1)}, bf16[4,1,96,768]{3,2,1,0:T(8,128)(2,1)S(1)}, u32[]{:S(2)}, u32[]{:S(2)}) collective-permute-start(bf16[4,1,96,768]{3,2,1,0:T(8,128)(2,1)S(1)} %add.198), channel_id=1, source_target_pairs={{0,8},{4,12},{8,0},{12,4},{16,24},{20,28},{24,16},{28,20},{1,9},{5... | collective-permute-start | bytes 1769480 | tf_op jit(solution)/shard_map/ppermute | solution.py:381
  173.5 16.4 %collective-permute-start.29 = (bf16[4,1,96,768]{3,2,1,0:T(8,128)(2,1)S(1)}, bf16[4,1,96,768]{3,2,1,0:T(8,128)(2,1)S(1)}, u32[]{:S(2)}, u32[]{:S(2)}) collective-permute-start(bf16[4,1,96,768]{3,2,1,0:T(8,128)(2,1)S(1)} %add.197), channel_id=1, source_target_pairs={{0,16},{4,20},{8,24},{12,28},{16,0},{20,4},{24,8},{28,12},{1,17},{... | collective-permute-start | bytes 1769480 | tf_op jit(solution)/shard_map/ppermute | solution.py:381
  175.3 14.6 %collective-permute-start.32 = (bf16[3,40,768]{2,1,0:T(8,128)(2,1)S(1)}, bf16[3,40,768]{2,1,0:T(8,128)(2,1)S(1)}, u32[]{:S(2)}, u32[]{:S(2)}) collective-permute-start(bf16[3,40,768]{2,1,0:T(8,128)(2,1)S(1)} %get-tuple-element.249), channel_id=1, source_target_pairs={{0,2},{1,3},{2,0},{3,1},{4,6},{5,7},{6,4},{7,5},{8,10},{9,11},{10,... | collective-permute-start | bytes 552968 | tf_op jit(solution)/shard_map/ppermute | solution.py:381
  175.6 14.3 %collective-permute-start.33 = (bf16[3,40,768]{2,1,0:T(8,128)(2,1)S(1)}, bf16[3,40,768]{2,1,0:T(8,128)(2,1)S(1)}, u32[]{:S(2)}, u32[]{:S(2)}) collective-permute-start(bf16[3,40,768]{2,1,0:T(8,128)(2,1)S(1)} %get-tuple-element.250), channel_id=1, source_target_pairs={{0,3},{1,2},{2,1},{3,0},{4,7},{5,6},{6,5},{7,4},{8,11},{9,10},{10,... | collective-permute-start | bytes 552968 | tf_op jit(solution)/shard_map/ppermute | solution.py:381
  192.4 15.2 %collective-permute-start.34 = (bf16[4,2,48,768]{3,2,1,0:T(8,128)(2,1)S(1)}, bf16[4,2,48,768]{3,2,1,0:T(8,128)(2,1)S(1)}, u32[]{:S(2)}, u32[]{:S(2)}) collective-permute-start(bf16[4,2,48,768]{3,2,1,0:T(8,128)(2,1)S(1)} %add.201), channel_id=1, source_target_pairs={{0,8},{4,12},{8,0},{12,4},{16,24},{20,28},{24,16},{28,20},{1,9},{5... | collective-permute-start | bytes 1769480 | tf_op jit(solution)/shard_map/ppermute | solution.py:381
  193.2 14.9 %collective-permute-start.35 = (bf16[4,2,48,768]{3,2,1,0:T(8,128)(2,1)S(1)}, bf16[4,2,48,768]{3,2,1,0:T(8,128)(2,1)S(1)}, u32[]{:S(2)}, u32[]{:S(2)}) collective-permute-start(bf16[4,2,48,768]{3,2,1,0:T(8,128)(2,1)S(1)} %add.202), channel_id=1, source_target_pairs={{0,16},{4,20},{8,24},{12,28},{16,0},{20,4},{24,8},{28,12},{1,17},{... | collective-permute-start | bytes 1769480 | tf_op jit(solution)/shard_map/ppermute | solution.py:381
  194.7 16.4 %collective-permute-start.36 = (bf16[2,192,768]{2,1,0:T(8,128)(2,1)S(1)}, bf16[2,192,768]{2,1,0:T(8,128)(2,1)S(1)}, u32[]{:S(2)}, u32[]{:S(2)}) collective-permute-start(bf16[2,192,768]{2,1,0:T(8,128)(2,1)S(1)} %pad_maximum_fusion.13), channel_id=1, source_target_pairs={{0,1},{1,0},{2,3},{3,2},{4,5},{5,4},{6,7},{7,6},{8,9},{9,8},{10,11... | collective-permute-start | bytes 1769480 | tf_op jit(solution)/shard_map/ppermute | solution.py:381
  211.2 15.3 %collective-permute-start.40 = (bf16[192,768]{1,0:T(8,128)(2,1)S(1)}, bf16[192,768]{1,0:T(8,128)(2,1)S(1)}, u32[]{:S(2)}, u32[]{:S(2)}) collective-permute-start(bf16[192,768]{1,0:T(8,128)(2,1)S(1)} %fusion.2), channel_id=1, source_target_pairs={{0,2},{1,3},{2,0},{3,1},{4,6},{5,7},{6,4},{7,5},{8,10},{9,11},{10,... | collective-permute-start | bytes 884744 | tf_op jit(solution)/shard_map/ppermute | solution.py:381
  214.1 12.3 %collective-permute-start.39 = (bf16[4,1,48,768]{3,2,1,0:T(8,128)(2,1)S(1)}, bf16[4,1,48,768]{3,2,1,0:T(8,128)(2,1)S(1)}, u32[]{:S(2)}, u32[]{:S(2)}) collective-permute-start(bf16[4,1,48,768]{3,2,1,0:T(8,128)(2,1)S(1)} %add.204), channel_id=1, source_target_pairs={{0,8},{4,12},{8,0},{12,4},{16,24},{20,28},{24,16},{28,20},{1,9},{5... | collective-permute-start | bytes 884744 | tf_op jit(solution)/shard_map/ppermute | solution.py:381
  215.1 11.3 %collective-permute-start.38 = (bf16[4,1,48,768]{3,2,1,0:T(8,128)(2,1)S(1)}, bf16[4,1,48,768]{3,2,1,0:T(8,128)(2,1)S(1)}, u32[]{:S(2)}, u32[]{:S(2)}) collective-permute-start(bf16[4,1,48,768]{3,2,1,0:T(8,128)(2,1)S(1)} %add.203), channel_id=1, source_target_pairs={{0,16},{4,20},{8,24},{12,28},{16,0},{20,4},{24,8},{28,12},{1,17},{... | collective-permute-start | bytes 884744 | tf_op jit(solution)/shard_map/ppermute | solution.py:381
  216.6 9.9 %collective-permute-start.41 = (bf16[3,40,768]{2,1,0:T(8,128)(2,1)S(1)}, bf16[3,40,768]{2,1,0:T(8,128)(2,1)S(1)}, u32[]{:S(2)}, u32[]{:S(2)}) collective-permute-start(bf16[3,40,768]{2,1,0:T(8,128)(2,1)S(1)} %get-tuple-element.278), channel_id=1, source_target_pairs={{0,1},{1,0},{2,3},{3,2},{4,5},{5,4},{6,7},{7,6},{8,9},{9,8},{10,11... | collective-permute-start | bytes 552968 | tf_op jit(solution)/shard_map/ppermute | solution.py:381
  227.5 7.4 %collective-permute-start.45 = (bf16[2,96,768]{2,1,0:T(8,128)(2,1)S(1)}, bf16[2,96,768]{2,1,0:T(8,128)(2,1)S(1)}, u32[]{:S(2)}, u32[]{:S(2)}) collective-permute-start(bf16[2,96,768]{2,1,0:T(8,128)(2,1)S(1)} %pad_maximum_fusion.21), channel_id=1, source_target_pairs={{0,1},{1,0},{2,3},{3,2},{4,5},{5,4},{6,7},{7,6},{8,9},{9,8},{10,11... | collective-permute-start | bytes 884744 | tf_op jit(solution)/shard_map/ppermute | solution.py:381
  227.6 7.3 %collective-permute-start.43 = (bf16[1,1,1,96,768]{4,3,2,1,0:T(8,128)(2,1)S(1)}, bf16[1,1,1,96,768]{4,3,2,1,0:T(8,128)(2,1)S(1)}, u32[]{:S(2)}, u32[]{:S(2)}) collective-permute-start(bf16[1,1,1,96,768]{4,3,2,1,0:T(8,128)(2,1)S(1)} %get-tuple-element.284), channel_id=1, source_target_pairs={{0,8},{4,12},{8,0},{12,4},{16,24},{20,28},{24,16},{28,20},{1,9},{5... | collective-permute-start | bytes 442376 | tf_op jit(solution)/shard_map/ppermute | solution.py:381
  235.0 11.7 %collective-permute-start.48 = (bf16[1,2,1,96,768]{4,3,2,1,0:T(8,128)(2,1)S(1)}, bf16[1,2,1,96,768]{4,3,2,1,0:T(8,128)(2,1)S(1)}, u32[]{:S(2)}, u32[]{:S(2)}) collective-permute-start(bf16[1,2,1,96,768]{4,3,2,1,0:T(8,128)(2,1)S(1)} %pad_maximum_fusion.24), channel_id=1, source_target_pairs={{0,8},{4,12},{8,0},{12,4},{16,24},{20,28},{24,16},{28,20},{1,9},{5... | collective-permute-start | bytes 884744 | tf_op jit(solution)/shard_map/ppermute | solution.py:381
  236.5 10.2 %collective-permute-start.47 = (bf16[1,1,2,96,768]{4,3,2,1,0:T(8,128)(2,1)S(1)}, bf16[1,1,2,96,768]{4,3,2,1,0:T(8,128)(2,1)S(1)}, u32[]{:S(2)}, u32[]{:S(2)}) collective-permute-start(bf16[1,1,2,96,768]{4,3,2,1,0:T(8,128)(2,1)S(1)} %pad_maximum_fusion.23), channel_id=1, source_target_pairs={{0,16},{4,20},{8,24},{12,28},{16,0},{20,4},{24,8},{28,12},{1,17},{... | collective-permute-start | bytes 884744 | tf_op jit(solution)/shard_map/ppermute | solution.py:381
  237.9 8.9 %collective-permute-start.49 = (bf16[96,768]{1,0:T(8,128)(2,1)S(1)}, bf16[96,768]{1,0:T(8,128)(2,1)S(1)}, u32[]{:S(2)}, u32[]{:S(2)}) collective-permute-start(bf16[96,768]{1,0:T(8,128)(2,1)S(1)} %fusion.4), channel_id=1, source_target_pairs={{0,2},{1,3},{2,0},{3,1},{4,6},{5,7},{6,4},{7,5},{8,10},{9,11},{10,... | collective-permute-start | bytes 442376 | tf_op jit(solution)/shard_map/ppermute | solution.py:381
  252.6 8.2 %collective-permute-start.57 = (bf16[1,2,1,48,768]{4,3,2,1,0:T(8,128)(2,1)S(1)}, bf16[1,2,1,48,768]{4,3,2,1,0:T(8,128)(2,1)S(1)}, u32[]{:S(2)}, u32[]{:S(2)}) collective-permute-start(bf16[1,2,1,48,768]{4,3,2,1,0:T(8,128)(2,1)S(1)} %pad_maximum_fusion.28), channel_id=1, source_target_pairs={{0,8},{4,12},{8,0},{12,4},{16,24},{20,28},{24,16},{28,20},{1,9},{5... | collective-permute-start | bytes 442376 | tf_op jit(solution)/shard_map/ppermute | solution.py:381
  254.5 6.4 %collective-permute-start.56 = (bf16[1,1,2,48,768]{4,3,2,1,0:T(8,128)(2,1)S(1)}, bf16[1,1,2,48,768]{4,3,2,1,0:T(8,128)(2,1)S(1)}, u32[]{:S(2)}, u32[]{:S(2)}) collective-permute-start(bf16[1,1,2,48,768]{4,3,2,1,0:T(8,128)(2,1)S(1)} %pad_maximum_fusion.27), channel_id=1, source_target_pairs={{0,16},{4,20},{8,24},{12,28},{16,0},{20,4},{24,8},{28,12},{1,17},{... | collective-permute-start | bytes 442376 | tf_op jit(solution)/shard_map/ppermute | solution.py:381
  260.9 10.5 %collective-permute-start.58 = (bf16[1,192,768]{2,1,0:T(8,128)(2,1)S(1)}, bf16[1,192,768]{2,1,0:T(8,128)(2,1)}, u32[]{:S(2)}, u32[]{:S(2)}) collective-permute-start(bf16[1,192,768]{2,1,0:T(8,128)(2,1)S(1)} %bitcast.249), channel_id=1, source_target_pairs={{0,4},{4,0},{8,12},{12,8},{16,20},{20,16},{24,28},{28,24},{1,5},{5... | collective-permute-start | bytes 884744 | tf_op jit(solution)/shard_map/ppermute | solution.py:381
  261.8 10.7 %collective-permute-start.59 = (bf16[1,192,768]{2,1,0:T(8,128)(2,1)}, bf16[1,192,768]{2,1,0:T(8,128)(2,1)}, u32[]{:S(2)}, u32[]{:S(2)}) collective-permute-start(bf16[1,192,768]{2,1,0:T(8,128)(2,1)} %bitcast.87), channel_id=1, source_target_pairs={{0,4},{4,0},{8,12},{12,8},{16,20},{20,16},{24,28},{28,24},{1,5},{5... | collective-permute-start | bytes 884744 | tf_op jit(solution)/shard_map/ppermute | solution.py:381
  (74 other events, 638.7 us)

commit v4 on v3

--- a/solution.py
+++ b/solution.py
@@ -56,8 +56,8 @@
     return total
 
 
-def head_weights(here_ref, own_ref, one_ref, two_ref):
-    first, low = pl.program_id(0) == 0, here_ref[0] == 0
+def head_weights(first, here_ref, own_ref, one_ref, two_ref):
+    low = here_ref[0] == 0
     half = one_ref.shape[1]
     one, two = one_ref[0], two_ref[0]
     return (
@@ -75,8 +75,8 @@
     heads = cols // HEAD
     slots = x_ref.shape[0] // pairs
     x = x_ref[...]
-    w_q, w_k = head_weights(here_ref, own_qk, qk_one, qk_two)
-    w_v, w_o = head_weights(here_ref, own_vo, vo_one, vo_two)
+    w_q, w_k = head_weights(step == 0, here_ref, own_qk, qk_one, qk_two)
+    w_v, w_o = head_weights(step == 0, here_ref, own_vo, vo_one, vo_two)
     q_ref[0] = (dot(x, w_q, 1, 1) + small_ref[0, 0:1, :cols]).astype(BF16)
     k_ref[0] = dot(x, w_k, 1, 1).astype(BF16)
     v_ref[0] = (dot(x, w_v, 1, 1) + small_ref[0, 1:2, :cols]).astype(BF16)
@@ -118,105 +118,183 @@
     return parts[0] if len(parts) == 1 else jnp.concatenate(parts, axis=0)
 
 
+def unit_columns(one, two, start, stop):
+    half = one.shape[1]
+    parts = []
+    if start < half:
+        parts.append(one[:, start : min(stop, half)])
+    if stop > half:
+        parts.append(two[:, max(start - half, 0) : stop - half])
+    return parts[0] if len(parts) == 1 else jnp.concatenate(parts, axis=1)
+
+
 def blocks_of(units):
     size = min(256, units)
     return [(start, start + size) for start in range(0, units, size)]
 
 
+def join_rows(refs):
+    pairs = refs[0].shape[0]
+    return jnp.concatenate([ref[p].astype(F32) for p in range(pairs) for ref in refs], axis=0)
+
+
+def leave_rows(array, refs):
+    pairs, rows = refs[0].shape[:2]
+    for p in range(pairs):
+        for j, ref in enumerate(refs):
+            start = (p * len(refs) + j) * rows
+            ref[p] = array[start : start + rows].astype(BF16)
+
+
 def ffn_kernel(
-    here_ref, low_ref, normed_ref, own_in_one, own_in_two, in_one, in_two, own_down_one, own_down_two, down_one,
-    down_two, bias_one, bias_two, cot_ref, vectors_ref,
-    out_ref, delta_ref, pre_grad_ref, in_keep_ref, in_send_ref, down_keep_ref, down_send_ref, sum_in_ref, sums_ref,
-    act_ref, slope_ref, ffn_low_ref, total_ref,
+    count, here_ref, low_hbm, normed_hbm, w_in_hbm, in_one_hbm, in_two_hbm, w_down_hbm, down_one_hbm, down_two_hbm,
+    small_ref, vectors_ref, *refs,
+):
+    cot_hbm, out_refs = refs[:count], refs[count : 2 * count]
+    (
+        delta_hbm, pre_grad_hbm, in_keep_hbm, in_send_hbm, down_keep_hbm, down_send_hbm, sum_in_ref, sums_ref,
+        low_ref, normed_ref, w_in_ref, in_one, in_two, w_down_ref, down_one, down_two, cot_ref, act_ref, slope_ref,
+        total_ref, delta_ref, pre_grad_ref, in_keep_ref, in_send_ref, down_keep_ref, down_send_ref, sems,
+    ) = refs[2 * count :]
+    core = here_ref[0]
+    half = in_one.shape[1]
+    started = [0]
+
+    def start(*pairs):
+        copies = []
+        for source, target in pairs:
+            copies.append(pltpu.make_async_copy(source, target, sems.at[started[0]]))
+            copies[-1].start()
+            started[0] += 1
+        return copies
+
+    def wait(copies):
+        for copy in copies:
+            copy.wait()
+
+    def shard(slot):
+        k = slot - 1
+        return start(
+            (in_one_hbm.at[k], in_one.at[k]),
+            (in_two_hbm.at[k], in_two.at[k]),
+            (down_one_hbm.at[k], down_one.at[k]),
+            (down_two_hbm.at[k], down_two.at[k]),
+        )
+
+    def halves(start_, stop):
+        parts = []
+        if start_ < half:
+            parts.append((0, start_, min(stop, half)))
+        if stop > half:
+            parts.append((1, max(start_ - half, 0), stop - half))
+        return parts
+
+    def own(which, first, last):
+        side = core if which == 0 else 1 - core
+        return pl.ds(pl.multiple_of(side * half + first, 128), last - first)
+
+    def down_rows(slot, start_, stop):
+        if slot == 0:
+            parts = [w_down_ref[own(w, a, b)] for w, a, b in halves(start_, stop)]
+        else:
+            parts = [(down_one, down_two)[w][slot - 1, a:b] for w, a, b in halves(start_, stop)]
+        return jnp.concatenate(parts, axis=0)
+
+    def forward(slot):
+        low = low_ref[...]
+        branch = None
+        for first, last in blocks_of(2 * half):
+            parts = halves(first, last)
+            if slot == 0:
+                w_in = jnp.concatenate([w_in_ref[:, own(*p)] for p in parts], axis=1)
+                pre_act = dot(low, w_in, 1, 0)
+            else:
+                w_in = jnp.concatenate([(in_one, in_two)[w][slot - 1, a:b] for w, a, b in parts], axis=0)
+                pre_act = dot(low, w_in, 1, 1)
+            bias = jnp.concatenate([small_ref[slot, 2:3, own(*p)] for p in parts], axis=1)
+            pre_act = pre_act + bias
+            share = 0.5 * (1.0 + lax.erf(pre_act * SQRT_HALF))
+            act = (pre_act * share).astype(BF16)
+            act_ref[slot, :, first:last] = act
+            slope_ref[slot, :, first:last] = share + pre_act * (DENSITY * jnp.exp(-0.5 * pre_act * pre_act))
+            term = dot(act, down_rows(slot, first, last), 1, 0)
+            branch = term if branch is None else branch + term
+        if slot == 0:
+            total_ref[...] = branch
+        else:
+            total_ref[...] += branch
+
+    first_copies = start((low_hbm, low_ref), (w_in_hbm, w_in_ref), (w_down_hbm, w_down_ref))
+    ahead = shard(1)
+    wait(first_copies)
+    forward(0)
+    for slot in range(1, count):
+        copies = ahead
+        if slot + 1 < count:
+            ahead = shard(slot + 1)
+        else:
+            ahead = start((normed_hbm, normed_ref), *[(cot_hbm[k], cot_ref.at[k]) for k in range(count)])
+        wait(copies)
+        forward(slot)
+    wait(ahead)
+
+    hidden = normed_ref[...] * vectors_ref[1:2] + vectors_ref[2:3]
+    second = total_ref[...] + vectors_ref[3:4] + hidden
+    gain = vectors_ref[4:5]
+    output, normed, scale = normalize(second, gain, vectors_ref[5:6])
+    leave_rows(output, out_refs)
+    upstream = join_rows([cot_ref.at[k] for k in range(count)])
+    delta = normalize_back(upstream, normed, scale, gain)
+    delta_ref[...] = delta
+    leaving = start((delta_ref, delta_hbm))
+    sums_ref[...] = jnp.zeros_like(sums_ref)
+    sums_ref[0:1] = column_sum(upstream * normed)
+    sums_ref[1:2] = column_sum(upstream)
+    sums_ref[2:3] = column_sum(delta)
+    ffn_low = delta.astype(BF16)
+    low = low_ref[...]
+    for slot in range(count):
+        for first, last in blocks_of(2 * half):
+            act_grad = dot(ffn_low, down_rows(slot, first, last), 1, 1)
+            pre_grad_ref[slot, :, first:last] = (act_grad * slope_ref[slot, :, first:last]).astype(BF16)
+        leaving += start((pre_grad_ref.at[slot], pre_grad_hbm.at[slot]))
+        down_send_ref[slot] = dot(act_ref[slot, :, half:], ffn_low, 0, 0).astype(BF16)
+        leaving += start((down_send_ref.at[slot], down_send_hbm.at[slot]))
+        down_keep_ref[slot] = dot(act_ref[slot, :, :half], ffn_low, 0, 0).astype(BF16)
+        leaving += start((down_keep_ref.at[slot], down_keep_hbm.at[slot]))
+        one, two = pre_grad_ref[slot, :, :half], pre_grad_ref[slot, :, half:]
+        in_send_ref[slot] = dot(two, low, 0, 0).astype(BF16)
+        leaving += start((in_send_ref.at[slot], in_send_hbm.at[slot]))
+        in_keep_ref[slot] = dot(one, low, 0, 0).astype(BF16)
+        leaving += start((in_keep_ref.at[slot], in_keep_hbm.at[slot]))
+        natural = slot ^ here_ref[1]
+        sum_in_ref[natural, :, own(0, 0, half)] = column_sum(one.astype(F32))
+        sum_in_ref[natural, :, own(1, 0, half)] = column_sum(two.astype(F32))
+    wait(leaving)
+
+
+def ffn_back_kernel(
+    here_ref, pre_grad_ref, own_in_one, own_in_two, in_one, in_two, delta_ref, normed_ref, scale_ref, vectors_ref,
+    delta_attn_ref, attn_low_ref, sums_ref, total_ref,
 ):
     step = pl.program_id(0)
-    shards_ = pl.num_programs(0) // 2
-    core = here_ref[0]
-    half = in_one.shape[1]
-
-    def down_of(first, slot):
-        if first:
-            return own_down_one, own_down_two
-        other = pl.ds(slot - 1, 1)
-        return down_one.at[other], down_two.at[other]
-
-    def forward(first):
-        low = low_ref[...]
-        bias = jnp.concatenate([bias_one[0, 2:3], bias_two[0, 2:3]], axis=1)
-        w_in = (own_in_one, own_in_two) if first else (in_one, in_two)
-        w_down = down_of(first, step)
+
+    def body(first):
         branch = None
-        for start, stop in blocks_of(2 * half):
-            pre_act = dot(low, unit_rows(*w_in, start, stop), 1, 1) + bias[:, start:stop]
-            share = 0.5 * (1.0 + lax.erf(pre_act * SQRT_HALF))
-            act = (pre_act * share).astype(BF16)
-            act_ref[step, :, start:stop] = act
-            slope_ref[step, :, start:stop] = share + pre_act * (DENSITY * jnp.exp(-0.5 * pre_act * pre_act))
-            term = dot(act, unit_rows(*w_down, start, stop), 1, 0)
+        for start, stop in blocks_of(pre_grad_ref.shape[2]):
+            pre_grad = pre_grad_ref[0, :, start:stop]
+            if first:
+                term = dot(pre_grad, unit_columns(own_in_one, own_in_two, start, stop), 1, 1)
+            else:
+                term = dot(pre_grad, unit_rows(in_one, in_two, start, stop), 1, 0)
             branch = term if branch is None else branch + term
         if first:
             total_ref[...] = branch
         else:
             total_ref[...] += branch
 
-    def backward(first):
-        slot = 0 if first else step - shards_
-        ffn_low = ffn_low_ref[...]
-        w_down = down_of(first, slot)
-        for start, stop in blocks_of(2 * half):
-            act_grad = dot(ffn_low, unit_rows(*w_down, start, stop), 1, 1)
-            pre_grad_ref[0, :, start:stop] = (act_grad * slope_ref[slot, :, start:stop]).astype(BF16)
-        down_send_ref[0] = dot(act_ref[slot, :, half:], ffn_low, 0, 0).astype(BF16)
-        down_keep_ref[0] = dot(act_ref[slot, :, :half], ffn_low, 0, 0).astype(BF16)
-        low = low_ref[...]
-        one, two = pre_grad_ref[0, :, :half], pre_grad_ref[0, :, half:]
-        sum_in_ref[0, :, pl.ds(pl.multiple_of(core * half, half), half)] = column_sum(one.astype(F32))
-        sum_in_ref[0, :, pl.ds(pl.multiple_of((1 - core) * half, half), half)] = column_sum(two.astype(F32))
-        in_send_ref[0] = dot(two, low, 0, 0).astype(BF16)
-        in_keep_ref[0] = dot(one, low, 0, 0).astype(BF16)
-
-    pl.when(step == 0)(partial(forward, True))
-    pl.when((step > 0) & (step < shards_))(partial(forward, False))
-
-    @pl.when(step == shards_ - 1)
-    def _():
-        hidden = normed_ref[...] * vectors_ref[1:2] + vectors_ref[2:3]
-        second = total_ref[...] + vectors_ref[3:4] + hidden
-        gain = vectors_ref[4:5]
-        output, normed, scale = normalize(second, gain, vectors_ref[5:6])
-        out_ref[...] = output.astype(BF16)
-        upstream = cot_ref[...].astype(F32)
-        delta = normalize_back(upstream, normed, scale, gain)
-        delta_ref[...] = delta
-        ffn_low_ref[...] = delta.astype(BF16)
-        sums_ref[...] = jnp.zeros_like(sums_ref)
-        sums_ref[0:1] = column_sum(upstream * normed)
-        sums_ref[1:2] = column_sum(upstream)
-        sums_ref[2:3] = column_sum(delta)
-
-    pl.when(step == shards_)(partial(backward, True))
-    pl.when(step > shards_)(partial(backward, False))
-
-
-def ffn_back_kernel(
-    here_ref, pre_grad_ref, own_in_one, own_in_two, in_one, in_two, delta_ref, normed_ref, scale_ref, vectors_ref,
-    delta_attn_ref, attn_low_ref, sums_ref, total_ref,
-):
-    step = pl.program_id(0)
-    units = pre_grad_ref.shape[2]
-
-    def body(first, w_in_one, w_in_two):
-        branch = None
-        for start, stop in blocks_of(units):
-            term = dot(pre_grad_ref[0, :, start:stop], unit_rows(w_in_one, w_in_two, start, stop), 1, 0)
-            branch = term if branch is None else branch + term
-        if first:
-            total_ref[...] = branch
-        else:
-            total_ref[...] += branch
-
-    pl.when(step == 0)(partial(body, True, own_in_one, own_in_two))
-    pl.when(step > 0)(partial(body, False, in_one, in_two))
+    pl.when(step == 0)(partial(body, True))
+    pl.when(step > 0)(partial(body, False))
 
     @pl.when(step == pl.num_programs(0) - 1)
     def _():
@@ -232,11 +310,24 @@
 
 
 def attention_back_kernel(
-    pairs, here_ref, x_ref, attn_low_ref, delta_ref, own_qk, qk_one, qk_two, own_vo, vo_one, vo_two, q_ref, k_ref, v_ref, weights_ref, context_ref,
-    sums_one_ref, sums_two_ref, sum_in_ref,
-    qk_keep_ref, vo_keep_ref, send_ref, sums_ref, rows_ref, dq_ref, dk_ref, dv_ref, total_ref,
+    pairs, here_ref, x_ref, attn_low_ref, delta_ref, own_qk, qk_one, qk_two, own_vo, vo_one, vo_two, q_ref, k_ref,
+    v_ref, weights_ref, context_ref, sums_one_ref, sums_two_ref, sum_in_ref,
+    qk_keep_ref, vo_keep_ref, send_ref, sums_ref, *refs,
 ):
     step = pl.program_id(0)
+    shards_ = pl.num_programs(0)
+    out_refs = refs[:shards_]
+    dq_ref, dk_ref, dv_ref, total_ref = refs[shards_:]
+
+    @pl.when(step == 0)
+    def _():
+        total_ref[...] = delta_ref[...]
+        sums_ref[...] = jnp.zeros_like(sums_ref)
+        sums_ref[0:8] = sums_one_ref[...]
+        sums_ref[8:16] = sums_two_ref[...]
+        for j in range(shards_):
+            sums_ref[16 + j : 17 + j] = sum_in_ref[j]
+
     core = here_ref[0]
     cols = q_ref.shape[2]
     heads = cols // HEAD
@@ -244,8 +335,8 @@
     scale = HEAD ** (-0.5)
     x = x_ref[...]
     attn_low = attn_low_ref[...]
-    w_q, w_k = head_weights(here_ref, own_qk, qk_one, qk_two)
-    w_v, w_o = head_weights(here_ref, own_vo, vo_one, vo_two)
+    w_q, w_k = head_weights(step == 0, here_ref, own_qk, qk_one, qk_two)
+    w_v, w_o = head_weights(step == 0, here_ref, own_vo, vo_one, vo_two)
     context_grad = dot(attn_low, w_o, 1, 1).astype(BF16)
     grad_out = dot(context_ref[0], attn_low, 0, 0).astype(BF16)
     for p in range(pairs):
@@ -261,16 +352,6 @@
         key_grad = dot(score_grad, head_stack(q_ref[0, rows], heads), 0, 0)
         dk_ref[rows] = (key_grad * scale).astype(BF16)
     dq, dk, dv = dq_ref[...], dk_ref[...], dv_ref[...]
-    shards_ = pl.num_programs(0)
-
-    @pl.when(step == 0)
-    def _():
-        sums_ref[...] = jnp.zeros_like(sums_ref)
-        sums_ref[0:8] = sums_one_ref[...]
-        sums_ref[8:16] = sums_two_ref[...]
-        for j in range(sum_in_ref.shape[0]):
-            sums_ref[16 + j : 17 + j] = sum_in_ref[j]
-
     row = pl.ds(16 + shards_ + (step ^ here_ref[1]), 1)
     sums_ref[row, :cols] = column_sum(dq.astype(F32))
     sums_ref[row, 2 * cols : 3 * cols] = column_sum(dv.astype(F32))
@@ -288,19 +369,37 @@
         qk_keep_ref[0], send_ref[0, 0] = grad_k, grad_q
         vo_keep_ref[0], send_ref[1, 0] = grad_out, grad_v
 
-    branch = dot(dq, w_q, 1, 0) + dot(dk, w_k, 1, 0) + dot(dv, w_v, 1, 0)
-
-    @pl.when(step == 0)
+    total_ref[...] += dot(dq, w_q, 1, 0) + dot(dk, w_k, 1, 0) + dot(dv, w_v, 1, 0)
+
+    @pl.when(step == shards_ - 1)
     def _():
-        total_ref[...] = branch + delta_ref[...]
-
-    @pl.when(step > 0)
-    def _():
-        total_ref[...] += branch
-
-    @pl.when(step == pl.num_programs(0) - 1)
-    def _():
-        rows_ref[...] = total_ref[...].astype(BF16)
+        leave_rows(total_ref[...], out_refs)
+
+
+def place_kernel(pairs, here_ref, *refs):
+    out_ref = refs[-1]
+    for k, ref in enumerate(refs[:-1]):
+        out_ref[pl.ds((here_ref[1] ^ k) * pairs, pairs)] = ref[...].astype(out_ref.dtype)
+
+
+def head_grads_kernel(here_ref, qk_ref, vo_ref, qk_other, vo_other, grad_qkv_ref, grad_out_ref):
+    low = here_ref[0] == 0
+    pick_two = lambda a, b: (jnp.where(low, a[0], b[0]), jnp.where(low, b[0], a[0]))
+    grad_q, grad_k = pick_two(qk_ref, qk_other)
+    grad_v, grad_out = pick_two(vo_ref, vo_other)
+    for j, grad in enumerate((grad_q, grad_k, grad_v)):
+        grad_qkv_ref[j] = grad.astype(F32)
+    grad_out_ref[...] = grad_out.astype(F32)
+
+
+def unit_grads_kernel(here_ref, in_ref, down_ref, in_other, down_other, grad_in_ref, grad_down_ref):
+    half = in_ref.shape[1]
+    mine = pl.multiple_of(here_ref[0] * half, half)
+    other = pl.multiple_of((1 - here_ref[0]) * half, half)
+    grad_in_ref[:, pl.ds(mine, half)] = in_ref[0].astype(F32).T
+    grad_in_ref[:, pl.ds(other, half)] = in_other[0].astype(F32).T
+    grad_down_ref[pl.ds(mine, half)] = down_ref[0].astype(F32)
+    grad_down_ref[pl.ds(other, half)] = down_other[0].astype(F32)
 
 
 def whole(array):
@@ -309,6 +408,16 @@
 
 def per_step(array):
     return pl.BlockSpec((1,) + array.shape[1:], lambda s, *_: (s,) + (0,) * (len(array.shape) - 1))
+
+
+def in_place(array):
+    if array.size * array.dtype.itemsize < MIB:
+        return array
+    return pltpu.with_memory_space_constraint(array, pltpu.HBM)
+
+
+def where_it_is(array):
+    return pl.BlockSpec(memory_space=pl.ANY)
 
 
 def call(kernel, steps, name, vmem, inputs, outputs, scratch, scalar, kept=()):
@@ -326,7 +435,7 @@
         name=name,
         cost_estimate=pl.CostEstimate(flops=0, bytes_accessed=0, transcendentals=0),
         compiler_params=pltpu.CompilerParams(vmem_limit_bytes=vmem * MIB),
-    )(scalar, *[a for _, a in inputs])
+    )(scalar, *[in_place(a) for _, a in inputs])
 
 
 def shape(dims, dtype):
@@ -423,13 +532,6 @@
 
     def halves(self):
         return [h.reshape(self.n, -1, self.cols) for h in self.held]
-
-    def finish(self, halves, got):
-        low = (lax.axis_index("dp") & 1) == 0
-        return [
-            jnp.concatenate([jnp.where(low, h, g), jnp.where(low, g, h)], axis=1)
-            for h, g in zip(halves, got)
-        ]
 
 
 class Reduce:
@@ -514,6 +616,7 @@
         "in": w_in.T,
         "down": w_down,
     }
+    own_qk, own_vo = own["qk"], own["vo"]
 
     def piece(name):
         part = own[name].shape[0] // dp
@@ -545,30 +648,28 @@
         slot_index[None, :] - WORDS < regions[:, None],
     ).astype(F32)[:, None, :]
 
-    att_two = flip(att_send, "mp", 2)
-    att_two, ffn_send, tok, vectors, key_valid, here, own = tie(
-        att_two, ffn_send, tok, vectors, key_valid, here, own
-    )
-    att_odd = flip(jnp.stack([att_send, att_two]), "mp", 1)
-    ffn_two = flip(ffn_send, "mp", 2)
-    att_odd, ffn_two = tie(att_odd, ffn_two)
-    att_got = [att_odd[0], att_two, att_odd[1]]
+    att_got = [flip(att_send, "mp", k) for k in range(1, mp)]
+    att_got, ffn_send, tok, vectors, key_valid, here, own_qk, own_vo = tie(
+        att_got, ffn_send, tok, vectors, key_valid, here, own_qk, own_vo
+    )
     att = Gather(
         [
             jnp.stack([g[:att_part] for g in att_got]),
             jnp.stack([g[att_part : 2 * att_part] for g in att_got]),
         ]
     )
-    ffn_odd = flip(jnp.stack([ffn_send, ffn_two]), "mp", 1)
+    ffn_two = flip(ffn_send, "mp", 2)
     got = att.send(0)
+    tok_one = flip(tok[1], "mp", 1)
+    ffn_two, got, tok_one, ffn_send, tok, att_got = tie(ffn_two, got, tok_one, ffn_send, tok, att_got)
     smalls = jnp.stack([small] + [g[2 * att_part :] for g in att_got]).astype(F32)
-    ffn_odd, got, tok, smalls = tie(ffn_odd, got, tok, smalls)
     for step in range(1, att.steps):
         att.take(step - 1, got)
         got = att.send(step)
         if step == 1:
-            tok_one, tok_three = flip(tok[1], "mp", 1), flip(tok[3], "mp", 3)
-        got, tok_one, tok_three, tok = tie(got, tok_one, tok_three, tok)
+            ffn_odd = flip(jnp.stack([ffn_send, ffn_two]), "mp", 1)
+            tok_three = flip(tok[3], "mp", 3)
+        got, ffn_odd, tok_three, tok, smalls = tie(got, ffn_odd, tok_three, tok, smalls)
     att.take(att.steps - 1, got)
     ffn_got = [ffn_odd[0], ffn_two, ffn_odd[1]]
     ffn = Gather(
@@ -582,24 +683,25 @@
     qk_two, vo_two = flip(qk_one, "dp", 1), flip(vo_one, "dp", 1)
     tok_two = flip(tok[2], "mp", 2)
     got, qk_two, vo_two, tok_two, cot = tie(got, qk_two, vo_two, tok_two, cot)
-    x = join([tok[0], tok_one, tok_two, tok_three])
     heads_low = shape((mp, rows, cols), BF16)
     low_shape = shape((rows, width), BF16)
     rows_shape = shape((rows, width), F32)
     sums_shape = shape((8, width), F32)
+    block_shape = shape((pairs, rows_local, width), BF16)
     for step in range(1, ffn.steps):
         ffn.take(step - 1, got)
         got = ffn.send(step)
         if step == 1:
-            cot_one, cot_two, cot_three = [flip(cot[k], "mp", k) for k in range(1, mp)]
+            cot_blocks = [cot[0]] + [flip(cot[k], "mp", k) for k in range(1, mp)]
         if step < ffn.steps - 1:
             got = tie(*got)
+    x = join([tok[0], tok_one, tok_two, tok_three])
     later = lambda a: pl.BlockSpec((1,) + a.shape[1:], lambda s, h: (jnp.clip(s - 1, 0, mp - 2), 0, 0))
     head_args = [
-        (whole, own["qk"]),
+        (whole, own_qk),
         (later, qk_one),
         (later, qk_two),
-        (whole, own["vo"]),
+        (whole, own_vo),
         (later, vo_one),
         (later, vo_two),
     ]
@@ -629,68 +731,80 @@
         here,
         range(5),
     )
-    got, hidden_low, cot_one, cot_two, cot_three = tie(got, hidden_low, cot_one, cot_two, cot_three)
+    got, hidden_low, cot_blocks = tie(got, hidden_low, cot_blocks)
     ffn.take(ffn.steps - 1, got)
     in_one, down_one = ffn.halves()
     in_two, down_two = flip(in_one, "dp", 1), flip(down_one, "dp", 1)
-    cot_rows = join([cot[0], cot_one, cot_two, cot_three])
-    in_two, down_two, hidden_low, cot_rows = tie(in_two, down_two, hidden_low, cot_rows)
-
-    half_block = (1, half_units, width)
-    mine = pl.BlockSpec(half_block, lambda s, h: (h[0], 0, 0))
-    other = pl.BlockSpec(half_block, lambda s, h: (1 - h[0], 0, 0))
-    own_in = own["in"].reshape(2, half_units, width)
-    own_down = own["down"].reshape(2, half_units, width)
-    in_args = [(mine, own_in), (other, own_in), (later, in_one), (later, in_two)]
-    down_args = [(mine, own_down), (other, own_down), (whole, down_one), (whole, down_two)]
+    in_two, down_two, hidden_low = tie(in_two, down_two, hidden_low)
+
+    column_mine = pl.BlockSpec((width, half_units), lambda s, h: (0, h[0]))
+    column_other = pl.BlockSpec((width, half_units), lambda s, h: (0, 1 - h[0]))
+    in_args = [(column_mine, w_in), (column_other, w_in), (later, in_one), (later, in_two)]
     half = shape((mp, half_units, width), BF16)
-    bias_block = (1, 8, half_units)
-    back_step = lambda s: jnp.maximum(s - mp, 0)
-    back = lambda a: pl.BlockSpec((1,) + a.shape[1:], lambda s, h: (back_step(s), 0, 0))
-    output, delta_ffn, pre_grad, in_keep, in_send, down_keep, down_send, sum_in, sums_two = call(
-        ffn_kernel,
-        2 * mp,
+    pre_shape = shape((mp, rows, units), BF16)
+    others = (mp - 1, half_units, width)
+    vmem = lambda a: pltpu.VMEM(a.shape, a.dtype)
+    results = call(
+        partial(ffn_kernel, mp),
+        1,
         "ffn",
         52,
         [
-            (whole, hidden_low),
-            (whole, normed_one),
-            *in_args,
-            *down_args,
-            (pl.BlockSpec(bias_block, lambda s, h: (jnp.minimum(s, mp - 1), 0, h[0])), smalls),
-            (pl.BlockSpec(bias_block, lambda s, h: (jnp.minimum(s, mp - 1), 0, 1 - h[0])), smalls),
-            (whole, cot_rows),
+            (where_it_is, hidden_low),
+            (where_it_is, normed_one),
+            (where_it_is, w_in),
+            (where_it_is, in_one),
+            (where_it_is, in_two),
+            (where_it_is, w_down),
+            (where_it_is, down_one),
+            (where_it_is, down_two),
+            (whole, smalls),
             (whole, vectors),
+            *[(where_it_is, c) for c in cot_blocks],
         ],
         [
-            (whole, low_shape),
-            (whole, rows_shape),
-            (back, shape((mp, rows, units), BF16)),
-            (back, half),
-            (back, half),
-            (back, half),
-            (back, half),
-            (
-                pl.BlockSpec((1, 1, units), lambda s, h: (back_step(s) ^ h[1], 0, 0)),
-                shape((mp, 1, units), F32),
-            ),
+            *[(whole, block_shape)] * mp,
+            (where_it_is, rows_shape),
+            (where_it_is, pre_shape),
+            (where_it_is, half),
+            (where_it_is, half),
+            (where_it_is, half),
+            (where_it_is, half),
+            (whole, shape((mp, 1, units), F32)),
             (whole, sums_shape),
         ],
         [
-            pltpu.VMEM((mp, rows, units), BF16),
-            pltpu.VMEM((mp, rows, units), F32),
-            pltpu.VMEM((rows, width), BF16),
-            pltpu.VMEM((rows, width), F32),
+            vmem(low_shape),
+            vmem(rows_shape),
+            pltpu.VMEM((width, units), BF16),
+            pltpu.VMEM(others, BF16),
+            pltpu.VMEM(others, BF16),
+            pltpu.VMEM((units, width), BF16),
+            pltpu.VMEM(others, BF16),
+            pltpu.VMEM(others, BF16),
+            pltpu.VMEM((mp,) + block_shape.shape, BF16),
+            vmem(pre_shape),
+            pltpu.VMEM(pre_shape.shape, F32),
+            vmem(rows_shape),
+            vmem(rows_shape),
+            vmem(pre_shape),
+            vmem(half),
+            vmem(half),
+            vmem(half),
+            vmem(half),
+            pltpu.SemaphoreType.DMA((3 + 4 * (mp - 1) + 1 + mp + 1 + 5 * mp,)),
         ],
         here,
-        range(2, 7),
-    )
+        range(mp, mp + 6),
+    )
+    out_blocks = results[:mp]
+    delta_ffn, pre_grad, in_keep, in_send, down_keep, down_send, sum_in, sums_two = results[mp:]
     in_got, down_got = flip(in_send, "dp", 1), flip(down_send, "dp", 1)
     delta_attn, attn_low, sums_one = call(
         ffn_back_kernel,
         mp,
         "ffn_back",
-        24,
+        32,
         [
             (per_step, pre_grad),
             *in_args,
@@ -703,20 +817,18 @@
         [pltpu.VMEM((rows, width), F32)],
         here,
     )
-    out_rows = output.reshape(pairs, mp, rows_local, width)
-    out_blocks = [out_rows[:, k] for k in range(mp)]
-    in_got, down_got, attn_low, out_blocks = tie(in_got, down_got, attn_low, out_blocks)
+    in_got, down_got, out_blocks, attn_low = tie(in_got, down_got, out_blocks, attn_low)
     ffn = Reduce([in_keep, down_keep], [in_got, down_got])
     packs = ffn.pack(0)
-    packs, attn_low = tie(packs, attn_low)
+    packs, attn_low, out_blocks = tie(packs, attn_low, out_blocks)
     got = ffn.send(0, packs)
     out_got = [out_blocks[0]] + [flip(out_blocks[k], "mp", k) for k in range(1, mp)]
     small_half = shape((mp, cols, width), BF16)
-    qk_keep, vo_keep, att_send, sums, grad_rows = call(
+    results = call(
         partial(attention_back_kernel, pairs),
         mp,
         "attention_back",
-        32,
+        40,
         [
             (whole, x),
             (whole, attn_low),
@@ -739,13 +851,14 @@
                 shape((2, mp, cols, width), BF16),
             ),
             (whole, shape((16 + 2 * mp, width), F32)),
-            (whole, low_shape),
+            *[(whole, block_shape)] * mp,
         ],
         [pltpu.VMEM((rows, cols), BF16)] * 3 + [pltpu.VMEM((rows, width), F32)],
         here,
-    )
-    grad_rows = grad_rows.reshape(pairs, mp, rows_local, width)
-    row_sends = [grad_rows[:, k] for k in range(mp)]
+        (0, 1, 2) + tuple(range(4, 4 + mp)),
+    )
+    qk_keep, vo_keep, att_send, sums = results[:4]
+    row_sends = results[4:]
     got, out_got, att_send, row_sends, sums = tie(got, out_got, att_send, row_sends, sums)
     for step in range(1, ffn.steps):
         ffn.take(got)
@@ -755,17 +868,27 @@
             att_got = flip(att_send, "dp", 1)
             row_two, row_three = flip(row_sends[2], "mp", 2), flip(row_sends[3], "mp", 3)
         got, att_got, row_two, row_three, row_sends = tie(got, att_got, row_two, row_three, row_sends)
+    place = lambda blocks, dtype: call(
+        partial(place_kernel, pairs),
+        1,
+        "place",
+        16,
+        [(whole, b) for b in blocks],
+        [(whole, shape((mp * pairs, rows_local, width), dtype))],
+        [],
+        here,
+    )[0]
+    layer_out = place(out_got, BF16)
     ffn.take(got)
     ffn_parts = ffn.finish()
     ffn_odd = jnp.concatenate([p[1::2] for p in ffn_parts], axis=1)
     ffn_even = jnp.concatenate([p[0::2] for p in ffn_parts], axis=1)
     att = Reduce([qk_keep, vo_keep], [att_got[0], att_got[1]])
-    packs = att.pack(0)
-    ffn_odd, ffn_even, packs, sums = tie(ffn_odd, ffn_even, packs, sums)
-    got = att.send(0, packs)
+    ffn_odd, ffn_even, sums = tie(ffn_odd, ffn_even, sums)
+    got = att.send(0, att.pack(0))
     ffn_got = flip(ffn_odd, "mp", 1)
     sums_got = flip(sums, "dp", 1)
-    got, ffn_got, sums_got, row_sends, out_got = tie(got, ffn_got, sums_got, row_sends, out_got)
+    got, ffn_got, sums_got, row_sends, layer_out = tie(got, ffn_got, sums_got, row_sends, layer_out)
     sums = sums + sums_got
     for mask in [1 << b for b in range(2, dp.bit_length() - 2)]:
         sums = sums + flip(sums, "dp", mask)
@@ -787,10 +910,11 @@
     ffn_sum = add_parts(ffn_even[0], ffn_got[0], ffn_last)
     ffn = Gather([ffn_sum[None, :ffn_part], ffn_sum[None, ffn_part:]])
     ffn.held, att_odd, att_even, sums = tie(ffn.held, att_odd, att_even, sums)
+    grad_input = place([row_sends[0], row_one, row_two, row_three], F32)
     got = ffn.send(0)
     att_got = flip(att_odd, "mp", 1)
     sums_got = flip(sums, "dp", dp // 2)
-    got, att_got, sums_got = tie(got, att_got, sums_got)
+    got, att_got, sums_got, grad_input = tie(got, att_got, sums_got, grad_input)
     sums = sums + sums_got
     att_two = add_parts(att_even[1], att_got[1])
     for step in range(1, ffn.steps):
@@ -808,35 +932,44 @@
     core_got = [flip(h, "dp", 1) for h in ffn_halves]
     got = att.send(0)
     sums_got = flip(sums, "mp", 2)
-    core_got, got, sums_got, row_one, row_two, row_three = tie(
-        core_got, got, sums_got, row_one, row_two, row_three
-    )
+    core_got, got, sums_got = tie(core_got, got, sums_got)
     sums = sums + sums_got
-    grad_in, grad_down = ffn.finish(ffn_halves, core_got)
-    grad_in, grad_down = grad_in[0].astype(F32).T, grad_down[0].astype(F32)
+    grad_in, grad_down = call(
+        unit_grads_kernel,
+        1,
+        "unit_grads",
+        24,
+        [(whole, a) for a in ffn_halves + core_got],
+        [(whole, shape((width, units), F32)), (whole, shape((units, width), F32))],
+        [],
+        here,
+    )
     for step in range(1, att.steps):
         att.take(step - 1, got)
         got = tie(*att.send(step))
-    grad_in, grad_down, got, row_one = tie(grad_in, grad_down, got, row_one)
+    grad_in, grad_down, got = tie(grad_in, grad_down, got)
     att.take(att.steps - 1, got)
     att_halves = att.halves()
-    grad_qk, grad_vo = att.finish(att_halves, [flip(h, "dp", 1) for h in att_halves])
-
-    def leave(blocks):
-        return jnp.take(jnp.stack(blocks), order, axis=0).reshape(mp * pairs, rows_local, width)
-
-    layer_out = leave(out_got)
-    grad_input = leave([row_sends[0], row_one, row_two, row_three]).astype(F32)
+    core_got = [flip(h, "dp", 1) for h in att_halves]
+    grad_qkv, grad_out = call(
+        head_grads_kernel,
+        1,
+        "head_grads",
+        24,
+        [(whole, a) for a in att_halves + core_got],
+        [(whole, shape((3, cols, width), F32)), (whole, shape((cols, width), F32))],
+        [],
+        here,
+    )
     sum_in_bias = lax.dynamic_index_in_dim(sums, 16 + mi, 0, keepdims=False)
     sum_qv = lax.dynamic_index_in_dim(sums, 16 + mp + mi, 0, keepdims=False)
     sum_qv = jnp.stack([sum_qv[:cols], sum_qv[2 * cols : 3 * cols]])
-    grad_qkv = jnp.concatenate([grad_qk[0], grad_vo[0, :cols]], axis=0).reshape(3, cols, width)
     return (
         layer_out,
         grad_input,
-        grad_qkv.astype(F32).transpose(0, 2, 1),
+        grad_qkv.transpose(0, 2, 1),
         sum_qv,
-        grad_vo[0, cols:].astype(F32),
+        grad_out,
         sums[0],
         sums[1],
         sums[2],

time: 277 us -> 258 us (0.931)
  other arithmetic: 19.8 us -> 3.57 us
  local copies, waits for them, and re-layouts: 24.5 us -> 14.5 us
  waiting for transfers between devices: 90.3 us -> 98.7 us
  starting transfers between devices: 72.7 us -> 65.5 us
  Pallas kernels: 66.5 us -> 73.5 us
    ppermute x60 -> x61, waiting for transfers between devices: 90.3 us -> 98.7 us  [flip(): return lax.ppermute(array, axis, [(i, i ^ mask) for i in range(size)])]
    ppermute x60 -> x61, starting transfers between devices: 72.7 us -> 65.5 us  [flip(): return lax.ppermute(array, axis, [(i, i ^ mask) for i in range(size)])]
    pallas_call x4 -> x8, Pallas kernels: 62.8 us -> 68.9 us  [call(): pl.pallas_call(kernel, grid_spec=spec, out_shape=[pltpu.HBM(a.shape, a.dt...]
    select_n x5 -> x0, other arithmetic: 5.72 us -> none  [the longest x3 3.3 us: finish(): jnp.where(low, h, g)]
    convert_element_type x3 -> x0, other arithmetic: 4.77 us -> none  [the longest x1 1.93 us: shards(): grad_vo[0, cols:].astype(F32)]
    unnamed x126 -> x77, local copies, waits for them, and re-layouts: 8.95 us -> 4.42 us
    gather x2 -> x0, local copies, waits for them, and re-layouts: 3.16 us -> none  [leave(): jnp.take(jnp.stack(blocks), order, axis=0)]
  transfers between devices with their start and end apart: 60 -> 61, of which waited for: 28 -> 24; matrix products, arithmetic and copies ran while one was open for 10% -> 3% of each run, Pallas kernels for 14% -> 18%
where the time goes in v4:
time: 258 us
  waiting for transfers between devices  98.7 us (38%)
  Pallas kernels  73.5 us (28%)
  starting transfers between devices  65.5 us (25%)
  local copies, waits for them, and re-layouts  14.5 us (6%)
  other arithmetic  3.57 us (1%)
    ppermute x61, waiting for transfers between devices, flip(): return lax.ppermute(array, axis, [(i, i ^ mask) for i in range(size)])  98.7 us
    pallas_call x8, Pallas kernels, call(): pl.pallas_call(kernel, grid_spec=spec, out_shape=[pltpu.HBM(a.shape, a.dt...  68.9 us
    ppermute x61, starting transfers between devices, flip(): return lax.ppermute(array, axis, [(i, i ^ mask) for i in range(size)])  65.5 us
  transfers between devices with their start and end apart: 61, of which 24 were waited for; matrix products, arithmetic and copies ran while one was open for 3% of the time, Pallas kernels for 18%

profile of v4, /device:TPU:0, one launch (start us, length us, event | category | flops | bytes accessed | tf_op | source)
XLA Modules:
  0.0 257.6 jit_solution(13957194776643840528)
XLA Ops:
  3.1 3.1 %collective-permute-start = (bf16[104,768]{1,0:T(8,128)(2,1)S(1)}, bf16[104,768]{1,0:T(8,128)(2,1)S(1)}, u32[]{:S(2)}, u32[]{:S(2)}) collective-permute-start(bf16[104,768]{1,0:T(8,128)(2,1)S(1)} %concatenate.77), channel_id=1, source_target_pairs={{0,1},{1,0},{2,3},{3,2},{4,5},{5,4},{6,7},{7,6},{8,9},{9,8},{10,11... | collective-permute-start | bytes 479240 | tf_op jit(solution)/shard_map/ppermute | solution.py:490
  6.2 2.6 %collective-permute-start.1 = (bf16[104,768]{1,0:T(8,128)(2,1)S(1)}, bf16[104,768]{1,0:T(8,128)(2,1)S(1)}, u32[]{:S(2)}, u32[]{:S(2)}) collective-permute-start(bf16[104,768]{1,0:T(8,128)(2,1)S(1)} %concatenate.77), channel_id=1, source_target_pairs={{0,2},{1,3},{2,0},{3,1},{4,6},{5,7},{6,4},{7,5},{8,10},{9,11},{10,... | collective-permute-start | bytes 479240 | tf_op jit(solution)/shard_map/ppermute | solution.py:490
  12.7 8.3 %collective-permute-done.1 = bf16[104,768]{1,0:T(8,128)(2,1)S(1)} collective-permute-done((bf16[104,768]{1,0:T(8,128)(2,1)S(1)}, bf16[104,768]{1,0:T(8,128)(2,1)S(1)}, u32[]{:S(2)}, u32[]{:S(2)}) %collective-permute-start.1) | collective-permute-done | bytes 159776 | tf_op jit(solution)/shard_map/ppermute | solution.py:490
  22.1 1.6 collective-permute-start.5
  23.6 3.6 %collective-permute-start.3 = (bf16[192,768]{1,0:T(8,128)(2,1)S(1)}, bf16[192,768]{1,0:T(8,128)(2,1)S(1)}, u32[]{:S(2)}, u32[]{:S(2)}) collective-permute-start(bf16[192,768]{1,0:T(8,128)(2,1)S(1)} %pad_maximum_fusion.15), channel_id=1, source_target_pairs={{0,2},{1,3},{2,0},{3,1},{4,6},{5,7},{6,4},{7,5},{8,10},{9,11},{10,... | collective-permute-start | bytes 884744 | tf_op jit(solution)/shard_map/ppermute | solution.py:490
  27.3 1.6 collective-permute-start.4
  28.9 7.5 %collective-permute-done.6 = bf16[3,40,768]{2,1,0:T(8,128)(2,1)S(1)} collective-permute-done((bf16[3,40,768]{2,1,0:T(8,128)(2,1)}, bf16[3,40,768]{2,1,0:T(8,128)(2,1)S(1)}, u32[]{:S(2)}, u32[]{:S(2)}) %collective-permute-start.6) | collective-permute-done | bytes 184352 | tf_op jit(solution)/shard_map/ppermute | solution.py:490
  36.4 3.0 %collective-permute-done.3 = bf16[192,768]{1,0:T(8,128)(2,1)S(1)} collective-permute-done((bf16[192,768]{1,0:T(8,128)(2,1)S(1)}, bf16[192,768]{1,0:T(8,128)(2,1)S(1)}, u32[]{:S(2)}, u32[]{:S(2)}) %collective-permute-start.3) | collective-permute-done | bytes 294944 | tf_op jit(solution)/shard_map/ppermute | solution.py:490
  41.1 1.5 collective-permute-start.8
  45.2 13.1 %collective-permute-done.10 = bf16[3,40,768]{2,1,0:T(8,128)(2,1)S(1)} collective-permute-done((bf16[3,40,768]{2,1,0:T(8,128)(2,1)S(1)}, bf16[3,40,768]{2,1,0:T(8,128)(2,1)S(1)}, u32[]{:S(2)}, u32[]{:S(2)}) %collective-permute-start.10) | collective-permute-done | bytes 184352 | tf_op jit(solution)/shard_map/ppermute | solution.py:490
  61.0 1.6 collective-permute-start.11
  62.7 10.2 %collective-permute-done.15 = bf16[3,40,768]{2,1,0:T(8,128)(2,1)S(1)} collective-permute-done((bf16[3,40,768]{2,1,0:T(8,128)(2,1)S(1)}, bf16[3,40,768]{2,1,0:T(8,128)(2,1)S(1)}, u32[]{:S(2)}, u32[]{:S(2)}) %collective-permute-start.15) | collective-permute-done | bytes 184352 | tf_op jit(solution)/shard_map/ppermute | solution.py:490
  73.1 1.5 collective-permute-start.17
  74.8 1.6 collective-permute-start.16
  76.4 2.7 %collective-permute-start.19 = (bf16[3,40,768]{2,1,0:T(8,128)(2,1)S(1)}, bf16[3,40,768]{2,1,0:T(8,128)(2,1)S(1)}, u32[]{:S(2)}, u32[]{:S(2)}) collective-permute-start(bf16[3,40,768]{2,1,0:T(8,128)(2,1)S(1)} %get-tuple-element.211), channel_id=1, source_target_pairs={{0,2},{1,3},{2,0},{3,1},{4,6},{5,7},{6,4},{7,5},{8,10},{9,11},{10,... | collective-permute-start | bytes 552968 | tf_op jit(solution)/shard_map/ppermute | solution.py:490
  79.1 1.7 collective-permute-start.20
  80.8 12.0 %attention.1 = (bf16[4,480,192]{2,1,0:T(8,128)(2,1)}, bf16[4,480,192]{2,1,0:T(8,128)(2,1)}, bf16[4,480,192]{2,1,0:T(8,128)(2,1)}, f32[4,3,480,160]{3,2,1,0:T(8,1...) custom-call(s32[2]{0:T(128)S(1)} %pad_add_fusion.here_ref, ...), custom_call_target="tpu_custom_call" | custom-call | tf_op jit(solution)/shard_map/attention/pallas_call | solution.py:431
  92.9 1.9 collective-permute-done.17
  97.3 2.1 collective-permute-done.22.down_two_hbm
  99.5 2.5 collective-permute-done.21.in_two_hbm.in_two
  103.2 21.0 %ffn.1 = (bf16[3,40,768]{2,1,0:T(8,128)(2,1)S(1)}, bf16[3,40,768]{2,1,0:T(8,128)(2,1)S(1)}, bf16[3,40,768]{2,1,0:T(8,128)(2,1)S(1)}, bf16[3,40,768]{2,1,0:T(8,12...) custom-call(s32[2]{0:T(128)S(1)} %pad_add_fusion.here_ref, ...), custom_call_target="tpu_custom_call" | custom-call | tf_op jit(solution)/shard_map/ffn/pallas_call | solution.py:431
  124.8 8.4 %ffn_back.1 = (f32[480,768]{1,0:T(8,128)S(1)}, bf16[480,768]{1,0:T(8,128)(2,1)S(1)}, f32[8,768]{1,0:T(8,128)S(1)}) custom-call(s32[2]{0:T(128)S(1)} %pad_add_fusion.here_ref, bf16[4,480,768]{2,1,0:T(8,128)(2,1)} %get-tuple-element.231.pre_grad_ref, bf16[768,768]{1,0:T(8,128)(2,1)} %own_in_two.1, bf16[768,768]{1,0:T(8,128)(2,1)} %own_in_two.1, ...), custom_call_target="tpu_custom_call" | custom-call | tf_op jit(solution)/shard_map/ffn_back/pallas_call | solution.py:431
  135.5 1.5 add.186
  138.4 1.5 collective-permute-start.26
  139.9 2.3 collective-permute-start.28
  142.2 2.1 collective-permute-start.29
  144.4 19.0 %attention_back.1 = (bf16[4,192,768]{2,1,0:T(8,128)(2,1)}, bf16[4,192,768]{2,1,0:T(8,128)(2,1)}, bf16[2,4,192,768]{3,2,1,0:T(8,128)(2,1)}, f32[24,768]{1,0:T(8,1...) custom-call(s32[2]{0:T(128)S(1)} %pad_add_fusion.here_ref, ...), custom_call_target="tpu_custom_call" | custom-call | tf_op jit(solution)/shard_map/attention_back/pallas_call | solution.py:431
  163.4 1.8 collective-permute-done.25.refs_3_
  167.3 1.6 collective-permute-start.30
  168.8 1.9 collective-permute-start.34
  170.7 12.7 %collective-permute-done.33.refs_2_ = bf16[3,40,768]{2,1,0:T(8,128)(2,1)S(1)} collective-permute-done((bf16[3,40,768]{2,1,0:T(8,128)(2,1)S(1)}, bf16[3,40,768]{2,1,0:T(8,128)(2,1)S(1)}, u32[]{:S(2)}, u32[]{:S(2)}) %collective-permute-start.33) | collective-permute-done | bytes 184352 | tf_op jit(solution)/shard_map/ppermute | solution.py:490
  184.2 4.5 %collective-permute-start.37 = (bf16[2,192,768]{2,1,0:T(8,128)(2,1)S(1)}, bf16[2,192,768]{2,1,0:T(8,128)(2,1)S(1)}, u32[]{:S(2)}, u32[]{:S(2)}) collective-permute-start(bf16[2,192,768]{2,1,0:T(8,128)(2,1)S(1)} %pad_maximum_fusion.9), channel_id=1, source_target_pairs={{0,1},{1,0},{2,3},{3,2},{4,5},{5,4},{6,7},{7,6},{8,9},{9,8},{10,11... | collective-permute-start | bytes 1769480 | tf_op jit(solution)/shard_map/ppermute | solution.py:490
  193.7 8.6 %collective-permute-done.37 = bf16[2,192,768]{2,1,0:T(8,128)(2,1)S(1)} collective-permute-done((bf16[2,192,768]{2,1,0:T(8,128)(2,1)S(1)}, bf16[2,192,768]{2,1,0:T(8,128)(2,1)S(1)}, u32[]{:S(2)}, u32[]{:S(2)}) %collective-permute-start.37) | collective-permute-done | bytes 589856 | tf_op jit(solution)/shard_map/ppermute | solution.py:490
  202.2 2.1 collective-permute-done.36.refs_3_
  204.3 1.5 collective-permute-done.35.refs_3_
  205.9 1.8 collective-permute-start.41
  207.9 1.6 collective-permute-start.40
  211.9 5.4 %collective-permute-done.43 = f32[24,768]{1,0:T(8,128)S(1)} collective-permute-done((f32[24,768]{1,0:T(8,128)S(1)}, f32[24,768]{1,0:T(8,128)S(1)}, u32[]{:S(2)}, u32[]{:S(2)}) %collective-permute-start.43) | collective-permute-done | bytes 73760 | tf_op jit(solution)/shard_map/ppermute | solution.py:490
  217.3 3.9 %collective-permute-done.42.refs_1_ = bf16[3,40,768]{2,1,0:T(8,128)(2,1)S(1)} collective-permute-done((bf16[3,40,768]{2,1,0:T(8,128)(2,1)S(1)}, bf16[3,40,768]{2,1,0:T(8,128)(2,1)S(1)}, u32[]{:S(2)}, u32[]{:S(2)}) %collective-permute-start.42) | collective-permute-done | bytes 184352 | tf_op jit(solution)/shard_map/ppermute | solution.py:490
  225.1 1.7 place.3
  226.8 2.2 collective-permute-done.47
  231.8 1.6 collective-permute-start.50
  234.6 3.2 %collective-permute-done.51 = f32[24,768]{1,0:T(8,128)S(1)} collective-permute-done((f32[24,768]{1,0:T(8,128)S(1)}, f32[24,768]{1,0:T(8,128)S(1)}, u32[]{:S(2)}, u32[]{:S(2)}) %collective-permute-start.51) | collective-permute-done | bytes 73760 | tf_op jit(solution)/shard_map/ppermute | solution.py:490
  237.8 1.7 collective-permute-done.50
  243.4 3.2 %collective-permute-done.56 = f32[24,768]{1,0:T(8,128)S(1)} collective-permute-done((f32[24,768]{1,0:T(8,128)S(1)}, f32[24,768]{1,0:T(8,128)S(1)}, u32[]{:S(2)}, u32[]{:S(2)}) %collective-permute-start.56) | collective-permute-done | bytes 73760 | tf_op jit(solution)/shard_map/ppermute | solution.py:490
  247.8 1.5 collective-permute-start.57
  249.3 3.1 %unit_grads.1 = (f32[768,768]{1,0:T(8,128)}, f32[768,768]{1,0:T(8,128)}) custom-call(s32[2]{0:T(128)S(1)} %pad_add_fusion.here_ref, bf16[1,384,768]{2,1,0:T(8,128)(2,1)S(1)} %bitcast.166, bf16[1,384,768]{2,1,0:T(8,128)(2,1)S(1)} %bitcast.164, bf16[1,384,768]{2,1,0:T(8,128)(2,1)S(1)} %collective-permute-done.52.in_other, ...), custom_call_target="tpu_custom_call" | custom-call | tf_op jit(solution)/shard_map/unit_grads/pallas_call | solution.py:431
  255.5 2.1 head_grads.1
  (275 shorter events, 48.7 us)
Async XLA Ops:
  3.1 9.6 %collective-permute-start = (bf16[104,768]{1,0:T(8,128)(2,1)S(1)}, bf16[104,768]{1,0:T(8,128)(2,1)S(1)}, u32[]{:S(2)}, u32[]{:S(2)}) collective-permute-start(bf16[104,768]{1,0:T(8,128)(2,1)S(1)} %concatenate.77), channel_id=1, source_target_pairs={{0,1},{1,0},{2,3},{3,2},{4,5},{5,4},{6,7},{7,6},{8,9},{9,8},{10,11... | collective-permute-start | bytes 479240 | tf_op jit(solution)/shard_map/ppermute | solution.py:490
  6.2 14.8 %collective-permute-start.1 = (bf16[104,768]{1,0:T(8,128)(2,1)S(1)}, bf16[104,768]{1,0:T(8,128)(2,1)S(1)}, u32[]{:S(2)}, u32[]{:S(2)}) collective-permute-start(bf16[104,768]{1,0:T(8,128)(2,1)S(1)} %concatenate.77), channel_id=1, source_target_pairs={{0,2},{1,3},{2,0},{3,1},{4,6},{5,7},{6,4},{7,5},{8,10},{9,11},{10,... | collective-permute-start | bytes 479240 | tf_op jit(solution)/shard_map/ppermute | solution.py:490
  8.8 12.2 %collective-permute-start.2 = (bf16[104,768]{1,0:T(8,128)(2,1)S(1)}, bf16[104,768]{1,0:T(8,128)(2,1)}, u32[]{:S(2)}, u32[]{:S(2)}) collective-permute-start(bf16[104,768]{1,0:T(8,128)(2,1)S(1)} %concatenate.77), channel_id=1, source_target_pairs={{0,3},{1,2},{2,1},{3,0},{4,7},{5,6},{6,5},{7,4},{8,11},{9,10},{10,... | collective-permute-start | bytes 479240 | tf_op jit(solution)/shard_map/ppermute | solution.py:490
  22.1 14.4 %collective-permute-start.5 = (bf16[3,1,1,48,768]{4,3,0,2,1:T(8,128)(2,1)S(1)}, bf16[3,1,1,48,768]{4,3,0,2,1:T(8,128)(2,1)S(1)}, u32[]{:S(2)}, u32[]{:S(2)}) collective-permute-start(bf16[3,1,1,48,768]{4,3,0,2,1:T(8,128)(2,1)S(1)} %maximum_bitcast_fusion.3), channel_id=1, source_target_pairs={{0,16},{4,20},{8,24},{12,28},{16,0},{20,4},{24,8},{28,12},{1,17},{... | collective-permute-start | bytes 663560 | tf_op jit(solution)/shard_map/ppermute | solution.py:490
  23.6 15.7 %collective-permute-start.3 = (bf16[192,768]{1,0:T(8,128)(2,1)S(1)}, bf16[192,768]{1,0:T(8,128)(2,1)S(1)}, u32[]{:S(2)}, u32[]{:S(2)}) collective-permute-start(bf16[192,768]{1,0:T(8,128)(2,1)S(1)} %pad_maximum_fusion.15), channel_id=1, source_target_pairs={{0,2},{1,3},{2,0},{3,1},{4,6},{5,7},{6,4},{7,5},{8,10},{9,11},{10,... | collective-permute-start | bytes 884744 | tf_op jit(solution)/shard_map/ppermute | solution.py:490
  27.3 9.1 %collective-permute-start.4 = (bf16[3,1,1,48,768]{4,3,0,2,1:T(8,128)(2,1)S(1)}, bf16[3,1,1,48,768]{4,3,0,2,1:T(8,128)(2,1)S(1)}, u32[]{:S(2)}, u32[]{:S(2)}) collective-permute-start(bf16[3,1,1,48,768]{4,3,0,2,1:T(8,128)(2,1)S(1)} %maximum_bitcast_fusion.2), channel_id=1, source_target_pairs={{0,8},{4,12},{8,0},{12,4},{16,24},{20,28},{24,16},{28,20},{1,9},{5... | collective-permute-start | bytes 663560 | tf_op jit(solution)/shard_map/ppermute | solution.py:490
  28.9 7.5 %collective-permute-start.6 = (bf16[3,40,768]{2,1,0:T(8,128)(2,1)}, bf16[3,40,768]{2,1,0:T(8,128)(2,1)S(1)}, u32[]{:S(2)}, u32[]{:S(2)}) collective-permute-start(bf16[3,40,768]{2,1,0:T(8,128)(2,1)} %get-tuple-element.177), channel_id=1, source_target_pairs={{0,1},{1,0},{2,3},{3,2},{4,5},{5,4},{6,7},{7,6},{8,9},{9,8},{10,11... | collective-permute-start | bytes 552968 | tf_op jit(solution)/shard_map/ppermute | solution.py:490
  40.9 18.3 %collective-permute-start.9 = (bf16[2,192,768]{2,1,0:T(8,128)(2,1)S(1)}, bf16[2,192,768]{2,1,0:T(8,128)(2,1)S(1)}, u32[]{:S(2)}, u32[]{:S(2)}) collective-permute-start(bf16[2,192,768]{2,1,0:T(8,128)(2,1)S(1)} %pad_maximum_fusion.8), channel_id=1, source_target_pairs={{0,1},{1,0},{2,3},{3,2},{4,5},{5,4},{6,7},{7,6},{8,9},{9,8},{10,11... | collective-permute-start | bytes 1769480 | tf_op jit(solution)/shard_map/ppermute | solution.py:490
  41.1 17.2 %collective-permute-start.8 = (bf16[3,2,1,48,768]{4,3,0,2,1:T(8,128)(2,1)S(1)}, bf16[3,2,1,48,768]{4,3,0,2,1:T(8,128)(2,1)S(1)}, u32[]{:S(2)}, u32[]{:S(2)}) collective-permute-start(bf16[3,2,1,48,768]{4,3,0,2,1:T(8,128)(2,1)S(1)} %pad_maximum_fusion.14), channel_id=1, source_target_pairs={{0,8},{4,12},{8,0},{12,4},{16,24},{20,28},{24,16},{28,20},{1,9},{5... | collective-permute-start | bytes 1327112 | tf_op jit(solution)/shard_map/ppermute | solution.py:490
  42.7 15.6 %collective-permute-start.7 = (bf16[3,1,2,48,768]{4,3,0,2,1:T(8,128)(2,1)S(1)}, bf16[3,1,2,48,768]{4,3,0,2,1:T(8,128)(2,1)S(1)}, u32[]{:S(2)}, u32[]{:S(2)}) collective-permute-start(bf16[3,1,2,48,768]{4,3,0,2,1:T(8,128)(2,1)S(1)} %pad_maximum_fusion.13), channel_id=1, source_target_pairs={{0,16},{4,20},{8,24},{12,28},{16,0},{20,4},{24,8},{28,12},{1,17},{... | collective-permute-start | bytes 1327112 | tf_op jit(solution)/shard_map/ppermute | solution.py:490
  44.0 14.3 %collective-permute-start.10 = (bf16[3,40,768]{2,1,0:T(8,128)(2,1)S(1)}, bf16[3,40,768]{2,1,0:T(8,128)(2,1)S(1)}, u32[]{:S(2)}, u32[]{:S(2)}) collective-permute-start(bf16[3,40,768]{2,1,0:T(8,128)(2,1)S(1)} %copy-done.22), channel_id=1, source_target_pairs={{0,3},{1,2},{2,1},{3,0},{4,7},{5,6},{6,5},{7,4},{8,11},{9,10},{10,... | collective-permute-start | bytes 552968 | tf_op jit(solution)/shard_map/ppermute | solution.py:490
  59.4 13.5 %collective-permute-start.14 = (bf16[3,192,768]{2,1,0:T(8,128)(2,1)S(1)}, bf16[3,192,768]{2,1,0:T(8,128)(2,1)S(1)}, u32[]{:S(2)}, u32[]{:S(2)}) collective-permute-start(bf16[3,192,768]{2,1,0:T(8,128)(2,1)S(1)} %bitcast.150), channel_id=1, source_target_pairs={{0,4},{4,0},{8,12},{12,8},{16,20},{20,16},{24,28},{28,24},{1,5},{5... | collective-permute-start | bytes 2654216 | tf_op jit(solution)/shard_map/ppermute | solution.py:490
  59.7 13.2 %collective-permute-start.13 = (bf16[3,192,768]{2,1,0:T(8,128)(2,1)S(1)}, bf16[3,192,768]{2,1,0:T(8,128)(2,1)S(1)}, u32[]{:S(2)}, u32[]{:S(2)}) collective-permute-start(bf16[3,192,768]{2,1,0:T(8,128)(2,1)S(1)} %bitcast.153), channel_id=1, source_target_pairs={{0,4},{4,0},{8,12},{12,8},{16,20},{20,16},{24,28},{28,24},{1,5},{5... | collective-permute-start | bytes 2654216 | tf_op jit(solution)/shard_map/ppermute | solution.py:490
  60.4 12.5 %collective-permute-start.12 = (bf16[3,1,1,96,768]{4,3,0,2,1:T(8,128)(2,1)S(1)}, bf16[3,1,1,96,768]{4,3,0,2,1:T(8,128)(2,1)S(1)}, u32[]{:S(2)}, u32[]{:S(2)}) collective-permute-start(bf16[3,1,1,96,768]{4,3,0,2,1:T(8,128)(2,1)S(1)} %maximum_bitcast_fusion.1), channel_id=1, source_target_pairs={{0,16},{4,20},{8,24},{12,28},{16,0},{20,4},{24,8},{28,12},{1,17},{... | collective-permute-start | bytes 1327112 | tf_op jit(solution)/shard_map/ppermute | solution.py:490
  61.0 11.9 %collective-permute-start.11 = (bf16[3,1,1,96,768]{4,3,0,2,1:T(8,128)(2,1)S(1)}, bf16[3,1,1,96,768]{4,3,0,2,1:T(8,128)(2,1)S(1)}, u32[]{:S(2)}, u32[]{:S(2)}) collective-permute-start(bf16[3,1,1,96,768]{4,3,0,2,1:T(8,128)(2,1)S(1)} %maximum_bitcast_fusion), channel_id=1, source_target_pairs={{0,8},{4,12},{8,0},{12,4},{16,24},{20,28},{24,16},{28,20},{1,9},{5... | collective-permute-start | bytes 1327112 | tf_op jit(solution)/shard_map/ppermute | solution.py:490
  62.6 10.3 %collective-permute-start.15 = (bf16[3,40,768]{2,1,0:T(8,128)(2,1)S(1)}, bf16[3,40,768]{2,1,0:T(8,128)(2,1)S(1)}, u32[]{:S(2)}, u32[]{:S(2)}) collective-permute-start(bf16[3,40,768]{2,1,0:T(8,128)(2,1)S(1)} %copy-done.21), channel_id=1, source_target_pairs={{0,2},{1,3},{2,0},{3,1},{4,6},{5,7},{6,4},{7,5},{8,10},{9,11},{10,... | collective-permute-start | bytes 552968 | tf_op jit(solution)/shard_map/ppermute | solution.py:490
  73.1 21.6 %collective-permute-start.17 = (bf16[3,2,1,96,768]{4,3,0,2,1:T(8,128)(2,1)S(1)}, bf16[3,2,1,96,768]{4,3,0,2,1:T(8,128)(2,1)S(1)}, u32[]{:S(2)}, u32[]{:S(2)}) collective-permute-start(bf16[3,2,1,96,768]{4,3,0,2,1:T(8,128)(2,1)S(1)} %pad_maximum_fusion.5), channel_id=1, source_target_pairs={{0,8},{4,12},{8,0},{12,4},{16,24},{20,28},{24,16},{28,20},{1,9},{5... | collective-permute-start | bytes 2654216 | tf_op jit(solution)/shard_map/ppermute | solution.py:490
  74.8 20.5 %collective-permute-start.16 = (bf16[3,1,2,96,768]{4,3,0,2,1:T(8,128)(2,1)S(1)}, bf16[3,1,2,96,768]{4,3,0,2,1:T(8,128)(2,1)S(1)}, u32[]{:S(2)}, u32[]{:S(2)}) collective-permute-start(bf16[3,1,2,96,768]{4,3,0,2,1:T(8,128)(2,1)S(1)} %pad_maximum_fusion.4), channel_id=1, source_target_pairs={{0,16},{4,20},{8,24},{12,28},{16,0},{20,4},{24,8},{28,12},{1,17},{... | collective-permute-start | bytes 2654216 | tf_op jit(solution)/shard_map/ppermute | solution.py:490
  76.4 16.5 %collective-permute-start.18 = (bf16[3,40,768]{2,1,0:T(8,128)(2,1)S(1)}, bf16[3,40,768]{2,1,0:T(8,128)(2,1)S(1)}, u32[]{:S(2)}, u32[]{:S(2)}) collective-permute-start(bf16[3,40,768]{2,1,0:T(8,128)(2,1)S(1)} %get-tuple-element.210), channel_id=1, source_target_pairs={{0,1},{1,0},{2,3},{3,2},{4,5},{5,4},{6,7},{7,6},{8,9},{9,8},{10,11... | collective-permute-start | bytes 552968 | tf_op jit(solution)/shard_map/ppermute | solution.py:490
  76.4 16.5 %collective-permute-start.19 = (bf16[3,40,768]{2,1,0:T(8,128)(2,1)S(1)}, bf16[3,40,768]{2,1,0:T(8,128)(2,1)S(1)}, u32[]{:S(2)}, u32[]{:S(2)}) collective-permute-start(bf16[3,40,768]{2,1,0:T(8,128)(2,1)S(1)} %get-tuple-element.211), channel_id=1, source_target_pairs={{0,2},{1,3},{2,0},{3,1},{4,6},{5,7},{6,4},{7,5},{8,10},{9,11},{10,... | collective-permute-start | bytes 552968 | tf_op jit(solution)/shard_map/ppermute | solution.py:490
  79.1 13.8 %collective-permute-start.20 = (bf16[3,40,768]{2,1,0:T(8,128)(2,1)S(1)}, bf16[3,40,768]{2,1,0:T(8,128)(2,1)S(1)}, u32[]{:S(2)}, u32[]{:S(2)}) collective-permute-start(bf16[3,40,768]{2,1,0:T(8,128)(2,1)S(1)} %get-tuple-element.212), channel_id=1, source_target_pairs={{0,3},{1,2},{2,1},{3,0},{4,7},{5,6},{6,5},{7,4},{8,11},{9,10},{10,... | collective-permute-start | bytes 552968 | tf_op jit(solution)/shard_map/ppermute | solution.py:490
  124.2 9.0 %collective-permute-start.23 = (bf16[4,384,768]{2,1,0:T(8,128)(2,1)}, bf16[4,384,768]{2,1,0:T(8,128)(2,1)S(1)}, u32[]{:S(2)}, u32[]{:S(2)}) collective-permute-start(bf16[4,384,768]{2,1,0:T(8,128)(2,1)} %get-tuple-element.225), channel_id=1, source_target_pairs={{0,4},{4,0},{8,12},{12,8},{16,20},{20,16},{24,28},{28,24},{1,5},{5... | collective-permute-start | bytes 7077896 | tf_op jit(solution)/shard_map/ppermute | solution.py:490
  124.4 8.8 %collective-permute-start.24 = (bf16[4,384,768]{2,1,0:T(8,128)(2,1)}, bf16[4,384,768]{2,1,0:T(8,128)(2,1)S(1)}, u32[]{:S(2)}, u32[]{:S(2)}) collective-permute-start(bf16[4,384,768]{2,1,0:T(8,128)(2,1)} %get-tuple-element.226), channel_id=1, source_target_pairs={{0,4},{4,0},{8,12},{12,8},{16,20},{20,16},{24,28},{28,24},{1,5},{5... | collective-permute-start | bytes 7077896 | tf_op jit(solution)/shard_map/ppermute | solution.py:490
  137.0 28.2 %collective-permute-start.25 = (bf16[4,2,96,768]{3,2,1,0:T(8,128)(2,1)}, bf16[4,2,96,768]{3,2,1,0:T(8,128)(2,1)S(1)}, u32[]{:S(2)}, u32[]{:S(2)}) collective-permute-start(bf16[4,2,96,768]{3,2,1,0:T(8,128)(2,1)} %add.186), channel_id=1, source_target_pairs={{0,8},{4,12},{8,0},{12,4},{16,24},{20,28},{24,16},{28,20},{1,9},{5... | collective-permute-start | bytes 3538952 | tf_op jit(solution)/shard_map/ppermute | solution.py:490
  138.4 27.7 %collective-permute-start.26 = (bf16[4,2,96,768]{3,2,1,0:T(8,128)(2,1)S(1)}, bf16[4,2,96,768]{3,2,1,0:T(8,128)(2,1)S(1)}, u32[]{:S(2)}, u32[]{:S(2)}) collective-permute-start(bf16[4,2,96,768]{3,2,1,0:T(8,128)(2,1)S(1)} %add.187), channel_id=1, source_target_pairs={{0,16},{4,20},{8,24},{12,28},{16,0},{20,4},{24,8},{28,12},{1,17},{... | collective-permute-start | bytes 3538952 | tf_op jit(solution)/shard_map/ppermute | solution.py:490
  139.9 23.4 %collective-permute-start.27 = (bf16[3,40,768]{2,1,0:T(8,128)(2,1)S(1)}, bf16[3,40,768]{2,1,0:T(8,128)(2,1)S(1)}, u32[]{:S(2)}, u32[]{:S(2)}) collective-permute-start(bf16[3,40,768]{2,1,0:T(8,128)(2,1)S(1)} %get-tuple-element.257), channel_id=1, source_target_pairs={{0,1},{1,0},{2,3},{3,2},{4,5},{5,4},{6,7},{7,6},{8,9},{9,8},{10,11... | collective-permute-start | bytes 552968 | tf_op jit(solution)/shard_map/ppermute | solution.py:490
  139.9 23.5 %collective-permute-start.28 = (bf16[3,40,768]{2,1,0:T(8,128)(2,1)S(1)}, bf16[3,40,768]{2,1,0:T(8,128)(2,1)S(1)}, u32[]{:S(2)}, u32[]{:S(2)}) collective-permute-start(bf16[3,40,768]{2,1,0:T(8,128)(2,1)S(1)} %get-tuple-element.258), channel_id=1, source_target_pairs={{0,2},{1,3},{2,0},{3,1},{4,6},{5,7},{6,4},{7,5},{8,10},{9,11},{10,... | collective-permute-start | bytes 552968 | tf_op jit(solution)/shard_map/ppermute | solution.py:490
  142.2 21.2 %collective-permute-start.29 = (bf16[3,40,768]{2,1,0:T(8,128)(2,1)S(1)}, bf16[3,40,768]{2,1,0:T(8,128)(2,1)S(1)}, u32[]{:S(2)}, u32[]{:S(2)}) collective-permute-start(bf16[3,40,768]{2,1,0:T(8,128)(2,1)S(1)} %get-tuple-element.259), channel_id=1, source_target_pairs={{0,3},{1,2},{2,1},{3,0},{4,7},{5,6},{6,5},{7,4},{8,11},{9,10},{10,... | collective-permute-start | bytes 552968 | tf_op jit(solution)/shard_map/ppermute | solution.py:490
  166.2 17.3 %collective-permute-start.32 = (bf16[2,4,192,768]{3,2,1,0:T(8,128)(2,1)}, bf16[2,4,192,768]{3,2,1,0:T(8,128)(2,1)S(1)}, u32[]{:S(2)}, u32[]{:S(2)}) collective-permute-start(bf16[2,4,192,768]{3,2,1,0:T(8,128)(2,1)} %get-tuple-element.268), channel_id=1, source_target_pairs={{0,4},{4,0},{8,12},{12,8},{16,20},{20,16},{24,28},{28,24},{1,5},{5... | collective-permute-start | bytes 7077896 | tf_op jit(solution)/shard_map/ppermute | solution.py:490
  166.4 17.0 %collective-permute-start.31 = (bf16[4,1,96,768]{3,2,1,0:T(8,128)(2,1)S(1)}, bf16[4,1,96,768]{3,2,1,0:T(8,128)(2,1)S(1)}, u32[]{:S(2)}, u32[]{:S(2)}) collective-permute-start(bf16[4,1,96,768]{3,2,1,0:T(8,128)(2,1)S(1)} %add.189), channel_id=1, source_target_pairs={{0,8},{4,12},{8,0},{12,4},{16,24},{20,28},{24,16},{28,20},{1,9},{5... | collective-permute-start | bytes 1769480 | tf_op jit(solution)/shard_map/ppermute | solution.py:490
  167.3 16.2 %collective-permute-start.30 = (bf16[4,1,96,768]{3,2,1,0:T(8,128)(2,1)S(1)}, bf16[4,1,96,768]{3,2,1,0:T(8,128)(2,1)S(1)}, u32[]{:S(2)}, u32[]{:S(2)}) collective-permute-start(bf16[4,1,96,768]{3,2,1,0:T(8,128)(2,1)S(1)} %add.188), channel_id=1, source_target_pairs={{0,16},{4,20},{8,24},{12,28},{16,0},{20,4},{24,8},{28,12},{1,17},{... | collective-permute-start | bytes 1769480 | tf_op jit(solution)/shard_map/ppermute | solution.py:490
  168.8 14.6 %collective-permute-start.33 = (bf16[3,40,768]{2,1,0:T(8,128)(2,1)S(1)}, bf16[3,40,768]{2,1,0:T(8,128)(2,1)S(1)}, u32[]{:S(2)}, u32[]{:S(2)}) collective-permute-start(bf16[3,40,768]{2,1,0:T(8,128)(2,1)S(1)} %copy-done.35), channel_id=1, source_target_pairs={{0,2},{1,3},{2,0},{3,1},{4,6},{5,7},{6,4},{7,5},{8,10},{9,11},{10,... | collective-permute-start | bytes 552968 | tf_op jit(solution)/shard_map/ppermute | solution.py:490
  168.8 14.6 %collective-permute-start.34 = (bf16[3,40,768]{2,1,0:T(8,128)(2,1)S(1)}, bf16[3,40,768]{2,1,0:T(8,128)(2,1)S(1)}, u32[]{:S(2)}, u32[]{:S(2)}) collective-permute-start(bf16[3,40,768]{2,1,0:T(8,128)(2,1)S(1)} %copy-done.34), channel_id=1, source_target_pairs={{0,3},{1,2},{2,1},{3,0},{4,7},{5,6},{6,5},{7,4},{8,11},{9,10},{10,... | collective-permute-start | bytes 552968 | tf_op jit(solution)/shard_map/ppermute | solution.py:490
  184.2 18.0 %collective-permute-start.37 = (bf16[2,192,768]{2,1,0:T(8,128)(2,1)S(1)}, bf16[2,192,768]{2,1,0:T(8,128)(2,1)S(1)}, u32[]{:S(2)}, u32[]{:S(2)}) collective-permute-start(bf16[2,192,768]{2,1,0:T(8,128)(2,1)S(1)} %pad_maximum_fusion.9), channel_id=1, source_target_pairs={{0,1},{1,0},{2,3},{3,2},{4,5},{5,4},{6,7},{7,6},{8,9},{9,8},{10,11... | collective-permute-start | bytes 1769480 | tf_op jit(solution)/shard_map/ppermute | solution.py:490
  189.3 15.0 %collective-permute-start.36 = (bf16[4,2,48,768]{3,2,1,0:T(8,128)(2,1)S(1)}, bf16[4,2,48,768]{3,2,1,0:T(8,128)(2,1)S(1)}, u32[]{:S(2)}, u32[]{:S(2)}) collective-permute-start(bf16[4,2,48,768]{3,2,1,0:T(8,128)(2,1)S(1)} %add.191), channel_id=1, source_target_pairs={{0,16},{4,20},{8,24},{12,28},{16,0},{20,4},{24,8},{28,12},{1,17},{... | collective-permute-start | bytes 1769480 | tf_op jit(solution)/shard_map/ppermute | solution.py:490
  190.8 15.0 %collective-permute-start.35 = (bf16[4,2,48,768]{3,2,1,0:T(8,128)(2,1)S(1)}, bf16[4,2,48,768]{3,2,1,0:T(8,128)(2,1)S(1)}, u32[]{:S(2)}, u32[]{:S(2)}) collective-permute-start(bf16[4,2,48,768]{3,2,1,0:T(8,128)(2,1)S(1)} %add.190), channel_id=1, source_target_pairs={{0,8},{4,12},{8,0},{12,4},{16,24},{20,28},{24,16},{28,20},{1,9},{5... | collective-permute-start | bytes 1769480 | tf_op jit(solution)/shard_map/ppermute | solution.py:490
  205.9 15.3 %collective-permute-start.41 = (bf16[192,768]{1,0:T(8,128)(2,1)S(1)}, bf16[192,768]{1,0:T(8,128)(2,1)S(1)}, u32[]{:S(2)}, u32[]{:S(2)}) collective-permute-start(bf16[192,768]{1,0:T(8,128)(2,1)S(1)} %fusion.1), channel_id=1, source_target_pairs={{0,2},{1,3},{2,0},{3,1},{4,6},{5,7},{6,4},{7,5},{8,10},{9,11},{10,... | collective-permute-start | bytes 884744 | tf_op jit(solution)/shard_map/ppermute | solution.py:490
  207.9 13.3 %collective-permute-start.40 = (bf16[4,1,48,768]{3,2,1,0:T(8,128)(2,1)S(1)}, bf16[4,1,48,768]{3,2,1,0:T(8,128)(2,1)S(1)}, u32[]{:S(2)}, u32[]{:S(2)}) collective-permute-start(bf16[4,1,48,768]{3,2,1,0:T(8,128)(2,1)S(1)} %add.195), channel_id=1, source_target_pairs={{0,8},{4,12},{8,0},{12,4},{16,24},{20,28},{24,16},{28,20},{1,9},{5... | collective-permute-start | bytes 884744 | tf_op jit(solution)/shard_map/ppermute | solution.py:490
  209.5 11.7 %collective-permute-start.39 = (bf16[4,1,48,768]{3,2,1,0:T(8,128)(2,1)S(1)}, bf16[4,1,48,768]{3,2,1,0:T(8,128)(2,1)S(1)}, u32[]{:S(2)}, u32[]{:S(2)}) collective-permute-start(bf16[4,1,48,768]{3,2,1,0:T(8,128)(2,1)S(1)} %add.194), channel_id=1, source_target_pairs={{0,16},{4,20},{8,24},{12,28},{16,0},{20,4},{24,8},{28,12},{1,17},{... | collective-permute-start | bytes 884744 | tf_op jit(solution)/shard_map/ppermute | solution.py:490
  210.5 10.7 %collective-permute-start.42 = (bf16[3,40,768]{2,1,0:T(8,128)(2,1)S(1)}, bf16[3,40,768]{2,1,0:T(8,128)(2,1)S(1)}, u32[]{:S(2)}, u32[]{:S(2)}) collective-permute-start(bf16[3,40,768]{2,1,0:T(8,128)(2,1)S(1)} %copy-done.33), channel_id=1, source_target_pairs={{0,1},{1,0},{2,3},{3,2},{4,5},{5,4},{6,7},{7,6},{8,9},{9,8},{10,11... | collective-permute-start | bytes 552968 | tf_op jit(solution)/shard_map/ppermute | solution.py:490
  221.8 7.7 %collective-permute-start.46 = (bf16[2,96,768]{2,1,0:T(8,128)(2,1)S(1)}, bf16[2,96,768]{2,1,0:T(8,128)(2,1)S(1)}, u32[]{:S(2)}, u32[]{:S(2)}) collective-permute-start(bf16[2,96,768]{2,1,0:T(8,128)(2,1)S(1)} %pad_maximum_fusion.16), channel_id=1, source_target_pairs={{0,1},{1,0},{2,3},{3,2},{4,5},{5,4},{6,7},{7,6},{8,9},{9,8},{10,11... | collective-permute-start | bytes 884744 | tf_op jit(solution)/shard_map/ppermute | solution.py:490
  221.9 7.1 %collective-permute-start.44 = (bf16[1,1,1,96,768]{4,3,2,1,0:T(8,128)(2,1)S(1)}, bf16[1,1,1,96,768]{4,3,2,1,0:T(8,128)(2,1)S(1)}, u32[]{:S(2)}, u32[]{:S(2)}) collective-permute-start(bf16[1,1,1,96,768]{4,3,2,1,0:T(8,128)(2,1)S(1)} %get-tuple-element.297), channel_id=1, source_target_pairs={{0,8},{4,12},{8,0},{12,4},{16,24},{20,28},{24,16},{28,20},{1,9},{5... | collective-permute-start | bytes 442376 | tf_op jit(solution)/shard_map/ppermute | solution.py:490
  229.5 9.9 %collective-permute-start.49 = (bf16[1,2,1,96,768]{4,3,2,1,0:T(8,128)(2,1)S(1)}, bf16[1,2,1,96,768]{4,3,2,1,0:T(8,128)(2,1)S(1)}, u32[]{:S(2)}, u32[]{:S(2)}) collective-permute-start(bf16[1,2,1,96,768]{4,3,2,1,0:T(8,128)(2,1)S(1)} %pad_maximum_fusion.19), channel_id=1, source_target_pairs={{0,8},{4,12},{8,0},{12,4},{16,24},{20,28},{24,16},{28,20},{1,9},{5... | collective-permute-start | bytes 884744 | tf_op jit(solution)/shard_map/ppermute | solution.py:490
  231.0 8.5 %collective-permute-start.48 = (bf16[1,1,2,96,768]{4,3,2,1,0:T(8,128)(2,1)S(1)}, bf16[1,1,2,96,768]{4,3,2,1,0:T(8,128)(2,1)S(1)}, u32[]{:S(2)}, u32[]{:S(2)}) collective-permute-start(bf16[1,1,2,96,768]{4,3,2,1,0:T(8,128)(2,1)S(1)} %pad_maximum_fusion.18), channel_id=1, source_target_pairs={{0,16},{4,20},{8,24},{12,28},{16,0},{20,4},{24,8},{28,12},{1,17},{... | collective-permute-start | bytes 884744 | tf_op jit(solution)/shard_map/ppermute | solution.py:490
  231.8 7.7 %collective-permute-start.50 = (bf16[96,768]{1,0:T(8,128)(2,1)S(1)}, bf16[96,768]{1,0:T(8,128)(2,1)S(1)}, u32[]{:S(2)}, u32[]{:S(2)}) collective-permute-start(bf16[96,768]{1,0:T(8,128)(2,1)S(1)} %fusion.3), channel_id=1, source_target_pairs={{0,2},{1,3},{2,0},{3,1},{4,6},{5,7},{6,4},{7,5},{8,10},{9,11},{10,... | collective-permute-start | bytes 442376 | tf_op jit(solution)/shard_map/ppermute | solution.py:490
  239.6 7.0 %collective-permute-start.53 = (bf16[1,384,768]{2,1,0:T(8,128)(2,1)S(1)}, bf16[1,384,768]{2,1,0:T(8,128)(2,1)S(1)}, u32[]{:S(2)}, u32[]{:S(2)}) collective-permute-start(bf16[1,384,768]{2,1,0:T(8,128)(2,1)S(1)} %bitcast.163), channel_id=1, source_target_pairs={{0,4},{4,0},{8,12},{12,8},{16,20},{20,16},{24,28},{28,24},{1,5},{5... | collective-permute-start | bytes 1769480 | tf_op jit(solution)/shard_map/ppermute | solution.py:490
  239.8 6.8 %collective-permute-start.52 = (bf16[1,384,768]{2,1,0:T(8,128)(2,1)S(1)}, bf16[1,384,768]{2,1,0:T(8,128)(2,1)S(1)}, u32[]{:S(2)}, u32[]{:S(2)}) collective-permute-start(bf16[1,384,768]{2,1,0:T(8,128)(2,1)S(1)} %bitcast.165), channel_id=1, source_target_pairs={{0,4},{4,0},{8,12},{12,8},{16,20},{20,16},{24,28},{28,24},{1,5},{5... | collective-permute-start | bytes 1769480 | tf_op jit(solution)/shard_map/ppermute | solution.py:490
  240.4 6.2 %collective-permute-start.56 = (f32[24,768]{1,0:T(8,128)S(1)}, f32[24,768]{1,0:T(8,128)S(1)}, u32[]{:S(2)}, u32[]{:S(2)}) collective-permute-start(f32[24,768]{1,0:T(8,128)S(1)} %add.155), channel_id=1, source_target_pairs={{0,2},{1,3},{2,0},{3,1},{4,6},{5,7},{6,4},{7,5},{8,10},{9,11},{10,... | collective-permute-start | bytes 221192 | tf_op jit(solution)/shard_map/ppermute | solution.py:490
  (51 other events, 247.5 us)

commit v5 on v4

--- a/solution.py
+++ b/solution.py
@@ -147,14 +147,14 @@
 
 
 def ffn_kernel(
-    count, here_ref, low_hbm, normed_hbm, w_in_hbm, in_one_hbm, in_two_hbm, w_down_hbm, down_one_hbm, down_two_hbm,
-    small_ref, vectors_ref, *refs,
+    count, here_ref, low_hbm, normed_hbm, w_in_hbm, in_one, in_two, w_down_hbm, down_one, down_two, small_ref,
+    vectors_ref, *refs,
 ):
     cot_hbm, out_refs = refs[:count], refs[count : 2 * count]
     (
         delta_hbm, pre_grad_hbm, in_keep_hbm, in_send_hbm, down_keep_hbm, down_send_hbm, sum_in_ref, sums_ref,
-        low_ref, normed_ref, w_in_ref, in_one, in_two, w_down_ref, down_one, down_two, cot_ref, act_ref, slope_ref,
-        total_ref, delta_ref, pre_grad_ref, in_keep_ref, in_send_ref, down_keep_ref, down_send_ref, sems,
+        low_ref, normed_ref, w_in_ref, w_down_ref, cot_ref, act_ref, slope_ref, total_ref, delta_ref, pre_grad_ref,
+        in_keep_ref, in_send_ref, down_keep_ref, down_send_ref, sems,
     ) = refs[2 * count :]
     core = here_ref[0]
     half = in_one.shape[1]
@@ -171,15 +171,6 @@
     def wait(copies):
         for copy in copies:
             copy.wait()
-
-    def shard(slot):
-        k = slot - 1
-        return start(
-            (in_one_hbm.at[k], in_one.at[k]),
-            (in_two_hbm.at[k], in_two.at[k]),
-            (down_one_hbm.at[k], down_one.at[k]),
-            (down_two_hbm.at[k], down_two.at[k]),
-        )
 
     def halves(start_, stop):
         parts = []
@@ -225,18 +216,11 @@
             total_ref[...] += branch
 
     first_copies = start((low_hbm, low_ref), (w_in_hbm, w_in_ref), (w_down_hbm, w_down_ref))
-    ahead = shard(1)
+    later_copies = start((normed_hbm, normed_ref), *[(cot_hbm[k], cot_ref.at[k]) for k in range(count)])
     wait(first_copies)
-    forward(0)
-    for slot in range(1, count):
-        copies = ahead
-        if slot + 1 < count:
-            ahead = shard(slot + 1)
-        else:
-            ahead = start((normed_hbm, normed_ref), *[(cot_hbm[k], cot_ref.at[k]) for k in range(count)])
-        wait(copies)
+    for slot in range(count):
         forward(slot)
-    wait(ahead)
+    wait(later_copies)
 
     hidden = normed_ref[...] * vectors_ref[1:2] + vectors_ref[2:3]
     second = total_ref[...] + vectors_ref[3:4] + hidden
@@ -382,14 +366,21 @@
         out_ref[pl.ds((here_ref[1] ^ k) * pairs, pairs)] = ref[...].astype(out_ref.dtype)
 
 
-def head_grads_kernel(here_ref, qk_ref, vo_ref, qk_other, vo_other, grad_qkv_ref, grad_out_ref):
-    low = here_ref[0] == 0
-    pick_two = lambda a, b: (jnp.where(low, a[0], b[0]), jnp.where(low, b[0], a[0]))
-    grad_q, grad_k = pick_two(qk_ref, qk_other)
-    grad_v, grad_out = pick_two(vo_ref, vo_other)
-    for j, grad in enumerate((grad_q, grad_k, grad_v)):
-        grad_qkv_ref[j] = grad.astype(F32)
-    grad_out_ref[...] = grad_out.astype(F32)
+def head_grads_kernel(indices, here_ref, qk_mine, vo_mine, qk_other, vo_other, grad_qkv_ref, grad_out_ref):
+    core, place_here = here_ref[0], here_ref[2]
+    for side, qk_ref, vo_ref in ((core, qk_mine, vo_mine), (1 - core, qk_other, vo_other)):
+        for k, (qk_index, vo_index) in enumerate(zip(*indices)):
+            grad_qkv_ref[side, place_here ^ qk_index] = qk_ref[k].astype(F32)
+            place = place_here ^ vo_index
+            piece = vo_ref[k].astype(F32)
+
+            @pl.when(side == 0)
+            def _():
+                grad_qkv_ref[2, place] = piece
+
+            @pl.when(side != 0)
+            def _():
+                grad_out_ref[place] = piece
 
 
 def unit_grads_kernel(here_ref, in_ref, down_ref, in_other, down_other, grad_in_ref, grad_down_ref):
@@ -420,6 +411,10 @@
     return pl.BlockSpec(memory_space=pl.ANY)
 
 
+def in_vmem(array):
+    return pl.BlockSpec(memory_space=pltpu.VMEM)
+
+
 def call(kernel, steps, name, vmem, inputs, outputs, scratch, scalar, kept=()):
     spec = pltpu.PrefetchScalarGridSpec(
         num_scalar_prefetch=1,
@@ -435,26 +430,28 @@
         name=name,
         cost_estimate=pl.CostEstimate(flops=0, bytes_accessed=0, transcendentals=0),
         compiler_params=pltpu.CompilerParams(vmem_limit_bytes=vmem * MIB),
-    )(scalar, *[in_place(a) for _, a in inputs])
+    )(scalar, *[a if make is in_vmem else in_place(a) for make, a in inputs])
 
 
 def shape(dims, dtype):
     return jax.ShapeDtypeStruct(dims, dtype)
 
 
-def add_kernel(count, *refs):
-    total = refs[1][...].astype(F32)
-    for ref in refs[2 : 1 + count]:
-        total = total + ref[...].astype(F32)
-    refs[1 + count][...] = total.astype(BF16)
-
-
-def add_terms(terms, me, fixed):
-    first, bits = terms[0]
-    left = [b for b in bits if b not in fixed]
-    n, _, rows, cols = first.shape
-
-    def place(own_bits):
+def add_kernel(counts, *refs):
+    refs = refs[1:]
+    out_refs = refs[sum(counts) :]
+    for count, out_ref in zip(counts, out_refs):
+        total = refs[0][...].astype(F32)
+        for ref in refs[1:count]:
+            total = total + ref[...].astype(F32)
+        out_ref[...] = total.astype(BF16)
+        refs = refs[count:]
+
+
+def add_terms(sides, me):
+    in_specs, out_specs, arrays, outs, lefts = [], [], [], [], []
+
+    def place(own_bits, fixed, left):
         def index(g, me_ref):
             at = 0
             for b in own_bits:
@@ -468,21 +465,26 @@
 
         return index
 
-    spec = pltpu.PrefetchScalarGridSpec(
-        num_scalar_prefetch=1,
-        grid=(1 << len(left),),
-        in_specs=[pl.BlockSpec((n, 1, rows, cols), place(b)) for _, b in terms],
-        out_specs=pl.BlockSpec((n, 1, rows, cols), lambda g, _: (0, g, 0, 0)),
-    )
-    out = pl.pallas_call(
-        partial(add_kernel, len(terms)),
-        grid_spec=spec,
-        out_shape=shape((n, 1 << len(left), rows, cols), BF16),
+    for terms, fixed in sides:
+        first, bits = terms[0]
+        left = [b for b in bits if b not in fixed]
+        n, _, rows, cols = first.shape
+        in_specs += [pl.BlockSpec((n, 1, rows, cols), place(b, fixed, left)) for _, b in terms]
+        out_specs.append(pl.BlockSpec((n, 1, rows, cols), lambda g, _: (0, g, 0, 0)))
+        arrays += [a for a, _ in terms]
+        outs.append(shape((n, 1 << len(left), rows, cols), BF16))
+        lefts.append(left)
+    results = pl.pallas_call(
+        partial(add_kernel, [len(terms) for terms, _ in sides]),
+        grid_spec=pltpu.PrefetchScalarGridSpec(
+            num_scalar_prefetch=1, grid=(1 << len(lefts[0]),), in_specs=in_specs, out_specs=out_specs
+        ),
+        out_shape=outs,
         name="add",
         cost_estimate=pl.CostEstimate(flops=0, bytes_accessed=0, transcendentals=0),
-        compiler_params=pltpu.CompilerParams(vmem_limit_bytes=16 * MIB),
-    )(me, *[a for a, _ in terms])
-    return out, left
+        compiler_params=pltpu.CompilerParams(vmem_limit_bytes=24 * MIB),
+    )(me, *arrays)
+    return results, lefts
 
 
 def flip(array, axis, mask):
@@ -549,12 +551,12 @@
         self.left = [None, None]
 
     def pack(self, step):
-        sends = []
-        for side, order in enumerate(self.orders):
+        sides = []
+        for terms, order in zip(self.terms, self.orders):
             fixed = {b: True for b in order[:step]}
             fixed[order[step]] = False
-            out, self.left[side] = add_terms(self.terms[side], self.me, fixed)
-            sends.append(out)
+            sides.append((terms, fixed))
+        sends, self.left = add_terms(sides, self.me)
         return sends
 
     def send(self, step, packs):
@@ -566,7 +568,26 @@
 
     def finish(self):
         fixed = {b: True for b in self.bits}
-        return [add_terms(t, self.me, fixed)[0][:, 0] for t in self.terms]
+        sums, _ = add_terms([(t, fixed) for t in self.terms], self.me)
+        return [a[:, 0] for a in sums]
+
+
+class Pieces:
+    def __init__(self, pair):
+        self.bits, self.orders = outer_bits()
+        self.steps = len(self.bits)
+        self.held = [p[None] for p in pair]
+        self.indices = [[0], [0]]
+
+    def send(self, step):
+        return [flip(h, "dp", 1 << order[step]) for h, order in zip(self.held, self.orders)]
+
+    def take(self, step, got):
+        self.held = [jnp.concatenate([h, g]) for h, g in zip(self.held, got)]
+        self.indices = [
+            index + [i ^ (1 << (order[step] - 1)) for i in index]
+            for index, order in zip(self.indices, self.orders)
+        ]
 
 
 def add_parts(*parts):
@@ -606,21 +627,20 @@
     units = w_in.shape[1]
     half_units = units // 2
     order = jnp.arange(mp) ^ mi
-    here = jnp.stack([lax.axis_index("dp") & 1, mi]).astype(jnp.int32)
+    here = jnp.stack([lax.axis_index("dp") & 1, mi, lax.axis_index("dp") >> 1]).astype(jnp.int32)
     share = share_of()
 
-    turned = w_qkv.transpose(0, 2, 1)
-    own = {
-        "qk": turned[:2].reshape(2 * cols, width),
-        "vo": jnp.concatenate([turned[2], w_out], axis=0),
-        "in": w_in.T,
-        "down": w_down,
-    }
-    own_qk, own_vo = own["qk"], own["vo"]
-
-    def piece(name):
-        part = own[name].shape[0] // dp
-        return lax.dynamic_slice_in_dim(own[name], share * part, part, 0)
+    turned = w_qkv.transpose(0, 2, 1).reshape(3 * cols, width)
+    own_qk = turned[: 2 * cols]
+    own_vo = jnp.concatenate([turned[2 * cols :], w_out], axis=0)
+    att_part, ffn_part = 2 * cols // dp, units // dp
+    first = share * att_part
+    rows_of = lambda array, start, size: lax.dynamic_slice_in_dim(array, start, size, 0)
+    vo_piece = jnp.where(
+        first < cols,
+        rows_of(turned, 2 * cols + jnp.minimum(first, cols - att_part), att_part),
+        rows_of(w_out, jnp.maximum(first - cols, 0), att_part),
+    )
 
     def row_blocks(array):
         blocks = array.reshape((mp, pairs) + array.shape[1:])
@@ -631,9 +651,11 @@
 
     fill = lambda v: jnp.pad(v, ((0, 0), (0, width - v.shape[1])))
     small = jnp.concatenate([fill(qv_bias), in_bias.reshape(1, units), jnp.zeros((5, width), BF16)])
-    att_part, ffn_part = 2 * cols // dp, units // dp
-    att_send = jnp.concatenate([piece("qk"), piece("vo"), small], axis=0)
-    ffn_send = jnp.concatenate([piece("in"), piece("down")], axis=0)
+    att_send = jnp.concatenate([rows_of(turned, first, att_part), vo_piece], axis=0)
+    ffn_send = jnp.concatenate(
+        [rows_of(w_in.T, share * ffn_part, ffn_part), rows_of(w_down, share * ffn_part, ffn_part), small],
+        axis=0,
+    )
     tok = row_blocks(tokens)
     cot = row_blocks(cotangent)
     vectors = jnp.stack(
@@ -655,34 +677,34 @@
     att = Gather(
         [
             jnp.stack([g[:att_part] for g in att_got]),
-            jnp.stack([g[att_part : 2 * att_part] for g in att_got]),
+            jnp.stack([g[att_part:] for g in att_got]),
         ]
     )
     ffn_two = flip(ffn_send, "mp", 2)
     got = att.send(0)
     tok_one = flip(tok[1], "mp", 1)
-    ffn_two, got, tok_one, ffn_send, tok, att_got = tie(ffn_two, got, tok_one, ffn_send, tok, att_got)
-    smalls = jnp.stack([small] + [g[2 * att_part :] for g in att_got]).astype(F32)
+    ffn_two, got, tok_one, ffn_send, tok = tie(ffn_two, got, tok_one, ffn_send, tok)
     for step in range(1, att.steps):
         att.take(step - 1, got)
         got = att.send(step)
         if step == 1:
             ffn_odd = flip(jnp.stack([ffn_send, ffn_two]), "mp", 1)
             tok_three = flip(tok[3], "mp", 3)
-        got, ffn_odd, tok_three, tok, smalls = tie(got, ffn_odd, tok_three, tok, smalls)
+        got, ffn_odd, tok_three, tok = tie(got, ffn_odd, tok_three, tok)
     att.take(att.steps - 1, got)
     ffn_got = [ffn_odd[0], ffn_two, ffn_odd[1]]
     ffn = Gather(
         [
             jnp.stack([g[:ffn_part] for g in ffn_got]),
-            jnp.stack([g[ffn_part:] for g in ffn_got]),
+            jnp.stack([g[ffn_part : 2 * ffn_part] for g in ffn_got]),
         ]
     )
     got = ffn.send(0)
     qk_one, vo_one = att.halves()
     qk_two, vo_two = flip(qk_one, "dp", 1), flip(vo_one, "dp", 1)
     tok_two = flip(tok[2], "mp", 2)
-    got, qk_two, vo_two, tok_two, cot = tie(got, qk_two, vo_two, tok_two, cot)
+    smalls = jnp.stack([small] + [g[2 * ffn_part :] for g in ffn_got]).astype(F32)
+    got, qk_two, vo_two, tok_two, cot, smalls = tie(got, qk_two, vo_two, tok_two, cot, smalls)
     heads_low = shape((mp, rows, cols), BF16)
     low_shape = shape((rows, width), BF16)
     rows_shape = shape((rows, width), F32)
@@ -742,22 +764,21 @@
     in_args = [(column_mine, w_in), (column_other, w_in), (later, in_one), (later, in_two)]
     half = shape((mp, half_units, width), BF16)
     pre_shape = shape((mp, rows, units), BF16)
-    others = (mp - 1, half_units, width)
     vmem = lambda a: pltpu.VMEM(a.shape, a.dtype)
     results = call(
         partial(ffn_kernel, mp),
         1,
         "ffn",
-        52,
+        44,
         [
             (where_it_is, hidden_low),
             (where_it_is, normed_one),
             (where_it_is, w_in),
-            (where_it_is, in_one),
-            (where_it_is, in_two),
+            (in_vmem, in_one),
+            (in_vmem, in_two),
             (where_it_is, w_down),
-            (where_it_is, down_one),
-            (where_it_is, down_two),
+            (in_vmem, down_one),
+            (in_vmem, down_two),
             (whole, smalls),
             (whole, vectors),
             *[(where_it_is, c) for c in cot_blocks],
@@ -777,11 +798,7 @@
             vmem(low_shape),
             vmem(rows_shape),
             pltpu.VMEM((width, units), BF16),
-            pltpu.VMEM(others, BF16),
-            pltpu.VMEM(others, BF16),
             pltpu.VMEM((units, width), BF16),
-            pltpu.VMEM(others, BF16),
-            pltpu.VMEM(others, BF16),
             pltpu.VMEM((mp,) + block_shape.shape, BF16),
             vmem(pre_shape),
             pltpu.VMEM(pre_shape.shape, F32),
@@ -792,10 +809,10 @@
             vmem(half),
             vmem(half),
             vmem(half),
-            pltpu.SemaphoreType.DMA((3 + 4 * (mp - 1) + 1 + mp + 1 + 5 * mp,)),
+            pltpu.SemaphoreType.DMA((3 + 1 + mp + 1 + 5 * mp,)),
         ],
         here,
-        range(mp, mp + 6),
+        range(mp + 6),
     )
     out_blocks = results[:mp]
     delta_ffn, pre_grad, in_keep, in_send, down_keep, down_send, sum_in, sums_two = results[mp:]
@@ -866,8 +883,8 @@
         got = ffn.send(step, packs)
         if step == 1:
             att_got = flip(att_send, "dp", 1)
-            row_two, row_three = flip(row_sends[2], "mp", 2), flip(row_sends[3], "mp", 3)
-        got, att_got, row_two, row_three, row_sends = tie(got, att_got, row_two, row_three, row_sends)
+            row_three = flip(row_sends[3], "mp", 3)
+        got, att_got, row_three, row_sends = tie(got, att_got, row_three, row_sends)
     place = lambda blocks, dtype: call(
         partial(place_kernel, pairs),
         1,
@@ -888,7 +905,10 @@
     got = att.send(0, att.pack(0))
     ffn_got = flip(ffn_odd, "mp", 1)
     sums_got = flip(sums, "dp", 1)
-    got, ffn_got, sums_got, row_sends, layer_out = tie(got, ffn_got, sums_got, row_sends, layer_out)
+    row_two = flip(row_sends[2], "mp", 2)
+    got, ffn_got, sums_got, row_two, row_sends, layer_out = tie(
+        got, ffn_got, sums_got, row_two, row_sends, layer_out
+    )
     sums = sums + sums_got
     for mask in [1 << b for b in range(2, dp.bit_length() - 2)]:
         sums = sums + flip(sums, "dp", mask)
@@ -901,7 +921,7 @@
             ffn_last = flip(ffn_two, "mp", 2)
             row_one = flip(row_sends[1], "mp", 1)
             sums_got = flip(sums, "dp", 2)
-        got, ffn_last, row_one, sums_got = tie(got, ffn_last, row_one, sums_got)
+        got, ffn_last, row_one, sums_got, row_sends = tie(got, ffn_last, row_one, sums_got, row_sends)
     att.take(got)
     sums = sums + sums_got
     att_parts = att.finish()
@@ -910,11 +930,11 @@
     ffn_sum = add_parts(ffn_even[0], ffn_got[0], ffn_last)
     ffn = Gather([ffn_sum[None, :ffn_part], ffn_sum[None, ffn_part:]])
     ffn.held, att_odd, att_even, sums = tie(ffn.held, att_odd, att_even, sums)
-    grad_input = place([row_sends[0], row_one, row_two, row_three], F32)
     got = ffn.send(0)
     att_got = flip(att_odd, "mp", 1)
     sums_got = flip(sums, "dp", dp // 2)
-    got, att_got, sums_got, grad_input = tie(got, att_got, sums_got, grad_input)
+    got, att_got, sums_got, row_one = tie(got, att_got, sums_got, row_one)
+    grad_input = place([row_sends[0], row_one, row_two, row_three], F32)
     sums = sums + sums_got
     att_two = add_parts(att_even[1], att_got[1])
     for step in range(1, ffn.steps):
@@ -923,17 +943,22 @@
         if step == 1:
             att_last = flip(att_two, "mp", 2)
             sums_got = flip(sums, "mp", 1)
-        got, att_last, sums_got = tie(got, att_last, sums_got)
+        got, att_last, sums_got, grad_input = tie(got, att_last, sums_got, grad_input)
     ffn.take(ffn.steps - 1, got)
     sums = sums + sums_got
     att_sum = add_parts(att_even[0], att_got[0], att_last)
-    att = Gather([att_sum[None, :att_part], att_sum[None, att_part:]])
     ffn_halves = ffn.halves()
     core_got = [flip(h, "dp", 1) for h in ffn_halves]
+    att = Pieces([att_sum[:att_part], att_sum[att_part:]])
     got = att.send(0)
-    sums_got = flip(sums, "mp", 2)
-    core_got, got, sums_got = tie(core_got, got, sums_got)
-    sums = sums + sums_got
+    core_got, got, sums = tie(core_got, got, sums)
+    for step in range(1, att.steps):
+        att.take(step - 1, got)
+        got = att.send(step)
+        if step == 1:
+            sums_got = flip(sums, "mp", 2)
+        if step < att.steps - 1:
+            got = tie(*got)
     grad_in, grad_down = call(
         unit_grads_kernel,
         1,
@@ -944,20 +969,20 @@
         [],
         here,
     )
-    for step in range(1, att.steps):
-        att.take(step - 1, got)
-        got = tie(*att.send(step))
-    grad_in, grad_down, got = tie(grad_in, grad_down, got)
+    grad_in, grad_down, got, sums_got = tie(grad_in, grad_down, got, sums_got)
+    sums = sums + sums_got
     att.take(att.steps - 1, got)
-    att_halves = att.halves()
-    core_got = [flip(h, "dp", 1) for h in att_halves]
+    core_got = [flip(h, "dp", 1) for h in att.held]
     grad_qkv, grad_out = call(
-        head_grads_kernel,
+        partial(head_grads_kernel, att.indices),
         1,
         "head_grads",
         24,
-        [(whole, a) for a in att_halves + core_got],
-        [(whole, shape((3, cols, width), F32)), (whole, shape((cols, width), F32))],
+        [(whole, a) for a in att.held + core_got],
+        [
+            (whole, shape((3, cols // att_part, att_part, width), F32)),
+            (whole, shape((cols // att_part, att_part, width), F32)),
+        ],
         [],
         here,
     )
@@ -967,9 +992,9 @@
     return (
         layer_out,
         grad_input,
-        grad_qkv.transpose(0, 2, 1),
+        grad_qkv.reshape(3, cols, width).transpose(0, 2, 1),
         sum_qv,
-        grad_out,
+        grad_out.reshape(cols, width),
         sums[0],
         sums[1],
         sums[2],

time: 258 us -> 251 us (0.973)
  starting transfers between devices: 65.5 us -> 57.9 us
  waiting for transfers between devices: 98.7 us -> 102 us
  local copies, waits for them, and re-layouts: 14.5 us -> 11.5 us
    ppermute x61, starting transfers between devices: 65.5 us -> 57.9 us  [flip(): return lax.ppermute(array, axis, [(i, i ^ mask) for i in range(size)])]
    ppermute x61, waiting for transfers between devices: 98.7 us -> 102 us  [flip(): return lax.ppermute(array, axis, [(i, i ^ mask) for i in range(size)])]
  transfers between devices with their start and end apart: 61 -> 61, of which waited for: 24 -> 27; matrix products, arithmetic and copies ran while one was open for 3% -> 4% of each run, Pallas kernels for 18% -> 19%
where the time goes in v5:
time: 251 us
  waiting for transfers between devices  102 us (41%)
  Pallas kernels  72.8 us (29%)
  starting transfers between devices  57.9 us (23%)
  local copies, waits for them, and re-layouts  11.5 us (5%)
  other arithmetic  4.62 us (2%)
    ppermute x61, waiting for transfers between devices, flip(): return lax.ppermute(array, axis, [(i, i ^ mask) for i in range(size)])  102 us
    pallas_call x8, Pallas kernels, call(): pl.pallas_call(kernel, grid_spec=spec, out_shape=[pltpu.HBM(a.shape, a.dt...  68.3 us
    ppermute x61, starting transfers between devices, flip(): return lax.ppermute(array, axis, [(i, i ^ mask) for i in range(size)])  57.9 us
  transfers between devices with their start and end apart: 61, of which 27 were waited for; matrix products, arithmetic and copies ran while one was open for 4% of the time, Pallas kernels for 19%

profile of v5, /device:TPU:0, one launch (start us, length us, event | category | flops | bytes accessed | tf_op | source)
XLA Modules:
  0.0 250.8 jit_solution(1873940237438927644)
XLA Ops:
  1.8 3.1 %collective-permute-start = (bf16[96,768]{1,0:T(8,128)(2,1)S(1)}, bf16[96,768]{1,0:T(8,128)(2,1)S(1)}, u32[]{:S(2)}, u32[]{:S(2)}) collective-permute-start(bf16[96,768]{1,0:T(8,128)(2,1)S(1)} %pad_maximum_fusion.21), channel_id=1, source_target_pairs={{0,1},{1,0},{2,3},{3,2},{4,5},{5,4},{6,7},{7,6},{8,9},{9,8},{10,11... | collective-permute-start | bytes 442376 | tf_op jit(solution)/shard_map/ppermute | solution.py:492
  4.9 2.6 %collective-permute-start.1 = (bf16[96,768]{1,0:T(8,128)(2,1)S(1)}, bf16[96,768]{1,0:T(8,128)(2,1)}, u32[]{:S(2)}, u32[]{:S(2)}) collective-permute-start(bf16[96,768]{1,0:T(8,128)(2,1)S(1)} %pad_maximum_fusion.21), channel_id=1, source_target_pairs={{0,2},{1,3},{2,0},{3,1},{4,6},{5,7},{6,4},{7,5},{8,10},{9,11},{10,... | collective-permute-start | bytes 442376 | tf_op jit(solution)/shard_map/ppermute | solution.py:492
  13.7 5.3 %collective-permute-done.1 = bf16[96,768]{1,0:T(8,128)(2,1)} collective-permute-done((bf16[96,768]{1,0:T(8,128)(2,1)S(1)}, bf16[96,768]{1,0:T(8,128)(2,1)}, u32[]{:S(2)}, u32[]{:S(2)}) %collective-permute-start.1) | collective-permute-done | bytes 147488 | tf_op jit(solution)/shard_map/ppermute | solution.py:492
  20.1 1.6 collective-permute-start.5
  21.7 3.3 %collective-permute-start.3 = (bf16[200,768]{1,0:T(8,128)(2,1)S(1)}, bf16[200,768]{1,0:T(8,128)(2,1)S(1)}, u32[]{:S(2)}, u32[]{:S(2)}) collective-permute-start(bf16[200,768]{1,0:T(8,128)(2,1)S(1)} %concatenate.79), channel_id=1, source_target_pairs={{0,2},{1,3},{2,0},{3,1},{4,6},{5,7},{6,4},{7,5},{8,10},{9,11},{10,... | collective-permute-start | bytes 921608 | tf_op jit(solution)/shard_map/ppermute | solution.py:492
  25.0 1.6 collective-permute-start.4
  26.5 7.8 %collective-permute-done.6 = bf16[3,40,768]{2,1,0:T(8,128)(2,1)S(1)} collective-permute-done((bf16[3,40,768]{2,1,0:T(8,128)(2,1)}, bf16[3,40,768]{2,1,0:T(8,128)(2,1)S(1)}, u32[]{:S(2)}, u32[]{:S(2)}) %collective-permute-start.6) | collective-permute-done | bytes 184352 | tf_op jit(solution)/shard_map/ppermute | solution.py:492
  34.4 3.2 %collective-permute-done.3 = bf16[200,768]{1,0:T(8,128)(2,1)S(1)} collective-permute-done((bf16[200,768]{1,0:T(8,128)(2,1)S(1)}, bf16[200,768]{1,0:T(8,128)(2,1)S(1)}, u32[]{:S(2)}, u32[]{:S(2)}) %collective-permute-start.3) | collective-permute-done | bytes 307232 | tf_op jit(solution)/shard_map/ppermute | solution.py:492
  37.8 1.6 collective-permute-start.8
  41.4 14.1 %collective-permute-done.10 = bf16[3,40,768]{2,1,0:T(8,128)(2,1)S(1)} collective-permute-done((bf16[3,40,768]{2,1,0:T(8,128)(2,1)S(1)}, bf16[3,40,768]{2,1,0:T(8,128)(2,1)S(1)}, u32[]{:S(2)}, u32[]{:S(2)}) %collective-permute-start.10) | collective-permute-done | bytes 184352 | tf_op jit(solution)/shard_map/ppermute | solution.py:492
  58.4 1.6 collective-permute-start.11
  60.7 10.3 %collective-permute-done.15 = bf16[3,40,768]{2,1,0:T(8,128)(2,1)S(1)} collective-permute-done((bf16[3,40,768]{2,1,0:T(8,128)(2,1)S(1)}, bf16[3,40,768]{2,1,0:T(8,128)(2,1)S(1)}, u32[]{:S(2)}, u32[]{:S(2)}) %collective-permute-start.15) | collective-permute-done | bytes 184352 | tf_op jit(solution)/shard_map/ppermute | solution.py:492
  72.2 1.6 collective-permute-start.16
  73.8 2.7 %collective-permute-start.19 = (bf16[3,40,768]{2,1,0:T(8,128)(2,1)S(1)}, bf16[3,40,768]{2,1,0:T(8,128)(2,1)S(1)}, u32[]{:S(2)}, u32[]{:S(2)}) collective-permute-start(bf16[3,40,768]{2,1,0:T(8,128)(2,1)S(1)} %get-tuple-element.219), channel_id=1, source_target_pairs={{0,2},{1,3},{2,0},{3,1},{4,6},{5,7},{6,4},{7,5},{8,10},{9,11},{10,... | collective-permute-start | bytes 552968 | tf_op jit(solution)/shard_map/ppermute | solution.py:492
  76.4 1.7 collective-permute-start.20
  78.3 12.0 %attention.1 = (bf16[4,480,192]{2,1,0:T(8,128)(2,1)}, bf16[4,480,192]{2,1,0:T(8,128)(2,1)}, bf16[4,480,192]{2,1,0:T(8,128)(2,1)}, f32[4,3,480,160]{3,2,1,0:T(8,1...) custom-call(s32[3]{0:T(128)S(1)} %pad_add_fusion.here_ref, ...), custom_call_target="tpu_custom_call" | custom-call | tf_op jit(solution)/shard_map/attention/pallas_call | solution.py:426
  90.3 2.5 collective-permute-done.17
  94.8 2.7 %collective-permute-done.22.down_two = bf16[3,384,768]{2,1,0:T(8,128)(2,1)S(1)} collective-permute-done((bf16[3,384,768]{2,1,0:T(8,128)(2,1)S(1)}, bf16[3,384,768]{2,1,0:T(8,128)(2,1)S(1)}, u32[]{:S(2)}, u32[]{:S(2)}) %collective-permute-start.22) | collective-permute-done | bytes 1769504 | tf_op jit(solution)/shard_map/ppermute | solution.py:492
  97.5 2.5 %collective-permute-done.21.in_two = bf16[3,384,768]{2,1,0:T(8,128)(2,1)S(1)} collective-permute-done((bf16[3,384,768]{2,1,0:T(8,128)(2,1)S(1)}, bf16[3,384,768]{2,1,0:T(8,128)(2,1)S(1)}, u32[]{:S(2)}, u32[]{:S(2)}) %collective-permute-start.21) | collective-permute-done | bytes 1769504 | tf_op jit(solution)/shard_map/ppermute | solution.py:492
  100.0 20.2 %ffn.1 = (bf16[3,40,768]{2,1,0:T(8,128)(2,1)}, bf16[3,40,768]{2,1,0:T(8,128)(2,1)}, bf16[3,40,768]{2,1,0:T(8,128)(2,1)}, bf16[3,40,768]{2,1,0:T(8,128)(2,1)}, f3...) custom-call(s32[3]{0:T(128)S(1)} %pad_add_fusion.here_ref, ...), custom_call_target="tpu_custom_call" | custom-call | tf_op jit(solution)/shard_map/ffn/pallas_call | solution.py:426
  120.8 8.5 %ffn_back.1 = (f32[480,768]{1,0:T(8,128)S(1)}, bf16[480,768]{1,0:T(8,128)(2,1)S(1)}, f32[8,768]{1,0:T(8,128)S(1)}) custom-call(s32[3]{0:T(128)S(1)} %pad_add_fusion.here_ref, bf16[4,480,768]{2,1,0:T(8,128)(2,1)} %get-tuple-element.239.pre_grad_ref, bf16[768,768]{1,0:T(8,128)(2,1)} %own_in_two.1, bf16[768,768]{1,0:T(8,128)(2,1)} %own_in_two.1, ...), custom_call_target="tpu_custom_call" | custom-call | tf_op jit(solution)/shard_map/ffn_back/pallas_call | solution.py:426
  130.5 1.9 add.189
  132.4 1.5 collective-permute-start.25
  133.9 1.5 collective-permute-start.26
  135.5 2.3 collective-permute-start.28
  137.8 2.1 collective-permute-start.29
  139.9 19.2 %attention_back.1 = (bf16[4,192,768]{2,1,0:T(8,128)(2,1)}, bf16[4,192,768]{2,1,0:T(8,128)(2,1)}, bf16[2,4,192,768]{3,2,1,0:T(8,128)(2,1)}, f32[24,768]{1,0:T(8,1...) custom-call(s32[3]{0:T(128)S(1)} %pad_add_fusion.here_ref, ...), custom_call_target="tpu_custom_call" | custom-call | tf_op jit(solution)/shard_map/attention_back/pallas_call | solution.py:426
  159.1 1.5 collective-permute-done.25.refs_3_
  162.1 1.6 collective-permute-start.30
  164.3 1.7 collective-permute-start.33
  166.0 6.7 %collective-permute-done.33.refs_3_ = bf16[3,40,768]{2,1,0:T(8,128)(2,1)S(1)} collective-permute-done((bf16[3,40,768]{2,1,0:T(8,128)(2,1)S(1)}, bf16[3,40,768]{2,1,0:T(8,128)(2,1)S(1)}, u32[]{:S(2)}, u32[]{:S(2)}) %collective-permute-start.33) | collective-permute-done | bytes 184352 | tf_op jit(solution)/shard_map/ppermute | solution.py:492
  172.7 5.3 %collective-permute-done.30.refs_4_ = bf16[4,1,96,768]{3,2,1,0:T(8,128)(2,1)S(1)} collective-permute-done((bf16[4,1,96,768]{3,2,1,0:T(8,128)(2,1)S(1)}, bf16[4,1,96,768]{3,2,1,0:T(8,128)(2,1)S(1)}, u32[]{:S(2)}, u32[]{:S(2)}) %collective-permute-start.30) | collective-permute-done | bytes 589856 | tf_op jit(solution)/shard_map/ppermute | solution.py:492
  184.7 1.5 place.2
  186.2 10.4 %collective-permute-done.38.refs_2_ = bf16[3,40,768]{2,1,0:T(8,128)(2,1)S(1)} collective-permute-done((bf16[3,40,768]{2,1,0:T(8,128)(2,1)S(1)}, bf16[3,40,768]{2,1,0:T(8,128)(2,1)S(1)}, u32[]{:S(2)}, u32[]{:S(2)}) %collective-permute-start.38) | collective-permute-done | bytes 184352 | tf_op jit(solution)/shard_map/ppermute | solution.py:492
  196.5 2.2 collective-permute-done.36
  202.6 1.6 collective-permute-start.43
  204.2 5.6 %collective-permute-done.43 = f32[24,768]{1,0:T(8,128)S(1)} collective-permute-done((f32[24,768]{1,0:T(8,128)S(1)}, f32[24,768]{1,0:T(8,128)S(1)}, u32[]{:S(2)}, u32[]{:S(2)}) %collective-permute-start.43) | collective-permute-done | bytes 73760 | tf_op jit(solution)/shard_map/ppermute | solution.py:492
  209.8 3.7 %collective-permute-done.41 = bf16[192,768]{1,0:T(8,128)(2,1)S(1)} collective-permute-done((bf16[192,768]{1,0:T(8,128)(2,1)S(1)}, bf16[192,768]{1,0:T(8,128)(2,1)S(1)}, u32[]{:S(2)}, u32[]{:S(2)}) %collective-permute-start.41) | collective-permute-done | bytes 294944 | tf_op jit(solution)/shard_map/ppermute | solution.py:492
  217.0 4.6 %collective-permute-done.47 = f32[24,768]{1,0:T(8,128)S(1)} collective-permute-done((f32[24,768]{1,0:T(8,128)S(1)}, f32[24,768]{1,0:T(8,128)S(1)}, u32[]{:S(2)}, u32[]{:S(2)}) %collective-permute-start.47) | collective-permute-done | bytes 73760 | tf_op jit(solution)/shard_map/ppermute | solution.py:492
  226.4 1.7 place.3
  228.1 2.4 collective-permute-done.51
  230.5 1.6 collective-permute-done.50
  233.0 1.7 collective-permute-start.54
  237.4 1.6 collective-permute-done.55
  239.6 1.7 collective-permute-start.56
  241.5 3.1 %unit_grads.1 = (f32[768,768]{1,0:T(8,128)}, f32[768,768]{1,0:T(8,128)}) custom-call(s32[3]{0:T(128)S(1)} %pad_add_fusion.here_ref, bf16[1,384,768]{2,1,0:T(8,128)(2,1)S(1)} %bitcast.160, bf16[1,384,768]{2,1,0:T(8,128)(2,1)S(1)} %bitcast.158, bf16[1,384,768]{2,1,0:T(8,128)(2,1)S(1)} %collective-permute-done.52.in_other, ...), custom_call_target="tpu_custom_call" | custom-call | tf_op jit(solution)/shard_map/unit_grads/pallas_call | solution.py:426
  244.6 1.8 collective-permute-done.58
  248.6 2.1 head_grads.1
  (278 shorter events, 46.0 us)
Async XLA Ops:
  1.8 11.9 %collective-permute-start = (bf16[96,768]{1,0:T(8,128)(2,1)S(1)}, bf16[96,768]{1,0:T(8,128)(2,1)S(1)}, u32[]{:S(2)}, u32[]{:S(2)}) collective-permute-start(bf16[96,768]{1,0:T(8,128)(2,1)S(1)} %pad_maximum_fusion.21), channel_id=1, source_target_pairs={{0,1},{1,0},{2,3},{3,2},{4,5},{5,4},{6,7},{7,6},{8,9},{9,8},{10,11... | collective-permute-start | bytes 442376 | tf_op jit(solution)/shard_map/ppermute | solution.py:492
  4.9 14.1 %collective-permute-start.1 = (bf16[96,768]{1,0:T(8,128)(2,1)S(1)}, bf16[96,768]{1,0:T(8,128)(2,1)}, u32[]{:S(2)}, u32[]{:S(2)}) collective-permute-start(bf16[96,768]{1,0:T(8,128)(2,1)S(1)} %pad_maximum_fusion.21), channel_id=1, source_target_pairs={{0,2},{1,3},{2,0},{3,1},{4,6},{5,7},{6,4},{7,5},{8,10},{9,11},{10,... | collective-permute-start | bytes 442376 | tf_op jit(solution)/shard_map/ppermute | solution.py:492
  7.5 11.5 %collective-permute-start.2 = (bf16[96,768]{1,0:T(8,128)(2,1)S(1)}, bf16[96,768]{1,0:T(8,128)(2,1)}, u32[]{:S(2)}, u32[]{:S(2)}) collective-permute-start(bf16[96,768]{1,0:T(8,128)(2,1)S(1)} %pad_maximum_fusion.21), channel_id=1, source_target_pairs={{0,3},{1,2},{2,1},{3,0},{4,7},{5,6},{6,5},{7,4},{8,11},{9,10},{10,... | collective-permute-start | bytes 442376 | tf_op jit(solution)/shard_map/ppermute | solution.py:492
  20.1 14.3 %collective-permute-start.5 = (bf16[3,1,1,48,768]{4,3,0,2,1:T(8,128)(2,1)S(1)}, bf16[3,1,1,48,768]{4,3,0,2,1:T(8,128)(2,1)S(1)}, u32[]{:S(2)}, u32[]{:S(2)}) collective-permute-start(bf16[3,1,1,48,768]{4,3,0,2,1:T(8,128)(2,1)S(1)} %maximum_bitcast_fusion.3), channel_id=1, source_target_pairs={{0,16},{4,20},{8,24},{12,28},{16,0},{20,4},{24,8},{28,12},{1,17},{... | collective-permute-start | bytes 663560 | tf_op jit(solution)/shard_map/ppermute | solution.py:492
  21.7 15.9 %collective-permute-start.3 = (bf16[200,768]{1,0:T(8,128)(2,1)S(1)}, bf16[200,768]{1,0:T(8,128)(2,1)S(1)}, u32[]{:S(2)}, u32[]{:S(2)}) collective-permute-start(bf16[200,768]{1,0:T(8,128)(2,1)S(1)} %concatenate.79), channel_id=1, source_target_pairs={{0,2},{1,3},{2,0},{3,1},{4,6},{5,7},{6,4},{7,5},{8,10},{9,11},{10,... | collective-permute-start | bytes 921608 | tf_op jit(solution)/shard_map/ppermute | solution.py:492
  25.0 9.4 %collective-permute-start.4 = (bf16[3,1,1,48,768]{4,3,0,2,1:T(8,128)(2,1)S(1)}, bf16[3,1,1,48,768]{4,3,0,2,1:T(8,128)(2,1)S(1)}, u32[]{:S(2)}, u32[]{:S(2)}) collective-permute-start(bf16[3,1,1,48,768]{4,3,0,2,1:T(8,128)(2,1)S(1)} %maximum_bitcast_fusion.2), channel_id=1, source_target_pairs={{0,8},{4,12},{8,0},{12,4},{16,24},{20,28},{24,16},{28,20},{1,9},{5... | collective-permute-start | bytes 663560 | tf_op jit(solution)/shard_map/ppermute | solution.py:492
  26.5 7.8 %collective-permute-start.6 = (bf16[3,40,768]{2,1,0:T(8,128)(2,1)}, bf16[3,40,768]{2,1,0:T(8,128)(2,1)S(1)}, u32[]{:S(2)}, u32[]{:S(2)}) collective-permute-start(bf16[3,40,768]{2,1,0:T(8,128)(2,1)} %get-tuple-element.188), channel_id=1, source_target_pairs={{0,1},{1,0},{2,3},{3,2},{4,5},{5,4},{6,7},{7,6},{8,9},{9,8},{10,11... | collective-permute-start | bytes 552968 | tf_op jit(solution)/shard_map/ppermute | solution.py:492
  37.6 18.8 %collective-permute-start.9 = (bf16[2,200,768]{2,1,0:T(8,128)(2,1)S(1)}, bf16[2,200,768]{2,1,0:T(8,128)(2,1)S(1)}, u32[]{:S(2)}, u32[]{:S(2)}) collective-permute-start(bf16[2,200,768]{2,1,0:T(8,128)(2,1)S(1)} %pad_maximum_fusion.7), channel_id=1, source_target_pairs={{0,1},{1,0},{2,3},{3,2},{4,5},{5,4},{6,7},{7,6},{8,9},{9,8},{10,11... | collective-permute-start | bytes 1843208 | tf_op jit(solution)/shard_map/ppermute | solution.py:492
  37.8 17.7 %collective-permute-start.8 = (bf16[3,2,1,48,768]{4,3,0,2,1:T(8,128)(2,1)S(1)}, bf16[3,2,1,48,768]{4,3,0,2,1:T(8,128)(2,1)S(1)}, u32[]{:S(2)}, u32[]{:S(2)}) collective-permute-start(bf16[3,2,1,48,768]{4,3,0,2,1:T(8,128)(2,1)S(1)} %pad_maximum_fusion.14), channel_id=1, source_target_pairs={{0,8},{4,12},{8,0},{12,4},{16,24},{20,28},{24,16},{28,20},{1,9},{5... | collective-permute-start | bytes 1327112 | tf_op jit(solution)/shard_map/ppermute | solution.py:492
  39.5 16.1 %collective-permute-start.7 = (bf16[3,1,2,48,768]{4,3,0,2,1:T(8,128)(2,1)S(1)}, bf16[3,1,2,48,768]{4,3,0,2,1:T(8,128)(2,1)S(1)}, u32[]{:S(2)}, u32[]{:S(2)}) collective-permute-start(bf16[3,1,2,48,768]{4,3,0,2,1:T(8,128)(2,1)S(1)} %pad_maximum_fusion.13), channel_id=1, source_target_pairs={{0,16},{4,20},{8,24},{12,28},{16,0},{20,4},{24,8},{28,12},{1,17},{... | collective-permute-start | bytes 1327112 | tf_op jit(solution)/shard_map/ppermute | solution.py:492
  40.2 15.4 %collective-permute-start.10 = (bf16[3,40,768]{2,1,0:T(8,128)(2,1)S(1)}, bf16[3,40,768]{2,1,0:T(8,128)(2,1)S(1)}, u32[]{:S(2)}, u32[]{:S(2)}) collective-permute-start(bf16[3,40,768]{2,1,0:T(8,128)(2,1)S(1)} %copy-done.30), channel_id=1, source_target_pairs={{0,3},{1,2},{2,1},{3,0},{4,7},{5,6},{6,5},{7,4},{8,11},{9,10},{10,... | collective-permute-start | bytes 552968 | tf_op jit(solution)/shard_map/ppermute | solution.py:492
  56.7 14.2 %collective-permute-start.14 = (bf16[3,192,768]{2,1,0:T(8,128)(2,1)S(1)}, bf16[3,192,768]{2,1,0:T(8,128)(2,1)S(1)}, u32[]{:S(2)}, u32[]{:S(2)}) collective-permute-start(bf16[3,192,768]{2,1,0:T(8,128)(2,1)S(1)} %bitcast.145), channel_id=1, source_target_pairs={{0,4},{4,0},{8,12},{12,8},{16,20},{20,16},{24,28},{28,24},{1,5},{5... | collective-permute-start | bytes 2654216 | tf_op jit(solution)/shard_map/ppermute | solution.py:492
  57.1 13.9 %collective-permute-start.13 = (bf16[3,192,768]{2,1,0:T(8,128)(2,1)S(1)}, bf16[3,192,768]{2,1,0:T(8,128)(2,1)S(1)}, u32[]{:S(2)}, u32[]{:S(2)}) collective-permute-start(bf16[3,192,768]{2,1,0:T(8,128)(2,1)S(1)} %bitcast.148), channel_id=1, source_target_pairs={{0,4},{4,0},{8,12},{12,8},{16,20},{20,16},{24,28},{28,24},{1,5},{5... | collective-permute-start | bytes 2654216 | tf_op jit(solution)/shard_map/ppermute | solution.py:492
  57.7 13.2 %collective-permute-start.12 = (bf16[3,1,1,96,768]{4,3,0,2,1:T(8,128)(2,1)S(1)}, bf16[3,1,1,96,768]{4,3,0,2,1:T(8,128)(2,1)S(1)}, u32[]{:S(2)}, u32[]{:S(2)}) collective-permute-start(bf16[3,1,1,96,768]{4,3,0,2,1:T(8,128)(2,1)S(1)} %maximum_bitcast_fusion.1), channel_id=1, source_target_pairs={{0,16},{4,20},{8,24},{12,28},{16,0},{20,4},{24,8},{28,12},{1,17},{... | collective-permute-start | bytes 1327112 | tf_op jit(solution)/shard_map/ppermute | solution.py:492
  58.4 12.6 %collective-permute-start.11 = (bf16[3,1,1,96,768]{4,3,0,2,1:T(8,128)(2,1)S(1)}, bf16[3,1,1,96,768]{4,3,0,2,1:T(8,128)(2,1)S(1)}, u32[]{:S(2)}, u32[]{:S(2)}) collective-permute-start(bf16[3,1,1,96,768]{4,3,0,2,1:T(8,128)(2,1)S(1)} %maximum_bitcast_fusion), channel_id=1, source_target_pairs={{0,8},{4,12},{8,0},{12,4},{16,24},{20,28},{24,16},{28,20},{1,9},{5... | collective-permute-start | bytes 1327112 | tf_op jit(solution)/shard_map/ppermute | solution.py:492
  60.6 10.3 %collective-permute-start.15 = (bf16[3,40,768]{2,1,0:T(8,128)(2,1)S(1)}, bf16[3,40,768]{2,1,0:T(8,128)(2,1)S(1)}, u32[]{:S(2)}, u32[]{:S(2)}) collective-permute-start(bf16[3,40,768]{2,1,0:T(8,128)(2,1)S(1)} %copy-done.29), channel_id=1, source_target_pairs={{0,2},{1,3},{2,0},{3,1},{4,6},{5,7},{6,4},{7,5},{8,10},{9,11},{10,... | collective-permute-start | bytes 552968 | tf_op jit(solution)/shard_map/ppermute | solution.py:492
  71.2 21.6 %collective-permute-start.17 = (bf16[3,2,1,96,768]{4,3,0,2,1:T(8,128)(2,1)S(1)}, bf16[3,2,1,96,768]{4,3,0,2,1:T(8,128)(2,1)S(1)}, u32[]{:S(2)}, u32[]{:S(2)}) collective-permute-start(bf16[3,2,1,96,768]{4,3,0,2,1:T(8,128)(2,1)S(1)} %pad_maximum_fusion.5), channel_id=1, source_target_pairs={{0,8},{4,12},{8,0},{12,4},{16,24},{20,28},{24,16},{28,20},{1,9},{5... | collective-permute-start | bytes 2654216 | tf_op jit(solution)/shard_map/ppermute | solution.py:492
  72.2 21.1 %collective-permute-start.16 = (bf16[3,1,2,96,768]{4,3,0,2,1:T(8,128)(2,1)S(1)}, bf16[3,1,2,96,768]{4,3,0,2,1:T(8,128)(2,1)S(1)}, u32[]{:S(2)}, u32[]{:S(2)}) collective-permute-start(bf16[3,1,2,96,768]{4,3,0,2,1:T(8,128)(2,1)S(1)} %pad_maximum_fusion.4), channel_id=1, source_target_pairs={{0,16},{4,20},{8,24},{12,28},{16,0},{20,4},{24,8},{28,12},{1,17},{... | collective-permute-start | bytes 2654216 | tf_op jit(solution)/shard_map/ppermute | solution.py:492
  73.8 16.5 %collective-permute-start.18 = (bf16[3,40,768]{2,1,0:T(8,128)(2,1)S(1)}, bf16[3,40,768]{2,1,0:T(8,128)(2,1)S(1)}, u32[]{:S(2)}, u32[]{:S(2)}) collective-permute-start(bf16[3,40,768]{2,1,0:T(8,128)(2,1)S(1)} %get-tuple-element.218), channel_id=1, source_target_pairs={{0,1},{1,0},{2,3},{3,2},{4,5},{5,4},{6,7},{7,6},{8,9},{9,8},{10,11... | collective-permute-start | bytes 552968 | tf_op jit(solution)/shard_map/ppermute | solution.py:492
  73.8 16.5 %collective-permute-start.19 = (bf16[3,40,768]{2,1,0:T(8,128)(2,1)S(1)}, bf16[3,40,768]{2,1,0:T(8,128)(2,1)S(1)}, u32[]{:S(2)}, u32[]{:S(2)}) collective-permute-start(bf16[3,40,768]{2,1,0:T(8,128)(2,1)S(1)} %get-tuple-element.219), channel_id=1, source_target_pairs={{0,2},{1,3},{2,0},{3,1},{4,6},{5,7},{6,4},{7,5},{8,10},{9,11},{10,... | collective-permute-start | bytes 552968 | tf_op jit(solution)/shard_map/ppermute | solution.py:492
  76.4 13.9 %collective-permute-start.20 = (bf16[3,40,768]{2,1,0:T(8,128)(2,1)S(1)}, bf16[3,40,768]{2,1,0:T(8,128)(2,1)S(1)}, u32[]{:S(2)}, u32[]{:S(2)}) collective-permute-start(bf16[3,40,768]{2,1,0:T(8,128)(2,1)S(1)} %get-tuple-element.220), channel_id=1, source_target_pairs={{0,3},{1,2},{2,1},{3,0},{4,7},{5,6},{6,5},{7,4},{8,11},{9,10},{10,... | collective-permute-start | bytes 552968 | tf_op jit(solution)/shard_map/ppermute | solution.py:492
  120.2 10.2 %collective-permute-start.23 = (bf16[4,384,768]{2,1,0:T(8,128)(2,1)}, bf16[4,384,768]{2,1,0:T(8,128)(2,1)S(1)}, u32[]{:S(2)}, u32[]{:S(2)}) collective-permute-start(bf16[4,384,768]{2,1,0:T(8,128)(2,1)} %get-tuple-element.233), channel_id=1, source_target_pairs={{0,4},{4,0},{8,12},{12,8},{16,20},{20,16},{24,28},{28,24},{1,5},{5... | collective-permute-start | bytes 7077896 | tf_op jit(solution)/shard_map/ppermute | solution.py:492
  120.4 10.0 %collective-permute-start.24 = (bf16[4,384,768]{2,1,0:T(8,128)(2,1)}, bf16[4,384,768]{2,1,0:T(8,128)(2,1)S(1)}, u32[]{:S(2)}, u32[]{:S(2)}) collective-permute-start(bf16[4,384,768]{2,1,0:T(8,128)(2,1)} %get-tuple-element.234), channel_id=1, source_target_pairs={{0,4},{4,0},{8,12},{12,8},{16,20},{20,16},{24,28},{28,24},{1,5},{5... | collective-permute-start | bytes 7077896 | tf_op jit(solution)/shard_map/ppermute | solution.py:492
  132.4 28.2 %collective-permute-start.25 = (bf16[4,2,96,768]{3,2,1,0:T(8,128)(2,1)}, bf16[4,2,96,768]{3,2,1,0:T(8,128)(2,1)S(1)}, u32[]{:S(2)}, u32[]{:S(2)}) collective-permute-start(bf16[4,2,96,768]{3,2,1,0:T(8,128)(2,1)} %get-tuple-element.264), channel_id=1, source_target_pairs={{0,8},{4,12},{8,0},{12,4},{16,24},{20,28},{24,16},{28,20},{1,9},{5... | collective-permute-start | bytes 3538952 | tf_op jit(solution)/shard_map/ppermute | solution.py:492
  133.9 27.7 %collective-permute-start.26 = (bf16[4,2,96,768]{3,2,1,0:T(8,128)(2,1)S(1)}, bf16[4,2,96,768]{3,2,1,0:T(8,128)(2,1)S(1)}, u32[]{:S(2)}, u32[]{:S(2)}) collective-permute-start(bf16[4,2,96,768]{3,2,1,0:T(8,128)(2,1)S(1)} %get-tuple-element.265), channel_id=1, source_target_pairs={{0,16},{4,20},{8,24},{12,28},{16,0},{20,4},{24,8},{28,12},{1,17},{... | collective-permute-start | bytes 3538952 | tf_op jit(solution)/shard_map/ppermute | solution.py:492
  135.5 23.7 %collective-permute-start.27 = (bf16[3,40,768]{2,1,0:T(8,128)(2,1)S(1)}, bf16[3,40,768]{2,1,0:T(8,128)(2,1)S(1)}, u32[]{:S(2)}, u32[]{:S(2)}) collective-permute-start(bf16[3,40,768]{2,1,0:T(8,128)(2,1)S(1)} %copy-done.43), channel_id=1, source_target_pairs={{0,1},{1,0},{2,3},{3,2},{4,5},{5,4},{6,7},{7,6},{8,9},{9,8},{10,11... | collective-permute-start | bytes 552968 | tf_op jit(solution)/shard_map/ppermute | solution.py:492
  135.5 23.7 %collective-permute-start.28 = (bf16[3,40,768]{2,1,0:T(8,128)(2,1)S(1)}, bf16[3,40,768]{2,1,0:T(8,128)(2,1)S(1)}, u32[]{:S(2)}, u32[]{:S(2)}) collective-permute-start(bf16[3,40,768]{2,1,0:T(8,128)(2,1)S(1)} %copy-done.42), channel_id=1, source_target_pairs={{0,2},{1,3},{2,0},{3,1},{4,6},{5,7},{6,4},{7,5},{8,10},{9,11},{10,... | collective-permute-start | bytes 552968 | tf_op jit(solution)/shard_map/ppermute | solution.py:492
  137.8 21.4 %collective-permute-start.29 = (bf16[3,40,768]{2,1,0:T(8,128)(2,1)S(1)}, bf16[3,40,768]{2,1,0:T(8,128)(2,1)S(1)}, u32[]{:S(2)}, u32[]{:S(2)}) collective-permute-start(bf16[3,40,768]{2,1,0:T(8,128)(2,1)S(1)} %copy-done.41), channel_id=1, source_target_pairs={{0,3},{1,2},{2,1},{3,0},{4,7},{5,6},{6,5},{7,4},{8,11},{9,10},{10,... | collective-permute-start | bytes 552968 | tf_op jit(solution)/shard_map/ppermute | solution.py:492
  161.7 17.5 %collective-permute-start.32 = (bf16[2,4,192,768]{3,2,1,0:T(8,128)(2,1)}, bf16[2,4,192,768]{3,2,1,0:T(8,128)(2,1)S(1)}, u32[]{:S(2)}, u32[]{:S(2)}) collective-permute-start(bf16[2,4,192,768]{3,2,1,0:T(8,128)(2,1)} %get-tuple-element.280), channel_id=1, source_target_pairs={{0,4},{4,0},{8,12},{12,8},{16,20},{20,16},{24,28},{28,24},{1,5},{5... | collective-permute-start | bytes 7077896 | tf_op jit(solution)/shard_map/ppermute | solution.py:492
  162.1 15.8 %collective-permute-start.30 = (bf16[4,1,96,768]{3,2,1,0:T(8,128)(2,1)S(1)}, bf16[4,1,96,768]{3,2,1,0:T(8,128)(2,1)S(1)}, u32[]{:S(2)}, u32[]{:S(2)}) collective-permute-start(bf16[4,1,96,768]{3,2,1,0:T(8,128)(2,1)S(1)} %get-tuple-element.278), channel_id=1, source_target_pairs={{0,16},{4,20},{8,24},{12,28},{16,0},{20,4},{24,8},{28,12},{1,17},{... | collective-permute-start | bytes 1769480 | tf_op jit(solution)/shard_map/ppermute | solution.py:492
  163.7 15.5 %collective-permute-start.31 = (bf16[4,1,96,768]{3,2,1,0:T(8,128)(2,1)S(1)}, bf16[4,1,96,768]{3,2,1,0:T(8,128)(2,1)S(1)}, u32[]{:S(2)}, u32[]{:S(2)}) collective-permute-start(bf16[4,1,96,768]{3,2,1,0:T(8,128)(2,1)S(1)} %get-tuple-element.279), channel_id=1, source_target_pairs={{0,8},{4,12},{8,0},{12,4},{16,24},{20,28},{24,16},{28,20},{1,9},{5... | collective-permute-start | bytes 1769480 | tf_op jit(solution)/shard_map/ppermute | solution.py:492
  164.3 8.4 %collective-permute-start.33 = (bf16[3,40,768]{2,1,0:T(8,128)(2,1)S(1)}, bf16[3,40,768]{2,1,0:T(8,128)(2,1)S(1)}, u32[]{:S(2)}, u32[]{:S(2)}) collective-permute-start(bf16[3,40,768]{2,1,0:T(8,128)(2,1)S(1)} %copy-done.44), channel_id=1, source_target_pairs={{0,3},{1,2},{2,1},{3,0},{4,7},{5,6},{6,5},{7,4},{8,11},{9,10},{10,... | collective-permute-start | bytes 552968 | tf_op jit(solution)/shard_map/ppermute | solution.py:492
  180.1 18.7 %collective-permute-start.36 = (bf16[2,192,768]{2,1,0:T(8,128)(2,1)S(1)}, bf16[2,192,768]{2,1,0:T(8,128)(2,1)S(1)}, u32[]{:S(2)}, u32[]{:S(2)}) collective-permute-start(bf16[2,192,768]{2,1,0:T(8,128)(2,1)S(1)} %pad_maximum_fusion.9), channel_id=1, source_target_pairs={{0,1},{1,0},{2,3},{3,2},{4,5},{5,4},{6,7},{7,6},{8,9},{9,8},{10,11... | collective-permute-start | bytes 1769480 | tf_op jit(solution)/shard_map/ppermute | solution.py:492
  182.6 16.1 %collective-permute-start.34 = (bf16[4,2,48,768]{3,2,1,0:T(8,128)(2,1)S(1)}, bf16[4,2,48,768]{3,2,1,0:T(8,128)(2,1)S(1)}, u32[]{:S(2)}, u32[]{:S(2)}) collective-permute-start(bf16[4,2,48,768]{3,2,1,0:T(8,128)(2,1)S(1)} %get-tuple-element.287), channel_id=1, source_target_pairs={{0,8},{4,12},{8,0},{12,4},{16,24},{20,28},{24,16},{28,20},{1,9},{5... | collective-permute-start | bytes 1769480 | tf_op jit(solution)/shard_map/ppermute | solution.py:492
  183.2 15.5 %collective-permute-start.35 = (bf16[4,2,48,768]{3,2,1,0:T(8,128)(2,1)S(1)}, bf16[4,2,48,768]{3,2,1,0:T(8,128)(2,1)S(1)}, u32[]{:S(2)}, u32[]{:S(2)}) collective-permute-start(bf16[4,2,48,768]{3,2,1,0:T(8,128)(2,1)S(1)} %get-tuple-element.288), channel_id=1, source_target_pairs={{0,16},{4,20},{8,24},{12,28},{16,0},{20,4},{24,8},{28,12},{1,17},{... | collective-permute-start | bytes 1769480 | tf_op jit(solution)/shard_map/ppermute | solution.py:492
  183.7 12.8 %collective-permute-start.38 = (bf16[3,40,768]{2,1,0:T(8,128)(2,1)S(1)}, bf16[3,40,768]{2,1,0:T(8,128)(2,1)S(1)}, u32[]{:S(2)}, u32[]{:S(2)}) collective-permute-start(bf16[3,40,768]{2,1,0:T(8,128)(2,1)S(1)} %copy-done.40), channel_id=1, source_target_pairs={{0,2},{1,3},{2,0},{3,1},{4,6},{5,7},{6,4},{7,5},{8,10},{9,11},{10,... | collective-permute-start | bytes 552968 | tf_op jit(solution)/shard_map/ppermute | solution.py:492
  198.8 14.7 %collective-permute-start.41 = (bf16[192,768]{1,0:T(8,128)(2,1)S(1)}, bf16[192,768]{1,0:T(8,128)(2,1)S(1)}, u32[]{:S(2)}, u32[]{:S(2)}) collective-permute-start(bf16[192,768]{1,0:T(8,128)(2,1)S(1)} %fusion.1), channel_id=1, source_target_pairs={{0,2},{1,3},{2,0},{3,1},{4,6},{5,7},{6,4},{7,5},{8,10},{9,11},{10,... | collective-permute-start | bytes 884744 | tf_op jit(solution)/shard_map/ppermute | solution.py:492
  200.3 13.2 %collective-permute-start.39 = (bf16[4,1,48,768]{3,2,1,0:T(8,128)(2,1)S(1)}, bf16[4,1,48,768]{3,2,1,0:T(8,128)(2,1)S(1)}, u32[]{:S(2)}, u32[]{:S(2)}) collective-permute-start(bf16[4,1,48,768]{3,2,1,0:T(8,128)(2,1)S(1)} %get-tuple-element.308), channel_id=1, source_target_pairs={{0,16},{4,20},{8,24},{12,28},{16,0},{20,4},{24,8},{28,12},{1,17},{... | collective-permute-start | bytes 884744 | tf_op jit(solution)/shard_map/ppermute | solution.py:492
  201.0 12.6 %collective-permute-start.40 = (bf16[4,1,48,768]{3,2,1,0:T(8,128)(2,1)S(1)}, bf16[4,1,48,768]{3,2,1,0:T(8,128)(2,1)S(1)}, u32[]{:S(2)}, u32[]{:S(2)}) collective-permute-start(bf16[4,1,48,768]{3,2,1,0:T(8,128)(2,1)S(1)} %get-tuple-element.309), channel_id=1, source_target_pairs={{0,8},{4,12},{8,0},{12,4},{16,24},{20,28},{24,16},{28,20},{1,9},{5... | collective-permute-start | bytes 884744 | tf_op jit(solution)/shard_map/ppermute | solution.py:492
  201.5 8.3 %collective-permute-start.42 = (bf16[3,40,768]{2,1,0:T(8,128)(2,1)S(1)}, bf16[3,40,768]{2,1,0:T(8,128)(2,1)S(1)}, u32[]{:S(2)}, u32[]{:S(2)}) collective-permute-start(bf16[3,40,768]{2,1,0:T(8,128)(2,1)S(1)} %copy-done.39), channel_id=1, source_target_pairs={{0,1},{1,0},{2,3},{3,2},{4,5},{5,4},{6,7},{7,6},{8,9},{9,8},{10,11... | collective-permute-start | bytes 552968 | tf_op jit(solution)/shard_map/ppermute | solution.py:492
  202.6 7.2 %collective-permute-start.43 = (f32[24,768]{1,0:T(8,128)S(1)}, f32[24,768]{1,0:T(8,128)S(1)}, u32[]{:S(2)}, u32[]{:S(2)}) collective-permute-start(f32[24,768]{1,0:T(8,128)S(1)} %add.148), channel_id=1, source_target_pairs={{0,8},{4,12},{8,0},{12,4},{16,24},{20,28},{24,16},{28,20},{1,9},{5... | collective-permute-start | bytes 221192 | tf_op jit(solution)/shard_map/ppermute | solution.py:492
  214.1 8.6 %collective-permute-start.46 = (bf16[2,96,768]{2,1,0:T(8,128)(2,1)S(1)}, bf16[2,96,768]{2,1,0:T(8,128)(2,1)S(1)}, u32[]{:S(2)}, u32[]{:S(2)}) collective-permute-start(bf16[2,96,768]{2,1,0:T(8,128)(2,1)S(1)} %pad_maximum_fusion.15), channel_id=1, source_target_pairs={{0,1},{1,0},{2,3},{3,2},{4,5},{5,4},{6,7},{7,6},{8,9},{9,8},{10,11... | collective-permute-start | bytes 884744 | tf_op jit(solution)/shard_map/ppermute | solution.py:492
  214.2 7.4 %collective-permute-start.44 = (bf16[1,1,1,96,768]{4,3,2,1,0:T(8,128)(2,1)S(1)}, bf16[1,1,1,96,768]{4,3,2,1,0:T(8,128)(2,1)S(1)}, u32[]{:S(2)}, u32[]{:S(2)}) collective-permute-start(bf16[1,1,1,96,768]{4,3,2,1,0:T(8,128)(2,1)S(1)} %get-tuple-element.319), channel_id=1, source_target_pairs={{0,8},{4,12},{8,0},{12,4},{16,24},{20,28},{24,16},{28,20},{1,9},{5... | collective-permute-start | bytes 442376 | tf_op jit(solution)/shard_map/ppermute | solution.py:492
  222.8 9.3 %collective-permute-start.49 = (bf16[1,2,1,96,768]{4,3,2,1,0:T(8,128)(2,1)S(1)}, bf16[1,2,1,96,768]{4,3,2,1,0:T(8,128)(2,1)S(1)}, u32[]{:S(2)}, u32[]{:S(2)}) collective-permute-start(bf16[1,2,1,96,768]{4,3,2,1,0:T(8,128)(2,1)S(1)} %pad_maximum_fusion.18), channel_id=1, source_target_pairs={{0,8},{4,12},{8,0},{12,4},{16,24},{20,28},{24,16},{28,20},{1,9},{5... | collective-permute-start | bytes 884744 | tf_op jit(solution)/shard_map/ppermute | solution.py:492
  223.6 8.5 %collective-permute-start.48 = (bf16[1,1,2,96,768]{4,3,2,1,0:T(8,128)(2,1)S(1)}, bf16[1,1,2,96,768]{4,3,2,1,0:T(8,128)(2,1)S(1)}, u32[]{:S(2)}, u32[]{:S(2)}) collective-permute-start(bf16[1,1,2,96,768]{4,3,2,1,0:T(8,128)(2,1)S(1)} %pad_maximum_fusion.17), channel_id=1, source_target_pairs={{0,16},{4,20},{8,24},{12,28},{16,0},{20,4},{24,8},{28,12},{1,17},{... | collective-permute-start | bytes 884744 | tf_op jit(solution)/shard_map/ppermute | solution.py:492
  224.4 7.7 %collective-permute-start.50 = (bf16[96,768]{1,0:T(8,128)(2,1)S(1)}, bf16[96,768]{1,0:T(8,128)(2,1)S(1)}, u32[]{:S(2)}, u32[]{:S(2)}) collective-permute-start(bf16[96,768]{1,0:T(8,128)(2,1)S(1)} %fusion.3), channel_id=1, source_target_pairs={{0,2},{1,3},{2,0},{3,1},{4,6},{5,7},{6,4},{7,5},{8,10},{9,11},{10,... | collective-permute-start | bytes 442376 | tf_op jit(solution)/shard_map/ppermute | solution.py:492
  239.1 7.4 %collective-permute-start.57 = (bf16[2,48,768]{2,1,0:T(8,128)(2,1)S(1)}, bf16[2,48,768]{2,1,0:T(8,128)(2,1)S(1)}, u32[]{:S(2)}, u32[]{:S(2)}) collective-permute-start(bf16[2,48,768]{2,1,0:T(8,128)(2,1)S(1)} %pad_maximum_fusion.23), channel_id=1, source_target_pairs={{0,8},{4,12},{8,0},{12,4},{16,24},{20,28},{24,16},{28,20},{1,9},{5... | collective-permute-start | bytes 442376 | tf_op jit(solution)/shard_map/ppermute | solution.py:492
  239.6 6.9 %collective-permute-start.56 = (bf16[2,48,768]{2,1,0:T(8,128)(2,1)S(1)}, bf16[2,48,768]{2,1,0:T(8,128)(2,1)S(1)}, u32[]{:S(2)}, u32[]{:S(2)}) collective-permute-start(bf16[2,48,768]{2,1,0:T(8,128)(2,1)S(1)} %pad_maximum_fusion.22), channel_id=1, source_target_pairs={{0,16},{4,20},{8,24},{12,28},{16,0},{20,4},{24,8},{28,12},{1,17},{... | collective-permute-start | bytes 442376 | tf_op jit(solution)/shard_map/ppermute | solution.py:492
  (58 other events, 457.3 us)

commit v6 on v5

--- a/solution.py
+++ b/solution.py
@@ -210,16 +210,19 @@
             slope_ref[slot, :, first:last] = share + pre_act * (DENSITY * jnp.exp(-0.5 * pre_act * pre_act))
             term = dot(act, down_rows(slot, first, last), 1, 0)
             branch = term if branch is None else branch + term
-        if slot == 0:
+        if slot == 1:
             total_ref[...] = branch
         else:
             total_ref[...] += branch
 
-    first_copies = start((low_hbm, low_ref), (w_in_hbm, w_in_ref), (w_down_hbm, w_down_ref))
+    low_copies = start((low_hbm, low_ref))
+    own_copies = start((w_in_hbm, w_in_ref), (w_down_hbm, w_down_ref))
     later_copies = start((normed_hbm, normed_ref), *[(cot_hbm[k], cot_ref.at[k]) for k in range(count)])
-    wait(first_copies)
-    for slot in range(count):
+    wait(low_copies)
+    for slot in range(1, count):
         forward(slot)
+    wait(own_copies)
+    forward(0)
     wait(later_copies)
 
     hidden = normed_ref[...] * vectors_ref[1:2] + vectors_ref[2:3]
@@ -307,10 +310,10 @@
     def _():
         total_ref[...] = delta_ref[...]
         sums_ref[...] = jnp.zeros_like(sums_ref)
-        sums_ref[0:8] = sums_one_ref[...]
-        sums_ref[8:16] = sums_two_ref[...]
+        sums_ref[0:3] = sums_one_ref[0:3]
+        sums_ref[3:6] = sums_two_ref[0:3]
         for j in range(shards_):
-            sums_ref[16 + j : 17 + j] = sum_in_ref[j]
+            sums_ref[6 + j : 7 + j] = sum_in_ref[j]
 
     core = here_ref[0]
     cols = q_ref.shape[2]
@@ -336,7 +339,7 @@
         key_grad = dot(score_grad, head_stack(q_ref[0, rows], heads), 0, 0)
         dk_ref[rows] = (key_grad * scale).astype(BF16)
     dq, dk, dv = dq_ref[...], dk_ref[...], dv_ref[...]
-    row = pl.ds(16 + shards_ + (step ^ here_ref[1]), 1)
+    row = pl.ds(6 + shards_ + (step ^ here_ref[1]), 1)
     sums_ref[row, :cols] = column_sum(dq.astype(F32))
     sums_ref[row, 2 * cols : 3 * cols] = column_sum(dv.astype(F32))
     grad_q = dot(dq, x, 0, 0).astype(BF16)
@@ -366,21 +369,22 @@
         out_ref[pl.ds((here_ref[1] ^ k) * pairs, pairs)] = ref[...].astype(out_ref.dtype)
 
 
-def head_grads_kernel(indices, here_ref, qk_mine, vo_mine, qk_other, vo_other, grad_qkv_ref, grad_out_ref):
-    core, place_here = here_ref[0], here_ref[2]
-    for side, qk_ref, vo_ref in ((core, qk_mine, vo_mine), (1 - core, qk_other, vo_other)):
-        for k, (qk_index, vo_index) in enumerate(zip(*indices)):
-            grad_qkv_ref[side, place_here ^ qk_index] = qk_ref[k].astype(F32)
-            place = place_here ^ vo_index
-            piece = vo_ref[k].astype(F32)
+def head_grads_kernel(order, here_ref, mine_ref, other_ref, grad_qkv_ref, grad_out_ref):
+    core = here_ref[0]
+    part = grad_out_ref.shape[1]
+    for side, ref in ((core, mine_ref), (1 - core, other_ref)):
+        for k, index in enumerate(order):
+            place = here_ref[2] ^ index
+            piece = ref[k].astype(F32)
+            grad_qkv_ref[side, place] = piece[:part]
 
             @pl.when(side == 0)
             def _():
-                grad_qkv_ref[2, place] = piece
+                grad_qkv_ref[2, place] = piece[part:]
 
             @pl.when(side != 0)
             def _():
-                grad_out_ref[place] = piece
+                grad_out_ref[place] = piece[part:]
 
 
 def unit_grads_kernel(here_ref, in_ref, down_ref, in_other, down_other, grad_in_ref, grad_down_ref):
@@ -401,12 +405,6 @@
     return pl.BlockSpec((1,) + array.shape[1:], lambda s, *_: (s,) + (0,) * (len(array.shape) - 1))
 
 
-def in_place(array):
-    if array.size * array.dtype.itemsize < MIB:
-        return array
-    return pltpu.with_memory_space_constraint(array, pltpu.HBM)
-
-
 def where_it_is(array):
     return pl.BlockSpec(memory_space=pl.ANY)
 
@@ -435,6 +433,12 @@
 
 def shape(dims, dtype):
     return jax.ShapeDtypeStruct(dims, dtype)
+
+
+def in_place(array):
+    if array.size * array.dtype.itemsize < MIB:
+        return array
+    return pltpu.with_memory_space_constraint(array, pltpu.HBM)
 
 
 def add_kernel(counts, *refs):
@@ -572,22 +576,15 @@
         return [a[:, 0] for a in sums]
 
 
-class Pieces:
-    def __init__(self, pair):
-        self.bits, self.orders = outer_bits()
-        self.steps = len(self.bits)
-        self.held = [p[None] for p in pair]
-        self.indices = [[0], [0]]
-
-    def send(self, step):
-        return [flip(h, "dp", 1 << order[step]) for h, order in zip(self.held, self.orders)]
-
-    def take(self, step, got):
-        self.held = [jnp.concatenate([h, g]) for h, g in zip(self.held, got)]
-        self.indices = [
-            index + [i ^ (1 << (order[step] - 1)) for i in index]
-            for index, order in zip(self.indices, self.orders)
-        ]
+def gather_stack(piece):
+    bits, _ = outer_bits()
+    order = list(range(1 << len(bits)))
+    if len(order) <= 4:
+        return [piece] + [flip(piece, "dp", 2 * k) for k in order[1:]], order
+    held = piece[None]
+    for bit in bits:
+        held = jnp.concatenate([held, flip(held, "dp", 1 << bit)])
+    return [held[k] for k in order], order
 
 
 def add_parts(*parts):
@@ -833,6 +830,7 @@
         [(whole, rows_shape), (whole, low_shape), (whole, sums_shape)],
         [pltpu.VMEM((rows, width), F32)],
         here,
+        (0,),
     )
     in_got, down_got, out_blocks, attn_low = tie(in_got, down_got, out_blocks, attn_low)
     ffn = Reduce([in_keep, down_keep], [in_got, down_got])
@@ -867,7 +865,7 @@
                 pl.BlockSpec((2, 1, cols, width), lambda s, h: (0, s, 0, 0)),
                 shape((2, mp, cols, width), BF16),
             ),
-            (whole, shape((16 + 2 * mp, width), F32)),
+            (whole, shape((-(-(6 + 2 * mp) // 8) * 8, width), F32)),
             *[(whole, block_shape)] * mp,
         ],
         [pltpu.VMEM((rows, cols), BF16)] * 3 + [pltpu.VMEM((rows, width), F32)],
@@ -884,7 +882,9 @@
         if step == 1:
             att_got = flip(att_send, "dp", 1)
             row_three = flip(row_sends[3], "mp", 3)
-        got, att_got, row_three, row_sends = tie(got, att_got, row_three, row_sends)
+            sums_got = flip(sums, "mp", 2)
+        got, att_got, row_three, sums_got, row_sends = tie(got, att_got, row_three, sums_got, row_sends)
+    sums = sums + sums_got
     place = lambda blocks, dtype: call(
         partial(place_kernel, pairs),
         1,
@@ -904,7 +904,7 @@
     ffn_odd, ffn_even, sums = tie(ffn_odd, ffn_even, sums)
     got = att.send(0, att.pack(0))
     ffn_got = flip(ffn_odd, "mp", 1)
-    sums_got = flip(sums, "dp", 1)
+    sums_got = flip(sums, "dp", 2)
     row_two = flip(row_sends[2], "mp", 2)
     got, ffn_got, sums_got, row_two, row_sends, layer_out = tie(
         got, ffn_got, sums_got, row_two, row_sends, layer_out
@@ -920,7 +920,7 @@
         if step == 1:
             ffn_last = flip(ffn_two, "mp", 2)
             row_one = flip(row_sends[1], "mp", 1)
-            sums_got = flip(sums, "dp", 2)
+            sums_got = flip(sums, "dp", dp // 2)
         got, ffn_last, row_one, sums_got, row_sends = tie(got, ffn_last, row_one, sums_got, row_sends)
     att.take(got)
     sums = sums + sums_got
@@ -932,7 +932,7 @@
     ffn.held, att_odd, att_even, sums = tie(ffn.held, att_odd, att_even, sums)
     got = ffn.send(0)
     att_got = flip(att_odd, "mp", 1)
-    sums_got = flip(sums, "dp", dp // 2)
+    sums_got = flip(sums, "dp", 1)
     got, att_got, sums_got, row_one = tie(got, att_got, sums_got, row_one)
     grad_input = place([row_sends[0], row_one, row_two, row_three], F32)
     sums = sums + sums_got
@@ -949,16 +949,7 @@
     att_sum = add_parts(att_even[0], att_got[0], att_last)
     ffn_halves = ffn.halves()
     core_got = [flip(h, "dp", 1) for h in ffn_halves]
-    att = Pieces([att_sum[:att_part], att_sum[att_part:]])
-    got = att.send(0)
-    core_got, got, sums = tie(core_got, got, sums)
-    for step in range(1, att.steps):
-        att.take(step - 1, got)
-        got = att.send(step)
-        if step == 1:
-            sums_got = flip(sums, "mp", 2)
-        if step < att.steps - 1:
-            got = tie(*got)
+    att_mine, att_order = gather_stack(att_sum)
     grad_in, grad_down = call(
         unit_grads_kernel,
         1,
@@ -969,16 +960,15 @@
         [],
         here,
     )
-    grad_in, grad_down, got, sums_got = tie(grad_in, grad_down, got, sums_got)
-    sums = sums + sums_got
-    att.take(att.steps - 1, got)
-    core_got = [flip(h, "dp", 1) for h in att.held]
+    att_mine, grad_in, grad_down, sums = tie(att_mine, grad_in, grad_down, sums)
+    att_mine = jnp.stack(att_mine)
+    att_other = flip(att_mine, "dp", 1)
     grad_qkv, grad_out = call(
-        partial(head_grads_kernel, att.indices),
+        partial(head_grads_kernel, att_order),
         1,
         "head_grads",
         24,
-        [(whole, a) for a in att.held + core_got],
+        [(whole, att_mine), (whole, att_other)],
         [
             (whole, shape((3, cols // att_part, att_part, width), F32)),
             (whole, shape((cols // att_part, att_part, width), F32)),
@@ -986,8 +976,8 @@
         [],
         here,
     )
-    sum_in_bias = lax.dynamic_index_in_dim(sums, 16 + mi, 0, keepdims=False)
-    sum_qv = lax.dynamic_index_in_dim(sums, 16 + mp + mi, 0, keepdims=False)
+    sum_in_bias = lax.dynamic_index_in_dim(sums, 6 + mi, 0, keepdims=False)
+    sum_qv = lax.dynamic_index_in_dim(sums, 6 + mp + mi, 0, keepdims=False)
     sum_qv = jnp.stack([sum_qv[:cols], sum_qv[2 * cols : 3 * cols]])
     return (
         layer_out,
@@ -1001,9 +991,9 @@
         grad_in,
         sum_in_bias,
         grad_down,
-        sums[10],
-        sums[8],
-        sums[9],
+        sums[5],
+        sums[3],
+        sums[4],
     )
 
 

time: 251 us -> 248 us (0.988)
    ppermute x61 -> x59, starting transfers between devices: 57.9 us -> 55.8 us  [flip(): return lax.ppermute(array, axis, [(i, i ^ mask) for i in range(size)])]
    ppermute x61 -> x59, waiting for transfers between devices: 102 us -> 101 us  [flip(): return lax.ppermute(array, axis, [(i, i ^ mask) for i in range(size)])]
  transfers between devices with their start and end apart: 61 -> 59, of which waited for: 27 -> 28; matrix products, arithmetic and copies ran while one was open for 4% -> 4% of each run, Pallas kernels for 19% -> 20%
where the time goes in v6:
time: 248 us; the launch traced here: 247 us
  waiting for transfers between devices  101 us (41%)
  Pallas kernels  73.6 us (30%)
  starting transfers between devices  55.8 us (22%)
  local copies, waits for them, and re-layouts  10.4 us (4%)
  other arithmetic  4.58 us (2%)
    ppermute x59, waiting for transfers between devices, flip(): return lax.ppermute(array, axis, [(i, i ^ mask) for i in range(size)])  101 us
    pallas_call x8, Pallas kernels, call(): pl.pallas_call(kernel, grid_spec=spec, out_shape=[pltpu.HBM(a.shape, a.dt...  69.2 us
    ppermute x59, starting transfers between devices, flip(): return lax.ppermute(array, axis, [(i, i ^ mask) for i in range(size)])  55.8 us
  transfers between devices with their start and end apart: 59, of which 28 were waited for; matrix products, arithmetic and copies ran while one was open for 4% of the time, Pallas kernels for 20%

profile of v6, /device:TPU:0, one launch (start us, length us, event | category | flops | bytes accessed | tf_op | source)
XLA Modules:
  0.0 247.4 jit_solution(11221616854512799788)
XLA Ops:
  1.8 3.1 %collective-permute-start = (bf16[96,768]{1,0:T(8,128)(2,1)S(1)}, bf16[96,768]{1,0:T(8,128)(2,1)S(1)}, u32[]{:S(2)}, u32[]{:S(2)}) collective-permute-start(bf16[96,768]{1,0:T(8,128)(2,1)S(1)} %pad_maximum_fusion.20), channel_id=1, source_target_pairs={{0,1},{1,0},{2,3},{3,2},{4,5},{5,4},{6,7},{7,6},{8,9},{9,8},{10,11... | collective-permute-start | bytes 442376 | tf_op jit(solution)/shard_map/ppermute | solution.py:496
  4.9 2.6 %collective-permute-start.1 = (bf16[96,768]{1,0:T(8,128)(2,1)S(1)}, bf16[96,768]{1,0:T(8,128)(2,1)}, u32[]{:S(2)}, u32[]{:S(2)}) collective-permute-start(bf16[96,768]{1,0:T(8,128)(2,1)S(1)} %pad_maximum_fusion.20), channel_id=1, source_target_pairs={{0,2},{1,3},{2,0},{3,1},{4,6},{5,7},{6,4},{7,5},{8,10},{9,11},{10,... | collective-permute-start | bytes 442376 | tf_op jit(solution)/shard_map/ppermute | solution.py:496
  13.7 5.3 %collective-permute-done.1 = bf16[96,768]{1,0:T(8,128)(2,1)} collective-permute-done((bf16[96,768]{1,0:T(8,128)(2,1)S(1)}, bf16[96,768]{1,0:T(8,128)(2,1)}, u32[]{:S(2)}, u32[]{:S(2)}) %collective-permute-start.1) | collective-permute-done | bytes 147488 | tf_op jit(solution)/shard_map/ppermute | solution.py:496
  20.1 1.6 collective-permute-start.5
  21.7 3.3 %collective-permute-start.3 = (bf16[200,768]{1,0:T(8,128)(2,1)S(1)}, bf16[200,768]{1,0:T(8,128)(2,1)S(1)}, u32[]{:S(2)}, u32[]{:S(2)}) collective-permute-start(bf16[200,768]{1,0:T(8,128)(2,1)S(1)} %concatenate.65), channel_id=1, source_target_pairs={{0,2},{1,3},{2,0},{3,1},{4,6},{5,7},{6,4},{7,5},{8,10},{9,11},{10,... | collective-permute-start | bytes 921608 | tf_op jit(solution)/shard_map/ppermute | solution.py:496
  25.0 1.6 collective-permute-start.4
  26.5 7.8 %collective-permute-done.6 = bf16[3,40,768]{2,1,0:T(8,128)(2,1)S(1)} collective-permute-done((bf16[3,40,768]{2,1,0:T(8,128)(2,1)}, bf16[3,40,768]{2,1,0:T(8,128)(2,1)S(1)}, u32[]{:S(2)}, u32[]{:S(2)}) %collective-permute-start.6) | collective-permute-done | bytes 184352 | tf_op jit(solution)/shard_map/ppermute | solution.py:496
  34.4 3.2 %collective-permute-done.3 = bf16[200,768]{1,0:T(8,128)(2,1)S(1)} collective-permute-done((bf16[200,768]{1,0:T(8,128)(2,1)S(1)}, bf16[200,768]{1,0:T(8,128)(2,1)S(1)}, u32[]{:S(2)}, u32[]{:S(2)}) %collective-permute-start.3) | collective-permute-done | bytes 307232 | tf_op jit(solution)/shard_map/ppermute | solution.py:496
  37.8 1.6 collective-permute-start.8
  41.4 14.1 %collective-permute-done.10 = bf16[3,40,768]{2,1,0:T(8,128)(2,1)S(1)} collective-permute-done((bf16[3,40,768]{2,1,0:T(8,128)(2,1)S(1)}, bf16[3,40,768]{2,1,0:T(8,128)(2,1)S(1)}, u32[]{:S(2)}, u32[]{:S(2)}) %collective-permute-start.10) | collective-permute-done | bytes 184352 | tf_op jit(solution)/shard_map/ppermute | solution.py:496
  58.4 1.6 collective-permute-start.11
  60.7 10.3 %collective-permute-done.15 = bf16[3,40,768]{2,1,0:T(8,128)(2,1)S(1)} collective-permute-done((bf16[3,40,768]{2,1,0:T(8,128)(2,1)S(1)}, bf16[3,40,768]{2,1,0:T(8,128)(2,1)S(1)}, u32[]{:S(2)}, u32[]{:S(2)}) %collective-permute-start.15) | collective-permute-done | bytes 184352 | tf_op jit(solution)/shard_map/ppermute | solution.py:496
  72.2 1.6 collective-permute-start.16
  73.8 2.7 %collective-permute-start.19 = (bf16[3,40,768]{2,1,0:T(8,128)(2,1)S(1)}, bf16[3,40,768]{2,1,0:T(8,128)(2,1)S(1)}, u32[]{:S(2)}, u32[]{:S(2)}) collective-permute-start(bf16[3,40,768]{2,1,0:T(8,128)(2,1)S(1)} %get-tuple-element.217), channel_id=1, source_target_pairs={{0,2},{1,3},{2,0},{3,1},{4,6},{5,7},{6,4},{7,5},{8,10},{9,11},{10,... | collective-permute-start | bytes 552968 | tf_op jit(solution)/shard_map/ppermute | solution.py:496
  76.4 1.7 collective-permute-start.20
  78.3 12.0 %attention.1 = (bf16[4,480,192]{2,1,0:T(8,128)(2,1)}, bf16[4,480,192]{2,1,0:T(8,128)(2,1)}, bf16[4,480,192]{2,1,0:T(8,128)(2,1)}, f32[4,3,480,160]{3,2,1,0:T(8,1...) custom-call(s32[3]{0:T(128)S(1)} %pad_add_fusion.here_ref, ...), custom_call_target="tpu_custom_call" | custom-call | tf_op jit(solution)/shard_map/attention/pallas_call | solution.py:424
  90.3 2.5 %collective-permute-done.17 = bf16[3,2,1,96,768]{4,3,0,2,1:T(8,128)(2,1)S(1)} collective-permute-done((bf16[3,2,1,96,768]{4,3,0,2,1:T(8,128)(2,1)S(1)}, bf16[3,2,1,96,768]{4,3,0,2,1:T(8,128)(2,1)S(1)}, u32[]{:S(2)}, u32[]{:S(2)}) %collective-permute-start.17) | collective-permute-done | bytes 884768 | tf_op jit(solution)/shard_map/ppermute | solution.py:496
  94.8 2.7 %collective-permute-done.22.down_two = bf16[3,384,768]{2,1,0:T(8,128)(2,1)S(1)} collective-permute-done((bf16[3,384,768]{2,1,0:T(8,128)(2,1)S(1)}, bf16[3,384,768]{2,1,0:T(8,128)(2,1)S(1)}, u32[]{:S(2)}, u32[]{:S(2)}) %collective-permute-start.22) | collective-permute-done | bytes 1769504 | tf_op jit(solution)/shard_map/ppermute | solution.py:496
  97.5 2.5 %collective-permute-done.21.in_two = bf16[3,384,768]{2,1,0:T(8,128)(2,1)S(1)} collective-permute-done((bf16[3,384,768]{2,1,0:T(8,128)(2,1)S(1)}, bf16[3,384,768]{2,1,0:T(8,128)(2,1)S(1)}, u32[]{:S(2)}, u32[]{:S(2)}) %collective-permute-start.21) | collective-permute-done | bytes 1769504 | tf_op jit(solution)/shard_map/ppermute | solution.py:496
  100.0 19.9 %ffn.1 = (bf16[3,40,768]{2,1,0:T(8,128)(2,1)}, bf16[3,40,768]{2,1,0:T(8,128)(2,1)}, bf16[3,40,768]{2,1,0:T(8,128)(2,1)}, bf16[3,40,768]{2,1,0:T(8,128)(2,1)}, f3...) custom-call(s32[3]{0:T(128)S(1)} %pad_add_fusion.here_ref, ...), custom_call_target="tpu_custom_call" | custom-call | tf_op jit(solution)/shard_map/ffn/pallas_call | solution.py:424
  120.5 9.6 %ffn_back.1 = (f32[480,768]{1,0:T(8,128)}, bf16[480,768]{1,0:T(8,128)(2,1)S(1)}, f32[8,768]{1,0:T(8,128)S(1)}) custom-call(s32[3]{0:T(128)S(1)} %pad_add_fusion.here_ref, bf16[4,480,768]{2,1,0:T(8,128)(2,1)} %get-tuple-element.237.pre_grad_ref, bf16[768,768]{1,0:T(8,128)(2,1)} %own_in_two.1, bf16[768,768]{1,0:T(8,128)(2,1)} %own_in_two.1, ...), custom_call_target="tpu_custom_call" | custom-call | tf_op jit(solution)/shard_map/ffn_back/pallas_call | solution.py:424
  130.3 1.9 add.189
  132.1 1.5 collective-permute-start.25
  133.6 1.5 collective-permute-start.26
  135.2 2.3 collective-permute-start.28
  137.4 2.1 collective-permute-start.29
  139.6 19.2 %attention_back.1 = (bf16[4,192,768]{2,1,0:T(8,128)(2,1)}, bf16[4,192,768]{2,1,0:T(8,128)(2,1)}, bf16[2,4,192,768]{3,2,1,0:T(8,128)(2,1)}, f32[16,768]{1,0:T(8,1...) custom-call(s32[3]{0:T(128)S(1)} %pad_add_fusion.here_ref, ...), custom_call_target="tpu_custom_call" | custom-call | tf_op jit(solution)/shard_map/attention_back/pallas_call | solution.py:424
  158.8 1.6 collective-permute-done.25.refs_3_
  161.8 1.6 collective-permute-start.30
  163.9 1.7 collective-permute-start.33
  165.7 9.2 %collective-permute-done.34 = f32[16,768]{1,0:T(8,128)S(1)} collective-permute-done((f32[16,768]{1,0:T(8,128)S(1)}, f32[16,768]{1,0:T(8,128)S(1)}, u32[]{:S(2)}, u32[]{:S(2)}) %collective-permute-start.34) | collective-permute-done | bytes 49184 | tf_op jit(solution)/shard_map/ppermute | solution.py:496
  174.8 2.8 %collective-permute-done.30.refs_4_ = bf16[4,1,96,768]{3,2,1,0:T(8,128)(2,1)S(1)} collective-permute-done((bf16[4,1,96,768]{3,2,1,0:T(8,128)(2,1)S(1)}, bf16[4,1,96,768]{3,2,1,0:T(8,128)(2,1)S(1)}, u32[]{:S(2)}, u32[]{:S(2)}) %collective-permute-start.30) | collective-permute-done | bytes 589856 | tf_op jit(solution)/shard_map/ppermute | solution.py:496
  184.4 1.5 collective-permute-start.38
  185.9 1.5 place.2
  187.3 10.7 %collective-permute-done.38 = f32[16,768]{1,0:T(8,128)S(1)} collective-permute-done((f32[16,768]{1,0:T(8,128)S(1)}, f32[16,768]{1,0:T(8,128)S(1)}, u32[]{:S(2)}, u32[]{:S(2)}) %collective-permute-start.38) | collective-permute-done | bytes 49184 | tf_op jit(solution)/shard_map/ppermute | solution.py:496
  202.3 1.4 collective-permute-start.44
  203.7 4.8 %collective-permute-done.44 = f32[16,768]{1,0:T(8,128)S(1)} collective-permute-done((f32[16,768]{1,0:T(8,128)S(1)}, f32[16,768]{1,0:T(8,128)S(1)}, u32[]{:S(2)}, u32[]{:S(2)}) %collective-permute-start.44) | collective-permute-done | bytes 49184 | tf_op jit(solution)/shard_map/ppermute | solution.py:496
  209.0 4.2 %collective-permute-done.42 = bf16[192,768]{1,0:T(8,128)(2,1)S(1)} collective-permute-done((bf16[192,768]{1,0:T(8,128)(2,1)S(1)}, bf16[192,768]{1,0:T(8,128)(2,1)S(1)}, u32[]{:S(2)}, u32[]{:S(2)}) %collective-permute-start.42) | collective-permute-done | bytes 294944 | tf_op jit(solution)/shard_map/ppermute | solution.py:496
  217.0 2.4 collective-permute-done.45
  219.8 2.7 %collective-permute-done.47 = bf16[2,96,768]{2,1,0:T(8,128)(2,1)S(1)} collective-permute-done((bf16[2,96,768]{2,1,0:T(8,128)(2,1)S(1)}, bf16[2,96,768]{2,1,0:T(8,128)(2,1)S(1)}, u32[]{:S(2)}, u32[]{:S(2)}) %collective-permute-start.47) | collective-permute-done | bytes 294944 | tf_op jit(solution)/shard_map/ppermute | solution.py:496
  224.4 1.6 collective-permute-start.52
  226.0 1.7 place.3
  228.9 2.8 %collective-permute-done.51 = bf16[96,768]{1,0:T(8,128)(2,1)S(1)} collective-permute-done((bf16[96,768]{1,0:T(8,128)(2,1)S(1)}, bf16[96,768]{1,0:T(8,128)(2,1)S(1)}, u32[]{:S(2)}, u32[]{:S(2)}) %collective-permute-start.51) | collective-permute-done | bytes 147488 | tf_op jit(solution)/shard_map/ppermute | solution.py:496
  232.7 1.8 collective-permute-start.53
  234.5 1.4 collective-permute-start.54
  236.2 3.1 %unit_grads.1 = (f32[768,768]{1,0:T(8,128)}, f32[768,768]{1,0:T(8,128)}) custom-call(s32[3]{0:T(128)S(1)} %pad_add_fusion.here_ref, bf16[1,384,768]{2,1,0:T(8,128)(2,1)S(1)} %bitcast.160, bf16[1,384,768]{2,1,0:T(8,128)(2,1)S(1)} %bitcast.158, bf16[1,384,768]{2,1,0:T(8,128)(2,1)S(1)} %collective-permute-done.56.in_other, ...), custom_call_target="tpu_custom_call" | custom-call | tf_op jit(solution)/shard_map/unit_grads/pallas_call | solution.py:424
  239.4 3.7 %collective-permute-done.54 = bf16[96,768]{1,0:T(8,128)(2,1)S(1)} collective-permute-done((bf16[96,768]{1,0:T(8,128)(2,1)S(1)}, bf16[96,768]{1,0:T(8,128)(2,1)S(1)}, u32[]{:S(2)}, u32[]{:S(2)}) %collective-permute-start.54) | collective-permute-done | bytes 147488 | tf_op jit(solution)/shard_map/ppermute | solution.py:496
  245.3 2.2 head_grads.1
  (268 shorter events, 41.7 us)
Async XLA Ops:
  1.8 11.9 %collective-permute-start = (bf16[96,768]{1,0:T(8,128)(2,1)S(1)}, bf16[96,768]{1,0:T(8,128)(2,1)S(1)}, u32[]{:S(2)}, u32[]{:S(2)}) collective-permute-start(bf16[96,768]{1,0:T(8,128)(2,1)S(1)} %pad_maximum_fusion.20), channel_id=1, source_target_pairs={{0,1},{1,0},{2,3},{3,2},{4,5},{5,4},{6,7},{7,6},{8,9},{9,8},{10,11... | collective-permute-start | bytes 442376 | tf_op jit(solution)/shard_map/ppermute | solution.py:496
  4.9 14.1 %collective-permute-start.1 = (bf16[96,768]{1,0:T(8,128)(2,1)S(1)}, bf16[96,768]{1,0:T(8,128)(2,1)}, u32[]{:S(2)}, u32[]{:S(2)}) collective-permute-start(bf16[96,768]{1,0:T(8,128)(2,1)S(1)} %pad_maximum_fusion.20), channel_id=1, source_target_pairs={{0,2},{1,3},{2,0},{3,1},{4,6},{5,7},{6,4},{7,5},{8,10},{9,11},{10,... | collective-permute-start | bytes 442376 | tf_op jit(solution)/shard_map/ppermute | solution.py:496
  7.5 11.5 %collective-permute-start.2 = (bf16[96,768]{1,0:T(8,128)(2,1)S(1)}, bf16[96,768]{1,0:T(8,128)(2,1)}, u32[]{:S(2)}, u32[]{:S(2)}) collective-permute-start(bf16[96,768]{1,0:T(8,128)(2,1)S(1)} %pad_maximum_fusion.20), channel_id=1, source_target_pairs={{0,3},{1,2},{2,1},{3,0},{4,7},{5,6},{6,5},{7,4},{8,11},{9,10},{10,... | collective-permute-start | bytes 442376 | tf_op jit(solution)/shard_map/ppermute | solution.py:496
  20.1 14.3 %collective-permute-start.5 = (bf16[3,1,1,48,768]{4,3,0,2,1:T(8,128)(2,1)S(1)}, bf16[3,1,1,48,768]{4,3,0,2,1:T(8,128)(2,1)S(1)}, u32[]{:S(2)}, u32[]{:S(2)}) collective-permute-start(bf16[3,1,1,48,768]{4,3,0,2,1:T(8,128)(2,1)S(1)} %maximum_bitcast_fusion.3), channel_id=1, source_target_pairs={{0,16},{4,20},{8,24},{12,28},{16,0},{20,4},{24,8},{28,12},{1,17},{... | collective-permute-start | bytes 663560 | tf_op jit(solution)/shard_map/ppermute | solution.py:496
  21.7 15.9 %collective-permute-start.3 = (bf16[200,768]{1,0:T(8,128)(2,1)S(1)}, bf16[200,768]{1,0:T(8,128)(2,1)S(1)}, u32[]{:S(2)}, u32[]{:S(2)}) collective-permute-start(bf16[200,768]{1,0:T(8,128)(2,1)S(1)} %concatenate.65), channel_id=1, source_target_pairs={{0,2},{1,3},{2,0},{3,1},{4,6},{5,7},{6,4},{7,5},{8,10},{9,11},{10,... | collective-permute-start | bytes 921608 | tf_op jit(solution)/shard_map/ppermute | solution.py:496
  25.0 9.4 %collective-permute-start.4 = (bf16[3,1,1,48,768]{4,3,0,2,1:T(8,128)(2,1)S(1)}, bf16[3,1,1,48,768]{4,3,0,2,1:T(8,128)(2,1)S(1)}, u32[]{:S(2)}, u32[]{:S(2)}) collective-permute-start(bf16[3,1,1,48,768]{4,3,0,2,1:T(8,128)(2,1)S(1)} %maximum_bitcast_fusion.2), channel_id=1, source_target_pairs={{0,8},{4,12},{8,0},{12,4},{16,24},{20,28},{24,16},{28,20},{1,9},{5... | collective-permute-start | bytes 663560 | tf_op jit(solution)/shard_map/ppermute | solution.py:496
  26.5 7.8 %collective-permute-start.6 = (bf16[3,40,768]{2,1,0:T(8,128)(2,1)}, bf16[3,40,768]{2,1,0:T(8,128)(2,1)S(1)}, u32[]{:S(2)}, u32[]{:S(2)}) collective-permute-start(bf16[3,40,768]{2,1,0:T(8,128)(2,1)} %get-tuple-element.186), channel_id=1, source_target_pairs={{0,1},{1,0},{2,3},{3,2},{4,5},{5,4},{6,7},{7,6},{8,9},{9,8},{10,11... | collective-permute-start | bytes 552968 | tf_op jit(solution)/shard_map/ppermute | solution.py:496
  37.6 18.8 %collective-permute-start.9 = (bf16[2,200,768]{2,1,0:T(8,128)(2,1)S(1)}, bf16[2,200,768]{2,1,0:T(8,128)(2,1)S(1)}, u32[]{:S(2)}, u32[]{:S(2)}) collective-permute-start(bf16[2,200,768]{2,1,0:T(8,128)(2,1)S(1)} %pad_maximum_fusion.7), channel_id=1, source_target_pairs={{0,1},{1,0},{2,3},{3,2},{4,5},{5,4},{6,7},{7,6},{8,9},{9,8},{10,11... | collective-permute-start | bytes 1843208 | tf_op jit(solution)/shard_map/ppermute | solution.py:496
  37.8 17.7 %collective-permute-start.8 = (bf16[3,2,1,48,768]{4,3,0,2,1:T(8,128)(2,1)S(1)}, bf16[3,2,1,48,768]{4,3,0,2,1:T(8,128)(2,1)S(1)}, u32[]{:S(2)}, u32[]{:S(2)}) collective-permute-start(bf16[3,2,1,48,768]{4,3,0,2,1:T(8,128)(2,1)S(1)} %pad_maximum_fusion.15), channel_id=1, source_target_pairs={{0,8},{4,12},{8,0},{12,4},{16,24},{20,28},{24,16},{28,20},{1,9},{5... | collective-permute-start | bytes 1327112 | tf_op jit(solution)/shard_map/ppermute | solution.py:496
  39.5 16.1 %collective-permute-start.7 = (bf16[3,1,2,48,768]{4,3,0,2,1:T(8,128)(2,1)S(1)}, bf16[3,1,2,48,768]{4,3,0,2,1:T(8,128)(2,1)S(1)}, u32[]{:S(2)}, u32[]{:S(2)}) collective-permute-start(bf16[3,1,2,48,768]{4,3,0,2,1:T(8,128)(2,1)S(1)} %pad_maximum_fusion.14), channel_id=1, source_target_pairs={{0,16},{4,20},{8,24},{12,28},{16,0},{20,4},{24,8},{28,12},{1,17},{... | collective-permute-start | bytes 1327112 | tf_op jit(solution)/shard_map/ppermute | solution.py:496
  40.2 15.4 %collective-permute-start.10 = (bf16[3,40,768]{2,1,0:T(8,128)(2,1)S(1)}, bf16[3,40,768]{2,1,0:T(8,128)(2,1)S(1)}, u32[]{:S(2)}, u32[]{:S(2)}) collective-permute-start(bf16[3,40,768]{2,1,0:T(8,128)(2,1)S(1)} %copy-done.29), channel_id=1, source_target_pairs={{0,3},{1,2},{2,1},{3,0},{4,7},{5,6},{6,5},{7,4},{8,11},{9,10},{10,... | collective-permute-start | bytes 552968 | tf_op jit(solution)/shard_map/ppermute | solution.py:496
  56.7 14.2 %collective-permute-start.14 = (bf16[3,192,768]{2,1,0:T(8,128)(2,1)S(1)}, bf16[3,192,768]{2,1,0:T(8,128)(2,1)S(1)}, u32[]{:S(2)}, u32[]{:S(2)}) collective-permute-start(bf16[3,192,768]{2,1,0:T(8,128)(2,1)S(1)} %bitcast.145), channel_id=1, source_target_pairs={{0,4},{4,0},{8,12},{12,8},{16,20},{20,16},{24,28},{28,24},{1,5},{5... | collective-permute-start | bytes 2654216 | tf_op jit(solution)/shard_map/ppermute | solution.py:496
  57.1 13.9 %collective-permute-start.13 = (bf16[3,192,768]{2,1,0:T(8,128)(2,1)S(1)}, bf16[3,192,768]{2,1,0:T(8,128)(2,1)S(1)}, u32[]{:S(2)}, u32[]{:S(2)}) collective-permute-start(bf16[3,192,768]{2,1,0:T(8,128)(2,1)S(1)} %bitcast.148), channel_id=1, source_target_pairs={{0,4},{4,0},{8,12},{12,8},{16,20},{20,16},{24,28},{28,24},{1,5},{5... | collective-permute-start | bytes 2654216 | tf_op jit(solution)/shard_map/ppermute | solution.py:496
  57.7 13.2 %collective-permute-start.12 = (bf16[3,1,1,96,768]{4,3,0,2,1:T(8,128)(2,1)S(1)}, bf16[3,1,1,96,768]{4,3,0,2,1:T(8,128)(2,1)S(1)}, u32[]{:S(2)}, u32[]{:S(2)}) collective-permute-start(bf16[3,1,1,96,768]{4,3,0,2,1:T(8,128)(2,1)S(1)} %maximum_bitcast_fusion.1), channel_id=1, source_target_pairs={{0,16},{4,20},{8,24},{12,28},{16,0},{20,4},{24,8},{28,12},{1,17},{... | collective-permute-start | bytes 1327112 | tf_op jit(solution)/shard_map/ppermute | solution.py:496
  58.4 12.6 %collective-permute-start.11 = (bf16[3,1,1,96,768]{4,3,0,2,1:T(8,128)(2,1)S(1)}, bf16[3,1,1,96,768]{4,3,0,2,1:T(8,128)(2,1)S(1)}, u32[]{:S(2)}, u32[]{:S(2)}) collective-permute-start(bf16[3,1,1,96,768]{4,3,0,2,1:T(8,128)(2,1)S(1)} %maximum_bitcast_fusion), channel_id=1, source_target_pairs={{0,8},{4,12},{8,0},{12,4},{16,24},{20,28},{24,16},{28,20},{1,9},{5... | collective-permute-start | bytes 1327112 | tf_op jit(solution)/shard_map/ppermute | solution.py:496
  60.6 10.3 %collective-permute-start.15 = (bf16[3,40,768]{2,1,0:T(8,128)(2,1)S(1)}, bf16[3,40,768]{2,1,0:T(8,128)(2,1)S(1)}, u32[]{:S(2)}, u32[]{:S(2)}) collective-permute-start(bf16[3,40,768]{2,1,0:T(8,128)(2,1)S(1)} %copy-done.28), channel_id=1, source_target_pairs={{0,2},{1,3},{2,0},{3,1},{4,6},{5,7},{6,4},{7,5},{8,10},{9,11},{10,... | collective-permute-start | bytes 552968 | tf_op jit(solution)/shard_map/ppermute | solution.py:496
  71.2 21.6 %collective-permute-start.17 = (bf16[3,2,1,96,768]{4,3,0,2,1:T(8,128)(2,1)S(1)}, bf16[3,2,1,96,768]{4,3,0,2,1:T(8,128)(2,1)S(1)}, u32[]{:S(2)}, u32[]{:S(2)}) collective-permute-start(bf16[3,2,1,96,768]{4,3,0,2,1:T(8,128)(2,1)S(1)} %pad_maximum_fusion.5), channel_id=1, source_target_pairs={{0,8},{4,12},{8,0},{12,4},{16,24},{20,28},{24,16},{28,20},{1,9},{5... | collective-permute-start | bytes 2654216 | tf_op jit(solution)/shard_map/ppermute | solution.py:496
  72.2 21.1 %collective-permute-start.16 = (bf16[3,1,2,96,768]{4,3,0,2,1:T(8,128)(2,1)S(1)}, bf16[3,1,2,96,768]{4,3,0,2,1:T(8,128)(2,1)S(1)}, u32[]{:S(2)}, u32[]{:S(2)}) collective-permute-start(bf16[3,1,2,96,768]{4,3,0,2,1:T(8,128)(2,1)S(1)} %pad_maximum_fusion.4), channel_id=1, source_target_pairs={{0,16},{4,20},{8,24},{12,28},{16,0},{20,4},{24,8},{28,12},{1,17},{... | collective-permute-start | bytes 2654216 | tf_op jit(solution)/shard_map/ppermute | solution.py:496
  73.8 16.5 %collective-permute-start.18 = (bf16[3,40,768]{2,1,0:T(8,128)(2,1)S(1)}, bf16[3,40,768]{2,1,0:T(8,128)(2,1)S(1)}, u32[]{:S(2)}, u32[]{:S(2)}) collective-permute-start(bf16[3,40,768]{2,1,0:T(8,128)(2,1)S(1)} %get-tuple-element.216), channel_id=1, source_target_pairs={{0,1},{1,0},{2,3},{3,2},{4,5},{5,4},{6,7},{7,6},{8,9},{9,8},{10,11... | collective-permute-start | bytes 552968 | tf_op jit(solution)/shard_map/ppermute | solution.py:496
  73.8 16.5 %collective-permute-start.19 = (bf16[3,40,768]{2,1,0:T(8,128)(2,1)S(1)}, bf16[3,40,768]{2,1,0:T(8,128)(2,1)S(1)}, u32[]{:S(2)}, u32[]{:S(2)}) collective-permute-start(bf16[3,40,768]{2,1,0:T(8,128)(2,1)S(1)} %get-tuple-element.217), channel_id=1, source_target_pairs={{0,2},{1,3},{2,0},{3,1},{4,6},{5,7},{6,4},{7,5},{8,10},{9,11},{10,... | collective-permute-start | bytes 552968 | tf_op jit(solution)/shard_map/ppermute | solution.py:496
  76.4 13.9 %collective-permute-start.20 = (bf16[3,40,768]{2,1,0:T(8,128)(2,1)S(1)}, bf16[3,40,768]{2,1,0:T(8,128)(2,1)S(1)}, u32[]{:S(2)}, u32[]{:S(2)}) collective-permute-start(bf16[3,40,768]{2,1,0:T(8,128)(2,1)S(1)} %get-tuple-element.218), channel_id=1, source_target_pairs={{0,3},{1,2},{2,1},{3,0},{4,7},{5,6},{6,5},{7,4},{8,11},{9,10},{10,... | collective-permute-start | bytes 552968 | tf_op jit(solution)/shard_map/ppermute | solution.py:496
  120.0 10.2 %collective-permute-start.23 = (bf16[4,384,768]{2,1,0:T(8,128)(2,1)}, bf16[4,384,768]{2,1,0:T(8,128)(2,1)S(1)}, u32[]{:S(2)}, u32[]{:S(2)}) collective-permute-start(bf16[4,384,768]{2,1,0:T(8,128)(2,1)} %get-tuple-element.231), channel_id=1, source_target_pairs={{0,4},{4,0},{8,12},{12,8},{16,20},{20,16},{24,28},{28,24},{1,5},{5... | collective-permute-start | bytes 7077896 | tf_op jit(solution)/shard_map/ppermute | solution.py:496
  120.2 9.9 %collective-permute-start.24 = (bf16[4,384,768]{2,1,0:T(8,128)(2,1)}, bf16[4,384,768]{2,1,0:T(8,128)(2,1)S(1)}, u32[]{:S(2)}, u32[]{:S(2)}) collective-permute-start(bf16[4,384,768]{2,1,0:T(8,128)(2,1)} %get-tuple-element.232), channel_id=1, source_target_pairs={{0,4},{4,0},{8,12},{12,8},{16,20},{20,16},{24,28},{28,24},{1,5},{5... | collective-permute-start | bytes 7077896 | tf_op jit(solution)/shard_map/ppermute | solution.py:496
  132.1 28.2 %collective-permute-start.25 = (bf16[4,2,96,768]{3,2,1,0:T(8,128)(2,1)}, bf16[4,2,96,768]{3,2,1,0:T(8,128)(2,1)S(1)}, u32[]{:S(2)}, u32[]{:S(2)}) collective-permute-start(bf16[4,2,96,768]{3,2,1,0:T(8,128)(2,1)} %get-tuple-element.262), channel_id=1, source_target_pairs={{0,8},{4,12},{8,0},{12,4},{16,24},{20,28},{24,16},{28,20},{1,9},{5... | collective-permute-start | bytes 3538952 | tf_op jit(solution)/shard_map/ppermute | solution.py:496
  133.6 27.7 %collective-permute-start.26 = (bf16[4,2,96,768]{3,2,1,0:T(8,128)(2,1)S(1)}, bf16[4,2,96,768]{3,2,1,0:T(8,128)(2,1)S(1)}, u32[]{:S(2)}, u32[]{:S(2)}) collective-permute-start(bf16[4,2,96,768]{3,2,1,0:T(8,128)(2,1)S(1)} %get-tuple-element.263), channel_id=1, source_target_pairs={{0,16},{4,20},{8,24},{12,28},{16,0},{20,4},{24,8},{28,12},{1,17},{... | collective-permute-start | bytes 3538952 | tf_op jit(solution)/shard_map/ppermute | solution.py:496
  135.1 23.6 %collective-permute-start.27 = (bf16[3,40,768]{2,1,0:T(8,128)(2,1)S(1)}, bf16[3,40,768]{2,1,0:T(8,128)(2,1)S(1)}, u32[]{:S(2)}, u32[]{:S(2)}) collective-permute-start(bf16[3,40,768]{2,1,0:T(8,128)(2,1)S(1)} %copy-done.42), channel_id=1, source_target_pairs={{0,1},{1,0},{2,3},{3,2},{4,5},{5,4},{6,7},{7,6},{8,9},{9,8},{10,11... | collective-permute-start | bytes 552968 | tf_op jit(solution)/shard_map/ppermute | solution.py:496
  135.2 23.6 %collective-permute-start.28 = (bf16[3,40,768]{2,1,0:T(8,128)(2,1)S(1)}, bf16[3,40,768]{2,1,0:T(8,128)(2,1)S(1)}, u32[]{:S(2)}, u32[]{:S(2)}) collective-permute-start(bf16[3,40,768]{2,1,0:T(8,128)(2,1)S(1)} %copy-done.41), channel_id=1, source_target_pairs={{0,2},{1,3},{2,0},{3,1},{4,6},{5,7},{6,4},{7,5},{8,10},{9,11},{10,... | collective-permute-start | bytes 552968 | tf_op jit(solution)/shard_map/ppermute | solution.py:496
  137.4 21.4 %collective-permute-start.29 = (bf16[3,40,768]{2,1,0:T(8,128)(2,1)S(1)}, bf16[3,40,768]{2,1,0:T(8,128)(2,1)S(1)}, u32[]{:S(2)}, u32[]{:S(2)}) collective-permute-start(bf16[3,40,768]{2,1,0:T(8,128)(2,1)S(1)} %copy-done.40), channel_id=1, source_target_pairs={{0,3},{1,2},{2,1},{3,0},{4,7},{5,6},{6,5},{7,4},{8,11},{9,10},{10,... | collective-permute-start | bytes 552968 | tf_op jit(solution)/shard_map/ppermute | solution.py:496
  161.4 17.5 %collective-permute-start.32 = (bf16[2,4,192,768]{3,2,1,0:T(8,128)(2,1)}, bf16[2,4,192,768]{3,2,1,0:T(8,128)(2,1)S(1)}, u32[]{:S(2)}, u32[]{:S(2)}) collective-permute-start(bf16[2,4,192,768]{3,2,1,0:T(8,128)(2,1)} %get-tuple-element.278), channel_id=1, source_target_pairs={{0,4},{4,0},{8,12},{12,8},{16,20},{20,16},{24,28},{28,24},{1,5},{5... | collective-permute-start | bytes 7077896 | tf_op jit(solution)/shard_map/ppermute | solution.py:496
  161.8 15.8 %collective-permute-start.30 = (bf16[4,1,96,768]{3,2,1,0:T(8,128)(2,1)S(1)}, bf16[4,1,96,768]{3,2,1,0:T(8,128)(2,1)S(1)}, u32[]{:S(2)}, u32[]{:S(2)}) collective-permute-start(bf16[4,1,96,768]{3,2,1,0:T(8,128)(2,1)S(1)} %get-tuple-element.276), channel_id=1, source_target_pairs={{0,16},{4,20},{8,24},{12,28},{16,0},{20,4},{24,8},{28,12},{1,17},{... | collective-permute-start | bytes 1769480 | tf_op jit(solution)/shard_map/ppermute | solution.py:496
  163.4 15.5 %collective-permute-start.31 = (bf16[4,1,96,768]{3,2,1,0:T(8,128)(2,1)S(1)}, bf16[4,1,96,768]{3,2,1,0:T(8,128)(2,1)S(1)}, u32[]{:S(2)}, u32[]{:S(2)}) collective-permute-start(bf16[4,1,96,768]{3,2,1,0:T(8,128)(2,1)S(1)} %get-tuple-element.277), channel_id=1, source_target_pairs={{0,8},{4,12},{8,0},{12,4},{16,24},{20,28},{24,16},{28,20},{1,9},{5... | collective-permute-start | bytes 1769480 | tf_op jit(solution)/shard_map/ppermute | solution.py:496
  163.9 10.9 %collective-permute-start.33 = (bf16[3,40,768]{2,1,0:T(8,128)(2,1)S(1)}, bf16[3,40,768]{2,1,0:T(8,128)(2,1)S(1)}, u32[]{:S(2)}, u32[]{:S(2)}) collective-permute-start(bf16[3,40,768]{2,1,0:T(8,128)(2,1)S(1)} %copy-done.43), channel_id=1, source_target_pairs={{0,3},{1,2},{2,1},{3,0},{4,7},{5,6},{6,5},{7,4},{8,11},{9,10},{10,... | collective-permute-start | bytes 552968 | tf_op jit(solution)/shard_map/ppermute | solution.py:496
  165.7 9.2 %collective-permute-start.34 = (f32[16,768]{1,0:T(8,128)S(1)}, f32[16,768]{1,0:T(8,128)S(1)}, u32[]{:S(2)}, u32[]{:S(2)}) collective-permute-start(f32[16,768]{1,0:T(8,128)S(1)} %get-tuple-element.280), channel_id=1, source_target_pairs={{0,2},{1,3},{2,0},{3,1},{4,6},{5,7},{6,4},{7,5},{8,10},{9,11},{10,... | collective-permute-start | bytes 147464 | tf_op jit(solution)/shard_map/ppermute | solution.py:496
  179.8 18.7 %collective-permute-start.37 = (bf16[2,192,768]{2,1,0:T(8,128)(2,1)S(1)}, bf16[2,192,768]{2,1,0:T(8,128)(2,1)S(1)}, u32[]{:S(2)}, u32[]{:S(2)}) collective-permute-start(bf16[2,192,768]{2,1,0:T(8,128)(2,1)S(1)} %pad_maximum_fusion.9), channel_id=1, source_target_pairs={{0,1},{1,0},{2,3},{3,2},{4,5},{5,4},{6,7},{7,6},{8,9},{9,8},{10,11... | collective-permute-start | bytes 1769480 | tf_op jit(solution)/shard_map/ppermute | solution.py:496
  182.3 16.1 %collective-permute-start.35 = (bf16[4,2,48,768]{3,2,1,0:T(8,128)(2,1)S(1)}, bf16[4,2,48,768]{3,2,1,0:T(8,128)(2,1)S(1)}, u32[]{:S(2)}, u32[]{:S(2)}) collective-permute-start(bf16[4,2,48,768]{3,2,1,0:T(8,128)(2,1)S(1)} %get-tuple-element.286), channel_id=1, source_target_pairs={{0,8},{4,12},{8,0},{12,4},{16,24},{20,28},{24,16},{28,20},{1,9},{5... | collective-permute-start | bytes 1769480 | tf_op jit(solution)/shard_map/ppermute | solution.py:496
  182.9 15.5 %collective-permute-start.36 = (bf16[4,2,48,768]{3,2,1,0:T(8,128)(2,1)S(1)}, bf16[4,2,48,768]{3,2,1,0:T(8,128)(2,1)S(1)}, u32[]{:S(2)}, u32[]{:S(2)}) collective-permute-start(bf16[4,2,48,768]{3,2,1,0:T(8,128)(2,1)S(1)} %get-tuple-element.287), channel_id=1, source_target_pairs={{0,16},{4,20},{8,24},{12,28},{16,0},{20,4},{24,8},{28,12},{1,17},{... | collective-permute-start | bytes 1769480 | tf_op jit(solution)/shard_map/ppermute | solution.py:496
  183.4 14.7 %collective-permute-start.39 = (bf16[3,40,768]{2,1,0:T(8,128)(2,1)S(1)}, bf16[3,40,768]{2,1,0:T(8,128)(2,1)S(1)}, u32[]{:S(2)}, u32[]{:S(2)}) collective-permute-start(bf16[3,40,768]{2,1,0:T(8,128)(2,1)S(1)} %copy-done.39), channel_id=1, source_target_pairs={{0,2},{1,3},{2,0},{3,1},{4,6},{5,7},{6,4},{7,5},{8,10},{9,11},{10,... | collective-permute-start | bytes 552968 | tf_op jit(solution)/shard_map/ppermute | solution.py:496
  184.4 13.7 %collective-permute-start.38 = (f32[16,768]{1,0:T(8,128)S(1)}, f32[16,768]{1,0:T(8,128)S(1)}, u32[]{:S(2)}, u32[]{:S(2)}) collective-permute-start(f32[16,768]{1,0:T(8,128)S(1)} %add.145), channel_id=1, source_target_pairs={{0,8},{4,12},{8,0},{12,4},{16,24},{20,28},{24,16},{28,20},{1,9},{5... | collective-permute-start | bytes 147464 | tf_op jit(solution)/shard_map/ppermute | solution.py:496
  198.5 14.7 %collective-permute-start.42 = (bf16[192,768]{1,0:T(8,128)(2,1)S(1)}, bf16[192,768]{1,0:T(8,128)(2,1)S(1)}, u32[]{:S(2)}, u32[]{:S(2)}) collective-permute-start(bf16[192,768]{1,0:T(8,128)(2,1)S(1)} %fusion.1), channel_id=1, source_target_pairs={{0,2},{1,3},{2,0},{3,1},{4,6},{5,7},{6,4},{7,5},{8,10},{9,11},{10,... | collective-permute-start | bytes 884744 | tf_op jit(solution)/shard_map/ppermute | solution.py:496
  200.0 13.2 %collective-permute-start.40 = (bf16[4,1,48,768]{3,2,1,0:T(8,128)(2,1)S(1)}, bf16[4,1,48,768]{3,2,1,0:T(8,128)(2,1)S(1)}, u32[]{:S(2)}, u32[]{:S(2)}) collective-permute-start(bf16[4,1,48,768]{3,2,1,0:T(8,128)(2,1)S(1)} %get-tuple-element.307), channel_id=1, source_target_pairs={{0,16},{4,20},{8,24},{12,28},{16,0},{20,4},{24,8},{28,12},{1,17},{... | collective-permute-start | bytes 884744 | tf_op jit(solution)/shard_map/ppermute | solution.py:496
  200.7 12.6 %collective-permute-start.41 = (bf16[4,1,48,768]{3,2,1,0:T(8,128)(2,1)S(1)}, bf16[4,1,48,768]{3,2,1,0:T(8,128)(2,1)S(1)}, u32[]{:S(2)}, u32[]{:S(2)}) collective-permute-start(bf16[4,1,48,768]{3,2,1,0:T(8,128)(2,1)S(1)} %get-tuple-element.308), channel_id=1, source_target_pairs={{0,8},{4,12},{8,0},{12,4},{16,24},{20,28},{24,16},{28,20},{1,9},{5... | collective-permute-start | bytes 884744 | tf_op jit(solution)/shard_map/ppermute | solution.py:496
  201.2 7.8 %collective-permute-start.43 = (bf16[3,40,768]{2,1,0:T(8,128)(2,1)S(1)}, bf16[3,40,768]{2,1,0:T(8,128)(2,1)S(1)}, u32[]{:S(2)}, u32[]{:S(2)}) collective-permute-start(bf16[3,40,768]{2,1,0:T(8,128)(2,1)S(1)} %copy-done.38), channel_id=1, source_target_pairs={{0,1},{1,0},{2,3},{3,2},{4,5},{5,4},{6,7},{7,6},{8,9},{9,8},{10,11... | collective-permute-start | bytes 552968 | tf_op jit(solution)/shard_map/ppermute | solution.py:496
  213.8 8.6 %collective-permute-start.47 = (bf16[2,96,768]{2,1,0:T(8,128)(2,1)S(1)}, bf16[2,96,768]{2,1,0:T(8,128)(2,1)S(1)}, u32[]{:S(2)}, u32[]{:S(2)}) collective-permute-start(bf16[2,96,768]{2,1,0:T(8,128)(2,1)S(1)} %pad_maximum_fusion.16), channel_id=1, source_target_pairs={{0,1},{1,0},{2,3},{3,2},{4,5},{5,4},{6,7},{7,6},{8,9},{9,8},{10,11... | collective-permute-start | bytes 884744 | tf_op jit(solution)/shard_map/ppermute | solution.py:496
  222.5 9.2 %collective-permute-start.50 = (bf16[1,2,1,96,768]{4,3,2,1,0:T(8,128)(2,1)S(1)}, bf16[1,2,1,96,768]{4,3,2,1,0:T(8,128)(2,1)S(1)}, u32[]{:S(2)}, u32[]{:S(2)}) collective-permute-start(bf16[1,2,1,96,768]{4,3,2,1,0:T(8,128)(2,1)S(1)} %pad_maximum_fusion.19), channel_id=1, source_target_pairs={{0,8},{4,12},{8,0},{12,4},{16,24},{20,28},{24,16},{28,20},{1,9},{5... | collective-permute-start | bytes 884744 | tf_op jit(solution)/shard_map/ppermute | solution.py:496
  223.2 8.5 %collective-permute-start.49 = (bf16[1,1,2,96,768]{4,3,2,1,0:T(8,128)(2,1)S(1)}, bf16[1,1,2,96,768]{4,3,2,1,0:T(8,128)(2,1)S(1)}, u32[]{:S(2)}, u32[]{:S(2)}) collective-permute-start(bf16[1,1,2,96,768]{4,3,2,1,0:T(8,128)(2,1)S(1)} %pad_maximum_fusion.18), channel_id=1, source_target_pairs={{0,16},{4,20},{8,24},{12,28},{16,0},{20,4},{24,8},{28,12},{1,17},{... | collective-permute-start | bytes 884744 | tf_op jit(solution)/shard_map/ppermute | solution.py:496
  224.0 7.7 %collective-permute-start.51 = (bf16[96,768]{1,0:T(8,128)(2,1)S(1)}, bf16[96,768]{1,0:T(8,128)(2,1)S(1)}, u32[]{:S(2)}, u32[]{:S(2)}) collective-permute-start(bf16[96,768]{1,0:T(8,128)(2,1)S(1)} %fusion.3), channel_id=1, source_target_pairs={{0,2},{1,3},{2,0},{3,1},{4,6},{5,7},{6,4},{7,5},{8,10},{9,11},{10,... | collective-permute-start | bytes 442376 | tf_op jit(solution)/shard_map/ppermute | solution.py:496
  234.5 8.7 %collective-permute-start.54 = (bf16[96,768]{1,0:T(8,128)(2,1)S(1)}, bf16[96,768]{1,0:T(8,128)(2,1)S(1)}, u32[]{:S(2)}, u32[]{:S(2)}) collective-permute-start(bf16[96,768]{1,0:T(8,128)(2,1)S(1)} %fusion.2), channel_id=1, source_target_pairs={{0,16},{4,20},{8,24},{12,28},{16,0},{20,4},{24,8},{28,12},{1,17},{... | collective-permute-start | bytes 442376 | tf_op jit(solution)/shard_map/ppermute | solution.py:496
  235.9 7.2 %collective-permute-start.55 = (bf16[96,768]{1,0:T(8,128)(2,1)S(1)}, bf16[96,768]{1,0:T(8,128)(2,1)S(1)}, u32[]{:S(2)}, u32[]{:S(2)}) collective-permute-start(bf16[96,768]{1,0:T(8,128)(2,1)S(1)} %fusion.2), channel_id=1, source_target_pairs={{0,24},{4,28},{8,16},{12,20},{16,8},{20,12},{24,0},{28,4},{1,25},{... | collective-permute-start | bytes 442376 | tf_op jit(solution)/shard_map/ppermute | solution.py:496
  (55 other events, 446.3 us)
